TPU v7x, 32 devices: a whole 2x2x4 slice. The times are simulated.
32 devices in a mesh: fsdp: 8 (over y, x, core), replica: 4 (over z).
Axes of the slice: x: 2, y: 2, z: 4, core: 2. Of those that a mesh axis runs over, the one named last changes fastest.
Arguments:
- tokens: bfloat16 [8192, 1152], P(('fsdp', 'replica')), may hold values from -6 to 6
- cond: bfloat16 [16, 1152], replicated, may hold values from -6 to 6
- latent_len: int32 [16], replicated, may hold values from 1 to 1024, 8192 in all
- first_ada_weight: bfloat16 [1152, 6912], P('fsdp'), may hold values from -0.1875 to 0.1875
- first_ada_bias: bfloat16 [6912], P('fsdp'), may hold values from -6 to 6
- first_qkv_weight: bfloat16 [1152, 3456], P('fsdp'), may hold values from -0.1875 to 0.1875
- first_qkv_bias: bfloat16 [2304], P('fsdp'), may hold values from -3.5 to 3.5
- first_out_weight: bfloat16 [1152, 1152], P('fsdp'), may hold values from -1.5 to 1.5
- first_out_bias: bfloat16 [1152], P('fsdp'), may hold values from -6 to 6
- first_up_weight: bfloat16 [1152, 4608], P('fsdp'), may hold values from -0.1875 to 0.1875
- first_up_bias: bfloat16 [4608], P('fsdp'), may hold values from -6 to 6
- first_down_weight: bfloat16 [4608, 1152], P('fsdp'), may hold values from -0.09375 to 0.09375
- first_down_bias: bfloat16 [1152], P('fsdp'), may hold values from -6 to 6
- second_ada_weight: bfloat16 [1152, 6912], P('fsdp'), may hold values from -0.1875 to 0.1875
- second_ada_bias: bfloat16 [6912], P('fsdp'), may hold values from -6 to 6
- second_qkv_weight: bfloat16 [1152, 3456], P('fsdp'), may hold values from -0.1875 to 0.1875
- second_qkv_bias: bfloat16 [2304], P('fsdp'), may hold values from -3.5 to 3.5
- second_out_weight: bfloat16 [1152, 1152], P('fsdp'), may hold values from -1.5 to 1.5
- second_out_bias: bfloat16 [1152], P('fsdp'), may hold values from -6 to 6
- second_up_weight: bfloat16 [1152, 4608], P('fsdp'), may hold values from -0.1875 to 0.1875
- second_up_bias: bfloat16 [4608], P('fsdp'), may hold values from -6 to 6
- second_down_weight: bfloat16 [4608, 1152], P('fsdp'), may hold values from -0.09375 to 0.09375
- second_down_bias: bfloat16 [1152], P('fsdp'), may hold values from -6 to 6
- cotangent: bfloat16 [8192, 1152], P(('fsdp', 'replica')), may hold values from -6 to 6
Outputs:
- output: bfloat16 [8192, 1152], P(('fsdp', 'replica'))
- token_grad: float32 [8192, 1152], P(('fsdp', 'replica'))
- cond_grad: float32 [16, 1152], P(None, 'fsdp')
- grad_first_ada_weight: float32 [1152, 6912], P('fsdp')
- grad_first_ada_bias: float32 [6912], P('fsdp')
- grad_first_qkv_weight: float32 [1152, 3456], P('fsdp')
- grad_first_qkv_bias: float32 [2304], P('fsdp')
- grad_first_out_weight: float32 [1152, 1152], P('fsdp')
- grad_first_out_bias: float32 [1152], P('fsdp')
- grad_first_up_weight: float32 [1152, 4608], P('fsdp')
- grad_first_up_bias: float32 [4608], P('fsdp')
- grad_first_down_weight: float32 [4608, 1152], P('fsdp')
- grad_first_down_bias: float32 [1152], P('fsdp')
- grad_second_ada_weight: float32 [1152, 6912], P('fsdp')
- grad_second_ada_bias: float32 [6912], P('fsdp')
- grad_second_qkv_weight: float32 [1152, 3456], P('fsdp')
- grad_second_qkv_bias: float32 [2304], P('fsdp')
- grad_second_out_weight: float32 [1152, 1152], P('fsdp')
- grad_second_out_bias: float32 [1152], P('fsdp')
- grad_second_up_weight: float32 [1152, 4608], P('fsdp')
- grad_second_up_bias: float32 [4608], P('fsdp')
- grad_second_down_weight: float32 [4608, 1152], P('fsdp')
- grad_second_down_bias: float32 [1152], P('fsdp')
Inputs may be any that keep to these rules, and one draw needn't show every extreme that they name: `latent_len`: the latents lie end to end and their lengths sum to 8192; the longest holds exactly 1024 tokens.
All inputs are finite; a program needn't handle non-finite values.
Results may differ from a plain program's by a relative error of at most 0.02.
Values may be sent and summed in bfloat16 or wider, within the bound.
A program may use at most 448 MiB of HBM per device.

v0:
```python
import math

import jax
import jax.numpy as jnp
from jax import lax
from jax.sharding import PartitionSpec as P

HEADS = 16
REACH = 4


NORM_EPS = 1e-06
HIGH = lax.Precision.HIGHEST


def shifted(value, axis, steps):
    count = lax.axis_size(axis)
    first, last = (max(0, -steps), min(count, count - steps))
    return lax.ppermute(value, axis, [(source, source + steps) for source in range(first, last)])


def pre_norm(stream, shift, scale):
    centred = stream - jnp.mean(stream, axis=-1, keepdims=True)
    spread = jnp.mean(centred * centred, axis=-1, keepdims=True)
    return centred * lax.rsqrt(spread + NORM_EPS) * (1.0 + scale) + shift


def gelu_tanh(values):
    return jax.nn.gelu(values, approximate=True)


def latent_ids(latent_len, positions, token_total):
    starts = jnp.cumsum(latent_len) - latent_len
    found = jnp.sum((starts[None, :] <= positions[:, None]).astype(jnp.int32), axis=1) - 1
    inside = (positions >= 0) & (positions < token_total)
    return jnp.where(inside, found, -1)


def low_dot(left, right):
    return jnp.dot(left, right, preferred_element_type=jnp.float32)


def shift_list():
    return list(range(REACH, 0, -1)) + [0] + list(range(-1, -REACH - 1, -1))


def neighbour_window(key_value):
    pieces = []
    for shift_by in shift_list():
        if shift_by == 0:
            pieces.append(key_value)
        else:
            pieces.append(shifted(key_value, ("fsdp", "replica"), shift_by))
    return jnp.concatenate(pieces, axis=0)


def return_key_grads(grad_window, tok_rows):
    summed = jnp.zeros((tok_rows, grad_window.shape[1]), jnp.float32)
    for place_at, shift_by in enumerate(shift_list()):
        piece = grad_window[place_at * tok_rows : (place_at + 1) * tok_rows]
        if shift_by == 0:
            summed = summed + piece
        else:
            summed = summed + shifted(piece, ("fsdp", "replica"), -shift_by)
    return summed


def split_heads(matrix):
    return matrix.reshape(matrix.shape[0], HEADS, -1).transpose(1, 0, 2)


def merge_heads(stacked):
    return stacked.transpose(1, 0, 2).reshape(stacked.shape[1], -1)


def head_scores(q_head, k_head, same):
    scale = 1.0 / math.sqrt(q_head.shape[1])
    scores = jnp.einsum("td,wd->tw", q_head, k_head, preferred_element_type=jnp.float32) * scale
    return jnp.where(same, scores, -1e30)


def attend(query, key_value, same):
    width = query.shape[1]

    def one_head(parts):
        q_head, k_head, v_head = parts
        scores = head_scores(q_head, k_head, same)
        top = jnp.max(scores, axis=1, keepdims=True)
        expo = jnp.exp(scores - top)
        denom = jnp.sum(expo, axis=1, keepdims=True)
        probs = (expo / denom).astype(jnp.bfloat16)
        mixed = jnp.einsum("tw,wd->td", probs, v_head, preferred_element_type=jnp.float32)
        return (mixed, (top + jnp.log(denom))[:, 0])

    mixed, log_norm = lax.map(
        one_head,
        (split_heads(query), split_heads(key_value[:, :width]), split_heads(key_value[:, width:])),
    )
    return (merge_heads(mixed), log_norm)


def attend_back(query, key_value, same, log_norm, grad_mixed):
    width = query.shape[1]
    scale = 1.0 / math.sqrt(width // HEADS)

    def one_head(parts):
        q_head, k_head, v_head, norm_head, g_head = parts
        probs = jnp.exp(head_scores(q_head, k_head, same) - norm_head[:, None])
        grad_v = jnp.einsum(
            "tw,td->wd", probs.astype(jnp.bfloat16), g_head, preferred_element_type=jnp.float32
        )
        grad_p = jnp.einsum("td,wd->tw", g_head, v_head, preferred_element_type=jnp.float32)
        row_total = jnp.sum(probs * grad_p, axis=1, keepdims=True)
        grad_s = (probs * (grad_p - row_total)).astype(jnp.bfloat16)
        grad_q = jnp.einsum("tw,wd->td", grad_s, k_head, preferred_element_type=jnp.float32) * scale
        grad_k = jnp.einsum("tw,td->wd", grad_s, q_head, preferred_element_type=jnp.float32) * scale
        return (grad_q, grad_k, grad_v)

    grad_q, grad_k, grad_v = lax.map(
        one_head,
        (
            split_heads(query),
            split_heads(key_value[:, :width]),
            split_heads(key_value[:, width:]),
            log_norm,
            split_heads(grad_mixed),
        ),
    )
    return (
        merge_heads(grad_q),
        jnp.concatenate([merge_heads(grad_k), merge_heads(grad_v)], axis=1),
    )


def layer_forward(stream, mod_tok, full, same):
    qkv_w, qkv_b, out_w, out_b, up_w, up_b, down_w, down_b = full
    width = stream.shape[1]
    shift_one, scale_one, gate_one, shift_two, scale_two, gate_two = jnp.split(mod_tok, 6, axis=1)
    normed = pre_norm(stream, shift_one, scale_one).astype(jnp.bfloat16)
    qkv_bias = qkv_b.astype(jnp.float32)
    bias_full = jnp.concatenate(
        [qkv_bias[:width], jnp.zeros((width,), jnp.float32), qkv_bias[width:]]
    )
    projected = low_dot(normed, qkv_w) + bias_full
    query = projected[:, :width].astype(jnp.bfloat16)
    key_value = neighbour_window(projected[:, width:].astype(jnp.bfloat16))
    mixed, log_norm = attend(query, key_value, same)
    mixed = mixed.astype(jnp.bfloat16)
    branch = low_dot(mixed, out_w) + out_b.astype(jnp.float32)
    middle = stream + gate_one * branch
    normed_two = pre_norm(middle, shift_two, scale_two).astype(jnp.bfloat16)
    hidden = low_dot(normed_two, up_w) + up_b.astype(jnp.float32)
    active = gelu_tanh(hidden).astype(jnp.bfloat16)
    result = low_dot(active, down_w) + down_b.astype(jnp.float32)
    saved = (
        normed,
        query,
        key_value,
        mixed,
        log_norm,
        branch,
        middle,
        normed_two,
        hidden,
        active,
        result,
    )
    return (middle + gate_two * result, saved)


def layer_backward(stream, mod_tok, full, same, pick, grad_next):
    qkv_w, qkv_b, out_w, out_b, up_w, up_b, down_w, down_b = full
    width = stream.shape[1]
    tok_rows = stream.shape[0]
    shift_one, scale_one, gate_one, shift_two, scale_two, gate_two = jnp.split(mod_tok, 6, axis=1)
    _, saved = layer_forward(stream, mod_tok, full, same)
    (
        normed,
        query,
        key_value,
        mixed,
        log_norm,
        branch,
        middle,
        normed_two,
        hidden,
        active,
        result,
    ) = saved
    grad_result = (gate_two * grad_next).astype(jnp.bfloat16)
    grad_gate_two = grad_next * result
    grad_down_w = jnp.einsum("tf,td->fd", active, grad_result, preferred_element_type=jnp.float32)
    grad_down_b = jnp.sum(grad_result.astype(jnp.float32), axis=0)
    grad_active = jnp.einsum("td,fd->tf", grad_result, down_w, preferred_element_type=jnp.float32)
    _, gelu_back = jax.vjp(gelu_tanh, hidden)
    grad_hidden = gelu_back(grad_active)[0].astype(jnp.bfloat16)
    grad_up_w = jnp.einsum("td,tf->df", normed_two, grad_hidden, preferred_element_type=jnp.float32)
    grad_up_b = jnp.sum(grad_hidden.astype(jnp.float32), axis=0)
    grad_normed_two = jnp.einsum("tf,df->td", grad_hidden, up_w, preferred_element_type=jnp.float32)
    _, norm_back_two = jax.vjp(pre_norm, middle, shift_two, scale_two)
    grad_middle_part, grad_shift_two, grad_scale_two = norm_back_two(grad_normed_two)
    grad_middle = grad_next + grad_middle_part
    grad_branch = (gate_one * grad_middle).astype(jnp.bfloat16)
    grad_gate_one = grad_middle * branch
    grad_out_w = jnp.einsum("td,te->de", mixed, grad_branch, preferred_element_type=jnp.float32)
    grad_out_b = jnp.sum(grad_branch.astype(jnp.float32), axis=0)
    grad_mixed = jnp.einsum(
        "te,de->td", grad_branch, out_w, preferred_element_type=jnp.float32
    ).astype(jnp.bfloat16)
    grad_query, grad_window = attend_back(query, key_value, same, log_norm, grad_mixed)
    grad_key_value = return_key_grads(grad_window, tok_rows).astype(jnp.bfloat16)
    grad_query = grad_query.astype(jnp.bfloat16)
    grad_projected = jnp.concatenate([grad_query, grad_key_value], axis=1)
    grad_qkv_w = jnp.einsum("td,te->de", normed, grad_projected, preferred_element_type=jnp.float32)
    grad_qkv_b = jnp.concatenate(
        [
            jnp.sum(grad_query.astype(jnp.float32), axis=0),
            jnp.sum(grad_key_value[:, width:].astype(jnp.float32), axis=0),
        ]
    )
    grad_normed = jnp.einsum("te,de->td", grad_projected, qkv_w, preferred_element_type=jnp.float32)
    _, norm_back_one = jax.vjp(pre_norm, stream, shift_one, scale_one)
    grad_stream_part, grad_shift_one, grad_scale_one = norm_back_one(grad_normed)
    grad_stream = grad_middle + grad_stream_part
    grad_mod_tok = jnp.concatenate(
        [
            grad_shift_one,
            grad_scale_one,
            grad_gate_one,
            grad_shift_two,
            grad_scale_two,
            grad_gate_two,
        ],
        axis=1,
    )
    grad_mod = jnp.einsum(
        "tl,tm->lm", pick, grad_mod_tok, precision=HIGH, preferred_element_type=jnp.float32
    )
    local_grads = (
        grad_qkv_w,
        grad_qkv_b,
        grad_out_w,
        grad_out_b,
        grad_up_w,
        grad_up_b,
        grad_down_w,
        grad_down_b,
    )
    return (grad_stream, grad_mod, local_grads)


def gather_layer(params):
    return (
        lax.all_gather(params[2], "fsdp", axis=0, tiled=True),
        lax.all_gather(params[3], "fsdp", axis=0, tiled=True),
        lax.all_gather(params[4], "fsdp", axis=0, tiled=True),
        lax.all_gather(params[5], "fsdp", axis=0, tiled=True),
        lax.all_gather(params[6], "fsdp", axis=0, tiled=True),
        lax.all_gather(params[7], "fsdp", axis=0, tiled=True),
        lax.all_gather(params[8], "fsdp", axis=0, tiled=True),
        lax.all_gather(params[9], "fsdp", axis=0, tiled=True),
    )


def owner_sums(local_grads):
    return (
        lax.psum_scatter(local_grads[0], "fsdp", scatter_dimension=0, tiled=True),
        lax.psum_scatter(local_grads[1], "fsdp", scatter_dimension=0, tiled=True),
        lax.psum_scatter(local_grads[2], "fsdp", scatter_dimension=0, tiled=True),
        lax.psum_scatter(local_grads[3], "fsdp", scatter_dimension=0, tiled=True),
        lax.psum_scatter(local_grads[4], "fsdp", scatter_dimension=0, tiled=True),
        lax.psum_scatter(local_grads[5], "fsdp", scatter_dimension=0, tiled=True),
        lax.psum_scatter(local_grads[6], "fsdp", scatter_dimension=0, tiled=True),
        lax.psum_scatter(local_grads[7], "fsdp", scatter_dimension=0, tiled=True),
    )


def replica_total(shares):
    return lax.psum(
        (shares[0], shares[1], shares[2], shares[3], shares[4], shares[5], shares[6], shares[7]),
        "replica",
    )


def shards(
    tokens,
    cond,
    latent_len,
    first_ada_weight,
    first_ada_bias,
    first_qkv_weight,
    first_qkv_bias,
    first_out_weight,
    first_out_bias,
    first_up_weight,
    first_up_bias,
    first_down_weight,
    first_down_bias,
    second_ada_weight,
    second_ada_bias,
    second_qkv_weight,
    second_qkv_bias,
    second_out_weight,
    second_out_bias,
    second_up_weight,
    second_up_bias,
    second_down_weight,
    second_down_bias,
    cotangent,
):
    tok_rows = tokens.shape[0]
    group_place = lax.axis_index("fsdp")
    device_at = lax.axis_index(("fsdp", "replica"))
    token_total = tok_rows * lax.axis_size(("fsdp", "replica"))
    latent_count = cond.shape[0]
    local_pos = jnp.arange(tok_rows, dtype=jnp.int32)
    own_ids = latent_ids(latent_len, device_at * tok_rows + local_pos, token_total)
    window_ids = jnp.concatenate(
        [
            latent_ids(latent_len, (device_at - shift_by) * tok_rows + local_pos, token_total)
            for shift_by in shift_list()
        ]
    )
    same = own_ids[:, None] == window_ids[None, :]
    pick = (own_ids[:, None] == jnp.arange(latent_count, dtype=jnp.int32)[None, :]).astype(
        jnp.float32
    )
    layers = (
        (
            first_ada_weight,
            first_ada_bias,
            first_qkv_weight,
            first_qkv_bias,
            first_out_weight,
            first_out_bias,
            first_up_weight,
            first_up_bias,
            first_down_weight,
            first_down_bias,
        ),
        (
            second_ada_weight,
            second_ada_bias,
            second_qkv_weight,
            second_qkv_bias,
            second_out_weight,
            second_out_bias,
            second_up_weight,
            second_up_bias,
            second_down_weight,
            second_down_bias,
        ),
    )
    col_width = first_ada_weight.shape[0]
    own_cond = lax.dynamic_slice_in_dim(
        cond.astype(jnp.float32), group_place * col_width, col_width, 1
    )
    own_silu = jax.nn.silu(own_cond).astype(jnp.bfloat16)
    partial_terms = []
    for params in layers:
        term = low_dot(own_silu, params[0])
        bias_share = params[1].astype(jnp.float32)
        spread = lax.dynamic_update_slice_in_dim(
            jnp.zeros((term.shape[1],), jnp.float32),
            bias_share,
            group_place * bias_share.shape[0],
            0,
        )
        partial_terms.append(term + spread[None, :])
    mod_first, mod_second = lax.psum((partial_terms[0], partial_terms[1]), "fsdp")
    mod_tokens = (
        jnp.dot(pick, mod_first, precision=HIGH, preferred_element_type=jnp.float32),
        jnp.dot(pick, mod_second, precision=HIGH, preferred_element_type=jnp.float32),
    )
    stream = tokens.astype(jnp.float32)
    inputs = []
    kept = []
    for layer_at in range(2):
        full = gather_layer(layers[layer_at])
        kept.append(full)
        inputs.append(stream)
        stream = layer_forward(stream, mod_tokens[layer_at], full, same)[0]
    output = stream.astype(jnp.bfloat16)
    grad_stream = cotangent.astype(jnp.float32)
    weight_grads = [None, None]
    mod_grads = [None, None]
    for layer_at in (1, 0):
        full = gather_layer(layers[layer_at])
        grad_stream, grad_mod, local_grads = layer_backward(
            inputs[layer_at], mod_tokens[layer_at], full, same, pick, grad_stream
        )
        shares = owner_sums(local_grads)
        shares = replica_total(shares)
        weight_grads[layer_at] = shares
        mod_grads[layer_at] = grad_mod
    grad_mod_first, grad_mod_second = lax.psum((mod_grads[0], mod_grads[1]), ("fsdp", "replica"))
    grad_silu = jnp.zeros(own_cond.shape, jnp.float32)
    ada_grads = []
    for params, grad_mod in zip(layers, (grad_mod_first, grad_mod_second)):
        low_mod = grad_mod.astype(jnp.bfloat16)
        weight_grad = jnp.einsum("ld,lm->dm", own_silu, low_mod, preferred_element_type=jnp.float32)
        column_sums = jnp.sum(low_mod.astype(jnp.float32), axis=0)
        bias_rows = params[1].shape[0]
        bias_grad = lax.dynamic_slice_in_dim(column_sums, group_place * bias_rows, bias_rows, 0)
        grad_silu = grad_silu + jnp.einsum(
            "lm,dm->ld", low_mod, params[0], preferred_element_type=jnp.float32
        )
        ada_grads.append((weight_grad, bias_grad))
    _, silu_back = jax.vjp(jax.nn.silu, own_cond)
    cond_grad = silu_back(grad_silu)[0]
    first_grads = weight_grads[0]
    second_grads = weight_grads[1]
    return (
        output,
        grad_stream,
        cond_grad,
        ada_grads[0][0],
        ada_grads[0][1],
        first_grads[0],
        first_grads[1],
        first_grads[2],
        first_grads[3],
        first_grads[4],
        first_grads[5],
        first_grads[6],
        first_grads[7],
        ada_grads[1][0],
        ada_grads[1][1],
        second_grads[0],
        second_grads[1],
        second_grads[2],
        second_grads[3],
        second_grads[4],
        second_grads[5],
        second_grads[6],
        second_grads[7],
    )


def solution(mesh):
    in_specs = (
        P(("fsdp", "replica"), None),
        P(),
        P(),
        P("fsdp", None),
        P("fsdp"),
        P("fsdp", None),
        P("fsdp"),
        P("fsdp", None),
        P("fsdp"),
        P("fsdp", None),
        P("fsdp"),
        P("fsdp", None),
        P("fsdp"),
        P("fsdp", None),
        P("fsdp"),
        P("fsdp", None),
        P("fsdp"),
        P("fsdp", None),
        P("fsdp"),
        P("fsdp", None),
        P("fsdp"),
        P("fsdp", None),
        P("fsdp"),
        P(("fsdp", "replica"), None),
    )
    out_specs = (
        P(("fsdp", "replica"), None),
        P(("fsdp", "replica"), None),
        P(None, "fsdp"),
        P("fsdp", None),
        P("fsdp"),
        P("fsdp", None),
        P("fsdp"),
        P("fsdp", None),
        P("fsdp"),
        P("fsdp", None),
        P("fsdp"),
        P("fsdp", None),
        P("fsdp"),
        P("fsdp", None),
        P("fsdp"),
        P("fsdp", None),
        P("fsdp"),
        P("fsdp", None),
        P("fsdp"),
        P("fsdp", None),
        P("fsdp"),
        P("fsdp", None),
        P("fsdp"),
    )
    return jax.shard_map(shards, mesh=mesh, in_specs=in_specs, out_specs=out_specs, check_vma=False)
```

profile of v0, /device:TPU:0, one launch (start us, length us, event | category | flops | bytes accessed | tf_op | source)
XLA Modules:
  0.0 3481.5 jit_solution(2569165371428138478)
XLA Ops:
  24.4 26.6 all-reduce.21
  51.0 21.7 all-reduce.29.cloned.1.call-done
  80.0 46.4 %all-gather.9.cloned.1.call-done = bf16[1152,3456]{1,0:T(8,128)(2,1)} async-done(((bf16[144,3456]{1,0:T(8,128)(2,1)}), bf16[1152,3456]{1,0:T(8,128)(2,1)}) %all-gather.9.cloned.1.call-update) | async-done | bytes 7962640 | tf_op jit(solution)/shard_map/all_gather | solution.py:254
  173.4 21.6 collective-permute-done.2
  198.6 21.6 collective-permute-done.3
  223.8 34.8 collective-permute-done.4
  259.6 61.7 %collective-permute-done.5 = bf16[256,2304]{1,0:T(8,128)(2,1)S(1)} collective-permute-done((bf16[256,2304]{1,0:T(8,128)(2,1)}, bf16[256,2304]{1,0:T(8,128)(2,1)S(1)}, u32[]{:S(2)}, u32[]{:S(2)}) %collective-permute-start.5) | collective-permute-done | bytes 1179680 | tf_op jit(solution)/shard_map/ppermute | solution.py:19
  373.9 63.6 %while.78 = (s32[]{:T(128)}, bf16[16,256,72]{1,2,0:T(8,128)(2,1)S(1)}, bf16[16,256,72]{2,1,0:T(8,128)(2,1)}, bf16[16,2304,72]{2,1,0:T(8,128)(2,1)}, bf16[16,2304...) while((s32[]{:T(128)}, bf16[16,256,72]{1,2,0:T(8,128)(2,1)S(1)}, ...), condition=%wide.region_16.17_spmd.clone, body=%wide.region_13.16_spmd.clone.sunk | while | flops 175177216 | bytes 8414301 | solution.py:95
  534.3 21.6 collective-permute-done.10
  584.6 34.0 collective-permute-done.12
  619.7 61.2 %collective-permute-done.13 = bf16[256,2304]{1,0:T(8,128)(2,1)S(1)} collective-permute-done((bf16[256,2304]{1,0:T(8,128)(2,1)}, bf16[256,2304]{1,0:T(8,128)(2,1)S(1)}, u32[]{:S(2)}, u32[]{:S(2)}) %collective-permute-start.13) | collective-permute-done | bytes 1179680 | tf_op jit(solution)/shard_map/ppermute | solution.py:19
  734.0 73.6 %while.80 = (s32[]{:T(128)}, bf16[16,256,72]{1,2,0:T(8,128)(2,1)}, f32[16,256]{1,0:T(8,128)S(1)}, bf16[16,256,72]{2,1,0:T(8,128)(2,1)}, bf16[16,2304,72]{2,1,0:T...) while((s32[]{:T(128)}, bf16[16,256,72]{1,2,0:T(8,128)(2,1)}, ...), condition=%wide.region_31.32_spmd.clone, body=%wide.region_28.31_spmd.clone.sunk | while | flops 175177472 | bytes 8419441 | solution.py:95
  868.1 163.4 %while.81 = (s32[]{:T(128)}, bf16[16,256,72]{1,2,0:T(8,128)(2,1)}, f32[16,2304,72]{1,2,0:T(8,128)}, f32[16,2304,72]{1,2,0:T(8,128)}, bf16[16,256,72]{2,1,0:T(8,1...) while((s32[]{:T(128)}, bf16[16,256,72]{1,2,0:T(8,128)(2,1)}, ...), condition=%wide.region_38.39_spmd.clone, body=%wide.region_36.38_spmd.clone.sunk | while | flops 430755584 | bytes 21090432 | solution.py:119
  1050.4 30.1 collective-permute-start.20
  1080.4 40.2 %collective-permute-start.21 = (f32[256,2304]{0,1:T(8,128)}, f32[256,2304]{0,1:T(8,128)}, u32[]{:S(2)}, u32[]{:S(2)}) collective-permute-start(f32[256,2304]{0,1:T(8,128)} %get-tuple-element.769), channel_id=1, source_target_pairs={{0,2},{1,3},{2,4},{3,5},{4,6},{5,7},{6,8},{7,9},{8,10},{9,11},{10,... | collective-permute-start | bytes 7077896 | tf_op jit(solution)/shard_map/ppermute | solution.py:19
  1134.1 93.2 %collective-permute-done.18 = f32[256,2304]{0,1:T(8,128)} collective-permute-done((f32[256,2304]{0,1:T(8,128)}, f32[256,2304]{0,1:T(8,128)}, u32[]{:S(2)}, u32[]{:S(2)}) %collective-permute-start.18) | collective-permute-done | bytes 2359328 | tf_op jit(solution)/shard_map/ppermute | solution.py:19
  1227.3 45.9 %collective-permute-start.22 = (f32[256,2304]{0,1:T(8,128)}, f32[256,2304]{0,1:T(8,128)}, u32[]{:S(2)}, u32[]{:S(2)}) collective-permute-start(f32[256,2304]{0,1:T(8,128)} %get-tuple-element.771), channel_id=1, source_target_pairs={{0,3},{1,4},{2,5},{3,6},{4,7},{5,8},{6,9},{7,10},{8,11},{9,12},{10... | collective-permute-start | bytes 7077896 | tf_op jit(solution)/shard_map/ppermute | solution.py:19
  1274.1 73.7 %while.82 = (s32[]{:T(128)}, bf16[16,256,72]{1,2,0:T(8,128)(2,1)}, f32[16,256]{1,0:T(8,128)S(1)}, bf16[16,256,72]{2,1,0:T(8,128)(2,1)}, bf16[16,2304,72]{2,1,0:T...) while((s32[]{:T(128)}, bf16[16,256,72]{1,2,0:T(8,128)(2,1)}, ...), condition=%wide.region_44.45_spmd.clone, body=%wide.region_41.44_spmd.clone.sunk | while | flops 175177472 | bytes 8419441 | solution.py:95
  1445.1 164.0 %while.83 = (s32[]{:T(128)}, bf16[16,256,72]{1,2,0:T(8,128)(2,1)}, f32[16,2304,72]{1,2,0:T(8,128)}, f32[16,2304,72]{1,2,0:T(8,128)}, bf16[16,256,72]{2,1,0:T(8,1...) while((s32[]{:T(128)}, bf16[16,256,72]{1,2,0:T(8,128)(2,1)}, ...), condition=%wide.region_51.52_spmd.clone, body=%wide.region_49.51_spmd.clone.sunk | while | flops 430755584 | bytes 21090432 | solution.py:119
  1636.1 22.9 collective-permute-done.25
  1659.1 170.2 %collective-permute-start.29 = (f32[256,2304]{0,1:T(8,128)}, f32[256,2304]{0,1:T(8,128)S(1)}, u32[]{:S(2)}, u32[]{:S(2)}) collective-permute-start(f32[256,2304]{0,1:T(8,128)} %get-tuple-element.761), channel_id=1, source_target_pairs={{0,2},{1,3},{2,4},{3,5},{4,6},{5,7},{6,8},{7,9},{8,10},{9,11},{10,... | collective-permute-start | bytes 7077896 | tf_op jit(solution)/shard_map/ppermute | solution.py:19
  1829.3 72.2 %collective-permute-start.31 = (f32[256,2304]{0,1:T(8,128)}, f32[256,2304]{0,1:T(8,128)S(1)}, u32[]{:S(2)}, u32[]{:S(2)}) collective-permute-start(f32[256,2304]{0,1:T(8,128)} %get-tuple-element.762), channel_id=1, source_target_pairs={{0,4},{1,5},{2,6},{3,7},{4,8},{5,9},{6,10},{7,11},{8,12},{9,13},{1... | collective-permute-start | bytes 7077896 | tf_op jit(solution)/shard_map/ppermute | solution.py:19
  1912.0 38.6 %collective-permute-done.30 = f32[256,2304]{0,1:T(8,128)} collective-permute-done((f32[256,2304]{0,1:T(8,128)S(1)}, f32[256,2304]{0,1:T(8,128)}, u32[]{:S(2)}, u32[]{:S(2)}) %collective-permute-start.30) | collective-permute-done | bytes 2359328 | tf_op jit(solution)/shard_map/ppermute | solution.py:19
  2027.6 259.3 %reduce-scatter.9.cloned.1.call-done = f32[144,3456]{1,0:T(8,128)} async-done(((f32[1152,3456]{1,0:T(8,128)}), f32[144,3456]{1,0:T(8,128)}) %reduce-scatter.9.cloned.1.call-update) | async-done | bytes 1990672 | tf_op jit(solution)/shard_map/reduce_scatter | solution.py:267
  2286.9 140.6 %reduce-scatter.23.cloned.1.call-done = f32[576,1152]{1,0:T(8,128)} async-done(((f32[4608,1152]{1,0:T(8,128)}), f32[576,1152]{1,0:T(8,128)}) %reduce-scatter.23.cloned.1.call-update) | async-done | bytes 2654224 | tf_op jit(solution)/shard_map/reduce_scatter | solution.py:273
  2427.5 140.7 %reduce-scatter.21.cloned.1.call-done = f32[144,4608]{1,0:T(8,128)} async-done(((f32[1152,4608]{1,0:T(8,128)}), f32[144,4608]{1,0:T(8,128)}) %reduce-scatter.21.cloned.1.call-update) | async-done | bytes 2654224 | tf_op jit(solution)/shard_map/reduce_scatter | solution.py:271
  2568.2 140.7 %reduce-scatter.15.cloned.1.call-done = f32[576,1152]{1,0:T(8,128)} async-done(((f32[4608,1152]{1,0:T(8,128)}), f32[576,1152]{1,0:T(8,128)}) %reduce-scatter.15.cloned.1.call-update) | async-done | bytes 2654224 | tf_op jit(solution)/shard_map/reduce_scatter | solution.py:273
  2708.8 140.7 %reduce-scatter.13.cloned.1.call-done = f32[144,4608]{1,0:T(8,128)} async-done(((f32[1152,4608]{1,0:T(8,128)}), f32[144,4608]{1,0:T(8,128)}) %reduce-scatter.13.cloned.1.call-update) | async-done | bytes 2654224 | tf_op jit(solution)/shard_map/reduce_scatter | solution.py:271
  2850.4 73.3 %while.79 = (s32[]{:T(128)}, bf16[16,256,72]{1,2,0:T(8,128)(2,1)}, bf16[16,256,72]{2,1,0:T(8,128)(2,1)}, bf16[16,2304,72]{2,1,0:T(8,128)(2,1)}, bf16[16,2304,72]...) while((s32[]{:T(128)}, bf16[16,256,72]{1,2,0:T(8,128)(2,1)}, ...), condition=%wide.region_25.26_spmd.clone, body=%wide.region_22.25_spmd.clone.sunk | while | flops 175177216 | bytes 8414301 | solution.py:95
  2985.9 58.3 %all-reduce.32 = (bf16[16,6912]{1,0:T(8,128)(2,1)S(1)}, bf16[16,6912]{1,0:T(8,128)(2,1)S(1)}) all-reduce(f32[16,6912]{1,0:T(8,128)S(1)} %fusion.229, f32[16,6912]{1,0:T(8,128)S(1)} %fusion.228), channel_id=1, replica_groups=mesh['fsdp'=8,'replica'=4] {'fsdp','replica'}, use_global_device_ids=true, to_apply=%region_54.55 | all-reduce | flops 221184 | bytes 1327104 | tf_op jit(solution)/shard_map/psum | solution.py:396
  3059.3 21.7 all-reduce.19
  3081.0 377.4 %all-reduce.31.cloned.1.call-done = (f32[144,3456]{1,0:T(8,128)}, f32[144,1152]{1,0:T(8,128)}, f32[144,4608]{1,0:T(8,128)}, f32[576,1152]{1,0:T(8,128)}, f32[144...) async-done(((f32[144,3456]{1,0:T(8,128)}, f32[144,1152]{1,0:T(8,128)}, f32[144,4608]{1,0:T(8,128)}, f32[576,1152]{1,0:T(8,128)}, ...) | async-done | bytes 15925264 | tf_op jit(solution)/shard_map/psum | solution.py:279
  (1019 shorter events, 1315.6 us)
Async XLA Ops:
  14.5 423.0 %all-gather.11.cloned.1.call-start = ((), (), s32[]{:S(2)}) async-start(), calls=%async_computation.9 | async-start | bytes 2985984 | tf_op jit(solution)/shard_map/all_gather | solution.py:256
  15.2 426.9 %all-gather.13.cloned.1.call-start = ((), (), s32[]{:S(2)}) async-start(), calls=%async_computation.10 | async-start | bytes 11943936 | tf_op jit(solution)/shard_map/all_gather | solution.py:258
  15.9 426.3 %all-gather.15.cloned.1.call-start = ((), (), s32[]{:S(2)}) async-start(), calls=%async_computation.11 | async-start | bytes 11943936 | tf_op jit(solution)/shard_map/all_gather | solution.py:260
  16.5 444.5 %all-gather.17.cloned.1.call-start = ((), (), s32[]{:S(2)}) async-start(), calls=%async_computation.12 | async-start | bytes 8957952 | tf_op jit(solution)/shard_map/all_gather | solution.py:254
  17.1 790.5 %all-gather.19.cloned.1.call-start = ((), (), s32[]{:S(2)}) async-start(), calls=%async_computation.13 | async-start | bytes 2985984 | tf_op jit(solution)/shard_map/all_gather | solution.py:256
  17.9 799.2 %all-gather.23.cloned.1.call-start = ((), (), s32[]{:S(2)}) async-start(), calls=%async_computation.15 | async-start | bytes 11943936 | tf_op jit(solution)/shard_map/all_gather | solution.py:260
  18.6 808.1 %all-gather.21.cloned.1.call-start = ((), (), s32[]{:S(2)}) async-start(), calls=%async_computation.14 | async-start | bytes 11943936 | tf_op jit(solution)/shard_map/all_gather | solution.py:258
  156.6 166.9 %collective-permute-start.7 = (bf16[256,2304]{1,0:T(8,128)(2,1)}, bf16[256,2304]{1,0:T(8,128)(2,1)}, u32[]{:S(2)}, u32[]{:S(2)}) collective-permute-start(bf16[256,2304]{1,0:T(8,128)(2,1)} %slice.151), channel_id=1, source_target_pairs={{4,0},{5,1},{6,2},{7,3},{8,4},{9,5},{10,6},{11,7},{12,8},{13,9},{1... | collective-permute-start | bytes 3538952 | tf_op jit(solution)/shard_map/ppermute | solution.py:19
  161.2 161.3 %collective-permute-start.6 = (bf16[256,2304]{1,0:T(8,128)(2,1)}, bf16[256,2304]{1,0:T(8,128)(2,1)S(1)}, u32[]{:S(2)}, u32[]{:S(2)}) collective-permute-start(bf16[256,2304]{1,0:T(8,128)(2,1)} %slice.151), channel_id=1, source_target_pairs={{3,0},{4,1},{5,2},{6,3},{7,4},{8,5},{9,6},{10,7},{11,8},{12,9},{13... | collective-permute-start | bytes 3538952 | tf_op jit(solution)/shard_map/ppermute | solution.py:19
  169.7 151.6 %collective-permute-start.5 = (bf16[256,2304]{1,0:T(8,128)(2,1)}, bf16[256,2304]{1,0:T(8,128)(2,1)S(1)}, u32[]{:S(2)}, u32[]{:S(2)}) collective-permute-start(bf16[256,2304]{1,0:T(8,128)(2,1)} %slice.151), channel_id=1, source_target_pairs={{2,0},{3,1},{4,2},{5,3},{6,4},{7,5},{8,6},{9,7},{10,8},{11,9},{12,... | collective-permute-start | bytes 3538952 | tf_op jit(solution)/shard_map/ppermute | solution.py:19
  510.3 1517.2 %reduce-scatter.19.cloned.1.call-start = ((), (), s32[]{:S(2)}) async-start(), calls=%async_computation.21 | async-start | bytes 5971968 | tf_op jit(solution)/shard_map/reduce_scatter | solution.py:269
  512.4 170.8 %collective-permute-start.15 = (bf16[256,2304]{1,0:T(8,128)(2,1)}, bf16[256,2304]{1,0:T(8,128)(2,1)}, u32[]{:S(2)}, u32[]{:S(2)}) collective-permute-start(bf16[256,2304]{1,0:T(8,128)(2,1)} %slice.157), channel_id=1, source_target_pairs={{4,0},{5,1},{6,2},{7,3},{8,4},{9,5},{10,6},{11,7},{12,8},{13,9},{1... | collective-permute-start | bytes 3538952 | tf_op jit(solution)/shard_map/ppermute | solution.py:19
  518.0 164.0 %collective-permute-start.14 = (bf16[256,2304]{1,0:T(8,128)(2,1)}, bf16[256,2304]{1,0:T(8,128)(2,1)S(1)}, u32[]{:S(2)}, u32[]{:S(2)}) collective-permute-start(bf16[256,2304]{1,0:T(8,128)(2,1)} %slice.157), channel_id=1, source_target_pairs={{3,0},{4,1},{5,2},{6,3},{7,4},{8,5},{9,6},{10,7},{11,8},{12,9},{13... | collective-permute-start | bytes 3538952 | tf_op jit(solution)/shard_map/ppermute | solution.py:19
  1047.8 179.5 %collective-permute-start.18 = (f32[256,2304]{0,1:T(8,128)}, f32[256,2304]{0,1:T(8,128)}, u32[]{:S(2)}, u32[]{:S(2)}) collective-permute-start(f32[256,2304]{0,1:T(8,128)} %get-tuple-element.766), channel_id=1, source_target_pairs={{2,0},{3,1},{4,2},{5,3},{6,4},{7,5},{8,6},{9,7},{10,8},{11,9},{12,... | collective-permute-start | bytes 7077896 | tf_op jit(solution)/shard_map/ppermute | solution.py:19
  1049.1 308.1 %collective-permute-start.19 = (f32[256,2304]{0,1:T(8,128)}, f32[256,2304]{0,1:T(8,128)}, u32[]{:S(2)}, u32[]{:S(2)}) collective-permute-start(f32[256,2304]{0,1:T(8,128)} %get-tuple-element.767), channel_id=1, source_target_pairs={{1,0},{2,1},{3,2},{4,3},{5,4},{6,5},{7,6},{8,7},{9,8},{10,9},{11,1... | collective-permute-start | bytes 7077896 | tf_op jit(solution)/shard_map/ppermute | solution.py:19
  1050.4 306.8 %collective-permute-start.20 = (f32[256,2304]{0,1:T(8,128)}, f32[256,2304]{0,1:T(8,128)}, u32[]{:S(2)}, u32[]{:S(2)}) collective-permute-start(f32[256,2304]{0,1:T(8,128)} %get-tuple-element.768), channel_id=1, source_target_pairs={{0,1},{1,2},{2,3},{3,4},{4,5},{5,6},{6,7},{7,8},{8,9},{9,10},{10,1... | collective-permute-start | bytes 7077896 | tf_op jit(solution)/shard_map/ppermute | solution.py:19
  1080.4 276.7 %collective-permute-start.21 = (f32[256,2304]{0,1:T(8,128)}, f32[256,2304]{0,1:T(8,128)}, u32[]{:S(2)}, u32[]{:S(2)}) collective-permute-start(f32[256,2304]{0,1:T(8,128)} %get-tuple-element.769), channel_id=1, source_target_pairs={{0,2},{1,3},{2,4},{3,5},{4,6},{5,7},{6,8},{7,9},{8,10},{9,11},{10,... | collective-permute-start | bytes 7077896 | tf_op jit(solution)/shard_map/ppermute | solution.py:19
  1120.6 236.5 %collective-permute-start.23 = (f32[256,2304]{0,1:T(8,128)}, f32[256,2304]{0,1:T(8,128)}, u32[]{:S(2)}, u32[]{:S(2)}) collective-permute-start(f32[256,2304]{0,1:T(8,128)} %get-tuple-element.770), channel_id=1, source_target_pairs={{0,4},{1,5},{2,6},{3,7},{4,8},{5,9},{6,10},{7,11},{8,12},{9,13},{1... | collective-permute-start | bytes 7077896 | tf_op jit(solution)/shard_map/ppermute | solution.py:19
  1357.1 670.5 %reduce-scatter.11.cloned.1.call-start = ((), (), s32[]{:S(2)}) async-start(), calls=%async_computation.17 | async-start | bytes 5971968 | tf_op jit(solution)/shard_map/reduce_scatter | solution.py:269
  1418.8 608.8 %reduce-scatter.17.cloned.1.call-start = ((), (), s32[]{:S(2)}) async-start(), calls=%async_computation.20 | async-start | bytes 17915904 | tf_op jit(solution)/shard_map/reduce_scatter | solution.py:267
  1434.0 852.8 %reduce-scatter.9.cloned.1.call-start = ((), (), s32[]{:S(2)}) async-start(), calls=%async_computation.16 | async-start | bytes 17915904 | tf_op jit(solution)/shard_map/reduce_scatter | solution.py:267
  1627.5 201.8 %collective-permute-start.24 = (f32[256,2304]{0,1:T(8,128)}, f32[256,2304]{0,1:T(8,128)S(1)}, u32[]{:S(2)}, u32[]{:S(2)}) collective-permute-start(f32[256,2304]{0,1:T(8,128)} %get-tuple-element.757), channel_id=1, source_target_pairs={{4,0},{5,1},{6,2},{7,3},{8,4},{9,5},{10,6},{11,7},{12,8},{13,9},{1... | collective-permute-start | bytes 7077896 | tf_op jit(solution)/shard_map/ppermute | solution.py:19
  1628.8 272.7 %collective-permute-start.26 = (f32[256,2304]{0,1:T(8,128)}, f32[256,2304]{0,1:T(8,128)S(1)}, u32[]{:S(2)}, u32[]{:S(2)}) collective-permute-start(f32[256,2304]{0,1:T(8,128)} %get-tuple-element.758), channel_id=1, source_target_pairs={{2,0},{3,1},{4,2},{5,3},{6,4},{7,5},{8,6},{9,7},{10,8},{11,9},{12,... | collective-permute-start | bytes 7077896 | tf_op jit(solution)/shard_map/ppermute | solution.py:19
  1630.1 277.5 %collective-permute-start.27 = (f32[256,2304]{0,1:T(8,128)}, f32[256,2304]{0,1:T(8,128)S(1)}, u32[]{:S(2)}, u32[]{:S(2)}) collective-permute-start(f32[256,2304]{0,1:T(8,128)} %get-tuple-element.759), channel_id=1, source_target_pairs={{1,0},{2,1},{3,2},{4,3},{5,4},{6,5},{7,6},{8,7},{9,8},{10,9},{11,1... | collective-permute-start | bytes 7077896 | tf_op jit(solution)/shard_map/ppermute | solution.py:19
  1631.4 276.2 %collective-permute-start.28 = (f32[256,2304]{0,1:T(8,128)}, f32[256,2304]{0,1:T(8,128)S(1)}, u32[]{:S(2)}, u32[]{:S(2)}) collective-permute-start(f32[256,2304]{0,1:T(8,128)} %get-tuple-element.760), channel_id=1, source_target_pairs={{0,1},{1,2},{2,3},{3,4},{4,5},{5,6},{6,7},{7,8},{8,9},{9,10},{10,1... | collective-permute-start | bytes 7077896 | tf_op jit(solution)/shard_map/ppermute | solution.py:19
  1659.1 248.5 %collective-permute-start.29 = (f32[256,2304]{0,1:T(8,128)}, f32[256,2304]{0,1:T(8,128)S(1)}, u32[]{:S(2)}, u32[]{:S(2)}) collective-permute-start(f32[256,2304]{0,1:T(8,128)} %get-tuple-element.761), channel_id=1, source_target_pairs={{0,2},{1,3},{2,4},{3,5},{4,6},{5,7},{6,8},{7,9},{8,10},{9,11},{10,... | collective-permute-start | bytes 7077896 | tf_op jit(solution)/shard_map/ppermute | solution.py:19
  1967.8 459.7 %reduce-scatter.23.cloned.1.call-start = ((), (), s32[]{:S(2)}) async-start(), calls=%async_computation.23 | async-start | bytes 23887872 | tf_op jit(solution)/shard_map/reduce_scatter | solution.py:273
  1981.7 586.5 %reduce-scatter.21.cloned.1.call-start = ((), (), s32[]{:S(2)}) async-start(), calls=%async_computation.22 | async-start | bytes 23887872 | tf_op jit(solution)/shard_map/reduce_scatter | solution.py:271
  1993.7 715.1 %reduce-scatter.15.cloned.1.call-start = ((), (), s32[]{:S(2)}) async-start(), calls=%async_computation.19 | async-start | bytes 23887872 | tf_op jit(solution)/shard_map/reduce_scatter | solution.py:273
  2007.6 842.0 %reduce-scatter.13.cloned.1.call-start = ((), (), s32[]{:S(2)}) async-start(), calls=%async_computation.18 | async-start | bytes 23887872 | tf_op jit(solution)/shard_map/reduce_scatter | solution.py:271
  2019.7 1033.5 %all-reduce.27.cloned.1.call-start = ((), (), s32[]{:S(2)}) async-start(), calls=%async_computation.24 | async-start | bytes 196608
  2025.5 1432.9 %all-reduce.31.cloned.1.call-start = ((), (), s32[]{:S(2)}) async-start(), calls=%async_computation.26 | async-start | bytes 31850496 | tf_op jit(solution)/shard_map/psum | solution.py:279
  (133 other events, 5315.4 us)
Sparse Core Ops, SparseCore 0:
  13.9 58.8 all-reduce.28
  74.7 51.7 all-gather.8
  128.4 46.7 all-gather.10
  176.9 73.1 all-gather.12
  251.9 85.7 all-gather.14
  339.4 73.0 all-gather.16
  414.4 30.2 all-gather.18
  446.5 79.4 all-gather.22
  527.9 82.0 all-gather.20
  1357.2 150.6 reduce-scatter.18
  1511.7 86.5 reduce-scatter.10
  1601.8 112.9 reduce-scatter.16
  1967.9 318.9 reduce-scatter.8
  2290.3 137.1 reduce-scatter.22
  2431.0 137.1 reduce-scatter.20
  2571.6 137.1 reduce-scatter.14
  2712.3 137.1 reduce-scatter.12
  2854.4 53.2 all-reduce.26
  2911.6 546.7 all-reduce.30
where the time goes:
time: 3500 us; the launch traced here: 3480 us
  waiting for transfers between devices  1720 us (49%)
  matrix products  835 us (24%)
  starting transfers between devices  462 us (13%)
  local copies, waits for them, and re-layouts  217 us (6%)
  other arithmetic  121 us (3%)
  blocking collectives  107 us (3%)
    ppermute x32, starting transfers between devices, shifted(): lax.ppermute(value, axis, [(source, source + steps) for source in range(f...  460 us
    ppermute x32, waiting for transfers between devices, shifted(): lax.ppermute(value, axis, [(source, source + steps) for source in range(f...  446 us
    psum x1, waiting for transfers between devices, replica_total(): lax.psum((shares[0], shares[1], shares[2], shares[3], shares[4], shares[5...  377 us
    reduce_scatter x2, waiting for transfers between devices, owner_sums(): lax.psum_scatter(local_grads[4], 'fsdp', scatter_dimension=0, tiled=True)  281 us
    reduce_scatter x2, waiting for transfers between devices, owner_sums(): lax.psum_scatter(local_grads[6], 'fsdp', scatter_dimension=0, tiled=True)  281 us
    reduce_scatter x2, waiting for transfers between devices, owner_sums(): lax.psum_scatter(local_grads[0], 'fsdp', scatter_dimension=0, tiled=True)  259 us
    dot_general x96, matrix products, head_scores(): jnp.einsum('td,wd->tw', q_head, k_head, preferred_element_type=jnp.float32)  178 us
    dot_general x64, matrix products, one_head(): jnp.einsum('tw,wd->td', probs, v_head, preferred_element_type=jnp.float32)  141 us
  transfers between devices with their start and end apart: 51, of which 21 were waited for; matrix products, arithmetic and copies ran while one was open for 26% of the time, Pallas kernels for 0%

commit v1 on v0

v1 whole, which is shorter than its diff:
```python
import functools
import math

import jax
import jax.numpy as jnp
from jax import lax
from jax.experimental import pallas as pl
from jax.experimental.pallas import tpu as pltpu
from jax.sharding import PartitionSpec as P

HEADS = 16
MAXLEN = 1024
NORM_EPS = 1e-06
HIGH = lax.Precision.HIGHEST
BQ = 256
BK = 256
LANES = 128
NEG = -1e30
VM = pl.BlockSpec(memory_space=pltpu.VMEM)
SM = pl.BlockSpec(memory_space=pltpu.SMEM)
HB = pl.BlockSpec(memory_space=pl.ANY)
VMEM_LIMIT = 56 * 1024 * 1024


def pad_to(size, unit):
    return -(-size // unit) * unit


def take_head(ref, rows, at, dim):
    first, off = at // LANES * LANES, at % LANES
    wide = LANES if off + dim <= LANES else 2 * LANES
    block = ref[rows, first : first + wide].astype(jnp.float32)
    if off:
        block = pltpu.roll(block, wide - off, 1)
    block = block[:, :LANES]
    lane = lax.broadcasted_iota(jnp.int32, block.shape, 1)
    return jnp.where(lane < dim, block, 0.0)


def put_heads(blocks, places, width):
    tiles = [None] * (width // LANES)
    for block, at in zip(blocks, places):
        first, off = at // LANES, at % LANES
        wide = jnp.concatenate([block, jnp.zeros_like(block)], axis=1)
        if off:
            wide = pltpu.roll(wide, off, 1)
        for step in range(2):
            part = wide[:, step * LANES : (step + 1) * LANES]
            if first + step < len(tiles):
                old = tiles[first + step]
                tiles[first + step] = part if old is None else old + part
    rows = blocks[0].shape[0]
    return jnp.concatenate(
        [jnp.zeros((rows, LANES), jnp.float32) if t is None else t for t in tiles], axis=1
    )


def nt_dot(left, right):
    return lax.dot_general(left, right, (((1,), (1,)), ((), ())), preferred_element_type=jnp.float32)


def nn_dot(left, right):
    return jnp.dot(left, right, preferred_element_type=jnp.float32)


def rows_at(block, size):
    return pl.ds(pl.multiple_of(block * size, size), size)


def over_window(lo, hi, prev, own, after, action):
    edge, mid = prev.shape[0] // BK, own.shape[0] // BK

    def run(ref, first, count):
        def body(at, carry):
            action(ref, at - first, at)
            return carry

        lax.fori_loop(jnp.clip(lo, first, first + count), jnp.clip(hi, first, first + count), body, 0)

    run(prev, 0, edge)
    run(own, edge, mid)
    run(after, edge + mid, edge)


def attend_kernel(nh, hd, lo, hi, prev, own, after, kid, qid, o_ref, ot_ref, lse_ref, kh, vt, qh, acc, ml):
    dim = hd // nh
    width = o_ref.shape[1]
    count = own.shape[0] // BQ
    scale = math.log2(math.e) / math.sqrt(dim)

    def load(ref, at, to):
        for h in range(nh):
            kh[h, rows_at(to, BK), :] = take_head(ref, rows_at(at, BK), h * dim, dim).astype(jnp.bfloat16)
            vt[h, :, rows_at(to, BK)] = take_head(ref, rows_at(at, BK), hd + h * dim, dim).T.astype(jnp.bfloat16)

    over_window(lo[0], hi[count - 1], prev, own, after, load)
    lse_ref[...] = jnp.zeros_like(lse_ref)

    def query_block(qb, carry):
        rows = rows_at(qb, BQ)
        for h in range(nh):
            qh[h] = take_head(own, rows, 2 * hd + h * dim, dim).astype(jnp.bfloat16)
        acc[...] = jnp.zeros_like(acc)
        ml[0] = jnp.full(ml.shape[1:], NEG, jnp.float32)
        ml[1] = jnp.zeros(ml.shape[1:], jnp.float32)
        ids = qid[0:1, rows]

        def key_block(kb, inner):
            keys = rows_at(kb, BK)
            lanes = kid[keys, :]
            same = jnp.concatenate([lanes] * (BQ // LANES), axis=1) == ids
            for h in range(nh):
                s = jnp.where(same, nt_dot(kh[h, keys, :], qh[h]) * scale, NEG)
                old = ml[0, h : h + 1, :]
                top = jnp.maximum(old, jnp.max(s, axis=0, keepdims=True))
                p = jnp.exp2(s - top)
                alpha = jnp.exp2(old - top)
                ml[0, h : h + 1, :] = top
                ml[1, h : h + 1, :] = ml[1, h : h + 1, :] * alpha + jnp.sum(p, axis=0, keepdims=True)
                acc[h] = acc[h] * alpha + nn_dot(vt[h, :, keys], p.astype(jnp.bfloat16))
            return inner

        lax.fori_loop(lo[qb], hi[qb], key_block, 0)
        parts = []
        for h in range(nh):
            total = ml[1, h : h + 1, :]
            out = acc[h, :dim, :] / total
            parts.append(out)
            lse_ref[h : h + 1, rows] = ml[0, h : h + 1, :] + jnp.log2(total)
        parts.append(jnp.zeros((width - hd, BQ), jnp.float32))
        heads = jnp.concatenate(parts, axis=0)
        ot_ref[:, rows] = heads
        o_ref[rows, :] = heads.T.astype(jnp.bfloat16)
        return carry

    lax.fori_loop(0, count, query_block, 0)


def attend(nh, hd, lo, hi, prev, own, after, kid, qid):
    rows, window = own.shape[0], own.shape[0] + 2 * prev.shape[0]
    width = pad_to(hd, LANES)
    return pl.pallas_call(
        functools.partial(attend_kernel, nh, hd),
        out_shape=(
            jax.ShapeDtypeStruct((rows, width), jnp.bfloat16),
            jax.ShapeDtypeStruct((width, rows), jnp.float32),
            jax.ShapeDtypeStruct((8, rows), jnp.float32),
        ),
        in_specs=[SM, SM, VM, VM, VM, VM, VM],
        out_specs=(VM, VM, VM),
        scratch_shapes=[
            pltpu.VMEM((nh, window, LANES), jnp.bfloat16),
            pltpu.VMEM((nh, LANES, window), jnp.bfloat16),
            pltpu.VMEM((nh, BQ, LANES), jnp.bfloat16),
            pltpu.VMEM((nh, LANES, BQ), jnp.float32),
            pltpu.VMEM((2, 8, BQ), jnp.float32),
        ],
        compiler_params=pltpu.CompilerParams(vmem_limit_bytes=VMEM_LIMIT),
        cost_estimate=pl.CostEstimate(
            flops=4 * nh * rows * 1024 * LANES, bytes_accessed=8 << 20, transcendentals=nh * rows * 1024
        ),
    )(lo, hi, prev, own, after, kid, qid)


def attend_back_kernel(
    nh, hd, lo, hi, prev, own, after, kid, qid, do_ref, ot_ref, lse_ref,
    dq_ref, dprev, down, dafter, kh, vh, kt, qh, gh, dk, dv, dqt, delta,
):
    dim = hd // nh
    width = dq_ref.shape[1]
    count = own.shape[0] // BQ
    root = 1.0 / math.sqrt(dim)
    scale = math.log2(math.e) / math.sqrt(dim)

    def load(ref, at, to):
        for h in range(nh):
            k = take_head(ref, rows_at(at, BK), h * dim, dim)
            kh[h, rows_at(to, BK), :] = k.astype(jnp.bfloat16)
            kt[h, :, rows_at(to, BK)] = k.T.astype(jnp.bfloat16)
            vh[h, rows_at(to, BK), :] = take_head(ref, rows_at(at, BK), hd + h * dim, dim).astype(jnp.bfloat16)
            dk[h, rows_at(to, BK), :] = jnp.zeros((BK, LANES), jnp.float32)
            dv[h, rows_at(to, BK), :] = jnp.zeros((BK, LANES), jnp.float32)

    over_window(lo[0], hi[count - 1], prev, own, after, load)

    def query_block(qb, carry):
        rows = rows_at(qb, BQ)
        for h in range(nh):
            qh[h] = take_head(own, rows, 2 * hd + h * dim, dim).astype(jnp.bfloat16)
            gh[h] = take_head(do_ref, rows, h * dim, dim).astype(jnp.bfloat16)
        prod = do_ref[rows, :].astype(jnp.float32).T * ot_ref[:, rows]
        for h in range(nh):
            delta[h : h + 1, :] = jnp.sum(prod[h * dim : (h + 1) * dim], axis=0, keepdims=True)
        dqt[...] = jnp.zeros_like(dqt)
        ids = qid[0:1, rows]

        def key_block(kb, inner):
            keys = rows_at(kb, BK)
            lanes = kid[keys, :]
            same = jnp.concatenate([lanes] * (BQ // LANES), axis=1) == ids
            for h in range(nh):
                s = nt_dot(kh[h, keys, :], qh[h]) * scale - lse_ref[h : h + 1, rows]
                p = jnp.exp2(jnp.where(same, s, NEG))
                dp = nt_dot(vh[h, keys, :], gh[h])
                ds = (p * (dp - delta[h : h + 1, :])).astype(jnp.bfloat16)
                dv[h, keys, :] += nn_dot(p.astype(jnp.bfloat16), gh[h])
                dk[h, keys, :] += nn_dot(ds, qh[h])
                dqt[h] += nn_dot(kt[h, :, keys], ds)
            return inner

        lax.fori_loop(lo[qb], hi[qb], key_block, 0)
        parts = [dqt[h, :dim, :] * root for h in range(nh)]
        parts.append(jnp.zeros((width - hd, BQ), jnp.float32))
        dq_ref[rows, :] = jnp.concatenate(parts, axis=0).T.astype(jnp.bfloat16)
        return carry

    lax.fori_loop(0, count, query_block, 0)
    for ref in (dprev, dafter):
        ref[...] = jnp.zeros_like(ref)

    def store(ref, at, to):
        keys = rows_at(to, BK)
        blocks = [dk[h, keys, :] * root for h in range(nh)] + [dv[h, keys, :] for h in range(nh)]
        ref[rows_at(at, BK), :] = put_heads(blocks, [h * dim for h in range(2 * nh)], ref.shape[1]).astype(ref.dtype)

    over_window(lo[0], hi[count - 1], dprev, down, dafter, store)


def attend_back(nh, hd, lo, hi, prev, own, after, kid, qid, grad, ot, lse):
    rows, edge = own.shape[0], prev.shape[0]
    window = rows + 2 * edge
    width, kv = pad_to(hd, LANES), prev.shape[1]
    heads = lambda size, dtype: pltpu.VMEM((nh, size, LANES), dtype)
    return pl.pallas_call(
        functools.partial(attend_back_kernel, nh, hd),
        out_shape=(
            jax.ShapeDtypeStruct((rows, width), jnp.bfloat16),
            jax.ShapeDtypeStruct((edge, kv), jnp.bfloat16),
            jax.ShapeDtypeStruct((rows, kv), jnp.bfloat16),
            jax.ShapeDtypeStruct((edge, kv), jnp.bfloat16),
        ),
        in_specs=[SM, SM] + [VM] * 8,
        out_specs=(VM,) * 4,
        scratch_shapes=[
            heads(window, jnp.bfloat16),
            heads(window, jnp.bfloat16),
            pltpu.VMEM((nh, LANES, window), jnp.bfloat16),
            heads(BQ, jnp.bfloat16),
            heads(BQ, jnp.bfloat16),
            heads(window, jnp.float32),
            heads(window, jnp.float32),
            pltpu.VMEM((nh, LANES, BQ), jnp.float32),
            pltpu.VMEM((8, BQ), jnp.float32),
        ],
        compiler_params=pltpu.CompilerParams(vmem_limit_bytes=VMEM_LIMIT),
        cost_estimate=pl.CostEstimate(
            flops=10 * nh * rows * 1024 * LANES, bytes_accessed=16 << 20, transcendentals=nh * rows * 1024
        ),
    )(lo, hi, prev, own, after, kid, qid, grad, ot, lse)


MESH = pl.DeviceIdType.MESH


def greet(partners, count):
    barrier = pltpu.get_barrier_semaphore()
    for where, there in partners:
        @pl.when(there)
        def _():
            pl.semaphore_signal(barrier, inc=1, device_id=where, device_id_type=MESH)
    pl.semaphore_wait(barrier, count)


def wait_for(ref, sem):
    pltpu.make_async_copy(ref, ref, sem).wait()


def to_heads_kernel(reps, size, edge, kv, x_ref, own, prev, after, send, recv, edge_send, edge_recv):
    group, me = lax.axis_index("fsdp"), lax.axis_index("replica")
    groups = lax.axis_size("fsdp")
    wide = x_ref.shape[2]
    down, up = group > 0, group < groups - 1
    others = [(group, lax.rem(me + d, reps)) for d in range(1, reps)]
    greet(
        [(place, True) for place in others] + [((group - 1, me), down), ((group + 1, me), up)],
        reps - 1 + down.astype(jnp.int32) + up.astype(jnp.int32),
    )
    spans = [pl.ds(0, kv), pl.ds(kv, wide - kv)] if wide > kv else [pl.ds(0, kv)]

    def exchange(span, part, there):
        return pltpu.make_async_remote_copy(
            src_ref=x_ref.at[there, :, span], dst_ref=own.at[me, :, span], send_sem=send.at[part, there],
            recv_sem=recv.at[part, me], device_id=(group, there), device_id_type=MESH,
        )

    for part, span in enumerate(spans):
        for _, there in others:
            exchange(span, part, there).start()
        pltpu.make_async_copy(x_ref.at[me, :, span], own.at[me, :, span], recv.at[part, me]).start()

    def edges(piece, action):
        lo, hi = piece * size, (piece + 1) * size
        total = reps * size
        if lo >= total - edge:
            @pl.when(up)
            def _():
                action(0, piece, (group + 1, me), prev.at[pl.ds(lo - (total - edge), size), :])
        if hi <= edge:
            @pl.when(down)
            def _():
                action(1, piece, (group - 1, me), after.at[pl.ds(lo, size), :])

    def start_edge(way, piece, where, target):
        pltpu.make_async_remote_copy(
            src_ref=own.at[piece, :, spans[0]], dst_ref=target, send_sem=edge_send.at[way, piece],
            recv_sem=edge_recv.at[way, piece], device_id=where, device_id_type=MESH,
        ).start()

    def end_send(way, piece, where, target):
        wait_for(own.at[piece, :, spans[0]], edge_send.at[way, piece])

    def end_recv(way, piece, where, target):
        wait_for(target, edge_recv.at[way, piece])

    for piece in range(reps):
        wait_for(own.at[piece, :, spans[0]], recv.at[0, piece])
        edges(piece, start_edge)
    if len(spans) > 1:
        for piece in range(reps):
            wait_for(own.at[piece, :, spans[1]], recv.at[1, piece])
    for part, span in enumerate(spans):
        for _, there in others:
            wait_for(x_ref.at[there, :, span], send.at[part, there])
    for piece in range(reps):
        edges(piece, end_send)
        lo, hi = piece * size, (piece + 1) * size
        total = reps * size
        if lo >= total - edge:
            @pl.when(down)
            def _():
                wait_for(prev.at[pl.ds(lo - (total - edge), size), :], edge_recv.at[0, piece])
        if hi <= edge:
            @pl.when(up)
            def _():
                wait_for(after.at[pl.ds(lo, size), :], edge_recv.at[1, piece])


def to_heads(packed, edge, kv, collective_id):
    reps, size, wide = packed.shape
    sems = pltpu.SemaphoreType.DMA((2, reps))
    own, prev, after = pl.pallas_call(
        functools.partial(to_heads_kernel, reps, size, edge, kv),
        out_shape=(
            jax.ShapeDtypeStruct(packed.shape, packed.dtype),
            jax.ShapeDtypeStruct((edge, kv), packed.dtype),
            jax.ShapeDtypeStruct((edge, kv), packed.dtype),
        ),
        in_specs=[HB],
        out_specs=(HB, HB, HB),
        scratch_shapes=[sems, sems, sems, sems],
        compiler_params=pltpu.CompilerParams(collective_id=collective_id, has_side_effects=True),
    )(packed)
    return own.reshape(reps * size, wide), prev, after


def swap_kernel(reps, x_ref, y_ref, send, recv):
    group, me = lax.axis_index("fsdp"), lax.axis_index("replica")
    others = [(group, lax.rem(me + d, reps)) for d in range(1, reps)]
    greet([(place, True) for place in others], reps - 1)
    for _, there in others:
        pltpu.make_async_remote_copy(
            src_ref=x_ref.at[there], dst_ref=y_ref.at[me], send_sem=send.at[there], recv_sem=recv.at[me],
            device_id=(group, there), device_id_type=MESH,
        ).start()
    pltpu.make_async_copy(x_ref.at[me], y_ref.at[me], recv.at[me]).start()
    for piece in range(reps):
        wait_for(y_ref.at[piece], recv.at[piece])
    for _, there in others:
        wait_for(x_ref.at[there], send.at[there])


def swap(packed, collective_id):
    reps = packed.shape[0]
    sems = pltpu.SemaphoreType.DMA((reps,))
    return pl.pallas_call(
        functools.partial(swap_kernel, reps),
        out_shape=jax.ShapeDtypeStruct(packed.shape, packed.dtype),
        in_specs=[HB],
        out_specs=HB,
        scratch_shapes=[sems, sems],
        compiler_params=pltpu.CompilerParams(collective_id=collective_id, has_side_effects=True),
    )(packed)


def from_heads_kernel(reps, size, edge, dprev, own, dafter, dq, out_kv, out_q, from_up, from_down, total, mine, sends, recvs, send, recv):
    group, me = lax.axis_index("fsdp"), lax.axis_index("replica")
    groups = lax.axis_size("fsdp")
    rows = reps * size
    down, up = group > 0, group < groups - 1
    others = [(group, lax.rem(me + d, reps)) for d in range(1, reps)]
    greet(
        [(place, True) for place in others] + [((group - 1, me), down), ((group + 1, me), up)],
        reps - 1 + down.astype(jnp.int32) + up.astype(jnp.int32),
    )
    to_down = pltpu.make_async_remote_copy(
        src_ref=dprev, dst_ref=from_up, send_sem=sends.at[0], recv_sem=recvs.at[0],
        device_id=(group - 1, me), device_id_type=MESH,
    )
    to_up = pltpu.make_async_remote_copy(
        src_ref=dafter, dst_ref=from_down, send_sem=sends.at[1], recv_sem=recvs.at[1],
        device_id=(group + 1, me), device_id_type=MESH,
    )
    pl.when(down)(to_down.start)
    pl.when(up)(to_up.start)
    for _, there in others:
        pltpu.make_async_remote_copy(
            src_ref=dq.at[pl.ds(pl.multiple_of(there * size, size), size), :], dst_ref=out_q.at[me], send_sem=send.at[0, there],
            recv_sem=recv.at[0, me], device_id=(group, there), device_id_type=MESH,
        ).start()
    pltpu.make_async_copy(dq.at[pl.ds(pl.multiple_of(me * size, size), size), :], out_q.at[me], recv.at[0, me]).start()
    step = math.gcd(edge, 256)

    def chunk(at, carry):
        here = pl.ds(pl.multiple_of(at * step, step), step)
        total[here, :] = own[here, :].astype(jnp.float32)
        return carry

    lax.fori_loop(0, rows // step, chunk, 0)

    def add(ref, first):
        def body(at, carry):
            here = pl.ds(pl.multiple_of(first + at * step, step), step)
            there = pl.ds(pl.multiple_of(at * step, step), step)
            total[here, :] += ref[there, :].astype(jnp.float32)
            return carry

        lax.fori_loop(0, edge // step, body, 0)

    @pl.when(down)
    def _():
        wait_for(from_down, recvs.at[1])
        add(from_down, 0)

    @pl.when(up)
    def _():
        wait_for(from_up, recvs.at[0])
        add(from_up, rows - edge)

    def narrow(at, carry):
        here = pl.ds(pl.multiple_of(at * step, step), step)
        mine[here, :] = total[here, :].astype(jnp.bfloat16)
        return carry

    lax.fori_loop(0, rows // step, narrow, 0)
    for _, there in others:
        pltpu.make_async_remote_copy(
            src_ref=mine.at[pl.ds(pl.multiple_of(there * size, size), size), :], dst_ref=out_kv.at[me], send_sem=send.at[1, there],
            recv_sem=recv.at[1, me], device_id=(group, there), device_id_type=MESH,
        ).start()
    pltpu.make_async_copy(mine.at[pl.ds(pl.multiple_of(me * size, size), size), :], out_kv.at[me], recv.at[1, me]).start()
    for piece in range(reps):
        wait_for(out_q.at[piece], recv.at[0, piece])
        wait_for(out_kv.at[piece], recv.at[1, piece])
    for _, there in others:
        wait_for(out_q.at[0], send.at[0, there])
        wait_for(out_kv.at[0], send.at[1, there])
    pl.when(down)(to_down.wait_send)
    pl.when(up)(to_up.wait_send)


def from_heads(reps, dprev, own, dafter, dq, collective_id):
    rows, kv = own.shape
    edge, size = dprev.shape[0], own.shape[0] // reps
    pair, both = pltpu.SemaphoreType.DMA((2,)), pltpu.SemaphoreType.DMA((2, reps))
    return pl.pallas_call(
        functools.partial(from_heads_kernel, reps, size, edge),
        out_shape=(
            jax.ShapeDtypeStruct((reps, size, kv), own.dtype),
            jax.ShapeDtypeStruct((reps, size, dq.shape[1]), dq.dtype),
        ),
        in_specs=[HB, VM, HB, HB],
        out_specs=(HB, HB),
        scratch_shapes=[
            pltpu.VMEM((edge, kv), own.dtype),
            pltpu.VMEM((edge, kv), own.dtype),
            pltpu.VMEM((rows, kv), jnp.float32),
            pltpu.VMEM((rows, kv), own.dtype),
            pair,
            pair,
            both,
            both,
        ],
        compiler_params=pltpu.CompilerParams(
            collective_id=collective_id, has_side_effects=True, vmem_limit_bytes=VMEM_LIMIT
        ),
    )(dprev, own, dafter, dq)


def pre_norm(stream, shift, scale):
    centred = stream - jnp.mean(stream, axis=-1, keepdims=True)
    spread = jnp.mean(centred * centred, axis=-1, keepdims=True)
    return centred * lax.rsqrt(spread + NORM_EPS) * (1.0 + scale) + shift


def gelu_tanh(values):
    return jax.nn.gelu(values, approximate=True)


def latent_ids(latent_len, positions, token_total):
    starts = jnp.cumsum(latent_len) - latent_len
    found = jnp.sum((starts[None, :] <= positions[:, None]).astype(jnp.int32), axis=1) - 1
    inside = (positions >= 0) & (positions < token_total)
    return jnp.where(inside, found, -1)


def low_dot(left, right):
    return jnp.dot(left, right, preferred_element_type=jnp.float32)


def group_heads(matrix, reps):
    return matrix.reshape(matrix.shape[0], reps, -1).transpose(1, 0, 2)


def ungroup_heads(stacked):
    return stacked.transpose(1, 0, 2).reshape(stacked.shape[1], -1)


def widen(stacked, width):
    return jnp.pad(stacked, ((0, 0), (0, 0), (0, width - stacked.shape[2])))


def layer_forward(stream, mod_tok, full, plan):
    qkv_w, qkv_b, out_w, out_b, up_w, up_b, down_w, down_b = full
    reps, edge, bounds, ids = plan
    width = stream.shape[1]
    hd = width // reps
    nh = HEADS // reps
    shift_one, scale_one, gate_one, shift_two, scale_two, gate_two = jnp.split(mod_tok, 6, axis=1)
    normed = pre_norm(stream, shift_one, scale_one).astype(jnp.bfloat16)
    qkv_bias = qkv_b.astype(jnp.float32)
    bias_full = jnp.concatenate(
        [qkv_bias[:width], jnp.zeros((width,), jnp.float32), qkv_bias[width:]]
    )
    projected = (low_dot(normed, qkv_w) + bias_full).astype(jnp.bfloat16)
    query, key, value = (group_heads(part, reps) for part in jnp.split(projected, 3, axis=1))
    packed = widen(jnp.concatenate([key, value, query], axis=2), pad_to(3 * hd, LANES))
    own, prev, after = to_heads(packed, edge, pad_to(2 * hd, LANES), 1)
    mixed, mixed_t, log_norm = attend(nh, hd, *bounds, prev, own, after, *ids)
    mixed = swap(mixed.reshape(reps, -1, mixed.shape[1]), 2)
    mixed = ungroup_heads(mixed[:, :, :hd])
    branch = low_dot(mixed, out_w) + out_b.astype(jnp.float32)
    middle = stream + gate_one * branch
    normed_two = pre_norm(middle, shift_two, scale_two).astype(jnp.bfloat16)
    hidden = low_dot(normed_two, up_w) + up_b.astype(jnp.float32)
    active = gelu_tanh(hidden).astype(jnp.bfloat16)
    result = low_dot(active, down_w) + down_b.astype(jnp.float32)
    saved = (
        normed, (prev, own, after), mixed, (mixed_t, log_norm), branch, middle, normed_two, hidden, active, result,
    )
    return (middle + gate_two * result, saved)


def layer_backward(stream, mod_tok, full, saved, plan, pick, grad_next):
    qkv_w, qkv_b, out_w, out_b, up_w, up_b, down_w, down_b = full
    normed, window, mixed, kept, branch, middle, normed_two, hidden, active, result = saved
    reps, edge, bounds, ids = plan
    width = stream.shape[1]
    hd = width // reps
    nh = HEADS // reps
    shift_one, scale_one, gate_one, shift_two, scale_two, gate_two = jnp.split(mod_tok, 6, axis=1)
    grad_result = (gate_two * grad_next).astype(jnp.bfloat16)
    grad_gate_two = grad_next * result
    grad_down_w = jnp.einsum("tf,td->fd", active, grad_result, preferred_element_type=jnp.float32).astype(jnp.bfloat16)
    grad_down_b = jnp.sum(grad_result.astype(jnp.float32), axis=0)
    grad_active = jnp.einsum("td,fd->tf", grad_result, down_w, preferred_element_type=jnp.float32)
    _, gelu_back = jax.vjp(gelu_tanh, hidden)
    grad_hidden = gelu_back(grad_active)[0].astype(jnp.bfloat16)
    grad_up_w = jnp.einsum("td,tf->df", normed_two, grad_hidden, preferred_element_type=jnp.float32).astype(jnp.bfloat16)
    grad_up_b = jnp.sum(grad_hidden.astype(jnp.float32), axis=0)
    grad_normed_two = jnp.einsum("tf,df->td", grad_hidden, up_w, preferred_element_type=jnp.float32)
    _, norm_back_two = jax.vjp(pre_norm, middle, shift_two, scale_two)
    grad_middle_part, grad_shift_two, grad_scale_two = norm_back_two(grad_normed_two)
    grad_middle = grad_next + grad_middle_part
    grad_branch = (gate_one * grad_middle).astype(jnp.bfloat16)
    grad_gate_one = grad_middle * branch
    grad_out_w = jnp.einsum("td,te->de", mixed, grad_branch, preferred_element_type=jnp.float32).astype(jnp.bfloat16)
    grad_out_b = jnp.sum(grad_branch.astype(jnp.float32), axis=0)
    grad_mixed = jnp.einsum(
        "te,de->td", grad_branch, out_w, preferred_element_type=jnp.float32
    ).astype(jnp.bfloat16)
    grad_heads = swap(widen(group_heads(grad_mixed, reps), pad_to(hd, LANES)), 3)
    prev, own, after = window
    grad_q, grad_prev, grad_own, grad_after = attend_back(
        nh, hd, *bounds, prev, own, after, *ids, grad_heads.reshape(own.shape[0], -1), *kept
    )
    grad_kv, grad_q = from_heads(reps, grad_prev, grad_own, grad_after, grad_q, 4)
    grad_projected = jnp.concatenate(
        [ungroup_heads(grad_q[:, :, :hd]), ungroup_heads(grad_kv[:, :, :hd]), ungroup_heads(grad_kv[:, :, hd : 2 * hd])],
        axis=1,
    )
    grad_qkv_w = jnp.einsum("td,te->de", normed, grad_projected, preferred_element_type=jnp.float32).astype(jnp.bfloat16)
    sums = jnp.sum(grad_projected.astype(jnp.float32), axis=0)
    grad_qkv_b = jnp.concatenate([sums[:width], sums[2 * width :]])
    grad_normed = jnp.einsum("te,de->td", grad_projected, qkv_w, preferred_element_type=jnp.float32)
    _, norm_back_one = jax.vjp(pre_norm, stream, shift_one, scale_one)
    grad_stream_part, grad_shift_one, grad_scale_one = norm_back_one(grad_normed)
    grad_stream = grad_middle + grad_stream_part
    grad_mod = jnp.concatenate(
        [
            jnp.einsum("tl,tm->lm", pick, part, precision=HIGH, preferred_element_type=jnp.float32)
            for part in (
                grad_shift_one, grad_scale_one, grad_gate_one, grad_shift_two, grad_scale_two, grad_gate_two,
            )
        ],
        axis=1,
    )
    return (
        grad_stream, grad_mod, (grad_qkv_w, grad_out_w, grad_up_w, grad_down_w),
        (grad_qkv_b, grad_out_b, grad_up_b, grad_down_b),
    )


def gather_layer(params):
    rows = lambda value: lax.all_gather(value, "fsdp", axis=0, tiled=True)
    biases = jnp.concatenate([params[3], params[5], params[7], params[9]])
    biases = lax.all_gather(biases, "fsdp", axis=0)
    cuts = [0]
    for at in (3, 5, 7, 9):
        cuts.append(cuts[-1] + params[at].shape[0])
    qkv_b, out_b, up_b, down_b = (biases[:, a:b].reshape(-1) for a, b in zip(cuts[:-1], cuts[1:]))
    return (rows(params[2]), qkv_b, rows(params[4]), out_b, rows(params[6]), up_b, rows(params[8]), down_b)


def owner_sums(local_grads):
    shares = []
    for grad in local_grads:
        part = lax.psum_scatter(grad, "fsdp", scatter_dimension=0, tiled=True)
        shares.append(lax.psum(part, "replica").astype(jnp.float32))
    return shares


def attention_plan(latent_len, tok_rows, reps, device_at):
    column = tok_rows * reps
    edge = MAXLEN
    total = jnp.sum(latent_len)
    first = lax.axis_index("fsdp") * column
    positions = first - edge + jnp.arange(column + 2 * edge, dtype=jnp.int32)
    ends = jnp.cumsum(latent_len)
    ids = jnp.sum((ends[None, :] <= positions[:, None]).astype(jnp.int32), axis=1)
    ids = jnp.where(positions < 0, -1, ids)
    own = ids[edge : edge + column]
    count = column // BQ
    firsts, lasts = own[::BQ], own[BQ - 1 :: BQ]
    pick = lambda at: (at[:, None] == jnp.arange(latent_len.shape[0], dtype=jnp.int32)[None, :]).astype(jnp.int32)
    low = jnp.sum(pick(firsts) * (ends - latent_len)[None, :], axis=1) - (first - edge)
    high = jnp.sum(pick(lasts) * ends[None, :], axis=1) - (first - edge)
    bounds = ((low // BK).astype(jnp.int32), ((high + BK - 1) // BK).astype(jnp.int32))
    kid = jnp.broadcast_to(ids[:, None], (ids.shape[0], LANES))
    qid = jnp.broadcast_to(own[None, :], (8, column))
    return (reps, edge, bounds, (kid, qid))


def shards(
    tokens,
    cond,
    latent_len,
    first_ada_weight,
    first_ada_bias,
    first_qkv_weight,
    first_qkv_bias,
    first_out_weight,
    first_out_bias,
    first_up_weight,
    first_up_bias,
    first_down_weight,
    first_down_bias,
    second_ada_weight,
    second_ada_bias,
    second_qkv_weight,
    second_qkv_bias,
    second_out_weight,
    second_out_bias,
    second_up_weight,
    second_up_bias,
    second_down_weight,
    second_down_bias,
    cotangent,
):
    tok_rows = tokens.shape[0]
    group_place = lax.axis_index("fsdp")
    device_at = lax.axis_index(("fsdp", "replica"))
    token_total = tok_rows * lax.axis_size(("fsdp", "replica"))
    latent_count = cond.shape[0]
    local_pos = jnp.arange(tok_rows, dtype=jnp.int32)
    own_ids = latent_ids(latent_len, device_at * tok_rows + local_pos, token_total)
    pick = (own_ids[:, None] == jnp.arange(latent_count, dtype=jnp.int32)[None, :]).astype(
        jnp.float32
    )
    plan = attention_plan(latent_len, tok_rows, lax.axis_size("replica"), device_at)
    layers = (
        (
            first_ada_weight,
            first_ada_bias,
            first_qkv_weight,
            first_qkv_bias,
            first_out_weight,
            first_out_bias,
            first_up_weight,
            first_up_bias,
            first_down_weight,
            first_down_bias,
        ),
        (
            second_ada_weight,
            second_ada_bias,
            second_qkv_weight,
            second_qkv_bias,
            second_out_weight,
            second_out_bias,
            second_up_weight,
            second_up_bias,
            second_down_weight,
            second_down_bias,
        ),
    )
    col_width = first_ada_weight.shape[0]
    own_cond = lax.dynamic_slice_in_dim(
        cond.astype(jnp.float32), group_place * col_width, col_width, 1
    )
    own_silu = jax.nn.silu(own_cond).astype(jnp.bfloat16)
    partial_terms = []
    for params in layers:
        term = low_dot(own_silu, params[0])
        bias_share = params[1].astype(jnp.float32)
        spread = lax.dynamic_update_slice_in_dim(
            jnp.zeros((term.shape[1],), jnp.float32),
            bias_share,
            group_place * bias_share.shape[0],
            0,
        )
        partial_terms.append(term + spread[None, :])
    mod_first, mod_second = lax.psum((partial_terms[0], partial_terms[1]), "fsdp")
    mod_tokens = (
        jnp.dot(pick, mod_first, precision=HIGH, preferred_element_type=jnp.float32),
        jnp.dot(pick, mod_second, precision=HIGH, preferred_element_type=jnp.float32),
    )
    stream = tokens.astype(jnp.float32)
    inputs = []
    kept = []
    fulls = [gather_layer(params) for params in layers]
    for layer_at in range(2):
        inputs.append(stream)
        stream, saved = layer_forward(stream, mod_tokens[layer_at], fulls[layer_at], plan)
        kept.append(saved)
    output = stream.astype(jnp.bfloat16)
    grad_stream = cotangent.astype(jnp.float32)
    weight_grads = [None, None]
    mod_grads = [None, None]
    bias_grads = [None, None]
    for layer_at in (1, 0):
        grad_stream, grad_mod, local_grads, local_biases = layer_backward(
            inputs[layer_at], mod_tokens[layer_at], fulls[layer_at], kept[layer_at], plan, pick, grad_stream
        )
        weight_grads[layer_at] = owner_sums(local_grads)
        mod_grads[layer_at] = grad_mod
        bias_grads[layer_at] = local_biases
    flat = jnp.concatenate([part for grads in bias_grads for part in grads])
    grad_mod_first, grad_mod_second, flat = lax.psum((mod_grads[0], mod_grads[1], flat), ("fsdp", "replica"))
    place = 0
    bias_sums = []
    for grads in bias_grads:
        for part in grads:
            share = part.shape[0] // lax.axis_size("fsdp")
            bias_sums.append(lax.dynamic_slice_in_dim(flat, place + group_place * share, share, 0))
            place += part.shape[0]
    grad_silu = jnp.zeros(own_cond.shape, jnp.float32)
    ada_grads = []
    for params, grad_mod in zip(layers, (grad_mod_first, grad_mod_second)):
        low_mod = grad_mod.astype(jnp.bfloat16)
        weight_grad = jnp.einsum("ld,lm->dm", own_silu, low_mod, preferred_element_type=jnp.float32)
        column_sums = jnp.sum(low_mod.astype(jnp.float32), axis=0)
        bias_rows = params[1].shape[0]
        bias_grad = lax.dynamic_slice_in_dim(column_sums, group_place * bias_rows, bias_rows, 0)
        grad_silu = grad_silu + jnp.einsum(
            "lm,dm->ld", low_mod, params[0], preferred_element_type=jnp.float32
        )
        ada_grads.append((weight_grad, bias_grad))
    _, silu_back = jax.vjp(jax.nn.silu, own_cond)
    cond_grad = silu_back(grad_silu)[0]
    outs = [output, grad_stream, cond_grad]
    for layer_at in range(2):
        outs += list(ada_grads[layer_at])
        for weight, bias in zip(weight_grads[layer_at], bias_sums[4 * layer_at : 4 * layer_at + 4]):
            outs += [weight, bias]
    return tuple(outs)


def solution(mesh):
    in_specs = (
        P(("fsdp", "replica"), None),
        P(),
        P(),
        P("fsdp", None),
        P("fsdp"),
        P("fsdp", None),
        P("fsdp"),
        P("fsdp", None),
        P("fsdp"),
        P("fsdp", None),
        P("fsdp"),
        P("fsdp", None),
        P("fsdp"),
        P("fsdp", None),
        P("fsdp"),
        P("fsdp", None),
        P("fsdp"),
        P("fsdp", None),
        P("fsdp"),
        P("fsdp", None),
        P("fsdp"),
        P("fsdp", None),
        P("fsdp"),
        P(("fsdp", "replica"), None),
    )
    out_specs = (
        P(("fsdp", "replica"), None),
        P(("fsdp", "replica"), None),
        P(None, "fsdp"),
        P("fsdp", None),
        P("fsdp"),
        P("fsdp", None),
        P("fsdp"),
        P("fsdp", None),
        P("fsdp"),
        P("fsdp", None),
        P("fsdp"),
        P("fsdp", None),
        P("fsdp"),
        P("fsdp", None),
        P("fsdp"),
        P("fsdp", None),
        P("fsdp"),
        P("fsdp", None),
        P("fsdp"),
        P("fsdp", None),
        P("fsdp"),
        P("fsdp", None),
        P("fsdp"),
    )
    return jax.shard_map(shards, mesh=mesh, in_specs=in_specs, out_specs=out_specs, check_vma=False)
```

time: 3500 us -> 1750 us (0.50)
  waiting for transfers between devices: 1720 us -> 949 us
  matrix products: 835 us -> 213 us
  starting transfers between devices: 462 us -> 1.61 us
  Pallas kernels: 0 us -> 359 us
  local copies, waits for them, and re-layouts: 217 us -> 88.8 us
  other arithmetic: 121 us -> 49.5 us
  blocking collectives: 107 us -> 69.3 us
    dot_general x290 -> x12, matrix products: 577 us -> 14 us  [layer_backward(): jnp.einsum('tl,tm->lm', pick, part, precision=HIGH, preferred_element_typ...]
    ppermute x32 -> x0, starting transfers between devices: 460 us -> none  [shifted(): lax.ppermute(value, axis, [(source, source + steps) for source in range(f...]
    ppermute x32 -> x0, waiting for transfers between devices: 446 us -> none  [shifted(): lax.ppermute(value, axis, [(source, source + steps) for source in range(f...]
    reduce_scatter x8, waiting for transfers between devices: 822 us -> 403 us  [owner_sums(): part = lax.psum_scatter(grad, 'fsdp', scatter_dimension=0, tiled=True)]
    pallas_call x0 -> x12, Pallas kernels: none -> 359 us  [the longest x2 92.2 us: from_heads(): pl.pallas_call(functools.partial(from_heads_kernel, reps, size, edge), ou...]
    all_gather x8, waiting for transfers between devices: 46.5 us -> 187 us  [gather_layer(): rows = lambda value: lax.all_gather(value, 'fsdp', axis=0, tiled=True)]
    unnamed x283 -> x169, local copies, waits for them, and re-layouts: 123 us -> 7.41 us
    slice x13 -> x5, local copies, waits for them, and re-layouts: 59.4 us -> 0.33 us  [the longest x2 0.18 us: attention_plan(): firsts, lasts = (own[::BQ], own[BQ - 1::BQ])]
  transfers between devices with their start and end apart: 51 -> 19, of which waited for: 21 -> 12; matrix products, arithmetic and copies ran while one was open for 26% -> 15% of each run, Pallas kernels for 0% -> 15%
where the time goes in v1:
time: 1750 us
  waiting for transfers between devices  949 us (54%)
  Pallas kernels  359 us (21%)
  matrix products  213 us (12%)
  local copies, waits for them, and re-layouts  88.8 us (5%)
  blocking collectives  69.3 us (4%)
  other arithmetic  49.5 us (3%)
    reduce_scatter x8, waiting for transfers between devices, owner_sums(): part = lax.psum_scatter(grad, 'fsdp', scatter_dimension=0, tiled=True)  403 us
    psum x1, waiting for transfers between devices, owner_sums(): shares.append(lax.psum(part, 'replica').astype(jnp.float32))  284 us
    all_gather x8, waiting for transfers between devices, gather_layer(): rows = lambda value: lax.all_gather(value, 'fsdp', axis=0, tiled=True)  187 us
    pallas_call x2, Pallas kernels, from_heads(): pl.pallas_call(functools.partial(from_heads_kernel, reps, size, edge), ou...  92.2 us
    pallas_call x2, Pallas kernels, to_heads(): pl.pallas_call(functools.partial(to_heads_kernel, reps, size, edge, kv),...  84.8 us
    dot_general x10, matrix products, low_dot(): return jnp.dot(left, right, preferred_element_type=jnp.float32)  65.2 us
    pallas_call x2, Pallas kernels, attend_back(): pl.pallas_call(functools.partial(attend_back_kernel, nh, hd), out_shape=(...  64.4 us
    pallas_call x4, Pallas kernels, swap(): pl.pallas_call(functools.partial(swap_kernel, reps), out_shape=jax.ShapeD...  59.3 us
  transfers between devices with their start and end apart: 19, of which 12 were waited for; matrix products, arithmetic and copies ran while one was open for 15% of the time, Pallas kernels for 15%

profile of v1, /device:TPU:0, one launch (start us, length us, event | category | flops | bytes accessed | tf_op | source)
XLA Modules:
  0.0 1745.8 jit_solution(462652960799321587)
XLA Ops:
  20.1 10.5 all-gather.2
  43.1 29.6 %all-reduce.14.cloned.1.call-done = (f32[16,6912]{1,0:T(8,128)}, f32[16,6912]{1,0:T(8,128)}) async-done(((f32[16,6912]{1,0:T(8,128)}, f32[16,6912]{1,0:T(8,128)}), (f32[16,6912]{1,0:T(8,128)}, f32[16,6912]{1,0:T(8,128)})) %all-reduce.14.cloned.1.call-update) | async-done | bytes 884752 | tf_op jit(solution)/shard_map/psum | solution.py:742
  82.3 44.1 %all-gather.13.cloned.1.call-done = bf16[1152,3456]{1,0:T(8,128)(2,1)} async-done(((bf16[144,3456]{1,0:T(8,128)(2,1)}), bf16[1152,3456]{1,0:T(8,128)(2,1)}) %all-gather.13.cloned.1.call-update) | async-done | bytes 7962640 | tf_op jit(solution)/shard_map/all_gather | solution.py:624
  149.2 42.6 %shard_map.407 = (bf16[4,256,896]{2,1,0:T(8,128)(2,1)}, bf16[1024,640]{1,0:T(8,128)(2,1)}, bf16[1024,640]{1,0:T(8,128)(2,1)}) custom-call(bf16[4,256,896]{2,1,0:T(8,128)(2,1)} %fusion.23.x_ref), custom_call_target="tpu_custom_call" | custom-call | tf_op jit(solution)/shard_map/pallas_call | solution.py:351
  194.6 29.1 %shard_map.408 = (bf16[1024,384]{1,0:T(8,128)(2,1)}, f32[384,1024]{1,0:T(8,128)}, f32[8,1024]{1,0:T(8,128)}) custom-call(s32[4]{0:T(128)} %get-tuple-element.155.lo, s32[4]{0:T(128)} %get-tuple-element.154.hi, bf16[1024,640]{1,0:T(8,128)(2,1)} %get-tuple-element.47.prev, bf16[1024,896]{1,0:T(8,128)(2,1)} %bitcast.158, ...), custom_call_target="tpu_custom_call" | custom-call | flops 2147483648 | bytes 8388608 | tf_op jit(solution)/shard_map/pallas_call | solution.py:142
  223.8 13.3 shard_map.409
  257.2 52.0 %all-gather.19.cloned.1.call-done = bf16[4608,1152]{1,0:T(8,128)(2,1)} async-done(((bf16[576,1152]{1,0:T(8,128)(2,1)}), bf16[4608,1152]{1,0:T(8,128)(2,1)}) %all-gather.19.cloned.1.call-update) | async-done | bytes 10616848 | tf_op jit(solution)/shard_map/all_gather | solution.py:624
  309.2 10.6 fusion.114
  322.9 40.7 %all-gather.21.cloned.1.call-done = bf16[1152,3456]{1,0:T(8,128)(2,1)} async-done(((bf16[144,3456]{1,0:T(8,128)(2,1)}), bf16[1152,3456]{1,0:T(8,128)(2,1)}) %all-gather.21.cloned.1.call-update) | async-done | bytes 7962640 | tf_op jit(solution)/shard_map/all_gather | solution.py:624
  388.0 42.2 %shard_map.410 = (bf16[4,256,896]{2,1,0:T(8,128)(2,1)}, bf16[1024,640]{1,0:T(8,128)(2,1)}, bf16[1024,640]{1,0:T(8,128)(2,1)}) custom-call(bf16[4,256,896]{2,1,0:T(8,128)(2,1)} %fusion.25.x_ref), custom_call_target="tpu_custom_call" | custom-call | tf_op jit(solution)/shard_map/pallas_call | solution.py:351
  430.2 29.2 %shard_map.411 = (bf16[1024,384]{1,0:T(8,128)(2,1)}, f32[384,1024]{1,0:T(8,128)}, f32[8,1024]{1,0:T(8,128)}) custom-call(s32[4]{0:T(128)} %get-tuple-element.155.lo, s32[4]{0:T(128)} %get-tuple-element.154.hi, bf16[1024,640]{1,0:T(8,128)(2,1)} %get-tuple-element.51.prev, bf16[1024,896]{1,0:T(8,128)(2,1)} %bitcast.160, ...), custom_call_target="tpu_custom_call" | custom-call | flops 2147483648 | bytes 8388608 | tf_op jit(solution)/shard_map/pallas_call | solution.py:142
  459.4 13.4 shard_map.412
  486.0 10.0 fusion.123
  496.0 50.7 %all-gather.25.cloned.1.call-done = bf16[1152,4608]{1,0:T(8,128)(2,1)} async-done(((bf16[144,4608]{1,0:T(8,128)(2,1)}), bf16[1152,4608]{1,0:T(8,128)(2,1)}) %all-gather.25.cloned.1.call-update) | async-done | bytes 10616848 | tf_op jit(solution)/shard_map/all_gather | solution.py:624
  556.6 10.3 multiply_reduce_fusion.2
  566.9 10.2 fusion.112
  592.7 17.8 %shard_map.413 = bf16[4,256,384]{2,1,0:T(8,128)(2,1)} custom-call(bf16[4,256,384]{2,1,0:T(8,128)(2,1)} %pad.16.x_ref), custom_call_target="tpu_custom_call" | custom-call | tf_op jit(solution)/shard_map/pallas_call | solution.py:385
  610.5 32.2 %shard_map.414 = (bf16[1024,384]{1,0:T(8,128)(2,1)}, bf16[1024,640]{1,0:T(8,128)(2,1)}, bf16[1024,640]{1,0:T(8,128)(2,1)}, bf16[1024,640]{1,0:T(8,128)(2,1)}) custom-call(s32[4]{0:T(128)} %get-tuple-element.155.lo, s32[4]{0:T(128)} %get-tuple-element.154.hi, bf16[1024,640]{1,0:T(8,128)(2,1)} %get-tuple-element.51.prev, bf16[1024,896]{1,0:T(8,128)(2,1)} %bitcast.161, ...), custom_call_target="tpu_custom_call" | custom-call | flops 5368709120 | bytes 16777216 | tf_op jit(solution)/shard_map/pallas_call | solution.py:234
  642.8 39.0 %shard_map.415 = (bf16[4,256,640]{2,1,0:T(8,128)(2,1)}, bf16[4,256,384]{2,1,0:T(8,128)(2,1)}) custom-call(bf16[1024,640]{1,0:T(8,128)(2,1)} %get-tuple-element.57.dprev, bf16[1024,640]{1,0:T(8,128)(2,1)} %get-tuple-element.58.own, bf16[1024,640]{1,0:T(8,128)(2,1)} %get-tuple-element.59.dafter, bf16[1024,384]{1,0:T(8,128)(2,1)} %get-tuple-element.60.dq), custom_call_target="tpu_custom_call" | custom-call | tf_op jit(solution)/shard_map/pallas_call | solution.py:475
  747.5 14.8 shard_map.416
  762.4 32.2 %shard_map.417 = (bf16[1024,384]{1,0:T(8,128)(2,1)}, bf16[1024,640]{1,0:T(8,128)(2,1)}, bf16[1024,640]{1,0:T(8,128)(2,1)}, bf16[1024,640]{1,0:T(8,128)(2,1)}) custom-call(s32[4]{0:T(128)} %get-tuple-element.155.lo, s32[4]{0:T(128)} %get-tuple-element.154.hi, bf16[1024,640]{1,0:T(8,128)(2,1)} %get-tuple-element.47.prev, bf16[1024,896]{1,0:T(8,128)(2,1)} %bitcast.159, ...), custom_call_target="tpu_custom_call" | custom-call | flops 5368709120 | bytes 16777216 | tf_op jit(solution)/shard_map/pallas_call | solution.py:234
  794.6 53.2 %shard_map.418 = (bf16[4,256,640]{2,1,0:T(8,128)(2,1)}, bf16[4,256,384]{2,1,0:T(8,128)(2,1)}) custom-call(bf16[1024,640]{1,0:T(8,128)(2,1)} %get-tuple-element.65.dprev, bf16[1024,640]{1,0:T(8,128)(2,1)} %get-tuple-element.66.own, bf16[1024,640]{1,0:T(8,128)(2,1)} %get-tuple-element.67.dafter, bf16[1024,384]{1,0:T(8,128)(2,1)} %get-tuple-element.68.dq), custom_call_target="tpu_custom_call" | custom-call | tf_op jit(solution)/shard_map/pallas_call | solution.py:475
  875.9 10.7 convolution_convert_fusion
  886.7 10.6 convolution_convert_fusion.2
  910.1 61.0 %reduce-scatter.9.cloned.1.call-done = bf16[144,3456]{1,0:T(8,128)(2,1)} async-done(((bf16[1152,3456]{1,0:T(8,128)(2,1)}), bf16[144,3456]{1,0:T(8,128)(2,1)}) %reduce-scatter.9.cloned.1.call-update) | async-done | bytes 995344 | tf_op jit(solution)/shard_map/reduce_scatter | solution.py:637
  971.2 85.6 %reduce-scatter.21.cloned.1.call-done = bf16[144,4608]{1,0:T(8,128)(2,1)} async-done(((bf16[1152,4608]{1,0:T(8,128)(2,1)}), bf16[144,4608]{1,0:T(8,128)(2,1)}) %reduce-scatter.21.cloned.1.call-update) | async-done | bytes 1327120 | tf_op jit(solution)/shard_map/reduce_scatter | solution.py:637
  1056.8 85.6 %reduce-scatter.23.cloned.1.call-done = bf16[576,1152]{1,0:T(8,128)(2,1)} async-done(((bf16[4608,1152]{1,0:T(8,128)(2,1)}), bf16[576,1152]{1,0:T(8,128)(2,1)}) %reduce-scatter.23.cloned.1.call-update) | async-done | bytes 1327120 | tf_op jit(solution)/shard_map/reduce_scatter | solution.py:637
  1142.3 85.6 %reduce-scatter.15.cloned.1.call-done = bf16[576,1152]{1,0:T(8,128)(2,1)} async-done(((bf16[4608,1152]{1,0:T(8,128)(2,1)}), bf16[576,1152]{1,0:T(8,128)(2,1)}) %reduce-scatter.15.cloned.1.call-update) | async-done | bytes 1327120 | tf_op jit(solution)/shard_map/reduce_scatter | solution.py:637
  1228.0 85.6 %reduce-scatter.13.cloned.1.call-done = bf16[144,4608]{1,0:T(8,128)(2,1)} async-done(((bf16[1152,4608]{1,0:T(8,128)(2,1)}), bf16[144,4608]{1,0:T(8,128)(2,1)}) %reduce-scatter.13.cloned.1.call-update) | async-done | bytes 1327120 | tf_op jit(solution)/shard_map/reduce_scatter | solution.py:637
  1335.8 49.1 %all-reduce.17 = (bf16[16,6912]{1,0:T(8,128)(2,1)S(1)}, bf16[16,6912]{1,0:T(8,128)(2,1)S(1)}) all-reduce(f32[16,6912]{1,0:T(8,128)} %convolution_dynamic-update-slice_fusion.6, f32[16,6912]{1,0:T(8,128)S(1)} %copy-done.51), channel_id=1, replica_groups=mesh['fsdp'=8,'replica'=4] {'fsdp','replica'}, use_global_device_ids=true, to_apply=%region_23.24 | all-reduce | flops 221184 | bytes 1327104 | tf_op jit(solution)/shard_map/psum | solution.py:768
  1398.1 40.0 %all-reduce.12.cloned.1.call-done = f32[18432]{0:T(1024)} async-done(((f32[18432]{0:T(1024)}), f32[18432]{0:T(1024)}) %all-reduce.12.cloned.1.call-update) | async-done | bytes 73744 | tf_op jit(solution)/shard_map/psum | solution.py:768
  1442.3 283.5 %all-reduce.16.cloned.1.call-done = (bf16[144,3456]{1,0:T(8,128)(2,1)}, bf16[144,1152]{1,0:T(8,128)(2,1)}, bf16[144,4608]{1,0:T(8,128)(2,1)}, bf16[576,1152]{1,0...) async-done(((bf16[144,3456]{1,0:T(8,128)(2,1)}, bf16[144,1152]{1,0:T(8,128)(2,1)}, ...) | async-done | bytes 7962640 | tf_op jit(solution)/shard_map/psum | solution.py:638
  (385 shorter events, 305.3 us)
Async XLA Ops:
  7.2 65.5 %all-reduce.14.cloned.1.call-start = ((), (), s32[]{:S(2)}) async-start(), calls=%async_computation.25 | async-start | bytes 1769472 | tf_op jit(solution)/shard_map/psum | solution.py:742
  13.7 112.7 %all-gather.13.cloned.1.call-start = ((), (), s32[]{:S(2)}) async-start(), calls=%async_computation.8 | async-start | bytes 8957952 | tf_op jit(solution)/shard_map/all_gather | solution.py:624
  14.5 226.1 %all-gather.15.cloned.1.call-start = ((), (), s32[]{:S(2)}) async-start(), calls=%async_computation.9 | async-start | bytes 2985984 | tf_op jit(solution)/shard_map/all_gather | solution.py:624
  15.2 232.8 %all-gather.17.cloned.1.call-start = ((), (), s32[]{:S(2)}) async-start(), calls=%async_computation.10 | async-start | bytes 11943936 | tf_op jit(solution)/shard_map/all_gather | solution.py:624
  15.8 293.4 %all-gather.19.cloned.1.call-start = ((), (), s32[]{:S(2)}) async-start(), calls=%async_computation.11 | async-start | bytes 11943936 | tf_op jit(solution)/shard_map/all_gather | solution.py:624
  16.4 347.2 %all-gather.21.cloned.1.call-start = ((), (), s32[]{:S(2)}) async-start(), calls=%async_computation.12 | async-start | bytes 8957952 | tf_op jit(solution)/shard_map/all_gather | solution.py:624
  17.0 13.7 copy-start.67
  17.0 13.7 copy-start.69
  17.1 13.7 copy-start.73
  17.1 13.7 copy-start.74
  17.1 460.0 %all-gather.23.cloned.1.call-start = ((), (), s32[]{:S(2)}) async-start(), calls=%async_computation.13 | async-start | bytes 2985984 | tf_op jit(solution)/shard_map/all_gather | solution.py:624
  17.8 24.2 %copy-start.5 = (bf16[256,1152]{1,0:T(8,128)(2,1)S(1)}, bf16[256,1152]{1,0:T(8,128)(2,1)}, u32[]{:S(2)}) copy-start(bf16[256,1152]{1,0:T(8,128)(2,1)} %param.24) | copy-start | bytes 1769476
  17.8 468.1 %all-gather.27.cloned.1.call-start = ((), (), s32[]{:S(2)}) async-start(), calls=%async_computation.15 | async-start | bytes 11943936 | tf_op jit(solution)/shard_map/all_gather | solution.py:624
  18.6 528.1 %all-gather.25.cloned.1.call-start = ((), (), s32[]{:S(2)}) async-start(), calls=%async_computation.14 | async-start | bytes 11943936 | tf_op jit(solution)/shard_map/all_gather | solution.py:624
  19.3 890.7 %reduce-scatter.19.cloned.1.call-start = ((), (), s32[]{:S(2)}) async-start(), calls=%async_computation.22 | async-start | bytes 2985984 | tf_op jit(solution)/shard_map/reduce_scatter | solution.py:637
  42.2 39.7 %copy-start.60 = (f32[256]{0:T(256)}, f32[256]{0:T(256)S(1)}, u32[]{:S(2)}) copy-start(f32[256]{0:T(256)S(1)} %broadcast_multiply_fusion.3) | copy-start | bytes 3076
  42.5 34.2 %copy-start.64 = (f32[256]{0:T(256)}, f32[256]{0:T(256)S(1)}, u32[]{:S(2)}) copy-start(f32[256]{0:T(256)S(1)} %fusion.35) | copy-start | bytes 3076
  42.6 34.2 %copy-start.53 = (s32[256]{0:T(256)}, s32[256]{0:T(256)S(1)}, u32[]{:S(2)}) copy-start(s32[256]{0:T(256)S(1)} %and_select_fusion.2) | copy-start | bytes 3076
  42.6 39.3 %copy-start.62 = (f32[256]{0:T(256)}, f32[256]{0:T(256)S(1)}, u32[]{:S(2)}) copy-start(f32[256]{0:T(256)S(1)} %fusion.89) | copy-start | bytes 3076
  82.3 49.9 %copy-start.37 = (bf16[256,1152]{1,0:T(8,128)(2,1)}, bf16[256,1152]{1,0:T(8,128)(2,1)S(1)}, u32[]{:S(2)}) copy-start(bf16[256,1152]{1,0:T(8,128)(2,1)S(1)} %fusion.33) | copy-start | bytes 1769476
  703.4 206.7 %reduce-scatter.11.cloned.1.call-start = ((), (), s32[]{:S(2)}) async-start(), calls=%async_computation.18 | async-start | bytes 2985984 | tf_op jit(solution)/shard_map/reduce_scatter | solution.py:637
  703.5 11.9 slice-start
  706.2 18.6 %copy-start.21 = (f32[256,1152]{1,0:T(8,128)}, f32[256,1152]{1,0:T(8,128)S(1)}, u32[]{:S(2)}) copy-start(f32[256,1152]{1,0:T(8,128)S(1)} %get-tuple-element.91) | copy-start | bytes 3538948
  729.4 180.8 %reduce-scatter.17.cloned.1.call-start = ((), (), s32[]{:S(2)}) async-start(), calls=%async_computation.21 | async-start | bytes 8957952 | tf_op jit(solution)/shard_map/reduce_scatter | solution.py:637
  737.1 234.1 %reduce-scatter.9.cloned.1.call-start = ((), (), s32[]{:S(2)}) async-start(), calls=%async_computation.16 | async-start | bytes 8957952 | tf_op jit(solution)/shard_map/reduce_scatter | solution.py:637
  866.4 190.4 %reduce-scatter.21.cloned.1.call-start = ((), (), s32[]{:S(2)}) async-start(), calls=%async_computation.23 | async-start | bytes 11943936 | tf_op jit(solution)/shard_map/reduce_scatter | solution.py:637
  875.9 266.5 %reduce-scatter.23.cloned.1.call-start = ((), (), s32[]{:S(2)}) async-start(), calls=%async_computation.24 | async-start | bytes 11943936 | tf_op jit(solution)/shard_map/reduce_scatter | solution.py:637
  886.6 341.3 %reduce-scatter.15.cloned.1.call-start = ((), (), s32[]{:S(2)}) async-start(), calls=%async_computation.20 | async-start | bytes 11943936 | tf_op jit(solution)/shard_map/reduce_scatter | solution.py:637
  897.3 416.2 %reduce-scatter.13.cloned.1.call-start = ((), (), s32[]{:S(2)}) async-start(), calls=%async_computation.19 | async-start | bytes 11943936 | tf_op jit(solution)/shard_map/reduce_scatter | solution.py:637
  906.4 531.7 %all-reduce.12.cloned.1.call-start = ((), (), s32[]{:S(2)}) async-start(), calls=%async_computation.17 | async-start | bytes 147456 | tf_op jit(solution)/shard_map/psum | solution.py:768
  910.0 815.8 %all-reduce.16.cloned.1.call-start = ((), (), s32[]{:S(2)}) async-start(), calls=%async_computation.26 | async-start | bytes 15925248 | tf_op jit(solution)/shard_map/psum | solution.py:638
  1334.6 51.8 %copy-start.65 = (f32[256]{0:T(256)S(1)}, f32[256]{0:T(256)}, u32[]{:S(2)}) copy-start(f32[256]{0:T(256)} %copy-done.64) | copy-start | bytes 3076
  (65 other events, 236.2 us)
Sparse Core Ops, SparseCore 0:
  13.9 58.7 all-reduce.13
  74.6 51.7 all-gather.12
  128.3 30.2 all-gather.14
  160.3 78.1 all-gather.16
  240.2 68.9 all-gather.18
  311.0 52.5 all-gather.20
  365.5 30.2 all-gather.22
  397.6 79.3 all-gather.26
  478.9 67.7 all-gather.24
  703.6 65.3 reduce-scatter.18
  773.5 43.7 reduce-scatter.10
  820.7 76.4 reduce-scatter.16
  901.1 69.9 reduce-scatter.8
  974.5 82.2 reduce-scatter.20
  1060.1 82.1 reduce-scatter.22
  1145.7 82.2 reduce-scatter.14
  1231.3 82.1 reduce-scatter.12
  1319.5 118.5 all-reduce.11
  1441.6 284.1 all-reduce.15

commit v2 on v1

--- a/solution.py
+++ b/solution.py
@@ -496,6 +496,228 @@
     )(dprev, own, dafter, dq)
 
 
+UNITS = 12
+LEFT_ROWS = 4
+
+
+def reduce_kernel(layers, width, half, *refs):
+    count = layers * UNITS
+    ins, refs = refs[: 8 * layers], refs[8 * layers :]
+    (out, left, right, csend, crecv, own, xs, xr, ys, yr, tx, ty, x2s, x2r, y2s, y2r, zs, z1r, z2s, z2r, fin,
+     load_sem, core_s, core_r, x_s, x_r, y_s, y_r, x2_s, x2_r, y2_s, y2_r, z1_s, z1_r, z2_s, z2_r, fin_l, fin_s, fin_r,
+     credit) = refs
+    f, r = lax.axis_index("fsdp"), lax.axis_index("replica")
+    rows = own.shape[1]
+    tokens = left.shape[1]
+    c, x, y = lax.rem(f, 2), lax.rem(f // 2, 2), f // 4
+    core_at, x_at, y_at = f + 1 - 2 * c, f + 2 - 4 * x, f + 4 - 8 * y
+    inner = jnp.logical_and(r > 0, r < 3)
+    outer = jnp.logical_not(inner)
+    z_at = r + 1 - 2 * lax.rem(r, 2)
+    greet(
+        [((core_at, r), True), ((x_at, r), True), ((y_at, r), True), ((f, r - 1), r > 0), ((f, r + 1), r < 3)],
+        3 + (r > 0).astype(jnp.int32) + (r < 3).astype(jnp.int32),
+    )
+    loads = []
+    for layer in range(layers):
+        place = layer * (LEFT_ROWS + 3) * width
+        for at in range(4):
+            src = ins[8 * layer + at]
+            loads.append((src, left.at[pl.ds(place, src.shape[0]), :]))
+            place += src.shape[0]
+        slot = layer * 9
+        for at in range(4):
+            src = ins[8 * layer + 4 + at]
+            for part in range(src.shape[1] // width):
+                loads.append((src.at[:, pl.ds(part * width, width)], right.at[slot]))
+                slot += 1
+    for at, (src, dst) in enumerate(loads):
+        pltpu.make_async_copy(src, dst, load_sem.at[at]).start()
+    for at, (src, dst) in enumerate(loads):
+        pltpu.make_async_copy(src, dst, load_sem.at[at]).wait()
+
+    def send(src, dst, s_sem, r_sem, where):
+        return pltpu.make_async_remote_copy(
+            src_ref=src, dst_ref=dst, send_sem=s_sem, recv_sem=r_sem, device_id=where, device_id_type=MESH
+        )
+
+    def term(u, core, mx, my):
+        layer, w = u // UNITS, lax.rem(u, UNITS)
+        block = ((y + my * (1 - 2 * y)) * 2 + (x + mx * (1 - 2 * x))) * 2 + (c + core * (1 - 2 * c))
+        inside = jnp.where(
+            w < 4, rows * w, LEFT_ROWS * width + jnp.where(w < 8, 0, jnp.where(w < 9, width, 2 * width))
+        )
+        stride = jnp.where(w < 4, 4 * rows, rows)
+        start = pl.multiple_of(layer * ((LEFT_ROWS + 3) * width) + inside + stride * block, 16)
+        other = layer * 9 + jnp.maximum(w - 3, 0)
+        return nn_dot(left[pl.ds(start, rows), :], right[other])
+
+    places = ((0, 0), (1, 0), (0, 1), (1, 1))
+    top, low = pl.ds(0, half), pl.ds(half, rows - half)
+
+    def core_copy(slot):
+        return send(csend.at[slot], crecv.at[slot], core_s.at[slot], core_r.at[slot], (core_at, r))
+
+    def x_copy(slot):
+        return send(xs.at[slot], xr.at[slot], x_s.at[slot], x_r.at[slot], (x_at, r))
+
+    def y_copy(slot):
+        return send(ys.at[slot], yr.at[slot], y_s.at[slot], y_r.at[slot], (y_at, r))
+
+    def x2_copy(slot):
+        return send(x2s.at[slot], x2r.at[slot], x2_s.at[slot], x2_r.at[slot], (x_at, r))
+
+    def y2_copy(slot):
+        return send(y2s.at[slot], y2r.at[slot], y2_s.at[slot], y2_r.at[slot], (y_at, r))
+
+    def z1_copy(slot, to):
+        return send(zs.at[slot], z1r.at[to], z1_s.at[slot], z1_r.at[to], (f, z_at))
+
+    def z2_copy(slot):
+        return send(z2s.at[slot], z2r.at[slot], z2_s.at[slot], z2_r.at[slot], (f, 3 - r))
+
+    def fin_copy(slot, u):
+        return send(fin.at[slot], out.at[u], fin_s.at[slot], fin_r.at[u], (f, z_at))
+
+    def keep_copy(slot, u):
+        return pltpu.make_async_copy(fin.at[slot], out.at[u], fin_l.at[slot])
+
+    f32, bf16 = jnp.float32, jnp.bfloat16
+    z_slots = z1r.shape[0]
+
+    def stage(u, condition, body):
+        live = jnp.logical_and(u >= 0, u < count)
+        pl.when(live if condition is None else jnp.logical_and(live, condition))(lambda: body(u))
+
+    def close(u):
+        slot = lax.rem(u, 4)
+        fin_copy(slot, u).wait_send()
+        keep_copy(slot, u).wait()
+
+    def arrive(u):
+        fin_copy(lax.rem(u, 4), u).wait_recv()
+
+    def finish(u):
+        slot = lax.rem(u, 4)
+        z2_copy(slot).wait()
+        fin[slot] = (z2s[slot].astype(f32) + z2r[slot].astype(f32)).astype(bf16)
+        fin_copy(slot, u).start()
+        keep_copy(slot, u).start()
+
+    def middle(u):
+        slot, z_slot, at = lax.rem(u, 4), lax.rem(u, z_slots), lax.rem(u, own.shape[0])
+        z1_copy(slot, z_slot).wait_recv()
+        z2s[slot] = (own[at] + z1r[z_slot].astype(f32)).astype(bf16)
+        z2_copy(slot).start()
+
+        @pl.when(u + z_slots < count)
+        def _():
+            pl.semaphore_signal(credit, inc=1, device_id=(f, z_at), device_id_type=MESH)
+
+    def sent(u):
+        z1_copy(lax.rem(u, 4), lax.rem(u, z_slots)).wait_send()
+
+    def plane(u):
+        slot, at = lax.rem(u, 4), lax.rem(u, own.shape[0])
+        x2_copy(slot).wait()
+        y2_copy(slot).wait()
+        own[at, top, :] += y2r[slot].astype(f32)
+        own[at, low, :] += x2r[slot].astype(f32)
+
+        @pl.when(outer)
+        def _():
+            zs[slot] = own[at].astype(bf16)
+
+            @pl.when(u >= z_slots)
+            def _():
+                pl.semaphore_wait(credit, 1)
+
+            z1_copy(slot, lax.rem(u, z_slots)).start()
+
+    def cross(u):
+        slot, at = lax.rem(u, 4), lax.rem(u, own.shape[0])
+        x_copy(slot).wait()
+        y_copy(slot).wait()
+        y2s[slot] = (ty[slot] + xr[slot, 1].astype(f32)).astype(bf16)
+        y2_copy(slot).start()
+        x2s[slot] = (tx[slot] + yr[slot, 1].astype(f32)).astype(bf16)
+        x2_copy(slot).start()
+        own[at, top, :] += xr[slot, 0].astype(f32)
+        own[at, low, :] += yr[slot, 0].astype(f32)
+
+    def chip(u):
+        slot, pair, at = lax.rem(u, 4), lax.rem(u, 2), lax.rem(u, own.shape[0])
+        core_copy(pair).wait()
+        total = term(u, 0, 1, 1) + crecv[pair, 3].astype(f32)
+        xs[slot, 1] = total[:half].astype(bf16)
+        ys[slot, 1] = total[half:].astype(bf16)
+        total = term(u, 0, 1, 0) + crecv[pair, 1].astype(f32)
+        xs[slot, 0] = total[:half].astype(bf16)
+        tx[slot] = total[half:]
+        x_copy(slot).start()
+        total = term(u, 0, 0, 1) + crecv[pair, 2].astype(f32)
+        ys[slot, 0] = total[half:].astype(bf16)
+        ty[slot] = total[:half]
+        y_copy(slot).start()
+        own[at] = term(u, 0, 0, 0) + crecv[pair, 0].astype(f32)
+
+    def open_unit(u):
+        pair = lax.rem(u, 2)
+        for m, (mx, my) in enumerate(places):
+            csend[pair, m] = term(u, 1, mx, my).astype(bf16)
+        core_copy(pair).start()
+
+    def step(t, carry):
+        stage(t - 11, inner, close)
+        stage(t - 11, outer, arrive)
+        stage(t - 9, inner, finish)
+        stage(t - 7, inner, middle)
+        stage(t - 7, outer, sent)
+        stage(t - 5, None, plane)
+        stage(t - 3, None, cross)
+        stage(t - 1, None, chip)
+        stage(t, None, open_unit)
+        return carry
+
+    lax.fori_loop(0, count + 11, step, 0)
+
+
+def reduce_grads(pairs):
+    layers = len(pairs)
+    width, tokens = pairs[0][0][1].shape
+    rows = width // 8
+    half = pad_to(rows // 2, 16)
+    ins = [part for lefts, rights in pairs for part in (*lefts, *rights)]
+    count = layers * UNITS
+    bf16, f32 = jnp.bfloat16, jnp.float32
+    buf = lambda dtype, *shape: pltpu.VMEM((*shape, width), dtype)
+    sem = lambda size: pltpu.SemaphoreType.DMA((size,))
+    z_slots = 8
+    return pl.pallas_call(
+        functools.partial(reduce_kernel, layers, width, half),
+        out_shape=jax.ShapeDtypeStruct((count, rows, width), bf16),
+        in_specs=[HB] * len(ins),
+        out_specs=HB,
+        scratch_shapes=[
+            pltpu.VMEM((layers * (LEFT_ROWS + 3) * width, tokens), bf16),
+            buf(bf16, layers * 9, tokens),
+            buf(bf16, 2, 4, rows), buf(bf16, 2, 4, rows), buf(f32, 9, rows),
+            buf(bf16, 4, 2, half), buf(bf16, 4, 2, half), buf(bf16, 4, 2, rows - half), buf(bf16, 4, 2, rows - half),
+            buf(f32, 4, rows - half), buf(f32, 4, half),
+            buf(bf16, 4, rows - half), buf(bf16, 4, rows - half), buf(bf16, 4, half), buf(bf16, 4, half),
+            buf(bf16, 4, rows), buf(bf16, z_slots, rows), buf(bf16, 4, rows), buf(bf16, 4, rows), buf(bf16, 4, rows),
+            sem(13 * layers), sem(2), sem(2), sem(4), sem(4), sem(4), sem(4), sem(4), sem(4), sem(4), sem(4),
+            sem(4), sem(z_slots), sem(4), sem(4), sem(4), sem(4), sem(count), pltpu.SemaphoreType.REGULAR,
+        ],
+        compiler_params=pltpu.CompilerParams(
+            collective_id=5, has_side_effects=True, vmem_limit_bytes=60 * 1024 * 1024
+        ),
+        cost_estimate=pl.CostEstimate(
+            flops=2 * count * 8 * rows * tokens * width, bytes_accessed=100 << 20, transcendentals=0
+        ),
+    )(*ins)
+
+
 def pre_norm(stream, shift, scale):
     centred = stream - jnp.mean(stream, axis=-1, keepdims=True)
     spread = jnp.mean(centred * centred, axis=-1, keepdims=True)
@@ -570,12 +792,10 @@
     shift_one, scale_one, gate_one, shift_two, scale_two, gate_two = jnp.split(mod_tok, 6, axis=1)
     grad_result = (gate_two * grad_next).astype(jnp.bfloat16)
     grad_gate_two = grad_next * result
-    grad_down_w = jnp.einsum("tf,td->fd", active, grad_result, preferred_element_type=jnp.float32).astype(jnp.bfloat16)
     grad_down_b = jnp.sum(grad_result.astype(jnp.float32), axis=0)
     grad_active = jnp.einsum("td,fd->tf", grad_result, down_w, preferred_element_type=jnp.float32)
     _, gelu_back = jax.vjp(gelu_tanh, hidden)
     grad_hidden = gelu_back(grad_active)[0].astype(jnp.bfloat16)
-    grad_up_w = jnp.einsum("td,tf->df", normed_two, grad_hidden, preferred_element_type=jnp.float32).astype(jnp.bfloat16)
     grad_up_b = jnp.sum(grad_hidden.astype(jnp.float32), axis=0)
     grad_normed_two = jnp.einsum("tf,df->td", grad_hidden, up_w, preferred_element_type=jnp.float32)
     _, norm_back_two = jax.vjp(pre_norm, middle, shift_two, scale_two)
@@ -583,7 +803,6 @@
     grad_middle = grad_next + grad_middle_part
     grad_branch = (gate_one * grad_middle).astype(jnp.bfloat16)
     grad_gate_one = grad_middle * branch
-    grad_out_w = jnp.einsum("td,te->de", mixed, grad_branch, preferred_element_type=jnp.float32).astype(jnp.bfloat16)
     grad_out_b = jnp.sum(grad_branch.astype(jnp.float32), axis=0)
     grad_mixed = jnp.einsum(
         "te,de->td", grad_branch, out_w, preferred_element_type=jnp.float32
@@ -598,7 +817,6 @@
         [ungroup_heads(grad_q[:, :, :hd]), ungroup_heads(grad_kv[:, :, :hd]), ungroup_heads(grad_kv[:, :, hd : 2 * hd])],
         axis=1,
     )
-    grad_qkv_w = jnp.einsum("td,te->de", normed, grad_projected, preferred_element_type=jnp.float32).astype(jnp.bfloat16)
     sums = jnp.sum(grad_projected.astype(jnp.float32), axis=0)
     grad_qkv_b = jnp.concatenate([sums[:width], sums[2 * width :]])
     grad_normed = jnp.einsum("te,de->td", grad_projected, qkv_w, preferred_element_type=jnp.float32)
@@ -615,7 +833,8 @@
         axis=1,
     )
     return (
-        grad_stream, grad_mod, (grad_qkv_w, grad_out_w, grad_up_w, grad_down_w),
+        grad_stream, grad_mod,
+        ((active.T, normed_two.T, mixed.T, normed.T), (grad_result, grad_hidden, grad_branch, grad_projected)),
         (grad_qkv_b, grad_out_b, grad_up_b, grad_down_b),
     )
 
@@ -631,11 +850,26 @@
     return (rows(params[2]), qkv_b, rows(params[4]), out_b, rows(params[6]), up_b, rows(params[8]), down_b)
 
 
-def owner_sums(local_grads):
+def owner_sums(pairs):
+    if lax.axis_size("fsdp") == 8 and lax.axis_size("replica") == 4:
+        units = reduce_grads(pairs).reshape(len(pairs), UNITS, -1, pairs[0][0][1].shape[0])
+        rows, width = units.shape[2:]
+        across = lambda part: part.transpose(1, 0, 2).reshape(rows, -1).astype(jnp.float32)
+        return [
+            (
+                across(unit[9:12]), across(unit[8:9]), across(unit[4:8]),
+                unit[0:4].reshape(-1, width).astype(jnp.float32),
+            )
+            for unit in units
+        ]
     shares = []
-    for grad in local_grads:
-        part = lax.psum_scatter(grad, "fsdp", scatter_dimension=0, tiled=True)
-        shares.append(lax.psum(part, "replica").astype(jnp.float32))
+    for lefts, rights in pairs:
+        grads = []
+        for left, right in zip(lefts, rights):
+            grad = low_dot(left, right).astype(jnp.bfloat16)
+            part = lax.psum_scatter(grad, "fsdp", scatter_dimension=0, tiled=True)
+            grads.append(lax.psum(part, "replica").astype(jnp.float32))
+        shares.append(grads[::-1])
     return shares
 
 
@@ -754,16 +988,17 @@
         kept.append(saved)
     output = stream.astype(jnp.bfloat16)
     grad_stream = cotangent.astype(jnp.float32)
-    weight_grads = [None, None]
+    weight_pairs = [None, None]
     mod_grads = [None, None]
     bias_grads = [None, None]
     for layer_at in (1, 0):
         grad_stream, grad_mod, local_grads, local_biases = layer_backward(
             inputs[layer_at], mod_tokens[layer_at], fulls[layer_at], kept[layer_at], plan, pick, grad_stream
         )
-        weight_grads[layer_at] = owner_sums(local_grads)
+        weight_pairs[layer_at] = local_grads
         mod_grads[layer_at] = grad_mod
         bias_grads[layer_at] = local_biases
+    weight_grads = owner_sums(weight_pairs)
     flat = jnp.concatenate([part for grads in bias_grads for part in grads])
     grad_mod_first, grad_mod_second, flat = lax.psum((mod_grads[0], mod_grads[1], flat), ("fsdp", "replica"))
     place = 0

time: 1750 us -> 1450 us (0.83)
  waiting for transfers between devices: 949 us -> 313 us
  Pallas kernels: 359 us -> 709 us
  matrix products: 213 us -> 150 us
  local copies, waits for them, and re-layouts: 88.8 us -> 127 us
    reduce_scatter x8 -> x0, waiting for transfers between devices: 403 us -> none  [owner_sums(): part = lax.psum_scatter(grad, 'fsdp', scatter_dimension=0, tiled=True)]
    pallas_call x0 -> x1, Pallas kernels: none -> 336 us  [reduce_grads(): pl.pallas_call(functools.partial(reduce_kernel, layers, width, half), out...]
    psum x1 -> x0, waiting for transfers between devices: 284 us -> none  [owner_sums(): shares.append(lax.psum(part, 'replica').astype(jnp.float32))]
    psum x1, waiting for transfers between devices: 40 us -> 100 us  [shards(): lax.psum((mod_grads[0], mod_grads[1], flat), ('fsdp', 'replica'))]
    dot_general x8 -> x0, matrix products: 58.3 us -> none  [the longest x2 21.3 us: layer_backward(): jnp.einsum('tf,td->fd', active, grad_result, preferred_element_type=jnp.f...]
  transfers between devices with their start and end apart: 19 -> 10, of which waited for: 12 -> 6; matrix products, arithmetic and copies ran while one was open for 15% -> 9% of each run, Pallas kernels for 15% -> 12%
where the time goes in v2:
time: 1450 us; the launch traced here: 1440 us
  Pallas kernels  709 us (49%)
  waiting for transfers between devices  313 us (22%)
  matrix products  150 us (10%)
  local copies, waits for them, and re-layouts  127 us (9%)
  blocking collectives  68.1 us (5%)
  other arithmetic  56.3 us (4%)
  between operations  15.5 us (1%)
    pallas_call x1, Pallas kernels, reduce_grads(): pl.pallas_call(functools.partial(reduce_kernel, layers, width, half), out...  336 us
    all_gather x8, waiting for transfers between devices, gather_layer(): rows = lambda value: lax.all_gather(value, 'fsdp', axis=0, tiled=True)  178 us
    psum x1, waiting for transfers between devices, shards(): lax.psum((mod_grads[0], mod_grads[1], flat), ('fsdp', 'replica'))  100 us
    pallas_call x2, Pallas kernels, to_heads(): pl.pallas_call(functools.partial(to_heads_kernel, reps, size, edge, kv),...  84.7 us
    pallas_call x2, Pallas kernels, from_heads(): pl.pallas_call(functools.partial(from_heads_kernel, reps, size, edge), ou...  83.8 us
    pallas_call x4, Pallas kernels, swap(): pl.pallas_call(functools.partial(swap_kernel, reps), out_shape=jax.ShapeD...  74.1 us
    pallas_call x2, Pallas kernels, attend_back(): pl.pallas_call(functools.partial(attend_back_kernel, nh, hd), out_shape=(...  67.7 us
    dot_general x10, matrix products, low_dot(): return jnp.dot(left, right, preferred_element_type=jnp.float32)  66.4 us
  transfers between devices with their start and end apart: 10, of which 6 were waited for; matrix products, arithmetic and copies ran while one was open for 9% of the time, Pallas kernels for 12%

profile of v2, /device:TPU:0, one launch (start us, length us, event | category | flops | bytes accessed | tf_op | source)
XLA Modules:
  0.0 1439.2 jit_solution(9413012056997794845)
XLA Ops:
  20.1 10.6 all-gather.2
  31.0 9.3 all-gather.3
  42.8 29.8 %all-reduce.12.cloned.1.call-done = (f32[16,6912]{1,0:T(8,128)}, f32[16,6912]{1,0:T(8,128)}) async-done(((f32[16,6912]{1,0:T(8,128)}, f32[16,6912]{1,0:T(8,128)}), (f32[16,6912]{1,0:T(8,128)}, f32[16,6912]{1,0:T(8,128)})) %all-reduce.12.cloned.1.call-update) | async-done | bytes 884752 | tf_op jit(solution)/shard_map/psum | solution.py:976
  87.1 39.2 %all-gather.13.cloned.1.call-done = bf16[1152,3456]{1,0:T(8,128)(2,1)} async-done(((bf16[144,3456]{1,0:T(8,128)(2,1)}), bf16[1152,3456]{1,0:T(8,128)(2,1)}) %all-gather.13.cloned.1.call-update) | async-done | bytes 7962640 | tf_op jit(solution)/shard_map/all_gather | solution.py:843
  148.1 42.5 %shard_map.407 = (bf16[4,256,896]{2,1,0:T(8,128)(2,1)}, bf16[1024,640]{1,0:T(8,128)(2,1)}, bf16[1024,640]{1,0:T(8,128)(2,1)}) custom-call(bf16[4,256,896]{2,1,0:T(8,128)(2,1)} %fusion.47.x_ref), custom_call_target="tpu_custom_call" | custom-call | tf_op jit(solution)/shard_map/pallas_call | solution.py:351
  193.4 31.4 %shard_map.408 = (bf16[1024,384]{1,0:T(8,128)(2,1)}, f32[384,1024]{1,0:T(8,128)}, f32[8,1024]{1,0:T(8,128)}) custom-call(s32[4]{0:T(128)} %get-tuple-element.161.lo, s32[4]{0:T(128)} %get-tuple-element.160.hi, bf16[1024,640]{1,0:T(8,128)(2,1)} %get-tuple-element.47.prev, bf16[1024,896]{1,0:T(8,128)(2,1)} %bitcast.184, ...), custom_call_target="tpu_custom_call" | custom-call | flops 2147483648 | bytes 8388608 | tf_op jit(solution)/shard_map/pallas_call | solution.py:142
  224.8 13.3 shard_map.409
  248.3 10.4 fusion.23
  258.6 50.5 %all-gather.19.cloned.1.call-done = bf16[4608,1152]{1,0:T(8,128)(2,1)} async-done(((bf16[576,1152]{1,0:T(8,128)(2,1)}), bf16[4608,1152]{1,0:T(8,128)(2,1)}) %all-gather.19.cloned.1.call-update) | async-done | bytes 10616848 | tf_op jit(solution)/shard_map/all_gather | solution.py:843
  309.2 10.6 fusion.144
  322.9 40.7 %all-gather.21.cloned.1.call-done = bf16[1152,3456]{1,0:T(8,128)(2,1)} async-done(((bf16[144,3456]{1,0:T(8,128)(2,1)}), bf16[1152,3456]{1,0:T(8,128)(2,1)}) %all-gather.21.cloned.1.call-update) | async-done | bytes 7962640 | tf_op jit(solution)/shard_map/all_gather | solution.py:843
  388.0 42.2 %shard_map.410 = (bf16[4,256,896]{2,1,0:T(8,128)(2,1)}, bf16[1024,640]{1,0:T(8,128)(2,1)}, bf16[1024,640]{1,0:T(8,128)(2,1)}) custom-call(bf16[4,256,896]{2,1,0:T(8,128)(2,1)} %fusion.49.x_ref), custom_call_target="tpu_custom_call" | custom-call | tf_op jit(solution)/shard_map/pallas_call | solution.py:351
  430.2 31.2 %shard_map.411 = (bf16[1024,384]{1,0:T(8,128)(2,1)}, f32[384,1024]{1,0:T(8,128)}, f32[8,1024]{1,0:T(8,128)}) custom-call(s32[4]{0:T(128)} %get-tuple-element.161.lo, s32[4]{0:T(128)} %get-tuple-element.160.hi, bf16[1024,640]{1,0:T(8,128)(2,1)} %get-tuple-element.51.prev, bf16[1024,896]{1,0:T(8,128)(2,1)} %bitcast.186, ...), custom_call_target="tpu_custom_call" | custom-call | flops 2147483648 | bytes 8388608 | tf_op jit(solution)/shard_map/pallas_call | solution.py:142
  461.4 13.4 shard_map.412
  488.2 11.1 fusion.154
  499.3 47.3 %all-gather.25.cloned.1.call-done = bf16[1152,4608]{1,0:T(8,128)(2,1)} async-done(((bf16[144,4608]{1,0:T(8,128)(2,1)}), bf16[1152,4608]{1,0:T(8,128)(2,1)}) %all-gather.25.cloned.1.call-update) | async-done | bytes 10616848 | tf_op jit(solution)/shard_map/all_gather | solution.py:843
  546.6 10.4 convert_reduce_fusion
  557.0 8.6 multiply_reduce_fusion.2
  568.5 9.8 fusion.142
  589.5 17.8 %shard_map.413 = bf16[4,256,384]{2,1,0:T(8,128)(2,1)} custom-call(bf16[4,256,384]{2,1,0:T(8,128)(2,1)} %pad.16.x_ref), custom_call_target="tpu_custom_call" | custom-call | tf_op jit(solution)/shard_map/pallas_call | solution.py:385
  607.3 34.0 %shard_map.414 = (bf16[1024,384]{1,0:T(8,128)(2,1)}, bf16[1024,640]{1,0:T(8,128)(2,1)}, bf16[1024,640]{1,0:T(8,128)(2,1)}, bf16[1024,640]{1,0:T(8,128)(2,1)}) custom-call(s32[4]{0:T(128)} %get-tuple-element.161.lo, s32[4]{0:T(128)} %get-tuple-element.160.hi, bf16[1024,640]{1,0:T(8,128)(2,1)} %get-tuple-element.51.prev, bf16[1024,896]{1,0:T(8,128)(2,1)} %bitcast.187, ...), custom_call_target="tpu_custom_call" | custom-call | flops 5368709120 | bytes 16777216 | tf_op jit(solution)/shard_map/pallas_call | solution.py:234
  641.3 41.3 %shard_map.415 = (bf16[4,256,640]{2,1,0:T(8,128)(2,1)}, bf16[4,256,384]{2,1,0:T(8,128)(2,1)}) custom-call(bf16[1024,640]{1,0:T(8,128)(2,1)} %get-tuple-element.57.dprev, bf16[1024,640]{1,0:T(8,128)(2,1)} %get-tuple-element.58.own, bf16[1024,640]{1,0:T(8,128)(2,1)} %get-tuple-element.59.dafter, bf16[1024,384]{1,0:T(8,128)(2,1)} %get-tuple-element.60.dq), custom_call_target="tpu_custom_call" | custom-call | tf_op jit(solution)/shard_map/pallas_call | solution.py:475
  702.5 6.9 multiply_reduce_fusion.1
  714.2 9.1 convert_reduce_fusion.1
  723.3 8.3 multiply_reduce_fusion
  743.6 29.6 %shard_map.416 = bf16[4,256,384]{2,1,0:T(8,128)(2,1)} custom-call(bf16[4,256,384]{2,1,0:T(8,128)(2,1)} %pad.17.x_ref), custom_call_target="tpu_custom_call" | custom-call | tf_op jit(solution)/shard_map/pallas_call | solution.py:385
  773.2 33.7 %shard_map.417 = (bf16[1024,384]{1,0:T(8,128)(2,1)}, bf16[1024,640]{1,0:T(8,128)(2,1)}, bf16[1024,640]{1,0:T(8,128)(2,1)}, bf16[1024,640]{1,0:T(8,128)(2,1)}) custom-call(s32[4]{0:T(128)} %get-tuple-element.161.lo, s32[4]{0:T(128)} %get-tuple-element.160.hi, bf16[1024,640]{1,0:T(8,128)(2,1)} %get-tuple-element.47.prev, bf16[1024,896]{1,0:T(8,128)(2,1)} %bitcast.185, ...), custom_call_target="tpu_custom_call" | custom-call | flops 5368709120 | bytes 16777216 | tf_op jit(solution)/shard_map/pallas_call | solution.py:234
  807.0 42.5 %shard_map.418 = (bf16[4,256,640]{2,1,0:T(8,128)(2,1)}, bf16[4,256,384]{2,1,0:T(8,128)(2,1)}) custom-call(bf16[1024,640]{1,0:T(8,128)(2,1)} %get-tuple-element.65.dprev, bf16[1024,640]{1,0:T(8,128)(2,1)} %get-tuple-element.66.own, bf16[1024,640]{1,0:T(8,128)(2,1)} %get-tuple-element.67.dafter, bf16[1024,384]{1,0:T(8,128)(2,1)} %get-tuple-element.68.dq), custom_call_target="tpu_custom_call" | custom-call | tf_op jit(solution)/shard_map/pallas_call | solution.py:475
  883.1 336.3 %shard_map.419 = bf16[24,144,1152]{2,1,0:T(8,128)(2,1)} custom-call(bf16[4608,256]{1,0:T(8,128)(2,1)} %copy.175.refs_0_, bf16[1152,256]{1,0:T(8,128)(2,1)} %copy.176.refs_1_, bf16[1152,256]{1,0:T(8,128)(2,1)} %bitcast.170, bf16[1152,256]{1,0:T(8,128)(2,1)} %copy.177.refs_3_, bf16[256,1152]{1,0:T(8,128)(2,1)} %copy-done.48, bf16[256,4608]{1,0:T(8,128)(2,1)} %copy-done.76, ...), custom_call_target="tpu_custom_call" | custom-call | flops 16307453952 | bytes 104857600 | tf_op jit(solution)/shard_map/pallas_call | solution.py:696
  1237.9 7.0 fusion.60
  1252.8 48.3 %all-reduce.13 = (bf16[16,6912]{1,0:T(8,128)(2,1)S(1)}, bf16[16,6912]{1,0:T(8,128)(2,1)S(1)}) all-reduce(f32[16,6912]{1,0:T(8,128)} %convolution_dynamic-update-slice_fusion.6, f32[16,6912]{1,0:T(8,128)S(1)} %copy-done.45), channel_id=1, replica_groups=mesh['fsdp'=8,'replica'=4] {'fsdp','replica'}, use_global_device_ids=true, to_apply=%region_23.24 | all-reduce | flops 221184 | bytes 1327104 | tf_op jit(solution)/shard_map/psum | solution.py:1003
  1327.9 100.1 %all-reduce.10.cloned.1.call-done = f32[18432]{0:T(1024)} async-done(((f32[18432]{0:T(1024)}), f32[18432]{0:T(1024)}) %all-reduce.10.cloned.1.call-update) | async-done | bytes 73744 | tf_op jit(solution)/shard_map/psum | solution.py:1003
  (372 shorter events, 246.6 us)
Async XLA Ops:
  7.2 65.4 %all-reduce.12.cloned.1.call-start = ((), (), s32[]{:S(2)}) async-start(), calls=%async_computation.9 | async-start | bytes 1769472 | tf_op jit(solution)/shard_map/psum | solution.py:976
  13.7 112.6 %all-gather.13.cloned.1.call-start = ((), (), s32[]{:S(2)}) async-start(), calls=%async_computation | async-start | bytes 8957952 | tf_op jit(solution)/shard_map/all_gather | solution.py:843
  14.5 226.0 %all-gather.15.cloned.1.call-start = ((), (), s32[]{:S(2)}) async-start(), calls=%async_computation.1 | async-start | bytes 2985984 | tf_op jit(solution)/shard_map/all_gather | solution.py:843
  15.2 233.0 %all-gather.17.cloned.1.call-start = ((), (), s32[]{:S(2)}) async-start(), calls=%async_computation.2 | async-start | bytes 11943936 | tf_op jit(solution)/shard_map/all_gather | solution.py:843
  15.8 293.4 %all-gather.19.cloned.1.call-start = ((), (), s32[]{:S(2)}) async-start(), calls=%async_computation.3 | async-start | bytes 11943936 | tf_op jit(solution)/shard_map/all_gather | solution.py:843
  16.4 347.1 %all-gather.21.cloned.1.call-start = ((), (), s32[]{:S(2)}) async-start(), calls=%async_computation.4 | async-start | bytes 8957952 | tf_op jit(solution)/shard_map/all_gather | solution.py:843
  17.0 462.1 %all-gather.23.cloned.1.call-start = ((), (), s32[]{:S(2)}) async-start(), calls=%async_computation.5 | async-start | bytes 2985984 | tf_op jit(solution)/shard_map/all_gather | solution.py:843
  17.8 13.0 copy-start.66
  17.8 13.0 copy-start.69
  17.8 13.0 copy-start.73
  17.8 13.0 copy-start.74
  17.8 470.4 %all-gather.27.cloned.1.call-start = ((), (), s32[]{:S(2)}) async-start(), calls=%async_computation.7 | async-start | bytes 11943936 | tf_op jit(solution)/shard_map/all_gather | solution.py:843
  18.6 23.1 %copy-start.5 = (bf16[256,1152]{1,0:T(8,128)(2,1)S(1)}, bf16[256,1152]{1,0:T(8,128)(2,1)}, u32[]{:S(2)}) copy-start(bf16[256,1152]{1,0:T(8,128)(2,1)} %param.24) | copy-start | bytes 1769476
  18.6 528.0 %all-gather.25.cloned.1.call-start = ((), (), s32[]{:S(2)}) async-start(), calls=%async_computation.6 | async-start | bytes 11943936 | tf_op jit(solution)/shard_map/all_gather | solution.py:843
  19.3 1408.6 %all-reduce.10.cloned.1.call-start = ((), (), s32[]{:S(2)}) async-start(), calls=%async_computation.8 | async-start | bytes 147456 | tf_op jit(solution)/shard_map/psum | solution.py:1003
  41.9 34.7 %copy-start.56 = (f32[256]{0:T(256)}, f32[256]{0:T(256)S(1)}, u32[]{:S(2)}) copy-start(f32[256]{0:T(256)S(1)} %broadcast_multiply_fusion.3) | copy-start | bytes 3076
  42.2 34.4 %copy-start.63 = (f32[256]{0:T(256)}, f32[256]{0:T(256)S(1)}, u32[]{:S(2)}) copy-start(f32[256]{0:T(256)S(1)} %fusion.59) | copy-start | bytes 3076
  42.2 38.7 %copy-start.49 = (s32[256]{0:T(256)}, s32[256]{0:T(256)S(1)}, u32[]{:S(2)}) copy-start(s32[256]{0:T(256)S(1)} %and_select_fusion.2) | copy-start | bytes 3076
  42.3 34.4 %copy-start.60 = (f32[256]{0:T(256)}, f32[256]{0:T(256)S(1)}, u32[]{:S(2)}) copy-start(f32[256]{0:T(256)S(1)} %fusion.113) | copy-start | bytes 3076
  546.6 10.4 copy-start.8
  557.0 8.6 copy-start.75
  568.5 9.8 copy-start.11
  700.6 13.6 slice-start.2
  702.5 11.6 slice-start.3
  711.7 11.5 slice-start
  714.1 9.1 copy-start.48
  714.1 18.5 %copy-start.27 = (f32[256,1152]{1,0:T(8,128)}, f32[256,1152]{1,0:T(8,128)S(1)}, u32[]{:S(2)}) copy-start(f32[256,1152]{1,0:T(8,128)S(1)} %get-tuple-element.85) | copy-start | bytes 3538948
  714.2 9.1 slice-start.1
  714.2 9.1 copy-start.3
  723.2 8.3 copy-start.76
  1237.9 8.2 copy-start.61
  1251.6 49.5 %copy-start.53 = (bf16[16,1152]{1,0:T(8,128)(2,1)S(1)}, bf16[16,1152]{1,0:T(8,128)(2,1)}, u32[]{:S(2)}) copy-start(bf16[16,1152]{1,0:T(8,128)(2,1)} %param.25) | copy-start | bytes 110596
  (59 other events, 122.2 us)
Sparse Core Ops, SparseCore 0:
  13.9 58.7 all-reduce.11
  74.5 51.7 all-gather.12
  128.2 30.2 all-gather.14
  160.3 77.0 all-gather.16
  239.0 70.0 all-gather.18
  310.9 52.5 all-gather.20
  365.4 30.2 all-gather.22
  397.6 79.3 all-gather.26
  478.8 67.7 all-gather.24
  1309.8 118.0 all-reduce.9

commit v3 on v2

--- a/solution.py
+++ b/solution.py
@@ -275,15 +275,229 @@
     pltpu.make_async_copy(ref, ref, sem).wait()
 
 
-def to_heads_kernel(reps, size, edge, kv, x_ref, own, prev, after, send, recv, edge_send, edge_recv):
+class Gather:
+    COPIES = 9
+
+    def __init__(self, shards, fulls, halves, send, recv, load, store, *held):
+        self.shards, self.fulls, self.halves, self.held = shards, fulls, halves, held
+        self.send, self.recv, self.load, self.store = send, recv, load, store
+        self.f, self.r = lax.axis_index("fsdp"), lax.axis_index("replica")
+        f = self.f
+        c, x, y = lax.rem(f, 2), lax.rem(f // 2, 2), f // 4
+        self.core, self.x, self.y = f + 1 - 2 * c, f + 2 - 4 * x, f + 4 - 8 * y
+        self.xy = self.x + 4 - 8 * y
+
+    def rows(self, at, which):
+        rows, half = self.shards[at][0].shape[0], self.halves[at]
+        return {"all": (0, rows), "top": (0, half), "low": (half, rows - half)}[which]
+
+    def part(self, at, place, which):
+        first, size = self.rows(at, which)
+        rows = self.shards[at][0].shape[0]
+        return self.fulls[at].at[pl.ds(pl.multiple_of(place * rows + first, 16), size), :]
+
+    def remote(self, at, kind, src, dst, to):
+        return pltpu.make_async_remote_copy(
+            src_ref=src, dst_ref=dst, send_sem=self.send.at[at, kind],
+            recv_sem=self.recv.at[at, kind], device_id=(to, self.r), device_id_type=MESH,
+        )
+
+    def copy(self, at, kind, place, which, to, source=None):
+        dst = self.part(at, place, which)
+        src = dst if source is None else self.held[at].at[source, pl.ds(*self.rows(at, which)), :]
+        return self.remote(at, kind, src, dst, to)
+
+    def hop(self, at, source):
+        return self.remote(at, 6 + source, self.held[at].at[0], self.held[at].at[source], (self.x, self.y)[source - 1])
+
+    def keep(self, at, source):
+        place = (self.f, self.x, self.y)[source]
+        return pltpu.make_async_copy(self.held[at].at[source], self.part(at, place, "all"), self.store.at[at, source])
+
+    def fetch(self, at, source):
+        return pltpu.make_async_copy(self.shards[at][source], self.held[at].at[source], self.load.at[at, source])
+
+    def pass_on(self, at, source):
+        place = (self.f, self.x, self.y)[source]
+        self.copy(at, 2 + source, place, "all", self.core, source).start()
+        self.keep(at, source).start()
+
+    def begin(self):
+        places = range(len(self.shards))
+        for at in places:
+            for source in range(len(self.shards[at])):
+                self.fetch(at, source).start()
+        for at in places:
+            self.fetch(at, 0).wait()
+            if len(self.shards[at]) == 1:
+                self.hop(at, 1).start()
+                self.hop(at, 2).start()
+        for at in places:
+            self.pass_on(at, 0)
+
+    def onward(self, at):
+        ahead = len(self.shards[at]) == 3
+        self.fetch(at, 1).wait() if ahead else self.hop(at, 1).wait_recv()
+        self.copy(at, 0, self.x, "top", self.y, 1).start()
+        self.fetch(at, 2).wait() if ahead else self.hop(at, 2).wait_recv()
+        self.copy(at, 1, self.y, "low", self.x, 2).start()
+        self.pass_on(at, 1)
+        self.pass_on(at, 2)
+
+    def across(self, at):
+        self.copy(at, 0, self.xy, "top", self.y).wait_recv()
+        self.copy(at, 5, self.xy, "top", self.core).start()
+        self.copy(at, 1, self.xy, "low", self.x).wait_recv()
+        self.copy(at, 6, self.xy, "low", self.core).start()
+
+    def end(self, at):
+        for source in range(3):
+            self.keep(at, source).wait()
+            if source and len(self.shards[at]) == 1:
+                self.hop(at, source).wait_send()
+        for kind, which in ((0, "top"), (1, "low"), (2, "all"), (3, "all"), (4, "all"), (5, "top"), (6, "low")):
+            self.copy(at, kind, self.f, which, self.core).wait_send()
+            if kind >= 2:
+                self.copy(at, kind, self.f, which, self.core).wait_recv()
+
+
+def sent_ahead(shards, after):
+    shards, _ = lax.optimization_barrier((shards, after))
+    hop = lambda shard, step: lax.ppermute(shard, "fsdp", [(at, at ^ step) for at in range(8)])
+    return [(shard, hop(shard, 2), hop(shard, 4)) for shard in shards]
+
+
+def split_shards(refs, sizes):
+    shards = []
+    for size in sizes:
+        shards.append(refs[:size])
+        refs = refs[size:]
+    return shards, refs
+
+
+def gather_scratch(shards):
+    count = len(shards)
+    if not count:
+        return []
+    return [
+        pltpu.SemaphoreType.DMA((count, Gather.COPIES)),
+        pltpu.SemaphoreType.DMA((count, Gather.COPIES)),
+        pltpu.SemaphoreType.DMA((count, 3)),
+        pltpu.SemaphoreType.DMA((count, 3)),
+    ] + [pltpu.VMEM((3, *part.shape), part.dtype) for part, *_ in shards]
+
+
+def gathered_shapes(shards):
+    return tuple(jax.ShapeDtypeStruct((8 * part.shape[0], part.shape[1]), part.dtype) for part, *_ in shards)
+
+
+def halves_of(shards):
+    halves, ahead = [], 0
+    for part, *_ in shards:
+        rows, size = part.shape
+        half = rows // 32 * 16
+        if rows % 32 and ahead <= 0:
+            half += 16
+        ahead += (2 * half - rows) * size
+        halves.append(half)
+    return tuple(halves), tuple(len(shard) for shard in shards)
+
+
+def start_kernel(plan, part_in, bias_in, *refs):
+    halves, sizes = plan
+    count = len(halves)
+    shards, refs = split_shards(refs, sizes)
+    (mod, bias), fulls, refs = refs[:2], refs[2 : count + 2], refs[count + 2 :]
+    terms, total, m_s, m_r, b_s, b_r, t_s, t_r, keep, *sems = refs
+    f, r = lax.axis_index("fsdp"), lax.axis_index("replica")
+    others = [lax.rem(f + d, 8) for d in range(1, 8)]
+    greet([((there, r), True) for there in others], 7)
+
+    def remote(src, dst, s_sem, r_sem, there):
+        return pltpu.make_async_remote_copy(
+            src_ref=src, dst_ref=dst, send_sem=s_sem, recv_sem=r_sem, device_id=(there, r), device_id_type=MESH
+        )
+
+    def term_copy(block, source, there):
+        return remote(part_in.at[block], terms.at[source], t_s.at[there], t_r.at[source], there)
+
+    def bias_copy(source, there):
+        return remote(bias_in, bias.at[source], b_s.at[there], b_r.at[source], there)
+
+    def mod_copy(source, there):
+        return remote(total, mod.at[source], m_s.at[there], m_r.at[source], there)
+
+    gather = Gather(shards, fulls, halves, *sems)
+    for there in others:
+        term_copy(there, f, there).start()
+    mine = pltpu.make_async_copy(part_in.at[f], terms.at[f], keep.at[0])
+    mine.start()
+    gather.begin()
+    for there in others:
+        bias_copy(f, there).start()
+    own_bias = pltpu.make_async_copy(bias_in, bias.at[f], keep.at[1])
+    own_bias.start()
+    mine.wait()
+    for there in others:
+        term_copy(f, there, there).wait_recv()
+    total[...] = functools.reduce(lambda a, b: a + b, [terms[j] for j in range(8)])
+    for there in others:
+        mod_copy(f, there).start()
+    own_mod = pltpu.make_async_copy(total, mod.at[f], keep.at[2])
+    own_mod.start()
+    for at in range(count):
+        gather.onward(at)
+    for at in range(count):
+        gather.across(at)
+    for at in range(count):
+        gather.end(at)
+    own_bias.wait()
+    own_mod.wait()
+    for there in others:
+        term_copy(there, f, there).wait_send()
+        bias_copy(f, there).wait_send()
+        mod_copy(f, there).wait_send()
+        bias_copy(there, there).wait_recv()
+        mod_copy(there, there).wait_recv()
+
+
+def start(parts, biases, shards, collective_id):
+    sem = lambda: pltpu.SemaphoreType.DMA((8,))
+    return pl.pallas_call(
+        functools.partial(start_kernel, halves_of(shards)),
+        out_shape=(
+            jax.ShapeDtypeStruct(parts.shape, parts.dtype),
+            jax.ShapeDtypeStruct((8, *biases.shape), biases.dtype),
+            *gathered_shapes(shards),
+        ),
+        in_specs=[HB] * (2 + sum(len(shard) for shard in shards)),
+        out_specs=(HB,) * (2 + len(shards)),
+        scratch_shapes=[
+            pltpu.VMEM(parts.shape, parts.dtype), pltpu.VMEM(parts.shape[1:], parts.dtype),
+            sem(), sem(), sem(), sem(), sem(), sem(), pltpu.SemaphoreType.DMA((3,)), *gather_scratch(shards),
+        ],
+        compiler_params=pltpu.CompilerParams(
+            collective_id=collective_id, has_side_effects=True, vmem_limit_bytes=VMEM_LIMIT
+        ),
+    )(parts, biases, *(part for shard in shards for part in shard))
+
+
+def to_heads_kernel(reps, size, edge, kv, plan, x_ref, *refs):
+    halves, sizes = plan
+    count = len(halves)
+    shards, refs = split_shards(refs, sizes)
+    (own, prev, after), fulls, refs = refs[:3], refs[3 : count + 3], refs[count + 3 :]
+    send, recv, edge_send, edge_recv, *sems = refs
+    gather = Gather(shards, fulls, halves, *sems) if count else None
     group, me = lax.axis_index("fsdp"), lax.axis_index("replica")
     groups = lax.axis_size("fsdp")
     wide = x_ref.shape[2]
     down, up = group > 0, group < groups - 1
     others = [(group, lax.rem(me + d, reps)) for d in range(1, reps)]
     greet(
-        [(place, True) for place in others] + [((group - 1, me), down), ((group + 1, me), up)],
-        reps - 1 + down.astype(jnp.int32) + up.astype(jnp.int32),
+        [(place, True) for place in others] + [((group - 1, me), down), ((group + 1, me), up)]
+        + ([((there, me), True) for there in (gather.core, gather.x, gather.y)] if count else []),
+        reps - 1 + down.astype(jnp.int32) + up.astype(jnp.int32) + (3 if count else 0),
     )
     spans = [pl.ds(0, kv), pl.ds(kv, wide - kv)] if wide > kv else [pl.ds(0, kv)]
 
@@ -297,6 +511,11 @@
         for _, there in others:
             exchange(span, part, there).start()
         pltpu.make_async_copy(x_ref.at[me, :, span], own.at[me, :, span], recv.at[part, me]).start()
+
+    if count:
+        gather.begin()
+    for at in range(count):
+        gather.onward(at)
 
     def edges(piece, action):
         lo, hi = piece * size, (piece + 1) * size
@@ -328,6 +547,8 @@
     if len(spans) > 1:
         for piece in range(reps):
             wait_for(own.at[piece, :, spans[1]], recv.at[1, piece])
+    for at in range(count):
+        gather.across(at)
     for part, span in enumerate(spans):
         for _, there in others:
             wait_for(x_ref.at[there, :, span], send.at[part, there])
@@ -343,53 +564,75 @@
             @pl.when(up)
             def _():
                 wait_for(after.at[pl.ds(lo, size), :], edge_recv.at[1, piece])
-
-
-def to_heads(packed, edge, kv, collective_id):
+    for at in range(count):
+        gather.end(at)
+
+
+def to_heads(packed, edge, kv, shards, collective_id):
     reps, size, wide = packed.shape
     sems = pltpu.SemaphoreType.DMA((2, reps))
-    own, prev, after = pl.pallas_call(
-        functools.partial(to_heads_kernel, reps, size, edge, kv),
+    own, prev, after, *fulls = pl.pallas_call(
+        functools.partial(to_heads_kernel, reps, size, edge, kv, halves_of(shards)),
         out_shape=(
             jax.ShapeDtypeStruct(packed.shape, packed.dtype),
             jax.ShapeDtypeStruct((edge, kv), packed.dtype),
             jax.ShapeDtypeStruct((edge, kv), packed.dtype),
-        ),
-        in_specs=[HB],
-        out_specs=(HB, HB, HB),
-        scratch_shapes=[sems, sems, sems, sems],
-        compiler_params=pltpu.CompilerParams(collective_id=collective_id, has_side_effects=True),
-    )(packed)
-    return own.reshape(reps * size, wide), prev, after
-
-
-def swap_kernel(reps, x_ref, y_ref, send, recv):
+            *gathered_shapes(shards),
+        ),
+        in_specs=[HB] * (1 + sum(len(shard) for shard in shards)),
+        out_specs=(HB,) * (3 + len(shards)),
+        scratch_shapes=[sems, sems, sems, sems, *gather_scratch(shards)],
+        compiler_params=pltpu.CompilerParams(
+            collective_id=collective_id, has_side_effects=True, vmem_limit_bytes=VMEM_LIMIT
+        ),
+    )(packed, *(part for shard in shards for part in shard))
+    return own.reshape(reps * size, wide), prev, after, fulls
+
+
+def swap_kernel(reps, plan, x_ref, *refs):
+    halves, sizes = plan
+    count = len(halves)
+    shards, refs = split_shards(refs, sizes)
+    y_ref, fulls, (send, recv, *sems) = refs[0], refs[1 : count + 1], refs[count + 1 :]
+    gather = Gather(shards, fulls, halves, *sems) if count else None
     group, me = lax.axis_index("fsdp"), lax.axis_index("replica")
     others = [(group, lax.rem(me + d, reps)) for d in range(1, reps)]
-    greet([(place, True) for place in others], reps - 1)
+    planar = [(there, me) for there in (gather.core, gather.x, gather.y)] if count else []
+    greet([(place, True) for place in others + planar], reps - 1 + len(planar))
     for _, there in others:
         pltpu.make_async_remote_copy(
             src_ref=x_ref.at[there], dst_ref=y_ref.at[me], send_sem=send.at[there], recv_sem=recv.at[me],
             device_id=(group, there), device_id_type=MESH,
         ).start()
     pltpu.make_async_copy(x_ref.at[me], y_ref.at[me], recv.at[me]).start()
+    if count:
+        gather.begin()
+    for at in range(count):
+        gather.onward(at)
+    for at in range(count):
+        gather.across(at)
     for piece in range(reps):
         wait_for(y_ref.at[piece], recv.at[piece])
     for _, there in others:
         wait_for(x_ref.at[there], send.at[there])
-
-
-def swap(packed, collective_id):
+    for at in range(count):
+        gather.end(at)
+
+
+def swap(packed, shards, collective_id):
     reps = packed.shape[0]
     sems = pltpu.SemaphoreType.DMA((reps,))
-    return pl.pallas_call(
-        functools.partial(swap_kernel, reps),
-        out_shape=jax.ShapeDtypeStruct(packed.shape, packed.dtype),
-        in_specs=[HB],
-        out_specs=HB,
-        scratch_shapes=[sems, sems],
-        compiler_params=pltpu.CompilerParams(collective_id=collective_id, has_side_effects=True),
-    )(packed)
+    swapped, *fulls = pl.pallas_call(
+        functools.partial(swap_kernel, reps, halves_of(shards)),
+        out_shape=(jax.ShapeDtypeStruct(packed.shape, packed.dtype), *gathered_shapes(shards)),
+        in_specs=[HB] * (1 + sum(len(shard) for shard in shards)),
+        out_specs=(HB,) * (1 + len(shards)),
+        scratch_shapes=[sems, sems, *gather_scratch(shards)],
+        compiler_params=pltpu.CompilerParams(
+            collective_id=collective_id, has_side_effects=True, vmem_limit_bytes=VMEM_LIMIT
+        ),
+    )(packed, *(part for shard in shards for part in shard))
+    return swapped, fulls
 
 
 def from_heads_kernel(reps, size, edge, dprev, own, dafter, dq, out_kv, out_q, from_up, from_down, total, mine, sends, recvs, send, recv):
@@ -501,9 +744,9 @@
 
 
 def reduce_kernel(layers, width, half, *refs):
-    count = layers * UNITS
-    ins, refs = refs[: 8 * layers], refs[8 * layers :]
-    (out, left, right, csend, crecv, own, xs, xr, ys, yr, tx, ty, x2s, x2r, y2s, y2r, zs, z1r, z2s, z2r, fin,
+    count = layers * UNITS + 1
+    ins, extra_in, refs = refs[: 8 * layers], refs[8 * layers], refs[8 * layers + 1 :]
+    (out, shared, extra, share_s, share_r, left, right, csend, crecv, own, xs, xr, ys, yr, tx, ty, x2s, x2r, y2s, y2r, zs, z1r, z2s, z2r, fin,
      load_sem, core_s, core_r, x_s, x_r, y_s, y_r, x2_s, x2_r, y2_s, y2_r, z1_s, z1_r, z2_s, z2_r, fin_l, fin_s, fin_r,
      credit) = refs
     f, r = lax.axis_index("fsdp"), lax.axis_index("replica")
@@ -514,11 +757,13 @@
     inner = jnp.logical_and(r > 0, r < 3)
     outer = jnp.logical_not(inner)
     z_at = r + 1 - 2 * lax.rem(r, 2)
+    others = [lax.rem(f + d, 8) for d in range(1, 8)]
     greet(
-        [((core_at, r), True), ((x_at, r), True), ((y_at, r), True), ((f, r - 1), r > 0), ((f, r + 1), r < 3)],
-        3 + (r > 0).astype(jnp.int32) + (r < 3).astype(jnp.int32),
-    )
-    loads = []
+        [((there, r), True) for there in others] + [((f, r - 1), r > 0), ((f, r + 1), r < 3)],
+        7 + (r > 0).astype(jnp.int32) + (r < 3).astype(jnp.int32),
+    )
+    few = extra.shape[1]
+    loads = [(extra_in, extra)]
     for layer in range(layers):
         place = layer * (LEFT_ROWS + 3) * width
         for at in range(4):
@@ -541,9 +786,12 @@
             src_ref=src, dst_ref=dst, send_sem=s_sem, recv_sem=r_sem, device_id=where, device_id_type=MESH
         )
 
+    def place_of(core, mx, my):
+        return ((y + my * (1 - 2 * y)) * 2 + (x + mx * (1 - 2 * x))) * 2 + (c + core * (1 - 2 * c))
+
     def term(u, core, mx, my):
-        layer, w = u // UNITS, lax.rem(u, UNITS)
-        block = ((y + my * (1 - 2 * y)) * 2 + (x + mx * (1 - 2 * x))) * 2 + (c + core * (1 - 2 * c))
+        layer, w = (u - 1) // UNITS, lax.rem(u - 1, UNITS)
+        block = place_of(core, mx, my)
         inside = jnp.where(
             w < 4, rows * w, LEFT_ROWS * width + jnp.where(w < 8, 0, jnp.where(w < 9, width, 2 * width))
         )
@@ -644,6 +892,19 @@
         x2_copy(slot).start()
         own[at, top, :] += xr[slot, 0].astype(f32)
         own[at, low, :] += yr[slot, 0].astype(f32)
+
+    def chip_extra(u):
+        core_copy(0).wait()
+        for m, (mx, my) in enumerate(places):
+            total = extra[place_of(0, mx, my)] + crecv[0, m, :few, :].astype(f32)
+            if m == 0:
+                own[0, :few, :] = total
+            elif m == 2:
+                ty[0, :few, :] = total
+            else:
+                xs[0, m // 2, :few, :] = total.astype(bf16)
+        x_copy(0).start()
+        y_copy(0).start()
 
     def chip(u):
         slot, pair, at = lax.rem(u, 4), lax.rem(u, 2), lax.rem(u, own.shape[0])
@@ -661,6 +922,18 @@
         y_copy(slot).start()
         own[at] = term(u, 0, 0, 0) + crecv[pair, 0].astype(f32)
 
+    def open_extra(u):
+        for m, (mx, my) in enumerate(places):
+            csend[0, m, :few, :] = extra[place_of(1, mx, my)].astype(bf16)
+        core_copy(0).start()
+
+    def share_copy(there, where):
+        return send(out.at[0, pl.ds(0, few), :], shared.at[there], share_s.at[where], share_r.at[there], (where, r))
+
+    def share(u):
+        for there in others:
+            share_copy(f, there).start()
+
     def open_unit(u):
         pair = lax.rem(u, 2)
         for m, (mx, my) in enumerate(places):
@@ -668,6 +941,7 @@
         core_copy(pair).start()
 
     def step(t, carry):
+        pl.when(t == 12)(lambda: share(t))
         stage(t - 11, inner, close)
         stage(t - 11, outer, arrive)
         stage(t - 9, inner, finish)
@@ -675,30 +949,39 @@
         stage(t - 7, outer, sent)
         stage(t - 5, None, plane)
         stage(t - 3, None, cross)
-        stage(t - 1, None, chip)
-        stage(t, None, open_unit)
+        stage(t - 1, t > 1, chip)
+        pl.when(t == 1)(lambda: chip_extra(t - 1))
+        stage(t, t > 0, open_unit)
+        pl.when(t == 0)(lambda: open_extra(t))
         return carry
 
     lax.fori_loop(0, count + 11, step, 0)
-
-
-def reduce_grads(pairs):
+    for there in others:
+        share_copy(f, there).wait_send()
+        share_copy(there, there).wait_recv()
+
+
+def reduce_grads(pairs, extra):
     layers = len(pairs)
     width, tokens = pairs[0][0][1].shape
     rows = width // 8
     half = pad_to(rows // 2, 16)
-    ins = [part for lefts, rights in pairs for part in (*lefts, *rights)]
-    count = layers * UNITS
+    ins = [part for lefts, rights in pairs for part in (*lefts, *rights)] + [extra]
+    count = layers * UNITS + 1
     bf16, f32 = jnp.bfloat16, jnp.float32
     buf = lambda dtype, *shape: pltpu.VMEM((*shape, width), dtype)
     sem = lambda size: pltpu.SemaphoreType.DMA((size,))
     z_slots = 8
     return pl.pallas_call(
         functools.partial(reduce_kernel, layers, width, half),
-        out_shape=jax.ShapeDtypeStruct((count, rows, width), bf16),
+        out_shape=(
+            jax.ShapeDtypeStruct((count, rows, width), bf16),
+            jax.ShapeDtypeStruct(extra.shape, bf16),
+        ),
         in_specs=[HB] * len(ins),
-        out_specs=HB,
+        out_specs=(HB, HB),
         scratch_shapes=[
+            buf(f32, *extra.shape[:2]), sem(8), sem(8),
             pltpu.VMEM((layers * (LEFT_ROWS + 3) * width, tokens), bf16),
             buf(bf16, layers * 9, tokens),
             buf(bf16, 2, 4, rows), buf(bf16, 2, 4, rows), buf(f32, 9, rows),
@@ -706,7 +989,7 @@
             buf(f32, 4, rows - half), buf(f32, 4, half),
             buf(bf16, 4, rows - half), buf(bf16, 4, rows - half), buf(bf16, 4, half), buf(bf16, 4, half),
             buf(bf16, 4, rows), buf(bf16, z_slots, rows), buf(bf16, 4, rows), buf(bf16, 4, rows), buf(bf16, 4, rows),
-            sem(13 * layers), sem(2), sem(2), sem(4), sem(4), sem(4), sem(4), sem(4), sem(4), sem(4), sem(4),
+            sem(13 * layers + 1), sem(2), sem(2), sem(4), sem(4), sem(4), sem(4), sem(4), sem(4), sem(4), sem(4),
             sem(4), sem(z_slots), sem(4), sem(4), sem(4), sem(4), sem(count), pltpu.SemaphoreType.REGULAR,
         ],
         compiler_params=pltpu.CompilerParams(
@@ -751,7 +1034,7 @@
     return jnp.pad(stacked, ((0, 0), (0, 0), (0, width - stacked.shape[2])))
 
 
-def layer_forward(stream, mod_tok, full, plan):
+def layer_forward(stream, mod_tok, full, plan, in_first, shards_second, shards_ahead, collective_id):
     qkv_w, qkv_b, out_w, out_b, up_w, up_b, down_w, down_b = full
     reps, edge, bounds, ids = plan
     width = stream.shape[1]
@@ -766,9 +1049,13 @@
     projected = (low_dot(normed, qkv_w) + bias_full).astype(jnp.bfloat16)
     query, key, value = (group_heads(part, reps) for part in jnp.split(projected, 3, axis=1))
     packed = widen(jnp.concatenate([key, value, query], axis=2), pad_to(3 * hd, LANES))
-    own, prev, after = to_heads(packed, edge, pad_to(2 * hd, LANES), 1)
+    own, prev, after, fulls = to_heads(packed, edge, pad_to(2 * hd, LANES), in_first, collective_id)
+    first_gathered = fulls
+    in_second = sent_ahead(shards_second, own) if shards_second else ()
     mixed, mixed_t, log_norm = attend(nh, hd, *bounds, prev, own, after, *ids)
-    mixed = swap(mixed.reshape(reps, -1, mixed.shape[1]), 2)
+    mixed, fulls = swap(mixed.reshape(reps, -1, mixed.shape[1]), in_second, collective_id + 1)
+    up_w, down_w = first_gathered or (up_w, down_w)
+    in_next = sent_ahead(shards_ahead, mixed) if shards_ahead else ()
     mixed = ungroup_heads(mixed[:, :, :hd])
     branch = low_dot(mixed, out_w) + out_b.astype(jnp.float32)
     middle = stream + gate_one * branch
@@ -779,7 +1066,8 @@
     saved = (
         normed, (prev, own, after), mixed, (mixed_t, log_norm), branch, middle, normed_two, hidden, active, result,
     )
-    return (middle + gate_two * result, saved)
+    full = (qkv_w, qkv_b, out_w, out_b, up_w, up_b, down_w, down_b)
+    return (middle + gate_two * result, saved, full, fulls, in_next)
 
 
 def layer_backward(stream, mod_tok, full, saved, plan, pick, grad_next):
@@ -807,7 +1095,7 @@
     grad_mixed = jnp.einsum(
         "te,de->td", grad_branch, out_w, preferred_element_type=jnp.float32
     ).astype(jnp.bfloat16)
-    grad_heads = swap(widen(group_heads(grad_mixed, reps), pad_to(hd, LANES)), 3)
+    grad_heads, _ = swap(widen(group_heads(grad_mixed, reps), pad_to(hd, LANES)), (), 3)
     prev, own, after = window
     grad_q, grad_prev, grad_own, grad_after = attend_back(
         nh, hd, *bounds, prev, own, after, *ids, grad_heads.reshape(own.shape[0], -1), *kept
@@ -839,38 +1127,79 @@
     )
 
 
-def gather_layer(params):
-    rows = lambda value: lax.all_gather(value, "fsdp", axis=0, tiled=True)
-    biases = jnp.concatenate([params[3], params[5], params[7], params[9]])
-    biases = lax.all_gather(biases, "fsdp", axis=0)
+def bias_parts(stacked, params):
     cuts = [0]
     for at in (3, 5, 7, 9):
         cuts.append(cuts[-1] + params[at].shape[0])
-    qkv_b, out_b, up_b, down_b = (biases[:, a:b].reshape(-1) for a, b in zip(cuts[:-1], cuts[1:]))
-    return (rows(params[2]), qkv_b, rows(params[4]), out_b, rows(params[6]), up_b, rows(params[8]), down_b)
-
-
-def owner_sums(pairs):
-    if lax.axis_size("fsdp") == 8 and lax.axis_size("replica") == 4:
-        units = reduce_grads(pairs).reshape(len(pairs), UNITS, -1, pairs[0][0][1].shape[0])
-        rows, width = units.shape[2:]
+    return [stacked[:, a:b].reshape(-1) for a, b in zip(cuts[:-1], cuts[1:])]
+
+
+def modulation(partial_terms, layers):
+    shares = jnp.stack([jnp.concatenate([params[at] for at in (3, 5, 7, 9)]) for params in layers])
+    if not on_planes():
+        mods = lax.psum(tuple(partial_terms), "fsdp")
+        stacked = lax.all_gather(shares, "fsdp", axis=0)
+        fulls = [lax.all_gather(layers[0][at], "fsdp", axis=0, tiled=True) for at in (2, 4)]
+    else:
+        width = layers[0][4].shape[1]
+        parts = jnp.stack(partial_terms).reshape(8, -1, width)
+        mod, stacked, *fulls = start(
+            parts, jnp.pad(shares, ((0, 16 - shares.shape[0]), (0, 0))), [(layers[0][at],) for at in (2, 4)], 6
+        )
+        mods = mod.reshape(len(layers), -1, partial_terms[0].shape[1])
+    return mods, [bias_parts(stacked[:, at], params) for at, params in enumerate(layers)], fulls
+
+
+def on_planes():
+    return lax.axis_size("fsdp") == 8 and lax.axis_size("replica") == 4
+
+
+def owner_sums(pairs, grad_mods, grad_biases):
+    groups = lax.axis_size("fsdp")
+    width = pairs[0][0][1].shape[0]
+    if on_planes():
+        mods = jnp.stack(grad_mods).reshape(groups, -1, width)
+        biases = jnp.stack(
+            [jnp.concatenate([part.reshape(groups, -1) for part in parts], axis=1) for parts in grad_biases], axis=1
+        )
+        extra = jnp.concatenate([mods, biases], axis=1)
+        used = extra.shape[1]
+        extra = jnp.pad(extra, ((0, 0), (0, pad_to(used, 16) - used), (0, 0)))
+        out, shared = reduce_grads(pairs, extra)
+        shared = lax.dynamic_update_slice_in_dim(
+            shared, out[None, 0, : extra.shape[1]], lax.axis_index("fsdp"), 0
+        )
+        mods = shared[:, : mods.shape[1]].reshape(len(pairs), -1, grad_mods[0].shape[1])
+        units = out[1:].reshape(len(pairs), UNITS, -1, width)
+        rows = units.shape[2]
         across = lambda part: part.transpose(1, 0, 2).reshape(rows, -1).astype(jnp.float32)
-        return [
-            (
+        results = []
+        for layer_at, unit in enumerate(units):
+            share = out[0, used - len(pairs) + layer_at].astype(jnp.float32)
+            cuts = [0]
+            for part in grad_biases[layer_at]:
+                cuts.append(cuts[-1] + part.shape[0] // groups)
+            weights = (
                 across(unit[9:12]), across(unit[8:9]), across(unit[4:8]),
                 unit[0:4].reshape(-1, width).astype(jnp.float32),
             )
-            for unit in units
-        ]
-    shares = []
-    for lefts, rights in pairs:
-        grads = []
+            results.append((weights, [share[i:j] for i, j in zip(cuts[:-1], cuts[1:])]))
+        return results, mods
+    flat = jnp.concatenate([part for parts in grad_biases for part in parts])
+    *mods, flat = lax.psum((*grad_mods, flat), ("fsdp", "replica"))
+    results, place = [], 0
+    for (lefts, rights), parts in zip(pairs, grad_biases):
+        grads, biases = [], []
         for left, right in zip(lefts, rights):
             grad = low_dot(left, right).astype(jnp.bfloat16)
             part = lax.psum_scatter(grad, "fsdp", scatter_dimension=0, tiled=True)
             grads.append(lax.psum(part, "replica").astype(jnp.float32))
-        shares.append(grads[::-1])
-    return shares
+        for part in parts:
+            share = part.shape[0] // groups
+            biases.append(lax.dynamic_slice_in_dim(flat, place + lax.axis_index("fsdp") * share, share, 0))
+            place += part.shape[0]
+        results.append((grads[::-1], biases))
+    return results, mods
 
 
 def attention_plan(latent_len, tok_rows, reps, device_at):
@@ -973,7 +1302,7 @@
             0,
         )
         partial_terms.append(term + spread[None, :])
-    mod_first, mod_second = lax.psum((partial_terms[0], partial_terms[1]), "fsdp")
+    (mod_first, mod_second), biases, attention_weights = modulation(partial_terms, layers)
     mod_tokens = (
         jnp.dot(pick, mod_first, precision=HIGH, preferred_element_type=jnp.float32),
         jnp.dot(pick, mod_second, precision=HIGH, preferred_element_type=jnp.float32),
@@ -981,10 +1310,27 @@
     stream = tokens.astype(jnp.float32)
     inputs = []
     kept = []
-    fulls = [gather_layer(params) for params in layers]
-    for layer_at in range(2):
+    whole = lambda value: lax.all_gather(value, "fsdp", axis=0, tiled=True)
+    fulls = []
+    in_first = sent_ahead((first_up_weight, first_down_weight), mod_first) if on_planes() else ()
+    for layer_at, params in enumerate(layers):
         inputs.append(stream)
-        stream, saved = layer_forward(stream, mod_tokens[layer_at], fulls[layer_at], plan)
+        ahead = layers[layer_at + 1] if layer_at + 1 < len(layers) else None
+        qkv_w, out_w = attention_weights
+        qkv_b, out_b, up_b, down_b = biases[layer_at]
+        shards_second, shards_ahead, up_w, down_w = (), (), None, None
+        if on_planes():
+            shards_second = () if ahead is None else (ahead[2], ahead[4])
+            shards_ahead = () if ahead is None else (ahead[6], ahead[8])
+        else:
+            up_w, down_w = whole(params[6]), whole(params[8])
+        full = (qkv_w, qkv_b, out_w, out_b, up_w, up_b, down_w, down_b)
+        stream, saved, full, attention_weights, in_first = layer_forward(
+            stream, mod_tokens[layer_at], full, plan, in_first, shards_second, shards_ahead, 7 + 2 * layer_at
+        )
+        fulls.append(full)
+        if ahead is not None and not on_planes():
+            attention_weights = [whole(ahead[at]) for at in (2, 4)]
         kept.append(saved)
     output = stream.astype(jnp.bfloat16)
     grad_stream = cotangent.astype(jnp.float32)
@@ -998,16 +1344,7 @@
         weight_pairs[layer_at] = local_grads
         mod_grads[layer_at] = grad_mod
         bias_grads[layer_at] = local_biases
-    weight_grads = owner_sums(weight_pairs)
-    flat = jnp.concatenate([part for grads in bias_grads for part in grads])
-    grad_mod_first, grad_mod_second, flat = lax.psum((mod_grads[0], mod_grads[1], flat), ("fsdp", "replica"))
-    place = 0
-    bias_sums = []
-    for grads in bias_grads:
-        for part in grads:
-            share = part.shape[0] // lax.axis_size("fsdp")
-            bias_sums.append(lax.dynamic_slice_in_dim(flat, place + group_place * share, share, 0))
-            place += part.shape[0]
+    sums, (grad_mod_first, grad_mod_second) = owner_sums(weight_pairs, mod_grads, bias_grads)
     grad_silu = jnp.zeros(own_cond.shape, jnp.float32)
     ada_grads = []
     for params, grad_mod in zip(layers, (grad_mod_first, grad_mod_second)):
@@ -1025,7 +1362,7 @@
     outs = [output, grad_stream, cond_grad]
     for layer_at in range(2):
         outs += list(ada_grads[layer_at])
-        for weight, bias in zip(weight_grads[layer_at], bias_sums[4 * layer_at : 4 * layer_at + 4]):
+        for weight, bias in zip(*sums[layer_at]):
             outs += [weight, bias]
     return tuple(outs)
 

time: 1450 us -> 1270 us (0.88)
  waiting for transfers between devices: 313 us -> 29.2 us
  Pallas kernels: 709 us -> 859 us
  blocking collectives: 68.1 us -> 0 us
  starting transfers between devices: 0.38 us -> 24.5 us
    all_gather x8 -> x0, waiting for transfers between devices: 178 us -> none  [gather_layer(): rows = lambda value: lax.all_gather(value, 'fsdp', axis=0, tiled=True)]
    psum x2 -> x0, waiting for transfers between devices: 130 us -> none  [the longest x1 100 us: shards(): lax.psum((mod_grads[0], mod_grads[1], flat), ('fsdp', 'replica'))]
    pallas_call x6 -> x7, Pallas kernels: 159 us -> 239 us  [the longest x2 94.8 us: to_heads(): pl.pallas_call(functools.partial(to_heads_kernel, reps, size, edge, kv, h...]
    pallas_call x1, Pallas kernels: 336 us -> 397 us  [reduce_grads(): pl.pallas_call(functools.partial(reduce_kernel, layers, width, half), out...]
    psum x1 -> x0, blocking collectives: 48.3 us -> none  [shards(): lax.psum((mod_grads[0], mod_grads[1], flat), ('fsdp', 'replica'))]
    ppermute x0 -> x12, waiting for transfers between devices: none -> 29.2 us  [sent_ahead(): lax.ppermute(shard, 'fsdp', [(at, at ^ step) for at in range(8)])]
    ppermute x0 -> x12, starting transfers between devices: none -> 24.5 us  [sent_ahead(): lax.ppermute(shard, 'fsdp', [(at, at ^ step) for at in range(8)])]
    all_gather x2 -> x0, blocking collectives: 19.8 us -> none  [gather_layer(): biases = lax.all_gather(biases, 'fsdp', axis=0)]
  transfers between devices with their start and end apart: 10 -> 12, of which waited for: 6 -> 4; matrix products, arithmetic and copies ran while one was open for 9% -> 8% of each run, Pallas kernels for 12% -> 3%
where the time goes in v3:
time: 1270 us; the launch traced here: 1250 us
  Pallas kernels  859 us (68%)
  matrix products  146 us (11%)
  local copies, waits for them, and re-layouts  138 us (11%)
  other arithmetic  55.4 us (4%)
  waiting for transfers between devices  29.2 us (2%)
  starting transfers between devices  24.5 us (2%)
    pallas_call x1, Pallas kernels, reduce_grads(): pl.pallas_call(functools.partial(reduce_kernel, layers, width, half), out...  397 us
    pallas_call x2, Pallas kernels, to_heads(): pl.pallas_call(functools.partial(to_heads_kernel, reps, size, edge, kv, h...  94.8 us
    pallas_call x2, Pallas kernels, from_heads(): pl.pallas_call(functools.partial(from_heads_kernel, reps, size, edge), ou...  86.8 us
    pallas_call x1, Pallas kernels, start(): pl.pallas_call(functools.partial(start_kernel, halves_of(shards)), out_sh...  73.9 us
    pallas_call x4, Pallas kernels, swap(): pl.pallas_call(functools.partial(swap_kernel, reps, halves_of(shards)), o...  70.4 us
    pallas_call x2, Pallas kernels, attend_back(): pl.pallas_call(functools.partial(attend_back_kernel, nh, hd), out_shape=(...  69.8 us
    pallas_call x2, Pallas kernels, attend(): pl.pallas_call(functools.partial(attend_kernel, nh, hd), out_shape=(jax.S...  66.3 us
    dot_general x10, matrix products, low_dot(): return jnp.dot(left, right, preferred_element_type=jnp.float32)  63.1 us
  transfers between devices with their start and end apart: 12, of which 4 were waited for; matrix products, arithmetic and copies ran while one was open for 8% of the time, Pallas kernels for 3%

profile of v3, /device:TPU:0, one launch (start us, length us, event | category | flops | bytes accessed | tf_op | source)
XLA Modules:
  0.0 1254.8 jit_solution(3370924909732995635)
XLA Ops:
  12.3 73.9 %shard_map.407 = (f32[8,24,1152]{2,1,0:T(8,128)}, bf16[8,16,1152]{2,1,0:T(8,128)(2,1)}, bf16[1152,3456]{1,0:T(8,128)(2,1)}, bf16[1152,1152]{1,0:T(8,128)(2,1)}) custom-call(f32[8,24,1152]{2,1,0:T(8,128)} %reshape.435.part_in, bf16[16,1152]{1,0:T(8,128)(2,1)} %fusion.109.bias_in, bf16[144,3456]{1,0:T(8,128)(2,1)} %refs_0_.1, bf16[144,1152]{1,0:T(8,128)(2,1)} %refs_1_.1), custom_call_target="tpu_custom_call" | custom-call | tf_op jit(solution)/shard_map/pallas_call | solution.py:466
  122.9 26.4 %collective-permute-done.3.refs_5_ = bf16[576,1152]{1,0:T(8,128)(2,1)} collective-permute-done((bf16[576,1152]{1,0:T(8,128)(2,1)}, bf16[576,1152]{1,0:T(8,128)(2,1)}, u32[]{:S(2)}, u32[]{:S(2)}) %collective-permute-start.3) | collective-permute-done | bytes 1327136 | tf_op jit(solution)/shard_map/ppermute | solution.py:366
  150.5 47.8 %shard_map.408 = (bf16[4,256,896]{2,1,0:T(8,128)(2,1)}, bf16[1024,640]{1,0:T(8,128)(2,1)}, bf16[1024,640]{1,0:T(8,128)(2,1)}, bf16[1152,4608]{1,0:T(8,128)(2,1)}, bf16[4608,1152]{1,0:T(8,128)(2,1)}) custom-call(bf16[4,256,896]{2,1,0:T(8,128)(2,1)} %fusion.49.x_ref, bf16[144,4608]{1,0:T(8,128)(2,1)} %refs_0_.2, ...), custom_call_target="tpu_custom_call" | custom-call | tf_op jit(solution)/shard_map/pallas_call | solution.py:574
  198.3 14.2 %collective-permute-start.5 = (bf16[144,3456]{1,0:T(8,128)(2,1)}, bf16[144,3456]{1,0:T(8,128)(2,1)}, u32[]{:S(2)}, u32[]{:S(2)}) collective-permute-start(bf16[144,3456]{1,0:T(8,128)(2,1)} %refs_0_.3), channel_id=1, source_target_pairs={{0,16},{4,20},{8,24},{12,28},{16,0},{20,4},{24,8},{28,12},{1,17},{... | collective-permute-start | bytes 2985992 | tf_op jit(solution)/shard_map/ppermute | solution.py:366
  216.1 5.1 fusion.91
  226.0 33.1 %shard_map.409 = (bf16[1024,384]{1,0:T(8,128)(2,1)}, f32[384,1024]{1,0:T(8,128)}, f32[8,1024]{1,0:T(8,128)}) custom-call(s32[4]{0:T(128)} %get-tuple-element.204.lo, s32[4]{0:T(128)} %get-tuple-element.203.hi, bf16[1024,640]{1,0:T(8,128)(2,1)} %get-tuple-element.71.prev, bf16[1024,896]{1,0:T(8,128)(2,1)} %bitcast.192, ...), custom_call_target="tpu_custom_call" | custom-call | flops 2147483648 | bytes 8388608 | tf_op jit(solution)/shard_map/pallas_call | solution.py:142
  259.9 29.3 %shard_map.410 = (bf16[4,256,384]{2,1,0:T(8,128)(2,1)}, bf16[1152,3456]{1,0:T(8,128)(2,1)}, bf16[1152,1152]{1,0:T(8,128)(2,1)}) custom-call(bf16[4,256,384]{2,1,0:T(8,128)(2,1)} %bitcast.179, bf16[144,3456]{1,0:T(8,128)(2,1)} %refs_0_.3, bf16[144,3456]{1,0:T(8,128)(2,1)} %collective-permute-done.4.refs_1_, bf16[144,3456]{1,0:T(8,128)(2,1)} %collective-permute-done.5.refs_2_, ...), custom_call_target="tpu_custom_call" | custom-call | tf_op jit(solution)/shard_map/pallas_call | solution.py:625
  295.7 4.5 fusion.145
  305.5 11.1 fusion.25
  316.6 4.6 copy.134.refs_0_
  321.3 10.8 fusion.144
  337.2 6.0 fusion.3
  361.2 46.9 %shard_map.411 = (bf16[4,256,896]{2,1,0:T(8,128)(2,1)}, bf16[1024,640]{1,0:T(8,128)(2,1)}, bf16[1024,640]{1,0:T(8,128)(2,1)}, bf16[1152,4608]{1,0:T(8,128)(2,1)}, bf16[4608,1152]{1,0:T(8,128)(2,1)}) custom-call(bf16[4,256,896]{2,1,0:T(8,128)(2,1)} %fusion.51.x_ref, bf16[144,4608]{1,0:T(8,128)(2,1)} %refs_0_.4, ...), custom_call_target="tpu_custom_call" | custom-call | tf_op jit(solution)/shard_map/pallas_call | solution.py:574
  408.1 33.3 %shard_map.412 = (bf16[1024,384]{1,0:T(8,128)(2,1)}, f32[384,1024]{1,0:T(8,128)}, f32[8,1024]{1,0:T(8,128)}) custom-call(s32[4]{0:T(128)} %get-tuple-element.204.lo, s32[4]{0:T(128)} %get-tuple-element.203.hi, bf16[1024,640]{1,0:T(8,128)(2,1)} %get-tuple-element.84.prev, bf16[1024,896]{1,0:T(8,128)(2,1)} %bitcast.194, ...), custom_call_target="tpu_custom_call" | custom-call | flops 2147483648 | bytes 8388608 | tf_op jit(solution)/shard_map/pallas_call | solution.py:142
  441.4 12.8 %shard_map.413 = bf16[4,256,384]{2,1,0:T(8,128)(2,1)} custom-call(bf16[4,256,384]{2,1,0:T(8,128)(2,1)} %bitcast.182), custom_call_target="tpu_custom_call" | custom-call | tf_op jit(solution)/shard_map/pallas_call | solution.py:625
  458.6 4.4 fusion.143
  469.9 11.1 fusion.33
  481.0 4.3 copy.137.refs_8_
  485.3 8.7 convert_reduce_fusion
  494.0 8.6 multiply_reduce_fusion.2
  502.7 10.5 fusion.142
  524.2 13.3 %shard_map.414 = bf16[4,256,384]{2,1,0:T(8,128)(2,1)} custom-call(bf16[4,256,384]{2,1,0:T(8,128)(2,1)} %pad.25.x_ref), custom_call_target="tpu_custom_call" | custom-call | tf_op jit(solution)/shard_map/pallas_call | solution.py:625
  537.6 34.9 %shard_map.415 = (bf16[1024,384]{1,0:T(8,128)(2,1)}, bf16[1024,640]{1,0:T(8,128)(2,1)}, bf16[1024,640]{1,0:T(8,128)(2,1)}, bf16[1024,640]{1,0:T(8,128)(2,1)}) custom-call(s32[4]{0:T(128)} %get-tuple-element.204.lo, s32[4]{0:T(128)} %get-tuple-element.203.hi, bf16[1024,640]{1,0:T(8,128)(2,1)} %get-tuple-element.84.prev, bf16[1024,896]{1,0:T(8,128)(2,1)} %bitcast.195, ...), custom_call_target="tpu_custom_call" | custom-call | flops 5368709120 | bytes 16777216 | tf_op jit(solution)/shard_map/pallas_call | solution.py:234
  572.5 41.0 %shard_map.416 = (bf16[4,256,640]{2,1,0:T(8,128)(2,1)}, bf16[4,256,384]{2,1,0:T(8,128)(2,1)}) custom-call(bf16[1024,640]{1,0:T(8,128)(2,1)} %get-tuple-element.93.dprev, bf16[1024,640]{1,0:T(8,128)(2,1)} %get-tuple-element.94.own, bf16[1024,640]{1,0:T(8,128)(2,1)} %get-tuple-element.95.dafter, bf16[1024,384]{1,0:T(8,128)(2,1)} %get-tuple-element.96.dq), custom_call_target="tpu_custom_call" | custom-call | tf_op jit(solution)/shard_map/pallas_call | solution.py:718
  633.4 6.9 multiply_reduce_fusion.1
  650.4 9.0 convert_reduce_fusion.1
  659.5 6.5 multiply_reduce_fusion
  685.1 14.9 %shard_map.417 = bf16[4,256,384]{2,1,0:T(8,128)(2,1)} custom-call(bf16[4,256,384]{2,1,0:T(8,128)(2,1)} %pad.26.x_ref), custom_call_target="tpu_custom_call" | custom-call | tf_op jit(solution)/shard_map/pallas_call | solution.py:625
  700.0 34.9 %shard_map.418 = (bf16[1024,384]{1,0:T(8,128)(2,1)}, bf16[1024,640]{1,0:T(8,128)(2,1)}, bf16[1024,640]{1,0:T(8,128)(2,1)}, bf16[1024,640]{1,0:T(8,128)(2,1)}) custom-call(s32[4]{0:T(128)} %get-tuple-element.204.lo, s32[4]{0:T(128)} %get-tuple-element.203.hi, bf16[1024,640]{1,0:T(8,128)(2,1)} %get-tuple-element.71.prev, bf16[1024,896]{1,0:T(8,128)(2,1)} %bitcast.193, ...), custom_call_target="tpu_custom_call" | custom-call | flops 5368709120 | bytes 16777216 | tf_op jit(solution)/shard_map/pallas_call | solution.py:234
  734.9 45.8 %shard_map.419 = (bf16[4,256,640]{2,1,0:T(8,128)(2,1)}, bf16[4,256,384]{2,1,0:T(8,128)(2,1)}) custom-call(bf16[1024,640]{1,0:T(8,128)(2,1)} %get-tuple-element.101.dprev, bf16[1024,640]{1,0:T(8,128)(2,1)} %get-tuple-element.102.own, bf16[1024,640]{1,0:T(8,128)(2,1)} %get-tuple-element.103.dafter, bf16[1024,384]{1,0:T(8,128)(2,1)} %get-tuple-element.104.dq), custom_call_target="tpu_custom_call" | custom-call | tf_op jit(solution)/shard_map/pallas_call | solution.py:718
  800.5 7.8 fusion.62
  820.7 396.7 %shard_map.420 = (bf16[25,144,1152]{2,1,0:T(8,128)(2,1)}, bf16[8,32,1152]{2,1,0:T(8,128)(2,1)}) custom-call(bf16[4608,256]{1,0:T(8,128)(2,1)} %copy.134.refs_0_, bf16[1152,256]{1,0:T(8,128)(2,1)} %copy.135.refs_1_, bf16[1152,256]{1,0:T(8,128)(2,1)} %bitcast.176, bf16[1152,256]{1,0:T(8,128)(2,1)} %copy.136.refs_3_, bf16[256,1152]{1,0:T(8,128)(2,1)} %copy-done.42, ...), custom_call_target="tpu_custom_call" | custom-call | flops 16986931200 | bytes 104857600 | tf_op jit(solution)/shard_map/pallas_call | solution.py:975
  (346 shorter events, 233.5 us)
Async XLA Ops:
  0.7 7.5 copy-start
  86.2 7.0 copy-start.4
  88.2 6.0 copy-start.53
  89.1 7.0 copy-start.35
  89.1 32.3 %collective-permute-start.1 = (bf16[144,4608]{1,0:T(8,128)(2,1)}, bf16[144,4608]{1,0:T(8,128)(2,1)}, u32[]{:S(2)}, u32[]{:S(2)}) collective-permute-start(bf16[144,4608]{1,0:T(8,128)(2,1)} %refs_0_.2), channel_id=1, source_target_pairs={{0,16},{4,20},{8,24},{12,28},{16,0},{20,4},{24,8},{28,12},{1,17},{... | collective-permute-start | bytes 3981320 | tf_op jit(solution)/shard_map/ppermute | solution.py:366
  90.6 32.3 %collective-permute-start = (bf16[144,4608]{1,0:T(8,128)(2,1)}, bf16[144,4608]{1,0:T(8,128)(2,1)}, u32[]{:S(2)}, u32[]{:S(2)}) collective-permute-start(bf16[144,4608]{1,0:T(8,128)(2,1)} %refs_0_.2), channel_id=1, source_target_pairs={{0,8},{4,12},{8,0},{12,4},{16,24},{20,28},{24,16},{28,20},{1,9},{5... | collective-permute-start | bytes 3981320 | tf_op jit(solution)/shard_map/ppermute | solution.py:366
  91.2 58.1 %collective-permute-start.3 = (bf16[576,1152]{1,0:T(8,128)(2,1)}, bf16[576,1152]{1,0:T(8,128)(2,1)}, u32[]{:S(2)}, u32[]{:S(2)}) collective-permute-start(bf16[576,1152]{1,0:T(8,128)(2,1)} %refs_3_), channel_id=1, source_target_pairs={{0,16},{4,20},{8,24},{12,28},{16,0},{20,4},{24,8},{28,12},{1,17},{... | collective-permute-start | bytes 3981320 | tf_op jit(solution)/shard_map/ppermute | solution.py:366
  91.7 58.8 %collective-permute-start.2 = (bf16[576,1152]{1,0:T(8,128)(2,1)}, bf16[576,1152]{1,0:T(8,128)(2,1)}, u32[]{:S(2)}, u32[]{:S(2)}) collective-permute-start(bf16[576,1152]{1,0:T(8,128)(2,1)} %refs_3_), channel_id=1, source_target_pairs={{0,8},{4,12},{8,0},{12,4},{16,24},{20,28},{24,16},{28,20},{1,9},{5... | collective-permute-start | bytes 3981320 | tf_op jit(solution)/shard_map/ppermute | solution.py:366
  93.3 5.8 copy-start.47
  96.1 6.4 copy-start.54
  121.2 92.2 %copy-start.32 = (f32[4,24,1152]{2,1,0:T(8,128)S(1)}, f32[4,24,1152]{2,1,0:T(8,128)}, u32[]{:S(2)}) copy-start(f32[4,24,1152]{2,1,0:T(8,128)} %get-tuple-element.163) | copy-start | bytes 1327108
  198.3 16.5 %copy-start.31 = (bf16[256,1152]{1,0:T(8,128)(2,1)S(1)}, bf16[256,1152]{1,0:T(8,128)(2,1)}, u32[]{:S(2)}) copy-start(bf16[256,1152]{1,0:T(8,128)(2,1)} %copy-done.30) | copy-start | bytes 1769476
  198.3 60.8 %collective-permute-start.5 = (bf16[144,3456]{1,0:T(8,128)(2,1)}, bf16[144,3456]{1,0:T(8,128)(2,1)}, u32[]{:S(2)}, u32[]{:S(2)}) collective-permute-start(bf16[144,3456]{1,0:T(8,128)(2,1)} %refs_0_.3), channel_id=1, source_target_pairs={{0,16},{4,20},{8,24},{12,28},{16,0},{20,4},{24,8},{28,12},{1,17},{... | collective-permute-start | bytes 2985992 | tf_op jit(solution)/shard_map/ppermute | solution.py:366
  212.5 46.6 %collective-permute-start.4 = (bf16[144,3456]{1,0:T(8,128)(2,1)}, bf16[144,3456]{1,0:T(8,128)(2,1)}, u32[]{:S(2)}, u32[]{:S(2)}) collective-permute-start(bf16[144,3456]{1,0:T(8,128)(2,1)} %refs_0_.3), channel_id=1, source_target_pairs={{0,8},{4,12},{8,0},{12,4},{16,24},{20,28},{24,16},{28,20},{1,9},{5... | collective-permute-start | bytes 2985992 | tf_op jit(solution)/shard_map/ppermute | solution.py:366
  221.2 37.8 %collective-permute-start.7 = (bf16[144,1152]{1,0:T(8,128)(2,1)S(1)}, bf16[144,1152]{1,0:T(8,128)(2,1)S(1)}, u32[]{:S(2)}, u32[]{:S(2)}) collective-permute-start(bf16[144,1152]{1,0:T(8,128)(2,1)S(1)} %copy-done.43), channel_id=1, source_target_pairs={{0,16},{4,20},{8,24},{12,28},{16,0},{20,4},{24,8},{28,12},{1,17},{... | collective-permute-start | bytes 995336 | tf_op jit(solution)/shard_map/ppermute | solution.py:366
  222.4 36.6 %collective-permute-start.6 = (bf16[144,1152]{1,0:T(8,128)(2,1)S(1)}, bf16[144,1152]{1,0:T(8,128)(2,1)S(1)}, u32[]{:S(2)}, u32[]{:S(2)}) collective-permute-start(bf16[144,1152]{1,0:T(8,128)(2,1)S(1)} %copy-done.43), channel_id=1, source_target_pairs={{0,8},{4,12},{8,0},{12,4},{16,24},{20,28},{24,16},{28,20},{1,9},{5... | collective-permute-start | bytes 995336 | tf_op jit(solution)/shard_map/ppermute | solution.py:366
  290.4 70.7 %collective-permute-start.9 = (bf16[144,4608]{1,0:T(8,128)(2,1)}, bf16[144,4608]{1,0:T(8,128)(2,1)}, u32[]{:S(2)}, u32[]{:S(2)}) collective-permute-start(bf16[144,4608]{1,0:T(8,128)(2,1)} %refs_0_.4), channel_id=1, source_target_pairs={{0,16},{4,20},{8,24},{12,28},{16,0},{20,4},{24,8},{28,12},{1,17},{... | collective-permute-start | bytes 3981320 | tf_op jit(solution)/shard_map/ppermute | solution.py:366
  290.5 70.6 %collective-permute-start.8 = (bf16[144,4608]{1,0:T(8,128)(2,1)}, bf16[144,4608]{1,0:T(8,128)(2,1)}, u32[]{:S(2)}, u32[]{:S(2)}) collective-permute-start(bf16[144,4608]{1,0:T(8,128)(2,1)} %refs_0_.4), channel_id=1, source_target_pairs={{0,8},{4,12},{8,0},{12,4},{16,24},{20,28},{24,16},{28,20},{1,9},{5... | collective-permute-start | bytes 3981320 | tf_op jit(solution)/shard_map/ppermute | solution.py:366
  291.2 70.0 %collective-permute-start.11 = (bf16[576,1152]{1,0:T(8,128)(2,1)}, bf16[576,1152]{1,0:T(8,128)(2,1)}, u32[]{:S(2)}, u32[]{:S(2)}) collective-permute-start(bf16[576,1152]{1,0:T(8,128)(2,1)} %refs_3_.2), channel_id=1, source_target_pairs={{0,16},{4,20},{8,24},{12,28},{16,0},{20,4},{24,8},{28,12},{1,17},{... | collective-permute-start | bytes 3981320 | tf_op jit(solution)/shard_map/ppermute | solution.py:366
  292.6 68.6 %collective-permute-start.10 = (bf16[576,1152]{1,0:T(8,128)(2,1)}, bf16[576,1152]{1,0:T(8,128)(2,1)}, u32[]{:S(2)}, u32[]{:S(2)}) collective-permute-start(bf16[576,1152]{1,0:T(8,128)(2,1)} %refs_3_.2), channel_id=1, source_target_pairs={{0,8},{4,12},{8,0},{12,4},{16,24},{20,28},{24,16},{28,20},{1,9},{5... | collective-permute-start | bytes 3981320 | tf_op jit(solution)/shard_map/ppermute | solution.py:366
  485.3 8.7 copy-start.9
  494.0 8.6 copy-start.55
  494.0 8.7 copy-start.57
  502.6 10.5 copy-start.25
  633.4 6.9 copy-start.33
  647.2 12.2 slice-start
  650.4 9.0 copy-start.42
  650.4 9.0 copy-start.3
  650.4 9.0 slice-start.1
  650.4 9.0 slice-start.2
  659.4 6.5 copy-start.56
  800.5 7.9 copy-start.34
  (41 other events, 99.8 us)

commit v4 on v3

--- a/solution.py
+++ b/solution.py
@@ -9,6 +9,7 @@
 from jax.sharding import PartitionSpec as P
 
 HEADS = 16
+HEAD_DIM = 72
 MAXLEN = 1024
 NORM_EPS = 1e-06
 HIGH = lax.Precision.HIGHEST
@@ -109,15 +110,16 @@
             keys = rows_at(kb, BK)
             lanes = kid[keys, :]
             same = jnp.concatenate([lanes] * (BQ // LANES), axis=1) == ids
+            scores = [jnp.where(same, nt_dot(kh[h, keys, :], qh[h]) * scale, NEG) for h in range(nh)]
+            olds = [ml[0, h : h + 1, :] for h in range(nh)]
+            tops = [jnp.maximum(old, jnp.max(s, axis=0, keepdims=True)) for old, s in zip(olds, scores)]
+            probs = [jnp.exp2(s - top) for s, top in zip(scores, tops)]
+            outs = [nn_dot(vt[h, :, keys], probs[h].astype(jnp.bfloat16)) for h in range(nh)]
             for h in range(nh):
-                s = jnp.where(same, nt_dot(kh[h, keys, :], qh[h]) * scale, NEG)
-                old = ml[0, h : h + 1, :]
-                top = jnp.maximum(old, jnp.max(s, axis=0, keepdims=True))
-                p = jnp.exp2(s - top)
-                alpha = jnp.exp2(old - top)
-                ml[0, h : h + 1, :] = top
-                ml[1, h : h + 1, :] = ml[1, h : h + 1, :] * alpha + jnp.sum(p, axis=0, keepdims=True)
-                acc[h] = acc[h] * alpha + nn_dot(vt[h, :, keys], p.astype(jnp.bfloat16))
+                alpha = jnp.exp2(olds[h] - tops[h])
+                ml[0, h : h + 1, :] = tops[h]
+                ml[1, h : h + 1, :] = ml[1, h : h + 1, :] * alpha + jnp.sum(probs[h], axis=0, keepdims=True)
+                acc[h] = acc[h] * alpha + outs[h]
             return inner
 
         lax.fori_loop(lo[qb], hi[qb], key_block, 0)
@@ -198,14 +200,18 @@
             keys = rows_at(kb, BK)
             lanes = kid[keys, :]
             same = jnp.concatenate([lanes] * (BQ // LANES), axis=1) == ids
-            for h in range(nh):
-                s = nt_dot(kh[h, keys, :], qh[h]) * scale - lse_ref[h : h + 1, rows]
-                p = jnp.exp2(jnp.where(same, s, NEG))
-                dp = nt_dot(vh[h, keys, :], gh[h])
-                ds = (p * (dp - delta[h : h + 1, :])).astype(jnp.bfloat16)
-                dv[h, keys, :] += nn_dot(p.astype(jnp.bfloat16), gh[h])
-                dk[h, keys, :] += nn_dot(ds, qh[h])
-                dqt[h] += nn_dot(kt[h, :, keys], ds)
+            hs = range(nh)
+            scores = [nt_dot(kh[h, keys, :], qh[h]) * scale - lse_ref[h : h + 1, rows] for h in hs]
+            dps = [nt_dot(vh[h, keys, :], gh[h]) - delta[h : h + 1, :] for h in hs]
+            probs = [jnp.exp2(jnp.where(same, s, NEG)) for s in scores]
+            dss = [(p * dp).astype(jnp.bfloat16) for p, dp in zip(probs, dps)]
+            lows = [p.astype(jnp.bfloat16) for p in probs]
+            for h in hs:
+                dv[h, keys, :] += nn_dot(lows[h], gh[h])
+            for h in hs:
+                dk[h, keys, :] += nn_dot(dss[h], qh[h])
+            for h in hs:
+                dqt[h] += nn_dot(kt[h, :, keys], dss[h])
             return inner
 
         lax.fori_loop(lo[qb], hi[qb], key_block, 0)
@@ -273,6 +279,36 @@
 
 def wait_for(ref, sem):
     pltpu.make_async_copy(ref, ref, sem).wait()
+
+
+def assemble(rows, width, pieces):
+    tiles = [None] * (width // LANES)
+    for ref, src, dst, count in pieces:
+        off, to = src % LANES, dst % LANES
+        wide = max(off + count, to + count)
+        wide, have = pad_to(wide, LANES), pad_to(off + count, LANES)
+        first = src // LANES * LANES
+        block = ref[rows, first : first + have].astype(jnp.float32)
+        lane = lax.broadcasted_iota(jnp.int32, block.shape, 1)
+        block = jnp.where(jnp.logical_and(lane >= off, lane < off + count), block, 0.0)
+        if wide > have:
+            block = jnp.concatenate([block, jnp.zeros((block.shape[0], wide - have), jnp.float32)], axis=1)
+        if off != to:
+            block = pltpu.roll(block, (to - off) % wide, 1)
+        for step in range(pad_to(to + count, LANES) // LANES):
+            part = block[:, step * LANES : (step + 1) * LANES]
+            at = dst // LANES + step
+            tiles[at] = part if tiles[at] is None else tiles[at] + part
+    size = next(t for t in tiles if t is not None).shape
+    return jnp.concatenate([jnp.zeros(size, jnp.float32) if t is None else t for t in tiles], axis=1)
+
+
+def by_rows(size, action, step=64):
+    def body(at, carry):
+        action(pl.ds(pl.multiple_of(at * step, step), step))
+        return carry
+
+    lax.fori_loop(0, size // step, body, 0)
 
 
 class Gather:
@@ -482,16 +518,25 @@
     )(parts, biases, *(part for shard in shards for part in shard))
 
 
-def to_heads_kernel(reps, size, edge, kv, plan, x_ref, *refs):
+def to_heads_kernel(reps, size, edge, kv, plan, qkv, *refs):
     halves, sizes = plan
     count = len(halves)
     shards, refs = split_shards(refs, sizes)
     (own, prev, after), fulls, refs = refs[:3], refs[3 : count + 3], refs[count + 3 :]
-    send, recv, edge_send, edge_recv, *sems = refs
+    x_ref, send, recv, edge_send, edge_recv, *sems = refs
     gather = Gather(shards, fulls, halves, *sems) if count else None
     group, me = lax.axis_index("fsdp"), lax.axis_index("replica")
     groups = lax.axis_size("fsdp")
     wide = x_ref.shape[2]
+    width = qkv.shape[1] // 3
+    hd = width // reps
+    for place in range(reps):
+        def pack(rows, place=place):
+            at = place * hd
+            pieces = [(qkv, width + at, 0, hd), (qkv, 2 * width + at, hd, hd), (qkv, at, 2 * hd, hd)]
+            x_ref[place, rows, :] = assemble(rows, wide, pieces).astype(jnp.bfloat16)
+
+        by_rows(size, pack)
     down, up = group > 0, group < groups - 1
     others = [(group, lax.rem(me + d, reps)) for d in range(1, reps)]
     greet(
@@ -568,43 +613,55 @@
         gather.end(at)
 
 
-def to_heads(packed, edge, kv, shards, collective_id):
-    reps, size, wide = packed.shape
+def to_heads(qkv, reps, edge, kv, shards, collective_id):
+    size, wide = qkv.shape[0], pad_to(qkv.shape[1] // reps, LANES)
     sems = pltpu.SemaphoreType.DMA((2, reps))
     own, prev, after, *fulls = pl.pallas_call(
         functools.partial(to_heads_kernel, reps, size, edge, kv, halves_of(shards)),
         out_shape=(
-            jax.ShapeDtypeStruct(packed.shape, packed.dtype),
-            jax.ShapeDtypeStruct((edge, kv), packed.dtype),
-            jax.ShapeDtypeStruct((edge, kv), packed.dtype),
+            jax.ShapeDtypeStruct((reps, size, wide), qkv.dtype),
+            jax.ShapeDtypeStruct((edge, kv), qkv.dtype),
+            jax.ShapeDtypeStruct((edge, kv), qkv.dtype),
             *gathered_shapes(shards),
         ),
-        in_specs=[HB] * (1 + sum(len(shard) for shard in shards)),
+        in_specs=[VM] + [HB] * sum(len(shard) for shard in shards),
         out_specs=(HB,) * (3 + len(shards)),
-        scratch_shapes=[sems, sems, sems, sems, *gather_scratch(shards)],
+        scratch_shapes=[pltpu.VMEM((reps, size, wide), qkv.dtype), sems, sems, sems, sems, *gather_scratch(shards)],
         compiler_params=pltpu.CompilerParams(
             collective_id=collective_id, has_side_effects=True, vmem_limit_bytes=VMEM_LIMIT
         ),
-    )(packed, *(part for shard in shards for part in shard))
+    )(qkv, *(part for shard in shards for part in shard))
     return own.reshape(reps * size, wide), prev, after, fulls
 
 
-def swap_kernel(reps, plan, x_ref, *refs):
+def swap_kernel(reps, out, plan, x_ref, *refs):
     halves, sizes = plan
     count = len(halves)
     shards, refs = split_shards(refs, sizes)
-    y_ref, fulls, (send, recv, *sems) = refs[0], refs[1 : count + 1], refs[count + 1 :]
+    y_ref, fulls, (held, send, recv, *sems) = refs[0], refs[1 : count + 1], refs[count + 1 :]
     gather = Gather(shards, fulls, halves, *sems) if count else None
     group, me = lax.axis_index("fsdp"), lax.axis_index("replica")
     others = [(group, lax.rem(me + d, reps)) for d in range(1, reps)]
     planar = [(there, me) for there in (gather.core, gather.x, gather.y)] if count else []
+    size, lanes = held.shape[1:]
+    if out:
+        src, dst = x_ref, held
+        hd = y_ref.shape[1] // reps
+    else:
+        src, dst = held, y_ref
+        hd = x_ref.shape[1] // reps
+        for place in range(reps):
+            def pack(rows, place=place):
+                held[place, rows, :] = assemble(rows, lanes, [(x_ref, place * hd, 0, hd)]).astype(jnp.bfloat16)
+
+            by_rows(size, pack)
     greet([(place, True) for place in others + planar], reps - 1 + len(planar))
     for _, there in others:
         pltpu.make_async_remote_copy(
-            src_ref=x_ref.at[there], dst_ref=y_ref.at[me], send_sem=send.at[there], recv_sem=recv.at[me],
+            src_ref=src.at[there], dst_ref=dst.at[me], send_sem=send.at[there], recv_sem=recv.at[me],
             device_id=(group, there), device_id_type=MESH,
         ).start()
-    pltpu.make_async_copy(x_ref.at[me], y_ref.at[me], recv.at[me]).start()
+    pltpu.make_async_copy(src.at[me], dst.at[me], recv.at[me]).start()
     if count:
         gather.begin()
     for at in range(count):
@@ -612,30 +669,42 @@
     for at in range(count):
         gather.across(at)
     for piece in range(reps):
-        wait_for(y_ref.at[piece], recv.at[piece])
+        wait_for(dst.at[piece], recv.at[piece])
+    if out:
+        def unpack(rows):
+            pieces = [(held.at[place], 0, place * hd, hd) for place in range(reps)]
+            y_ref[rows, :] = assemble(rows, y_ref.shape[1], pieces).astype(jnp.bfloat16)
+
+        by_rows(size, unpack)
     for _, there in others:
-        wait_for(x_ref.at[there], send.at[there])
+        wait_for(src.at[there], send.at[there])
     for at in range(count):
         gather.end(at)
 
 
-def swap(packed, shards, collective_id):
-    reps = packed.shape[0]
+def swap(x, reps, out, shards, collective_id):
+    if out:
+        size, lanes = x.shape[0] // reps, x.shape[1]
+        x = x.reshape(reps, size, lanes)
+        shape = (size, HEADS * HEAD_DIM)
+    else:
+        size, lanes = x.shape[0], pad_to(x.shape[1] // reps, LANES)
+        shape = (reps, size, lanes)
     sems = pltpu.SemaphoreType.DMA((reps,))
     swapped, *fulls = pl.pallas_call(
-        functools.partial(swap_kernel, reps, halves_of(shards)),
-        out_shape=(jax.ShapeDtypeStruct(packed.shape, packed.dtype), *gathered_shapes(shards)),
-        in_specs=[HB] * (1 + sum(len(shard) for shard in shards)),
-        out_specs=(HB,) * (1 + len(shards)),
-        scratch_shapes=[sems, sems, *gather_scratch(shards)],
+        functools.partial(swap_kernel, reps, out, halves_of(shards)),
+        out_shape=(jax.ShapeDtypeStruct(shape, x.dtype), *gathered_shapes(shards)),
+        in_specs=[HB if out else VM] + [HB] * sum(len(shard) for shard in shards),
+        out_specs=(VM if out else HB,) + (HB,) * len(shards),
+        scratch_shapes=[pltpu.VMEM((reps, size, lanes), x.dtype), sems, sems, *gather_scratch(shards)],
         compiler_params=pltpu.CompilerParams(
             collective_id=collective_id, has_side_effects=True, vmem_limit_bytes=VMEM_LIMIT
         ),
-    )(packed, *(part for shard in shards for part in shard))
+    )(x, *(part for shard in shards for part in shard))
     return swapped, fulls
 
 
-def from_heads_kernel(reps, size, edge, dprev, own, dafter, dq, out_kv, out_q, from_up, from_down, total, mine, sends, recvs, send, recv):
+def from_heads_kernel(reps, size, edge, dprev, own, dafter, dq, out, out_kv, out_q, from_up, from_down, total, mine, sends, recvs, send, recv):
     group, me = lax.axis_index("fsdp"), lax.axis_index("replica")
     groups = lax.axis_size("fsdp")
     rows = reps * size
@@ -701,9 +770,23 @@
             recv_sem=recv.at[1, me], device_id=(group, there), device_id_type=MESH,
         ).start()
     pltpu.make_async_copy(mine.at[pl.ds(pl.multiple_of(me * size, size), size), :], out_kv.at[me], recv.at[1, me]).start()
+    width = out.shape[1] // 3
+    hd = width // reps
+
+    def unpack(ref, first, section):
+        def body(rows):
+            pieces = [(ref.at[place], first, place * hd, hd) for place in range(reps)]
+            out[rows, section * width : (section + 1) * width] = assemble(rows, width, pieces).astype(jnp.bfloat16)
+
+        by_rows(size, body)
+
     for piece in range(reps):
         wait_for(out_q.at[piece], recv.at[0, piece])
+    unpack(out_q, 0, 0)
+    for piece in range(reps):
         wait_for(out_kv.at[piece], recv.at[1, piece])
+    unpack(out_kv, 0, 1)
+    unpack(out_kv, hd, 2)
     for _, there in others:
         wait_for(out_q.at[0], send.at[0, there])
         wait_for(out_kv.at[0], send.at[1, there])
@@ -711,19 +794,18 @@
     pl.when(up)(to_up.wait_send)
 
 
-def from_heads(reps, dprev, own, dafter, dq, collective_id):
+def from_heads(reps, width, dprev, own, dafter, dq, collective_id):
     rows, kv = own.shape
     edge, size = dprev.shape[0], own.shape[0] // reps
     pair, both = pltpu.SemaphoreType.DMA((2,)), pltpu.SemaphoreType.DMA((2, reps))
     return pl.pallas_call(
         functools.partial(from_heads_kernel, reps, size, edge),
-        out_shape=(
-            jax.ShapeDtypeStruct((reps, size, kv), own.dtype),
-            jax.ShapeDtypeStruct((reps, size, dq.shape[1]), dq.dtype),
-        ),
+        out_shape=jax.ShapeDtypeStruct((size, 3 * width), own.dtype),
         in_specs=[HB, VM, HB, HB],
-        out_specs=(HB, HB),
+        out_specs=VM,
         scratch_shapes=[
+            pltpu.VMEM((reps, size, kv), own.dtype),
+            pltpu.VMEM((reps, size, dq.shape[1]), own.dtype),
             pltpu.VMEM((edge, kv), own.dtype),
             pltpu.VMEM((edge, kv), own.dtype),
             pltpu.VMEM((rows, kv), jnp.float32),
@@ -1022,19 +1104,7 @@
     return jnp.dot(left, right, preferred_element_type=jnp.float32)
 
 
-def group_heads(matrix, reps):
-    return matrix.reshape(matrix.shape[0], reps, -1).transpose(1, 0, 2)
-
-
-def ungroup_heads(stacked):
-    return stacked.transpose(1, 0, 2).reshape(stacked.shape[1], -1)
-
-
-def widen(stacked, width):
-    return jnp.pad(stacked, ((0, 0), (0, 0), (0, width - stacked.shape[2])))
-
-
-def layer_forward(stream, mod_tok, full, plan, in_first, shards_second, shards_ahead, collective_id):
+def layer_forward(stream, mod_tok, full, plan, in_first, shards_first, shards_second, shards_ahead, collective_id):
     qkv_w, qkv_b, out_w, out_b, up_w, up_b, down_w, down_b = full
     reps, edge, bounds, ids = plan
     width = stream.shape[1]
@@ -1047,16 +1117,15 @@
         [qkv_bias[:width], jnp.zeros((width,), jnp.float32), qkv_bias[width:]]
     )
     projected = (low_dot(normed, qkv_w) + bias_full).astype(jnp.bfloat16)
-    query, key, value = (group_heads(part, reps) for part in jnp.split(projected, 3, axis=1))
-    packed = widen(jnp.concatenate([key, value, query], axis=2), pad_to(3 * hd, LANES))
-    own, prev, after, fulls = to_heads(packed, edge, pad_to(2 * hd, LANES), in_first, collective_id)
+    in_second = sent_ahead(shards_first, projected) if shards_first else []
+    own, prev, after, fulls = to_heads(projected, reps, edge, pad_to(2 * hd, LANES), in_first, collective_id)
     first_gathered = fulls
-    in_second = sent_ahead(shards_second, own) if shards_second else ()
+    in_second += sent_ahead(shards_second, own) if shards_second else []
     mixed, mixed_t, log_norm = attend(nh, hd, *bounds, prev, own, after, *ids)
-    mixed, fulls = swap(mixed.reshape(reps, -1, mixed.shape[1]), in_second, collective_id + 1)
-    up_w, down_w = first_gathered or (up_w, down_w)
+    mixed, fulls = swap(mixed, reps, True, in_second, collective_id + 1)
+    if in_first:
+        (up_w,), (down_w, *fulls) = first_gathered, fulls
     in_next = sent_ahead(shards_ahead, mixed) if shards_ahead else ()
-    mixed = ungroup_heads(mixed[:, :, :hd])
     branch = low_dot(mixed, out_w) + out_b.astype(jnp.float32)
     middle = stream + gate_one * branch
     normed_two = pre_norm(middle, shift_two, scale_two).astype(jnp.bfloat16)
@@ -1095,16 +1164,12 @@
     grad_mixed = jnp.einsum(
         "te,de->td", grad_branch, out_w, preferred_element_type=jnp.float32
     ).astype(jnp.bfloat16)
-    grad_heads, _ = swap(widen(group_heads(grad_mixed, reps), pad_to(hd, LANES)), (), 3)
+    grad_heads, _ = swap(grad_mixed, reps, False, (), 3)
     prev, own, after = window
     grad_q, grad_prev, grad_own, grad_after = attend_back(
         nh, hd, *bounds, prev, own, after, *ids, grad_heads.reshape(own.shape[0], -1), *kept
     )
-    grad_kv, grad_q = from_heads(reps, grad_prev, grad_own, grad_after, grad_q, 4)
-    grad_projected = jnp.concatenate(
-        [ungroup_heads(grad_q[:, :, :hd]), ungroup_heads(grad_kv[:, :, :hd]), ungroup_heads(grad_kv[:, :, hd : 2 * hd])],
-        axis=1,
-    )
+    grad_projected = from_heads(reps, width, grad_prev, grad_own, grad_after, grad_q, 4)
     sums = jnp.sum(grad_projected.astype(jnp.float32), axis=0)
     grad_qkv_b = jnp.concatenate([sums[:width], sums[2 * width :]])
     grad_normed = jnp.einsum("te,de->td", grad_projected, qkv_w, preferred_element_type=jnp.float32)
@@ -1312,21 +1377,22 @@
     kept = []
     whole = lambda value: lax.all_gather(value, "fsdp", axis=0, tiled=True)
     fulls = []
-    in_first = sent_ahead((first_up_weight, first_down_weight), mod_first) if on_planes() else ()
+    in_first = sent_ahead((first_up_weight,), mod_first) if on_planes() else ()
     for layer_at, params in enumerate(layers):
         inputs.append(stream)
         ahead = layers[layer_at + 1] if layer_at + 1 < len(layers) else None
         qkv_w, out_w = attention_weights
         qkv_b, out_b, up_b, down_b = biases[layer_at]
-        shards_second, shards_ahead, up_w, down_w = (), (), None, None
+        shards_first, shards_second, shards_ahead, up_w, down_w = (), (), (), None, None
         if on_planes():
+            shards_first = (params[8],)
             shards_second = () if ahead is None else (ahead[2], ahead[4])
-            shards_ahead = () if ahead is None else (ahead[6], ahead[8])
+            shards_ahead = () if ahead is None else (ahead[6],)
         else:
             up_w, down_w = whole(params[6]), whole(params[8])
         full = (qkv_w, qkv_b, out_w, out_b, up_w, up_b, down_w, down_b)
         stream, saved, full, attention_weights, in_first = layer_forward(
-            stream, mod_tokens[layer_at], full, plan, in_first, shards_second, shards_ahead, 7 + 2 * layer_at
+            stream, mod_tokens[layer_at], full, plan, in_first, shards_first, shards_second, shards_ahead, 7 + 2 * layer_at
         )
         fulls.append(full)
         if ahead is not None and not on_planes():

time: 1270 us -> 1140 us (0.90)
  local copies, waits for them, and re-layouts: 138 us -> 65.5 us
  other arithmetic: 55.4 us -> 37.4 us
  Pallas kernels: 859 us -> 842 us
  waiting for transfers between devices: 29.2 us -> 14.7 us
    pallas_call x4, Pallas kernels: 70.4 us -> 118 us  [swap(): pl.pallas_call(functools.partial(swap_kernel, reps, out, halves_of(shards...]
    pallas_call x1, Pallas kernels: 397 us -> 366 us  [reduce_grads(): pl.pallas_call(functools.partial(reduce_kernel, layers, width, half), out...]
    transpose x14 -> x0, local copies, waits for them, and re-layouts: 29.9 us -> none  [ungroup_heads(): return stacked.transpose(1, 0, 2).reshape(stacked.shape[1], -1)]
    reshape x14 -> x0, local copies, waits for them, and re-layouts: 29.8 us -> none  [the longest x8 16.9 us: group_heads(): return matrix.reshape(matrix.shape[0], reps, -1).transpose(1, 0, 2)]
    pallas_call x2, Pallas kernels: 66.3 us -> 42.6 us  [attend(): pl.pallas_call(functools.partial(attend_kernel, nh, hd), out_shape=(jax.S...]
    ppermute x12, waiting for transfers between devices: 29.2 us -> 14.7 us  [sent_ahead(): lax.ppermute(shard, 'fsdp', [(at, at ^ step) for at in range(8)])]
    split x8 -> x0, local copies, waits for them, and re-layouts: 14.1 us -> none  [layer_forward(): jnp.split(projected, 3, axis=1)]
  transfers between devices with their start and end apart: 12 -> 12, of which waited for: 4 -> 2; matrix products, arithmetic and copies ran while one was open for 8% -> 6% of each run, Pallas kernels for 3% -> 12%
where the time goes in v4:
time: 1140 us; the launch traced here: 1130 us
  Pallas kernels  842 us (74%)
  matrix products  140 us (12%)
  local copies, waits for them, and re-layouts  65.5 us (6%)
  other arithmetic  37.4 us (3%)
  starting transfers between devices  31.1 us (3%)
  waiting for transfers between devices  14.7 us (1%)
    pallas_call x1, Pallas kernels, reduce_grads(): pl.pallas_call(functools.partial(reduce_kernel, layers, width, half), out...  366 us
    pallas_call x4, Pallas kernels, swap(): pl.pallas_call(functools.partial(swap_kernel, reps, out, halves_of(shards...  118 us
    pallas_call x2, Pallas kernels, to_heads(): pl.pallas_call(functools.partial(to_heads_kernel, reps, size, edge, kv, h...  96.5 us
    pallas_call x2, Pallas kernels, from_heads(): pl.pallas_call(functools.partial(from_heads_kernel, reps, size, edge), ou...  83.5 us
    pallas_call x1, Pallas kernels, start(): pl.pallas_call(functools.partial(start_kernel, halves_of(shards)), out_sh...  73.9 us
    pallas_call x2, Pallas kernels, attend_back(): pl.pallas_call(functools.partial(attend_back_kernel, nh, hd), out_shape=(...  61.7 us
    dot_general x10, matrix products, low_dot(): return jnp.dot(left, right, preferred_element_type=jnp.float32)  55 us
    pallas_call x2, Pallas kernels, attend(): pl.pallas_call(functools.partial(attend_kernel, nh, hd), out_shape=(jax.S...  42.6 us
  transfers between devices with their start and end apart: 12, of which 2 were waited for; matrix products, arithmetic and copies ran while one was open for 6% of the time, Pallas kernels for 12%

profile of v4, /device:TPU:0, one launch (start us, length us, event | category | flops | bytes accessed | tf_op | source)
XLA Modules:
  0.0 1132.1 jit_solution(3294365927914215345)
XLA Ops:
  12.6 73.9 %shard_map.407 = (f32[8,24,1152]{2,1,0:T(8,128)}, bf16[8,16,1152]{2,1,0:T(8,128)(2,1)}, bf16[1152,3456]{1,0:T(8,128)(2,1)}, bf16[1152,1152]{1,0:T(8,128)(2,1)}) custom-call(f32[8,24,1152]{2,1,0:T(8,128)} %reshape.387.part_in, bf16[16,1152]{1,0:T(8,128)(2,1)} %fusion.99.bias_in, bf16[144,3456]{1,0:T(8,128)(2,1)} %refs_0_.1, bf16[144,1152]{1,0:T(8,128)(2,1)} %refs_1_.1), custom_call_target="tpu_custom_call" | custom-call | tf_op jit(solution)/shard_map/pallas_call | solution.py:502
  101.0 3.7 fusion.2.qkv
  107.7 13.1 %collective-permute-done.1.refs_2_ = bf16[144,4608]{1,0:T(8,128)(2,1)} collective-permute-done((bf16[144,4608]{1,0:T(8,128)(2,1)}, bf16[144,4608]{1,0:T(8,128)(2,1)}, u32[]{:S(2)}, u32[]{:S(2)}) %collective-permute-start.1) | collective-permute-done | bytes 1327136 | tf_op jit(solution)/shard_map/ppermute | solution.py:402
  122.4 48.7 %shard_map.408 = (bf16[4,256,896]{2,1,0:T(8,128)(2,1)}, bf16[1024,640]{1,0:T(8,128)(2,1)}, bf16[1024,640]{1,0:T(8,128)(2,1)}, bf16[1152,4608]{1,0:T(8,128)(2,1)}) custom-call(bf16[256,3456]{1,0:T(8,128)(2,1)} %fusion.2.qkv, bf16[144,4608]{1,0:T(8,128)(2,1)} %refs_0_.2, bf16[144,4608]{1,0:T(8,128)(2,1)} %collective-permute-done.refs_1_, ...), custom_call_target="tpu_custom_call" | custom-call | tf_op jit(solution)/shard_map/pallas_call | solution.py:619
  171.1 20.8 %collective-permute-start.5 = (bf16[144,3456]{1,0:T(8,128)(2,1)}, bf16[144,3456]{1,0:T(8,128)(2,1)}, u32[]{:S(2)}, u32[]{:S(2)}) collective-permute-start(bf16[144,3456]{1,0:T(8,128)(2,1)} %refs_3_), channel_id=1, source_target_pairs={{0,16},{4,20},{8,24},{12,28},{16,0},{20,4},{24,8},{28,12},{1,17},{... | collective-permute-start | bytes 2985992 | tf_op jit(solution)/shard_map/ppermute | solution.py:402
  195.0 5.1 fusion.81
  205.5 21.3 %shard_map.409 = (bf16[1024,384]{1,0:T(8,128)(2,1)}, f32[384,1024]{1,0:T(8,128)}, f32[8,1024]{1,0:T(8,128)}) custom-call(s32[4]{0:T(128)} %get-tuple-element.184.lo, s32[4]{0:T(128)} %get-tuple-element.183.hi, bf16[1024,640]{1,0:T(8,128)(2,1)} %get-tuple-element.67.prev, bf16[1024,896]{1,0:T(8,128)(2,1)} %bitcast.132, ...), custom_call_target="tpu_custom_call" | custom-call | flops 2147483648 | bytes 8388608 | tf_op jit(solution)/shard_map/pallas_call | solution.py:144
  227.7 40.6 %shard_map.410 = (bf16[256,1152]{1,0:T(8,128)(2,1)}, bf16[4608,1152]{1,0:T(8,128)(2,1)}, bf16[1152,3456]{1,0:T(8,128)(2,1)}, bf16[1152,1152]{1,0:T(8,128)(2,1)}) custom-call(bf16[4,256,384]{2,1,0:T(8,128)(2,1)} %bitcast.115, bf16[576,1152]{1,0:T(8,128)(2,1)} %refs_0_.3, bf16[576,1152]{1,0:T(8,128)(2,1)} %collective-permute-done.2.refs_1_, ...), custom_call_target="tpu_custom_call" | custom-call | tf_op jit(solution)/shard_map/pallas_call | solution.py:694
  277.8 9.7 fusion.25
  287.6 6.9 fusion.134
  296.7 3.8 fusion.3.qkv
  307.9 4.4 copy.72.refs_0_
  314.4 47.8 %shard_map.411 = (bf16[4,256,896]{2,1,0:T(8,128)(2,1)}, bf16[1024,640]{1,0:T(8,128)(2,1)}, bf16[1024,640]{1,0:T(8,128)(2,1)}, bf16[1152,4608]{1,0:T(8,128)(2,1)}) custom-call(bf16[256,3456]{1,0:T(8,128)(2,1)} %fusion.3.qkv, bf16[144,4608]{1,0:T(8,128)(2,1)} %refs_0_.4, bf16[144,4608]{1,0:T(8,128)(2,1)} %collective-permute-done.8.refs_1_, ...), custom_call_target="tpu_custom_call" | custom-call | tf_op jit(solution)/shard_map/pallas_call | solution.py:619
  362.2 21.3 %shard_map.412 = (bf16[1024,384]{1,0:T(8,128)(2,1)}, f32[384,1024]{1,0:T(8,128)}, f32[8,1024]{1,0:T(8,128)}) custom-call(s32[4]{0:T(128)} %get-tuple-element.184.lo, s32[4]{0:T(128)} %get-tuple-element.183.hi, bf16[1024,640]{1,0:T(8,128)(2,1)} %get-tuple-element.80.prev, bf16[1024,896]{1,0:T(8,128)(2,1)} %bitcast.134, ...), custom_call_target="tpu_custom_call" | custom-call | flops 2147483648 | bytes 8388608 | tf_op jit(solution)/shard_map/pallas_call | solution.py:144
  383.6 40.1 %shard_map.413 = (bf16[256,1152]{1,0:T(8,128)(2,1)}, bf16[4608,1152]{1,0:T(8,128)(2,1)}) custom-call(bf16[4,256,384]{2,1,0:T(8,128)(2,1)} %bitcast.116, bf16[576,1152]{1,0:T(8,128)(2,1)} %refs_0_.5, bf16[576,1152]{1,0:T(8,128)(2,1)} %collective-permute-done.10.refs_1_, bf16[576,1152]{1,0:T(8,128)(2,1)} %collective-permute-done.11.refs_2_), custom_call_target="tpu_custom_call" | custom-call | tf_op jit(solution)/shard_map/pallas_call | solution.py:694
  425.8 4.3 fusion.133
  434.1 9.8 fusion.33
  443.9 9.8 convert_reduce_fusion
  453.8 8.3 multiply_reduce_fusion.2
  462.1 10.8 fusion.132
  477.2 20.1 %shard_map.414 = bf16[4,256,384]{2,1,0:T(8,128)(2,1)} custom-call(bf16[256,1152]{1,0:T(8,128)(2,1)} %convolution_convert_fusion.1.x_ref), custom_call_target="tpu_custom_call" | custom-call | tf_op jit(solution)/shard_map/pallas_call | solution.py:694
  497.3 30.8 %shard_map.415 = (bf16[1024,384]{1,0:T(8,128)(2,1)}, bf16[1024,640]{1,0:T(8,128)(2,1)}, bf16[1024,640]{1,0:T(8,128)(2,1)}, bf16[1024,640]{1,0:T(8,128)(2,1)}) custom-call(s32[4]{0:T(128)} %get-tuple-element.184.lo, s32[4]{0:T(128)} %get-tuple-element.183.hi, bf16[1024,640]{1,0:T(8,128)(2,1)} %get-tuple-element.80.prev, bf16[1024,896]{1,0:T(8,128)(2,1)} %bitcast.135, ...), custom_call_target="tpu_custom_call" | custom-call | flops 5368709120 | bytes 16777216 | tf_op jit(solution)/shard_map/pallas_call | solution.py:240
  528.1 36.4 %shard_map.416.refs_15_ = bf16[256,3456]{1,0:T(8,128)(2,1)} custom-call(bf16[1024,640]{1,0:T(8,128)(2,1)} %get-tuple-element.91.dprev, bf16[1024,640]{1,0:T(8,128)(2,1)} %get-tuple-element.92.own, bf16[1024,640]{1,0:T(8,128)(2,1)} %get-tuple-element.93.dafter, bf16[1024,384]{1,0:T(8,128)(2,1)} %get-tuple-element.94.dq), custom_call_target="tpu_custom_call" | custom-call | tf_op jit(solution)/shard_map/pallas_call | solution.py:801
  564.6 6.9 multiply_reduce_fusion.1
  575.9 7.9 convert_reduce_fusion.1
  583.9 8.3 multiply_reduce_fusion
  597.4 17.2 %shard_map.417 = bf16[4,256,384]{2,1,0:T(8,128)(2,1)} custom-call(bf16[256,1152]{1,0:T(8,128)(2,1)} %convolution_convert_fusion.x_ref), custom_call_target="tpu_custom_call" | custom-call | tf_op jit(solution)/shard_map/pallas_call | solution.py:694
  614.6 30.9 %shard_map.418 = (bf16[1024,384]{1,0:T(8,128)(2,1)}, bf16[1024,640]{1,0:T(8,128)(2,1)}, bf16[1024,640]{1,0:T(8,128)(2,1)}, bf16[1024,640]{1,0:T(8,128)(2,1)}) custom-call(s32[4]{0:T(128)} %get-tuple-element.184.lo, s32[4]{0:T(128)} %get-tuple-element.183.hi, bf16[1024,640]{1,0:T(8,128)(2,1)} %get-tuple-element.67.prev, bf16[1024,896]{1,0:T(8,128)(2,1)} %bitcast.133, ...), custom_call_target="tpu_custom_call" | custom-call | flops 5368709120 | bytes 16777216 | tf_op jit(solution)/shard_map/pallas_call | solution.py:240
  645.5 47.1 %shard_map.419.refs_7_ = bf16[256,3456]{1,0:T(8,128)(2,1)} custom-call(bf16[1024,640]{1,0:T(8,128)(2,1)} %get-tuple-element.97.dprev, bf16[1024,640]{1,0:T(8,128)(2,1)} %get-tuple-element.98.own, bf16[1024,640]{1,0:T(8,128)(2,1)} %get-tuple-element.99.dafter, bf16[1024,384]{1,0:T(8,128)(2,1)} %get-tuple-element.100.dq), custom_call_target="tpu_custom_call" | custom-call | tf_op jit(solution)/shard_map/pallas_call | solution.py:801
  692.6 7.8 fusion.52
  702.9 4.3 copy.75.refs_8_
  729.4 365.5 %shard_map.420 = (bf16[25,144,1152]{2,1,0:T(8,128)(2,1)}, bf16[8,32,1152]{2,1,0:T(8,128)(2,1)}) custom-call(bf16[4608,256]{1,0:T(8,128)(2,1)} %copy.72.refs_0_, bf16[1152,256]{1,0:T(8,128)(2,1)} %copy.73.refs_1_, bf16[1152,256]{1,0:T(8,128)(2,1)} %bitcast.121, bf16[1152,256]{1,0:T(8,128)(2,1)} %copy.74.refs_3_, bf16[256,1152]{1,0:T(8,128)(2,1)} %copy-done.43, ...), custom_call_target="tpu_custom_call" | custom-call | flops 16986931200 | bytes 104857600 | tf_op jit(solution)/shard_map/pallas_call | solution.py:1057
  (346 shorter events, 142.6 us)
Async XLA Ops:
  88.6 32.3 %collective-permute-start.1 = (bf16[144,4608]{1,0:T(8,128)(2,1)}, bf16[144,4608]{1,0:T(8,128)(2,1)}, u32[]{:S(2)}, u32[]{:S(2)}) collective-permute-start(bf16[144,4608]{1,0:T(8,128)(2,1)} %refs_0_.2), channel_id=1, source_target_pairs={{0,16},{4,20},{8,24},{12,28},{16,0},{20,4},{24,8},{28,12},{1,17},{... | collective-permute-start | bytes 3981320 | tf_op jit(solution)/shard_map/ppermute | solution.py:402
  90.1 32.3 %collective-permute-start = (bf16[144,4608]{1,0:T(8,128)(2,1)}, bf16[144,4608]{1,0:T(8,128)(2,1)}, u32[]{:S(2)}, u32[]{:S(2)}) collective-permute-start(bf16[144,4608]{1,0:T(8,128)(2,1)} %refs_0_.2), channel_id=1, source_target_pairs={{0,8},{4,12},{8,0},{12,4},{16,24},{20,28},{24,16},{28,20},{1,9},{5... | collective-permute-start | bytes 3981320 | tf_op jit(solution)/shard_map/ppermute | solution.py:402
  104.8 96.3 %collective-permute-start.3 = (bf16[576,1152]{1,0:T(8,128)(2,1)}, bf16[576,1152]{1,0:T(8,128)(2,1)}, u32[]{:S(2)}, u32[]{:S(2)}) collective-permute-start(bf16[576,1152]{1,0:T(8,128)(2,1)} %refs_0_.3), channel_id=1, source_target_pairs={{0,16},{4,20},{8,24},{12,28},{16,0},{20,4},{24,8},{28,12},{1,17},{... | collective-permute-start | bytes 3981320 | tf_op jit(solution)/shard_map/ppermute | solution.py:402
  105.3 121.5 %collective-permute-start.2 = (bf16[576,1152]{1,0:T(8,128)(2,1)}, bf16[576,1152]{1,0:T(8,128)(2,1)}, u32[]{:S(2)}, u32[]{:S(2)}) collective-permute-start(bf16[576,1152]{1,0:T(8,128)(2,1)} %refs_0_.3), channel_id=1, source_target_pairs={{0,8},{4,12},{8,0},{12,4},{16,24},{20,28},{24,16},{28,20},{1,9},{5... | collective-permute-start | bytes 3981320 | tf_op jit(solution)/shard_map/ppermute | solution.py:402
  107.7 85.5 %copy-start.48 = (f32[8,144]{1,0:T(8,128)S(1)}, f32[8,144]{1,0:T(8,128)}, u32[]{:S(2)}) copy-start(f32[8,144]{1,0:T(8,128)} %get-tuple-element.151) | copy-start | bytes 13828
  107.7 86.4 %copy-start.61 = (s32[16]{0:T(128)S(1)}, s32[16]{0:T(128)}, u32[]{:S(2)}) copy-start(s32[16]{0:T(128)} %copy-done.60) | copy-start | bytes 196
  171.1 55.8 %collective-permute-start.5 = (bf16[144,3456]{1,0:T(8,128)(2,1)}, bf16[144,3456]{1,0:T(8,128)(2,1)}, u32[]{:S(2)}, u32[]{:S(2)}) collective-permute-start(bf16[144,3456]{1,0:T(8,128)(2,1)} %refs_3_), channel_id=1, source_target_pairs={{0,16},{4,20},{8,24},{12,28},{16,0},{20,4},{24,8},{28,12},{1,17},{... | collective-permute-start | bytes 2985992 | tf_op jit(solution)/shard_map/ppermute | solution.py:402
  191.9 35.0 %collective-permute-start.4 = (bf16[144,3456]{1,0:T(8,128)(2,1)}, bf16[144,3456]{1,0:T(8,128)(2,1)}, u32[]{:S(2)}, u32[]{:S(2)}) collective-permute-start(bf16[144,3456]{1,0:T(8,128)(2,1)} %refs_3_), channel_id=1, source_target_pairs={{0,8},{4,12},{8,0},{12,4},{16,24},{20,28},{24,16},{28,20},{1,9},{5... | collective-permute-start | bytes 2985992 | tf_op jit(solution)/shard_map/ppermute | solution.py:402
  200.1 26.8 %collective-permute-start.7 = (bf16[144,1152]{1,0:T(8,128)(2,1)S(1)}, bf16[144,1152]{1,0:T(8,128)(2,1)S(1)}, u32[]{:S(2)}, u32[]{:S(2)}) collective-permute-start(bf16[144,1152]{1,0:T(8,128)(2,1)S(1)} %copy-done.44), channel_id=1, source_target_pairs={{0,16},{4,20},{8,24},{12,28},{16,0},{20,4},{24,8},{28,12},{1,17},{... | collective-permute-start | bytes 995336 | tf_op jit(solution)/shard_map/ppermute | solution.py:402
  201.1 25.8 %collective-permute-start.6 = (bf16[144,1152]{1,0:T(8,128)(2,1)S(1)}, bf16[144,1152]{1,0:T(8,128)(2,1)S(1)}, u32[]{:S(2)}, u32[]{:S(2)}) collective-permute-start(bf16[144,1152]{1,0:T(8,128)(2,1)S(1)} %copy-done.44), channel_id=1, source_target_pairs={{0,8},{4,12},{8,0},{12,4},{16,24},{20,28},{24,16},{28,20},{1,9},{5... | collective-permute-start | bytes 995336 | tf_op jit(solution)/shard_map/ppermute | solution.py:402
  227.7 44.2 %copy-start.29 = (bf16[1152,1152]{1,0:T(8,128)(2,1)S(1)}, bf16[1152,1152]{1,0:T(8,128)(2,1)}, u32[]{:S(2)}) copy-start(bf16[1152,1152]{1,0:T(8,128)(2,1)} %get-tuple-element.75) | copy-start | bytes 7962628
  268.3 46.1 %collective-permute-start.9 = (bf16[144,4608]{1,0:T(8,128)(2,1)}, bf16[144,4608]{1,0:T(8,128)(2,1)}, u32[]{:S(2)}, u32[]{:S(2)}) collective-permute-start(bf16[144,4608]{1,0:T(8,128)(2,1)} %refs_0_.4), channel_id=1, source_target_pairs={{0,16},{4,20},{8,24},{12,28},{16,0},{20,4},{24,8},{28,12},{1,17},{... | collective-permute-start | bytes 3981320 | tf_op jit(solution)/shard_map/ppermute | solution.py:402
  269.7 44.7 %collective-permute-start.8 = (bf16[144,4608]{1,0:T(8,128)(2,1)}, bf16[144,4608]{1,0:T(8,128)(2,1)}, u32[]{:S(2)}, u32[]{:S(2)}) collective-permute-start(bf16[144,4608]{1,0:T(8,128)(2,1)} %refs_0_.4), channel_id=1, source_target_pairs={{0,8},{4,12},{8,0},{12,4},{16,24},{20,28},{24,16},{28,20},{1,9},{5... | collective-permute-start | bytes 3981320 | tf_op jit(solution)/shard_map/ppermute | solution.py:402
  275.4 12.1 %copy-start.2 = (f32[256,1152]{1,0:T(8,128)}, f32[256,1152]{1,0:T(8,128)S(1)}, u32[]{:S(2)}) copy-start(f32[256,1152]{1,0:T(8,128)S(1)} %get-tuple-element.130) | copy-start | bytes 3538948
  275.7 11.8 %slice-start.4 = ((s8[10616832]{0:T(1024)(128)(4,1)}), s8[4194304]{0:T(1024)(128)(4,1)S(1)}, s32[]{:S(2)}) async-start(s8[10616832]{0:T(1024)(128)(4,1)} %bitcast.128), calls=%async_computation.4 | async-start | bytes 8388608
  277.8 9.7 copy-start.33
  277.8 9.7 slice-start.5
  277.8 18.9 %slice-start.7 = ((s8[7962624]{0:T(1024)(128)(4,1)}), s8[4194304]{0:T(1024)(128)(4,1)S(1)}, s32[]{:S(2)}) async-start(s8[7962624]{0:T(1024)(128)(4,1)} %bitcast.130), calls=%async_computation.7 | async-start | bytes 8388608
  300.5 83.0 %collective-permute-start.11 = (bf16[576,1152]{1,0:T(8,128)(2,1)}, bf16[576,1152]{1,0:T(8,128)(2,1)}, u32[]{:S(2)}, u32[]{:S(2)}) collective-permute-start(bf16[576,1152]{1,0:T(8,128)(2,1)} %refs_0_.5), channel_id=1, source_target_pairs={{0,16},{4,20},{8,24},{12,28},{16,0},{20,4},{24,8},{28,12},{1,17},{... | collective-permute-start | bytes 3981320 | tf_op jit(solution)/shard_map/ppermute | solution.py:402
  300.6 83.0 %collective-permute-start.10 = (bf16[576,1152]{1,0:T(8,128)(2,1)}, bf16[576,1152]{1,0:T(8,128)(2,1)}, u32[]{:S(2)}, u32[]{:S(2)}) collective-permute-start(bf16[576,1152]{1,0:T(8,128)(2,1)} %refs_0_.5), channel_id=1, source_target_pairs={{0,8},{4,12},{8,0},{12,4},{16,24},{20,28},{24,16},{28,20},{1,9},{5... | collective-permute-start | bytes 3981320 | tf_op jit(solution)/shard_map/ppermute | solution.py:402
  430.1 32.0 %copy-start.8 = (f32[256,1152]{1,0:T(8,128)}, f32[256,1152]{1,0:T(8,128)S(1)}, u32[]{:S(2)}) copy-start(f32[256,1152]{1,0:T(8,128)S(1)} %get-tuple-element.126) | copy-start | bytes 3538948
  434.1 9.9 copy-start.32
  434.1 9.9 copy-start.40
  434.1 19.7 %slice-start.2 = ((s8[7077888]{0:T(1024)(128)(4,1)}), s8[4194304]{0:T(1024)(128)(4,1)S(1)}, s32[]{:S(2)}) async-start(s8[7077888]{0:T(1024)(128)(4,1)} %bitcast.105), calls=%async_computation.2 | async-start | bytes 8388608
  443.9 9.8 copy-start.67
  443.9 9.9 slice-start.3
  462.1 10.8 copy-start.26
  528.1 46.7 %slice-start = ((s8[7077888]{0:T(1024)(128)(4,1)}), s8[2883584]{0:T(1024)(128)(4,1)S(1)}, s32[]{:S(2)}) async-start(s8[7077888]{0:T(1024)(128)(4,1)} %bitcast.103), calls=%async_computation | async-start | bytes 5767168
  564.6 10.3 slice-start.1
  575.3 18.0 %copy-start.20 = (f32[256,1152]{1,0:T(8,128)}, f32[256,1152]{1,0:T(8,128)S(1)}, u32[]{:S(2)}) copy-start(f32[256,1152]{1,0:T(8,128)S(1)} %get-tuple-element.105) | copy-start | bytes 3538948
  645.5 47.1 %copy-start.6 = (bf16[256,1152]{1,0:T(8,128)(2,1)S(1)}, bf16[256,1152]{1,0:T(8,128)(2,1)}, u32[]{:S(2)}) copy-start(bf16[256,1152]{1,0:T(8,128)(2,1)} %param.24) | copy-start | bytes 1769476
  645.5 47.1 %copy-start.50 = (f32[256]{0:T(256)S(1)}, f32[256]{0:T(256)}, u32[]{:S(2)}) copy-start(f32[256]{0:T(256)} %copy-done.49) | copy-start | bytes 3076
  (59 other events, 216.0 us)

commit v5 on v4

--- a/solution.py
+++ b/solution.py
@@ -158,9 +158,6 @@
             pltpu.VMEM((2, 8, BQ), jnp.float32),
         ],
         compiler_params=pltpu.CompilerParams(vmem_limit_bytes=VMEM_LIMIT),
-        cost_estimate=pl.CostEstimate(
-            flops=4 * nh * rows * 1024 * LANES, bytes_accessed=8 << 20, transcendentals=nh * rows * 1024
-        ),
     )(lo, hi, prev, own, after, kid, qid)
 
 
@@ -259,9 +256,6 @@
             pltpu.VMEM((8, BQ), jnp.float32),
         ],
         compiler_params=pltpu.CompilerParams(vmem_limit_bytes=VMEM_LIMIT),
-        cost_estimate=pl.CostEstimate(
-            flops=10 * nh * rows * 1024 * LANES, bytes_accessed=16 << 20, transcendentals=nh * rows * 1024
-        ),
     )(lo, hi, prev, own, after, kid, qid, grad, ot, lse)
 
 
@@ -821,21 +815,174 @@
     )(dprev, own, dafter, dq)
 
 
-UNITS = 12
+MATRICES = 12
+UNIT_WIDTH = 1152
 LEFT_ROWS = 4
-
-
-def reduce_kernel(layers, width, half, *refs):
-    count = layers * UNITS + 1
-    ins, extra_in, refs = refs[: 8 * layers], refs[8 * layers], refs[8 * layers + 1 :]
-    (out, shared, extra, share_s, share_r, left, right, csend, crecv, own, xs, xr, ys, yr, tx, ty, x2s, x2r, y2s, y2r, zs, z1r, z2s, z2r, fin,
-     load_sem, core_s, core_r, x_s, x_r, y_s, y_r, x2_s, x2_r, y2_s, y2_r, z1_s, z1_r, z2_s, z2_r, fin_l, fin_s, fin_r,
+PLACES = ((0, 0), (1, 0), (0, 1), (1, 1))
+
+
+class Terms:
+    def __init__(self, ins, left, right, rows, width, load_sem):
+        self.left, self.right, self.rows, self.width = left, right, rows, width
+        self.unit = right.shape[2]
+        self.parts = width // self.unit
+        f = lax.axis_index("fsdp")
+        self.c, self.x, self.y = lax.rem(f, 2), lax.rem(f // 2, 2), f // 4
+        self.core_at, self.x_at, self.y_at = f + 1 - 2 * self.c, f + 2 - 4 * self.x, f + 4 - 8 * self.y
+        self.loads, place, slot = [], 0, 0
+        for src in ins[:4]:
+            self.loads.append((src, left.at[pl.ds(place, src.shape[0]), :]))
+            place += src.shape[0]
+        for src in ins[4:]:
+            for part in range(src.shape[1] // self.unit):
+                self.loads.append((src.at[:, pl.ds(part * self.unit, self.unit)], right.at[slot]))
+                slot += 1
+        self.load_sem = load_sem
+
+    def start(self):
+        for at, (src, dst) in enumerate(self.loads):
+            pltpu.make_async_copy(src, dst, self.load_sem.at[at]).start()
+
+    def wait(self):
+        for at, (src, dst) in enumerate(self.loads):
+            pltpu.make_async_copy(src, dst, self.load_sem.at[at]).wait()
+
+    def block(self, core, mx, my):
+        x, y = self.x + mx * (1 - 2 * self.x), self.y + my * (1 - 2 * self.y)
+        return (y * 2 + x) * 2 + (self.c + core * (1 - 2 * self.c))
+
+    def stack(self, u, core):
+        rows, width = self.rows, self.width
+        m, part = u // self.parts, lax.rem(u, self.parts)
+        inside = jnp.where(
+            m < 4, rows * m, LEFT_ROWS * width + jnp.where(m < 8, 0, jnp.where(m < 9, width, 2 * width))
+        )
+        stride = jnp.where(m < 4, 4 * rows, rows)
+        other = jnp.maximum(m - 3, 0) * self.parts + part
+        blocks = []
+        for mx, my in PLACES:
+            start = pl.multiple_of(inside + stride * self.block(core, mx, my), 16)
+            blocks.append(self.left[pl.ds(start, rows), :])
+        return nn_dot(jnp.concatenate(blocks, axis=0), self.right[other])
+
+
+def term_scratch(ins, unit):
+    width, tokens = ins[1].shape
+    parts = width // unit
+    return [
+        pltpu.VMEM(((LEFT_ROWS + 3) * width, tokens), jnp.bfloat16),
+        pltpu.VMEM((9 * parts, tokens, unit), jnp.bfloat16),
+        pltpu.SemaphoreType.DMA((4 + 9 * parts,)),
+    ]
+
+
+def remote_copy(src, dst, s_sem, r_sem, where):
+    return pltpu.make_async_remote_copy(
+        src_ref=src, dst_ref=dst, send_sem=s_sem, recv_sem=r_sem, device_id=where, device_id_type=MESH
+    )
+
+
+def chip_kernel(width, half, *refs):
+    ins, (own, xs, ys, tx, ty), refs = refs[:8], refs[8:13], refs[13:]
+    left, right, load_sem, csend, crecv, own_b, xs_b, ys_b, tx_b, ty_b, core_s, core_r, out_sem = refs
+    r = lax.axis_index("replica")
+    count, rows = own.shape[:2]
+    terms = Terms(ins, left, right, rows, width, load_sem)
+    where = (terms.core_at, r)
+    greet([(where, True)], 1)
+    terms.start()
+    terms.wait()
+    bf16, f32 = jnp.bfloat16, jnp.float32
+
+    def core_copy(u):
+        pair, four = lax.rem(u, 2), lax.rem(u, 4)
+        return remote_copy(csend.at[pair], crecv.at[four], core_s.at[pair], core_r.at[four], where)
+
+    def stores(u):
+        pair = lax.rem(u, 2)
+        buffers = ((own_b, own), (xs_b, xs), (ys_b, ys), (tx_b, tx), (ty_b, ty))
+        return [
+            pltpu.make_async_copy(src.at[pair], dst.at[u], out_sem.at[at, pair]) for at, (src, dst) in enumerate(buffers)
+        ]
+
+    def close(u):
+        for copy in stores(u):
+            copy.wait()
+
+    def chip(u):
+        pair, four = lax.rem(u, 2), lax.rem(u, 4)
+        stacked = terms.stack(u, 0)
+        core_copy(u).wait()
+        totals = [stacked[m * rows : (m + 1) * rows] + crecv[four, m].astype(f32) for m in range(4)]
+        mine, along_x, along_y, opposite = [total.astype(bf16) for total in totals]
+        own_b[pair] = mine
+        xs_b[pair, 0] = along_x[:half]
+        tx_b[pair] = along_x[half:]
+        ty_b[pair] = along_y[:half]
+        ys_b[pair, 0] = along_y[half:]
+        xs_b[pair, 1] = opposite[:half]
+        ys_b[pair, 1] = opposite[half:]
+        for copy in stores(u):
+            copy.start()
+
+    def open_unit(u):
+        pair = lax.rem(u, 2)
+        csend[pair] = terms.stack(u, 1).astype(bf16).reshape(csend.shape[1:])
+        core_copy(u).start()
+
+    def step(t, carry):
+        pl.when(t < count)(lambda: open_unit(t))
+        pl.when(t >= 3)(lambda: close(t - 3))
+        pl.when(jnp.logical_and(t >= 1, t <= count))(lambda: chip(t - 1))
+        return carry
+
+    lax.fori_loop(0, count + 3, step, 0)
+
+
+def chip_sums(lefts, rights, collective_id):
+    ins = (*lefts, *rights)
+    width, tokens = lefts[1].shape
+    rows, unit = width // 8, UNIT_WIDTH
+    half = pad_to(rows // 2, 16)
+    count = MATRICES * (width // unit)
+    bf16 = jnp.bfloat16
+    shapes = ((rows, unit), (2, half, unit), (2, rows - half, unit), (rows - half, unit), (half, unit))
+    pair = pltpu.SemaphoreType.DMA((2,))
+    return pl.pallas_call(
+        functools.partial(chip_kernel, width, half),
+        out_shape=tuple(jax.ShapeDtypeStruct((count, *shape), bf16) for shape in shapes),
+        in_specs=[HB] * 8,
+        out_specs=(HB,) * 5,
+        scratch_shapes=[
+            *term_scratch(ins, unit),
+            pltpu.VMEM((2, 4, rows, unit), bf16),
+            pltpu.VMEM((4, 4, rows, unit), bf16),
+            *(pltpu.VMEM((2, *shape), bf16) for shape in shapes),
+            pair,
+            pltpu.SemaphoreType.DMA((4,)),
+            pltpu.SemaphoreType.DMA((5, 2)),
+        ],
+        compiler_params=pltpu.CompilerParams(
+            collective_id=collective_id, has_side_effects=True, vmem_limit_bytes=VMEM_LIMIT
+        ),
+        cost_estimate=pl.CostEstimate(flops=2 * 64 * width * width * tokens, bytes_accessed=40 << 20, transcendentals=0),
+    )(*ins)
+
+
+def reduce_kernel(width, half, *refs):
+    ins, (extra_in, own_in, xr_in, yr_in, tx_in, ty_in), (out, mine, shared), refs = refs[:8], refs[8:14], refs[14:17], refs[17:]
+    (left, right, load_sem, extra, extra_sem, cx_s, cx_r, cxs_sem, cxr_sem, share_s, share_r,
+     csend, crecv, own, xs, xr, ys, yr, tx, ty, x2s, x2r, y2s, y2r, zs, z1r, z2s, z2r, fin,
+     own_l, xr_l, yr_l, tx_l, ty_l, ready_sem,
+     core_s, core_r, x_s, x_r, y_s, y_r, x2_s, x2_r, y2_s, y2_r, z1_s, z1_r, z2_s, z2_r, fin_l, fin_s, fin_r,
      credit) = refs
     f, r = lax.axis_index("fsdp"), lax.axis_index("replica")
     rows = own.shape[1]
-    tokens = left.shape[1]
-    c, x, y = lax.rem(f, 2), lax.rem(f // 2, 2), f // 4
-    core_at, x_at, y_at = f + 1 - 2 * c, f + 2 - 4 * x, f + 4 - 8 * y
+    extras = extra.shape[0]
+    count = extras + 2 * own_in.shape[0]
+    unit = own.shape[2]
+    terms = Terms(ins, left, right, rows, width, load_sem)
+    core_at, x_at, y_at = terms.core_at, terms.x_at, terms.y_at
     inner = jnp.logical_and(r > 0, r < 3)
     outer = jnp.logical_not(inner)
     z_at = r + 1 - 2 * lax.rem(r, 2)
@@ -844,50 +991,20 @@
         [((there, r), True) for there in others] + [((f, r - 1), r > 0), ((f, r + 1), r < 3)],
         7 + (r > 0).astype(jnp.int32) + (r < 3).astype(jnp.int32),
     )
-    few = extra.shape[1]
-    loads = [(extra_in, extra)]
-    for layer in range(layers):
-        place = layer * (LEFT_ROWS + 3) * width
-        for at in range(4):
-            src = ins[8 * layer + at]
-            loads.append((src, left.at[pl.ds(place, src.shape[0]), :]))
-            place += src.shape[0]
-        slot = layer * 9
-        for at in range(4):
-            src = ins[8 * layer + 4 + at]
-            for part in range(src.shape[1] // width):
-                loads.append((src.at[:, pl.ds(part * width, width)], right.at[slot]))
-                slot += 1
-    for at, (src, dst) in enumerate(loads):
-        pltpu.make_async_copy(src, dst, load_sem.at[at]).start()
-    for at, (src, dst) in enumerate(loads):
-        pltpu.make_async_copy(src, dst, load_sem.at[at]).wait()
-
-    def send(src, dst, s_sem, r_sem, where):
-        return pltpu.make_async_remote_copy(
-            src_ref=src, dst_ref=dst, send_sem=s_sem, recv_sem=r_sem, device_id=where, device_id_type=MESH
-        )
-
-    def place_of(core, mx, my):
-        return ((y + my * (1 - 2 * y)) * 2 + (x + mx * (1 - 2 * x))) * 2 + (c + core * (1 - 2 * c))
-
-    def term(u, core, mx, my):
-        layer, w = (u - 1) // UNITS, lax.rem(u - 1, UNITS)
-        block = place_of(core, mx, my)
-        inside = jnp.where(
-            w < 4, rows * w, LEFT_ROWS * width + jnp.where(w < 8, 0, jnp.where(w < 9, width, 2 * width))
-        )
-        stride = jnp.where(w < 4, 4 * rows, rows)
-        start = pl.multiple_of(layer * ((LEFT_ROWS + 3) * width) + inside + stride * block, 16)
-        other = layer * 9 + jnp.maximum(w - 3, 0)
-        return nn_dot(left[pl.ds(start, rows), :], right[other])
-
-    places = ((0, 0), (1, 0), (0, 1), (1, 1))
+    few = extra.shape[2]
+    extra_load = pltpu.make_async_copy(extra_in, extra, extra_sem)
+    extra_load.start()
+    terms.start()
+    extra_load.wait()
+    send = remote_copy
     top, low = pl.ds(0, half), pl.ds(half, rows - half)
 
     def core_copy(slot):
         return send(csend.at[slot], crecv.at[slot], core_s.at[slot], core_r.at[slot], (core_at, r))
 
+    def extra_copy(u):
+        return send(cx_s.at[u], cx_r.at[u], cxs_sem.at[u], cxr_sem.at[u], (core_at, r))
+
     def x_copy(slot):
         return send(xs.at[slot], xr.at[slot], x_s.at[slot], x_r.at[slot], (x_at, r))
 
@@ -906,18 +1023,48 @@
     def z2_copy(slot):
         return send(z2s.at[slot], z2r.at[slot], z2_s.at[slot], z2_r.at[slot], (f, 3 - r))
 
+    def target(u):
+        v = u - extras
+        first = pl.multiple_of((v // 2) * unit, LANES)
+        return out.at[1 - lax.rem(v, 2), :, pl.ds(first, unit)]
+
     def fin_copy(slot, u):
-        return send(fin.at[slot], out.at[u], fin_s.at[slot], fin_r.at[u], (f, z_at))
+        return send(fin.at[slot], target(u), fin_s.at[slot], fin_r.at[u], (f, z_at))
 
     def keep_copy(slot, u):
-        return pltpu.make_async_copy(fin.at[slot], out.at[u], fin_l.at[slot])
+        return pltpu.make_async_copy(fin.at[slot], target(u), fin_l.at[slot])
+
+    def fin_extra(u):
+        slot = lax.rem(u, 4)
+        return send(fin.at[slot, pl.ds(0, few), :], mine.at[u], fin_s.at[slot], fin_r.at[u], (f, z_at))
+
+    def keep_extra(u):
+        slot = lax.rem(u, 4)
+        return pltpu.make_async_copy(fin.at[slot, pl.ds(0, few), :], mine.at[u], fin_l.at[slot])
+
+    def share_copy(u, there, where):
+        return send(
+            mine.at[u], shared.at[u, there], share_s.at[u, where], share_r.at[u, there], (where, r)
+        )
+
+    def ready_copies(u):
+        slot = lax.rem(u, 4)
+        buffers = ((own_in, own_l), (xr_in, xr_l), (yr_in, yr_l), (tx_in, tx_l), (ty_in, ty_l))
+        return [
+            pltpu.make_async_copy(src.at[(u - extras) // 2], dst.at[slot], ready_sem.at[at, slot])
+            for at, (src, dst) in enumerate(buffers)
+        ]
 
     f32, bf16 = jnp.float32, jnp.bfloat16
     z_slots = z1r.shape[0]
 
-    def stage(u, condition, body):
-        live = jnp.logical_and(u >= 0, u < count)
+    def stage(u, condition, body, first=0, last=count):
+        live = jnp.logical_and(u >= first, u < last)
         pl.when(live if condition is None else jnp.logical_and(live, condition))(lambda: body(u))
+
+    def share(u):
+        for there in others:
+            share_copy(u, f, there).start()
 
     def close(u):
         slot = lax.rem(u, 4)
@@ -927,12 +1074,27 @@
     def arrive(u):
         fin_copy(lax.rem(u, 4), u).wait_recv()
 
+    def close_extra(u):
+        fin_extra(u).wait_send()
+        keep_extra(u).wait()
+
+    def arrive_extra(u):
+        fin_extra(u).wait_recv()
+
     def finish(u):
         slot = lax.rem(u, 4)
         z2_copy(slot).wait()
         fin[slot] = (z2s[slot].astype(f32) + z2r[slot].astype(f32)).astype(bf16)
-        fin_copy(slot, u).start()
-        keep_copy(slot, u).start()
+
+        @pl.when(u >= extras)
+        def _():
+            fin_copy(slot, u).start()
+            keep_copy(slot, u).start()
+
+        @pl.when(u < extras)
+        def _():
+            fin_extra(u).start()
+            keep_extra(u).start()
 
     def middle(u):
         slot, z_slot, at = lax.rem(u, 4), lax.rem(u, z_slots), lax.rem(u, own.shape[0])
@@ -975,112 +1137,141 @@
         own[at, top, :] += xr[slot, 0].astype(f32)
         own[at, low, :] += yr[slot, 0].astype(f32)
 
-    def chip_extra(u):
-        core_copy(0).wait()
-        for m, (mx, my) in enumerate(places):
-            total = extra[place_of(0, mx, my)] + crecv[0, m, :few, :].astype(f32)
-            if m == 0:
-                own[0, :few, :] = total
-            elif m == 2:
-                ty[0, :few, :] = total
-            else:
-                xs[0, m // 2, :few, :] = total.astype(bf16)
-        x_copy(0).start()
-        y_copy(0).start()
+    def cross_ready(u):
+        slot, at = lax.rem(u, 4), lax.rem(u, own.shape[0])
+        for copy in ready_copies(u):
+            copy.wait()
+        y2s[slot] = (ty_l[slot].astype(f32) + xr_l[slot, 1].astype(f32)).astype(bf16)
+        y2_copy(slot).start()
+        x2s[slot] = (tx_l[slot].astype(f32) + yr_l[slot, 1].astype(f32)).astype(bf16)
+        x2_copy(slot).start()
+        own[at, top, :] = own_l[slot, top, :].astype(f32) + xr_l[slot, 0].astype(f32)
+        own[at, low, :] = own_l[slot, low, :].astype(f32) + yr_l[slot, 0].astype(f32)
 
     def chip(u):
-        slot, pair, at = lax.rem(u, 4), lax.rem(u, 2), lax.rem(u, own.shape[0])
+        slot, at = lax.rem(u, 4), lax.rem(u, own.shape[0])
+        w = (u - extras) // 2
+        pair = lax.rem(w, 2)
+        stacked = terms.stack(w, 0)
         core_copy(pair).wait()
-        total = term(u, 0, 1, 1) + crecv[pair, 3].astype(f32)
+        total = stacked[3 * rows :] + crecv[pair, 3].astype(f32)
         xs[slot, 1] = total[:half].astype(bf16)
         ys[slot, 1] = total[half:].astype(bf16)
-        total = term(u, 0, 1, 0) + crecv[pair, 1].astype(f32)
+        total = stacked[rows : 2 * rows] + crecv[pair, 1].astype(f32)
         xs[slot, 0] = total[:half].astype(bf16)
         tx[slot] = total[half:]
         x_copy(slot).start()
-        total = term(u, 0, 0, 1) + crecv[pair, 2].astype(f32)
+        total = stacked[2 * rows : 3 * rows] + crecv[pair, 2].astype(f32)
         ys[slot, 0] = total[half:].astype(bf16)
         ty[slot] = total[:half]
         y_copy(slot).start()
-        own[at] = term(u, 0, 0, 0) + crecv[pair, 0].astype(f32)
+        own[at] = stacked[:rows] + crecv[pair, 0].astype(f32)
+
+    def chip_extra(u):
+        slot, at = lax.rem(u, 4), lax.rem(u, own.shape[0])
+        extra_copy(u).wait()
+        for m, (mx, my) in enumerate(PLACES):
+            total = extra[u, terms.block(0, mx, my)] + cx_r[u, m].astype(f32)
+            if m == 0:
+                own[at, :few, :] = total
+            elif m == 2:
+                ty[slot, :few, :] = total
+            else:
+                xs[slot, m // 2, :few, :] = total.astype(bf16)
+        x_copy(slot).start()
+        y_copy(slot).start()
 
     def open_extra(u):
-        for m, (mx, my) in enumerate(places):
-            csend[0, m, :few, :] = extra[place_of(1, mx, my)].astype(bf16)
-        core_copy(0).start()
-
-    def share_copy(there, where):
-        return send(out.at[0, pl.ds(0, few), :], shared.at[there], share_s.at[where], share_r.at[there], (where, r))
-
-    def share(u):
+        for m, (mx, my) in enumerate(PLACES):
+            cx_s[u, m] = extra[u, terms.block(1, mx, my)].astype(bf16)
+        extra_copy(u).start()
+
+    def open_ready(u):
+        for copy in ready_copies(u):
+            copy.start()
+
+    def open_unit(u):
+        w = (u - extras) // 2
+        pair = lax.rem(w, 2)
+        csend[pair] = terms.stack(w, 1).astype(bf16).reshape(csend.shape[1:])
+        core_copy(pair).start()
+
+    def full(u):
+        return lax.rem(u - extras, 2) == 1
+
+    def prepared(u):
+        return lax.rem(u - extras, 2) == 0
+
+    def step(t, carry):
+        stage(t - 13, None, share, 0, extras)
+        stage(t - 12, inner, close, extras)
+        stage(t - 12, outer, arrive, extras)
+        stage(t - 12, inner, close_extra, 0, extras)
+        stage(t - 12, outer, arrive_extra, 0, extras)
+        stage(t - 10, inner, finish)
+        stage(t - 8, inner, middle)
+        stage(t - 8, outer, sent)
+        stage(t - 6, None, plane)
+        stage(t - 4, full(t - 4), cross, extras)
+        stage(t - 4, None, cross, 0, extras)
+        stage(t - 4, prepared(t - 4), cross_ready, extras)
+        stage(t - 2, full(t - 2), chip, extras)
+        stage(t - 2, None, chip_extra, 0, extras)
+        pl.when(t == extras)(terms.wait)
+        stage(t, full(t), open_unit, extras)
+        stage(t, prepared(t), open_ready, extras)
+        stage(t, None, open_extra, 0, extras)
+        return carry
+
+    lax.fori_loop(0, count + 12, step, 0)
+    for u in range(extras):
         for there in others:
-            share_copy(f, there).start()
-
-    def open_unit(u):
-        pair = lax.rem(u, 2)
-        for m, (mx, my) in enumerate(places):
-            csend[pair, m] = term(u, 1, mx, my).astype(bf16)
-        core_copy(pair).start()
-
-    def step(t, carry):
-        pl.when(t == 12)(lambda: share(t))
-        stage(t - 11, inner, close)
-        stage(t - 11, outer, arrive)
-        stage(t - 9, inner, finish)
-        stage(t - 7, inner, middle)
-        stage(t - 7, outer, sent)
-        stage(t - 5, None, plane)
-        stage(t - 3, None, cross)
-        stage(t - 1, t > 1, chip)
-        pl.when(t == 1)(lambda: chip_extra(t - 1))
-        stage(t, t > 0, open_unit)
-        pl.when(t == 0)(lambda: open_extra(t))
-        return carry
-
-    lax.fori_loop(0, count + 11, step, 0)
-    for there in others:
-        share_copy(f, there).wait_send()
-        share_copy(there, there).wait_recv()
-
-
-def reduce_grads(pairs, extra):
-    layers = len(pairs)
-    width, tokens = pairs[0][0][1].shape
-    rows = width // 8
+            share_copy(u, f, there).wait_send()
+            share_copy(u, there, there).wait_recv()
+
+
+def reduce_grads(lefts, rights, ready, extra):
+    width, tokens = lefts[1].shape
+    rows, unit = width // 8, UNIT_WIDTH
     half = pad_to(rows // 2, 16)
-    ins = [part for lefts, rights in pairs for part in (*lefts, *rights)] + [extra]
-    count = layers * UNITS + 1
+    ins = (*lefts, *rights)
+    extras, _, few, _ = extra.shape
+    count = extras + ready[0].shape[0] + MATRICES * (width // unit)
     bf16, f32 = jnp.bfloat16, jnp.float32
-    buf = lambda dtype, *shape: pltpu.VMEM((*shape, width), dtype)
-    sem = lambda size: pltpu.SemaphoreType.DMA((size,))
+    buf = lambda dtype, *shape: pltpu.VMEM((*shape, unit), dtype)
+    sem = lambda *size: pltpu.SemaphoreType.DMA(size)
     z_slots = 8
+    rest = rows - half
     return pl.pallas_call(
-        functools.partial(reduce_kernel, layers, width, half),
+        functools.partial(reduce_kernel, width, half),
         out_shape=(
-            jax.ShapeDtypeStruct((count, rows, width), bf16),
+            jax.ShapeDtypeStruct((2, rows, MATRICES * width), bf16),
+            jax.ShapeDtypeStruct((extras, few, unit), bf16),
             jax.ShapeDtypeStruct(extra.shape, bf16),
         ),
-        in_specs=[HB] * len(ins),
-        out_specs=(HB, HB),
+        in_specs=[HB] * 14,
+        out_specs=(HB, HB, HB),
         scratch_shapes=[
-            buf(f32, *extra.shape[:2]), sem(8), sem(8),
-            pltpu.VMEM((layers * (LEFT_ROWS + 3) * width, tokens), bf16),
-            buf(bf16, layers * 9, tokens),
+            *term_scratch(ins, unit),
+            pltpu.VMEM(extra.shape, f32), pltpu.SemaphoreType.DMA, buf(bf16, extras, 4, few), buf(bf16, extras, 4, few),
+            sem(extras), sem(extras), sem(extras, 8), sem(extras, 8),
             buf(bf16, 2, 4, rows), buf(bf16, 2, 4, rows), buf(f32, 9, rows),
-            buf(bf16, 4, 2, half), buf(bf16, 4, 2, half), buf(bf16, 4, 2, rows - half), buf(bf16, 4, 2, rows - half),
-            buf(f32, 4, rows - half), buf(f32, 4, half),
-            buf(bf16, 4, rows - half), buf(bf16, 4, rows - half), buf(bf16, 4, half), buf(bf16, 4, half),
+            buf(bf16, 4, 2, half), buf(bf16, 4, 2, half), buf(bf16, 4, 2, rest), buf(bf16, 4, 2, rest),
+            buf(f32, 4, rest), buf(f32, 4, half),
+            buf(bf16, 4, rest), buf(bf16, 4, rest), buf(bf16, 4, half), buf(bf16, 4, half),
             buf(bf16, 4, rows), buf(bf16, z_slots, rows), buf(bf16, 4, rows), buf(bf16, 4, rows), buf(bf16, 4, rows),
-            sem(13 * layers + 1), sem(2), sem(2), sem(4), sem(4), sem(4), sem(4), sem(4), sem(4), sem(4), sem(4),
+            buf(bf16, 4, rows), buf(bf16, 4, 2, half), buf(bf16, 4, 2, rest), buf(bf16, 4, rest), buf(bf16, 4, half),
+            sem(5, 4),
+            sem(2), sem(2), sem(4), sem(4), sem(4), sem(4), sem(4), sem(4), sem(4), sem(4),
             sem(4), sem(z_slots), sem(4), sem(4), sem(4), sem(4), sem(count), pltpu.SemaphoreType.REGULAR,
         ],
         compiler_params=pltpu.CompilerParams(
             collective_id=5, has_side_effects=True, vmem_limit_bytes=60 * 1024 * 1024
         ),
         cost_estimate=pl.CostEstimate(
-            flops=2 * count * 8 * rows * tokens * width, bytes_accessed=100 << 20, transcendentals=0
+            flops=2 * 64 * width * width * tokens, bytes_accessed=100 << 20, transcendentals=0
         ),
-    )(*ins)
+    )(*ins, extra, *ready)
 
 
 def pre_norm(stream, shift, scale):
@@ -1139,7 +1330,7 @@
     return (middle + gate_two * result, saved, full, fulls, in_next)
 
 
-def layer_backward(stream, mod_tok, full, saved, plan, pick, grad_next):
+def layer_backward(stream, mod_tok, full, saved, plan, pick, grad_next, beside):
     qkv_w, qkv_b, out_w, out_b, up_w, up_b, down_w, down_b = full
     normed, window, mixed, kept, branch, middle, normed_two, hidden, active, result = saved
     reps, edge, bounds, ids = plan
@@ -1170,6 +1361,7 @@
         nh, hd, *bounds, prev, own, after, *ids, grad_heads.reshape(own.shape[0], -1), *kept
     )
     grad_projected = from_heads(reps, width, grad_prev, grad_own, grad_after, grad_q, 4)
+    grad_projected, beside = lax.optimization_barrier((grad_projected, beside))
     sums = jnp.sum(grad_projected.astype(jnp.float32), axis=0)
     grad_qkv_b = jnp.concatenate([sums[:width], sums[2 * width :]])
     grad_normed = jnp.einsum("te,de->td", grad_projected, qkv_w, preferred_element_type=jnp.float32)
@@ -1188,7 +1380,7 @@
     return (
         grad_stream, grad_mod,
         ((active.T, normed_two.T, mixed.T, normed.T), (grad_result, grad_hidden, grad_branch, grad_projected)),
-        (grad_qkv_b, grad_out_b, grad_up_b, grad_down_b),
+        (grad_qkv_b, grad_out_b, grad_up_b, grad_down_b), beside,
     )
 
 
@@ -1219,7 +1411,13 @@
     return lax.axis_size("fsdp") == 8 and lax.axis_size("replica") == 4
 
 
-def owner_sums(pairs, grad_mods, grad_biases):
+def first_hop(lefts, rights):
+    own, xs, ys, tx, ty = chip_sums(lefts, rights, 11)
+    hop = lambda value, step: lax.ppermute(value, "fsdp", [(at, at ^ step) for at in range(8)])
+    return (own, hop(xs, 2), hop(ys, 4), tx, ty), own
+
+
+def owner_sums(pairs, ready, grad_mods, grad_biases):
     groups = lax.axis_size("fsdp")
     width = pairs[0][0][1].shape[0]
     if on_planes():
@@ -1228,26 +1426,25 @@
             [jnp.concatenate([part.reshape(groups, -1) for part in parts], axis=1) for parts in grad_biases], axis=1
         )
         extra = jnp.concatenate([mods, biases], axis=1)
-        used = extra.shape[1]
-        extra = jnp.pad(extra, ((0, 0), (0, pad_to(used, 16) - used), (0, 0)))
-        out, shared = reduce_grads(pairs, extra)
-        shared = lax.dynamic_update_slice_in_dim(
-            shared, out[None, 0, : extra.shape[1]], lax.axis_index("fsdp"), 0
-        )
+        used, parts = extra.shape[1], width // UNIT_WIDTH
+        lines = pad_to(used, 16) * parts
+        extras = -(-lines // pad_to(width // 16, 16))
+        extra = jnp.pad(extra, ((0, 0), (0, lines // parts - used), (0, 0)))
+        extra = extra.reshape(groups, extras, -1, UNIT_WIDTH).transpose(1, 0, 2, 3)
+        out, mine, shared = reduce_grads(*pairs[0], ready, extra)
+        shared = lax.dynamic_update_slice_in_dim(shared, mine[:, None], lax.axis_index("fsdp"), 1)
+        shared = shared.transpose(1, 0, 2, 3).reshape(groups, -1, width)
         mods = shared[:, : mods.shape[1]].reshape(len(pairs), -1, grad_mods[0].shape[1])
-        units = out[1:].reshape(len(pairs), UNITS, -1, width)
-        rows = units.shape[2]
-        across = lambda part: part.transpose(1, 0, 2).reshape(rows, -1).astype(jnp.float32)
+        mine = mine.reshape(-1, width)
+        columns = lambda layer_at, first, last: out[layer_at, :, first * width : last * width].astype(jnp.float32)
         results = []
-        for layer_at, unit in enumerate(units):
-            share = out[0, used - len(pairs) + layer_at].astype(jnp.float32)
+        for layer_at in range(2):
+            share = mine[used - 2 + layer_at].astype(jnp.float32)
             cuts = [0]
             for part in grad_biases[layer_at]:
                 cuts.append(cuts[-1] + part.shape[0] // groups)
-            weights = (
-                across(unit[9:12]), across(unit[8:9]), across(unit[4:8]),
-                unit[0:4].reshape(-1, width).astype(jnp.float32),
-            )
+            down = jnp.stack([columns(layer_at, m, m + 1) for m in range(4)]).reshape(-1, width)
+            weights = (columns(layer_at, 9, 12), columns(layer_at, 8, 9), columns(layer_at, 4, 8), down)
             results.append((weights, [share[i:j] for i, j in zip(cuts[:-1], cuts[1:])]))
         return results, mods
     flat = jnp.concatenate([part for parts in grad_biases for part in parts])
@@ -1401,16 +1598,20 @@
     output = stream.astype(jnp.bfloat16)
     grad_stream = cotangent.astype(jnp.float32)
     weight_pairs = [None, None]
+    ready = ()
     mod_grads = [None, None]
     bias_grads = [None, None]
     for layer_at in (1, 0):
-        grad_stream, grad_mod, local_grads, local_biases = layer_backward(
-            inputs[layer_at], mod_tokens[layer_at], fulls[layer_at], kept[layer_at], plan, pick, grad_stream
+        grad_stream, grad_mod, local_grads, local_biases, ready = layer_backward(
+            inputs[layer_at], mod_tokens[layer_at], fulls[layer_at], kept[layer_at], plan, pick, grad_stream, ready
         )
         weight_pairs[layer_at] = local_grads
+        if layer_at == 1 and on_planes():
+            ready, own = first_hop(*local_grads)
+            grad_stream, _ = lax.optimization_barrier((grad_stream, own))
         mod_grads[layer_at] = grad_mod
         bias_grads[layer_at] = local_biases
-    sums, (grad_mod_first, grad_mod_second) = owner_sums(weight_pairs, mod_grads, bias_grads)
+    sums, (grad_mod_first, grad_mod_second) = owner_sums(weight_pairs, ready, mod_grads, bias_grads)
     grad_silu = jnp.zeros(own_cond.shape, jnp.float32)
     ada_grads = []
     for params, grad_mod in zip(layers, (grad_mod_first, grad_mod_second)):

time: 1140 us -> 1100 us (0.965)
  Pallas kernels: 842 us -> 792 us
    pallas_call x1 -> x2, Pallas kernels: 366 us -> 325 us  [the longest x1 278 us: reduce_grads(): pl.pallas_call(functools.partial(reduce_kernel, width, half), out_shape=(...]
  transfers between devices with their start and end apart: 12 -> 14, of which waited for: 2 -> 4; matrix products, arithmetic and copies ran while one was open for 6% -> 8% of each run, Pallas kernels for 12% -> 20%
where the time goes in v5:
time: 1100 us; the launch traced here: 1090 us
  Pallas kernels  792 us (72%)
  matrix products  136 us (12%)
  local copies, waits for them, and re-layouts  62.9 us (6%)
  other arithmetic  48.4 us (4%)
  starting transfers between devices  36.6 us (3%)
  waiting for transfers between devices  16.5 us (2%)
    pallas_call x1, Pallas kernels, reduce_grads(): pl.pallas_call(functools.partial(reduce_kernel, width, half), out_shape=(...  278 us
    pallas_call x4, Pallas kernels, swap(): pl.pallas_call(functools.partial(swap_kernel, reps, out, halves_of(shards...  128 us
    pallas_call x2, Pallas kernels, to_heads(): pl.pallas_call(functools.partial(to_heads_kernel, reps, size, edge, kv, h...  97.2 us
    pallas_call x2, Pallas kernels, from_heads(): pl.pallas_call(functools.partial(from_heads_kernel, reps, size, edge), ou...  80.5 us
    pallas_call x1, Pallas kernels, start(): pl.pallas_call(functools.partial(start_kernel, halves_of(shards)), out_sh...  73.9 us
    dot_general x10, matrix products, low_dot(): return jnp.dot(left, right, preferred_element_type=jnp.float32)  55.4 us
    pallas_call x2, Pallas kernels, attend_back(): pl.pallas_call(functools.partial(attend_back_kernel, nh, hd), out_shape=(...  50.9 us
    pallas_call x1, Pallas kernels, chip_sums(): pl.pallas_call(functools.partial(chip_kernel, width, half), out_shape=tup...  47.2 us
  transfers between devices with their start and end apart: 14, of which 4 were waited for; matrix products, arithmetic and copies ran while one was open for 8% of the time, Pallas kernels for 20%

profile of v5, /device:TPU:0, one launch (start us, length us, event | category | flops | bytes accessed | tf_op | source)
XLA Modules:
  0.0 1094.5 jit_solution(13931226276931461248)
XLA Ops:
  12.3 73.9 %shard_map.407 = (f32[8,24,1152]{2,1,0:T(8,128)}, bf16[8,16,1152]{2,1,0:T(8,128)(2,1)}, bf16[1152,3456]{1,0:T(8,128)(2,1)}, bf16[1152,1152]{1,0:T(8,128)(2,1)}) custom-call(f32[8,24,1152]{2,1,0:T(8,128)} %reshape.390.part_in, bf16[16,1152]{1,0:T(8,128)(2,1)} %fusion.100.bias_in, bf16[144,3456]{1,0:T(8,128)(2,1)} %refs_0_.1, bf16[144,1152]{1,0:T(8,128)(2,1)} %refs_1_.1), custom_call_target="tpu_custom_call" | custom-call | tf_op jit(solution)/shard_map/pallas_call | solution.py:496
  107.1 13.5 %collective-permute-done.1.refs_2_ = bf16[144,4608]{1,0:T(8,128)(2,1)} collective-permute-done((bf16[144,4608]{1,0:T(8,128)(2,1)}, bf16[144,4608]{1,0:T(8,128)(2,1)}, u32[]{:S(2)}, u32[]{:S(2)}) %collective-permute-start.1) | collective-permute-done | bytes 1327136 | tf_op jit(solution)/shard_map/ppermute | solution.py:396
  122.1 48.8 %shard_map.408 = (bf16[4,256,896]{2,1,0:T(8,128)(2,1)}, bf16[1024,640]{1,0:T(8,128)(2,1)}, bf16[1024,640]{1,0:T(8,128)(2,1)}, bf16[1152,4608]{1,0:T(8,128)(2,1)}) custom-call(bf16[256,3456]{1,0:T(8,128)(2,1)} %fusion.2.qkv, bf16[144,4608]{1,0:T(8,128)(2,1)} %refs_0_.2, bf16[144,4608]{1,0:T(8,128)(2,1)} %collective-permute-done.refs_1_, ...), custom_call_target="tpu_custom_call" | custom-call | tf_op jit(solution)/shard_map/pallas_call | solution.py:613
  170.9 20.7 %collective-permute-start.5 = (bf16[144,3456]{1,0:T(8,128)(2,1)}, bf16[144,3456]{1,0:T(8,128)(2,1)}, u32[]{:S(2)}, u32[]{:S(2)}) collective-permute-start(bf16[144,3456]{1,0:T(8,128)(2,1)} %refs_3_), channel_id=1, source_target_pairs={{0,16},{4,20},{8,24},{12,28},{16,0},{20,4},{24,8},{28,12},{1,17},{... | collective-permute-start | bytes 2985992 | tf_op jit(solution)/shard_map/ppermute | solution.py:396
  194.9 5.1 fusion.82
  202.8 17.9 %shard_map.409 = (bf16[1024,384]{1,0:T(8,128)(2,1)}, f32[384,1024]{1,0:T(8,128)}, f32[8,1024]{1,0:T(8,128)}) custom-call(s32[4]{0:T(128)} %get-tuple-element.215.lo, s32[4]{0:T(128)} %get-tuple-element.214.hi, bf16[1024,640]{1,0:T(8,128)(2,1)} %get-tuple-element.80.prev, bf16[1024,896]{1,0:T(8,128)(2,1)} %bitcast.102, ...), custom_call_target="tpu_custom_call" | custom-call | tf_op jit(solution)/shard_map/pallas_call | solution.py:144
  222.9 44.3 %shard_map.410 = (bf16[256,1152]{1,0:T(8,128)(2,1)}, bf16[4608,1152]{1,0:T(8,128)(2,1)}, bf16[1152,3456]{1,0:T(8,128)(2,1)}, bf16[1152,1152]{1,0:T(8,128)(2,1)}) custom-call(bf16[4,256,384]{2,1,0:T(8,128)(2,1)} %bitcast.112, bf16[576,1152]{1,0:T(8,128)(2,1)} %refs_0_.3, bf16[576,1152]{1,0:T(8,128)(2,1)} %collective-permute-done.2.refs_1_, ...), custom_call_target="tpu_custom_call" | custom-call | tf_op jit(solution)/shard_map/pallas_call | solution.py:688
  274.5 9.7 fusion.33
  284.2 6.8 fusion.135
  306.8 12.0 %copy.71.refs_0_ = bf16[4608,256]{1,0:T(8,128)(2,1)} copy(bf16[4608,256]{0,1:T(8,128)(2,1)} %get-tuple-element.212) | data formatting | bytes 4718592 | tf_op jit(solution)/shard_map/convert_element_type | solution.py:1324
  321.0 48.5 %shard_map.411 = (bf16[4,256,896]{2,1,0:T(8,128)(2,1)}, bf16[1024,640]{1,0:T(8,128)(2,1)}, bf16[1024,640]{1,0:T(8,128)(2,1)}, bf16[1152,4608]{1,0:T(8,128)(2,1)}) custom-call(bf16[256,3456]{1,0:T(8,128)(2,1)} %fusion.3.qkv, bf16[144,4608]{1,0:T(8,128)(2,1)} %refs_0_.4, bf16[144,4608]{1,0:T(8,128)(2,1)} %collective-permute-done.8.refs_1_, ...), custom_call_target="tpu_custom_call" | custom-call | tf_op jit(solution)/shard_map/pallas_call | solution.py:613
  369.5 17.9 %shard_map.412 = (bf16[1024,384]{1,0:T(8,128)(2,1)}, f32[384,1024]{1,0:T(8,128)}, f32[8,1024]{1,0:T(8,128)}) custom-call(s32[4]{0:T(128)} %get-tuple-element.215.lo, s32[4]{0:T(128)} %get-tuple-element.214.hi, bf16[1024,640]{1,0:T(8,128)(2,1)} %get-tuple-element.93.prev, bf16[1024,896]{1,0:T(8,128)(2,1)} %bitcast.104, ...), custom_call_target="tpu_custom_call" | custom-call | tf_op jit(solution)/shard_map/pallas_call | solution.py:144
  387.4 40.4 %shard_map.413 = (bf16[256,1152]{1,0:T(8,128)(2,1)}, bf16[4608,1152]{1,0:T(8,128)(2,1)}) custom-call(bf16[4,256,384]{2,1,0:T(8,128)(2,1)} %bitcast.113, bf16[576,1152]{1,0:T(8,128)(2,1)} %refs_0_.5, bf16[576,1152]{1,0:T(8,128)(2,1)} %collective-permute-done.10.refs_1_, bf16[576,1152]{1,0:T(8,128)(2,1)} %collective-permute-done.11.refs_2_), custom_call_target="tpu_custom_call" | custom-call | tf_op jit(solution)/shard_map/pallas_call | solution.py:688
  429.9 4.3 fusion.134
  441.0 11.1 %fusion.25 = (bf16[4608,256]{0,1:T(8,128)(2,1)}, f32[256,4608]{1,0:T(8,128)}) fusion(f32[4608]{0:T(1024)S(1)} %reshape.412, bf16[256,1152]{1,0:T(8,128)(2,1)} %get-tuple-element.171, bf16[1152,4608]{1,0:T(8,128)(2,1)} %get-tuple-element.100), kind=kOutput, calls=%fused_computation.37 | convolution fusion | flops 2729705472 | bytes 18302976 | tf_op jit(solution)/shard_map/dot_general | solution.py:1295
  456.4 9.0 convert_reduce_fusion
  465.5 8.6 multiply_reduce_fusion.2
  474.1 10.1 fusion.133
  488.7 20.9 %shard_map.414 = bf16[4,256,384]{2,1,0:T(8,128)(2,1)} custom-call(bf16[256,1152]{1,0:T(8,128)(2,1)} %convolution_convert_fusion.1.x_ref), custom_call_target="tpu_custom_call" | custom-call | tf_op jit(solution)/shard_map/pallas_call | solution.py:688
  509.6 25.5 %shard_map.415 = (bf16[1024,384]{1,0:T(8,128)(2,1)}, bf16[1024,640]{1,0:T(8,128)(2,1)}, bf16[1024,640]{1,0:T(8,128)(2,1)}, bf16[1024,640]{1,0:T(8,128)(2,1)}) custom-call(s32[4]{0:T(128)} %get-tuple-element.215.lo, s32[4]{0:T(128)} %get-tuple-element.214.hi, bf16[1024,640]{1,0:T(8,128)(2,1)} %get-tuple-element.93.prev, bf16[1024,896]{1,0:T(8,128)(2,1)} %bitcast.105, ...), custom_call_target="tpu_custom_call" | custom-call | tf_op jit(solution)/shard_map/pallas_call | solution.py:237
  535.1 40.2 %shard_map.416.refs_7_ = bf16[256,3456]{1,0:T(8,128)(2,1)} custom-call(bf16[1024,640]{1,0:T(8,128)(2,1)} %get-tuple-element.104.dprev, bf16[1024,640]{1,0:T(8,128)(2,1)} %get-tuple-element.105.own, bf16[1024,640]{1,0:T(8,128)(2,1)} %get-tuple-element.106.dafter, bf16[1024,384]{1,0:T(8,128)(2,1)} %get-tuple-element.107.dq), custom_call_target="tpu_custom_call" | custom-call | tf_op jit(solution)/shard_map/pallas_call | solution.py:795
  575.3 6.7 multiply_reduce_fusion.1
  584.5 47.2 %shard_map.417 = (bf16[12,144,1152]{2,1,0:T(8,128)(2,1)}, bf16[12,2,80,1152]{3,2,1,0:T(8,128)(2,1)}, bf16[12,2,64,1152]{3,2,1,0:T(8,128)(2,1)}, bf16[12,64,1152]{2,1,0:T(8,128)(2,1)}, bf16[12,80,1152]{2,1,0:T(8,128)(2,1)}) custom-call(bf16[4608,256]{1,0:T(8,128)(2,1)} %copy.67.refs_0_, bf16[1152,256]{1,0:T(8,128)(2,1)} %copy.68.refs_1_, ...), custom_call_target="tpu_custom_call" | custom-call | flops 43486543872 | bytes 41943040 | tf_op jit(solution)/shard_map/pallas_call | solution.py:951
  633.3 8.8 convert_reduce_fusion.1
  642.1 5.6 collective-permute-start.13
  647.7 8.8 multiply_reduce_fusion
  666.7 22.5 %shard_map.418 = bf16[4,256,384]{2,1,0:T(8,128)(2,1)} custom-call(bf16[256,1152]{1,0:T(8,128)(2,1)} %convolution_convert_fusion.x_ref), custom_call_target="tpu_custom_call" | custom-call | tf_op jit(solution)/shard_map/pallas_call | solution.py:688
  689.2 25.4 %shard_map.419 = (bf16[1024,384]{1,0:T(8,128)(2,1)}, bf16[1024,640]{1,0:T(8,128)(2,1)}, bf16[1024,640]{1,0:T(8,128)(2,1)}, bf16[1024,640]{1,0:T(8,128)(2,1)}) custom-call(s32[4]{0:T(128)} %get-tuple-element.215.lo, s32[4]{0:T(128)} %get-tuple-element.214.hi, bf16[1024,640]{1,0:T(8,128)(2,1)} %get-tuple-element.80.prev, bf16[1024,896]{1,0:T(8,128)(2,1)} %bitcast.103, ...), custom_call_target="tpu_custom_call" | custom-call | tf_op jit(solution)/shard_map/pallas_call | solution.py:237
  714.6 40.3 %shard_map.420.refs_7_ = bf16[256,3456]{1,0:T(8,128)(2,1)} custom-call(bf16[1024,640]{1,0:T(8,128)(2,1)} %get-tuple-element.112.dprev, bf16[1024,640]{1,0:T(8,128)(2,1)} %get-tuple-element.113.own, bf16[1024,640]{1,0:T(8,128)(2,1)} %get-tuple-element.114.dafter, bf16[1024,384]{1,0:T(8,128)(2,1)} %get-tuple-element.115.dq), custom_call_target="tpu_custom_call" | custom-call | tf_op jit(solution)/shard_map/pallas_call | solution.py:795
  761.5 7.3 fusion.52
  780.5 278.0 %shard_map.421 = (bf16[2,144,13824]{2,1,0:T(8,128)(2,1)}, bf16[1,32,1152]{2,1,0:T(8,128)(2,1)}, bf16[1,8,32,1152]{3,2,1,0:T(8,128)(2,1)}) custom-call(bf16[4608,256]{1,0:T(8,128)(2,1)} %copy.71.refs_0_, bf16[1152,256]{1,0:T(8,128)(2,1)} %copy.72.refs_1_, bf16[1152,256]{1,0:T(8,128)(2,1)} %bitcast.116, bf16[1152,256]{1,0:T(8,128)(2,1)} %copy.73.refs_3_, ...), custom_call_target="tpu_custom_call" | custom-call | flops 43486543872 | bytes 104857600 | tf_op jit(solution)/shard_map/pallas_call | solution.py:1245
  1079.4 4.8 bitcast_convert_fusion.1
  (345 shorter events, 147.6 us)
Async XLA Ops:
  88.3 32.3 %collective-permute-start.1 = (bf16[144,4608]{1,0:T(8,128)(2,1)}, bf16[144,4608]{1,0:T(8,128)(2,1)}, u32[]{:S(2)}, u32[]{:S(2)}) collective-permute-start(bf16[144,4608]{1,0:T(8,128)(2,1)} %refs_0_.2), channel_id=1, source_target_pairs={{0,16},{4,20},{8,24},{12,28},{16,0},{20,4},{24,8},{28,12},{1,17},{... | collective-permute-start | bytes 3981320 | tf_op jit(solution)/shard_map/ppermute | solution.py:396
  89.8 32.3 %collective-permute-start = (bf16[144,4608]{1,0:T(8,128)(2,1)}, bf16[144,4608]{1,0:T(8,128)(2,1)}, u32[]{:S(2)}, u32[]{:S(2)}) collective-permute-start(bf16[144,4608]{1,0:T(8,128)(2,1)} %refs_0_.2), channel_id=1, source_target_pairs={{0,8},{4,12},{8,0},{12,4},{16,24},{20,28},{24,16},{28,20},{1,9},{5... | collective-permute-start | bytes 3981320 | tf_op jit(solution)/shard_map/ppermute | solution.py:396
  92.3 102.5 %copy-start.44 = (s32[256]{0:T(256)}, s32[256]{0:T(256)S(1)}, u32[]{:S(2)}) copy-start(s32[256]{0:T(256)S(1)} %and_select_fusion.2) | copy-start | bytes 3076
  104.5 89.2 %collective-permute-start.3 = (bf16[576,1152]{1,0:T(8,128)(2,1)}, bf16[576,1152]{1,0:T(8,128)(2,1)}, u32[]{:S(2)}, u32[]{:S(2)}) collective-permute-start(bf16[576,1152]{1,0:T(8,128)(2,1)} %refs_0_.3), channel_id=1, source_target_pairs={{0,16},{4,20},{8,24},{12,28},{16,0},{20,4},{24,8},{28,12},{1,17},{... | collective-permute-start | bytes 3981320 | tf_op jit(solution)/shard_map/ppermute | solution.py:396
  105.1 115.6 %collective-permute-start.2 = (bf16[576,1152]{1,0:T(8,128)(2,1)}, bf16[576,1152]{1,0:T(8,128)(2,1)}, u32[]{:S(2)}, u32[]{:S(2)}) collective-permute-start(bf16[576,1152]{1,0:T(8,128)(2,1)} %refs_0_.3), channel_id=1, source_target_pairs={{0,8},{4,12},{8,0},{12,4},{16,24},{20,28},{24,16},{28,20},{1,9},{5... | collective-permute-start | bytes 3981320 | tf_op jit(solution)/shard_map/ppermute | solution.py:396
  107.1 84.9 %copy-start.67 = (s32[16]{0:T(128)S(1)}, s32[16]{0:T(128)}, u32[]{:S(2)}) copy-start(s32[16]{0:T(128)} %copy-done.66) | copy-start | bytes 196
  107.1 85.6 %copy-start.46 = (bf16[144,1152]{1,0:T(8,128)(2,1)S(1)}, bf16[144,1152]{1,0:T(8,128)(2,1)}, u32[]{:S(2)}) copy-start(bf16[144,1152]{1,0:T(8,128)(2,1)} %refs_6_) | copy-start | bytes 995332
  170.9 51.3 %collective-permute-start.5 = (bf16[144,3456]{1,0:T(8,128)(2,1)}, bf16[144,3456]{1,0:T(8,128)(2,1)}, u32[]{:S(2)}, u32[]{:S(2)}) collective-permute-start(bf16[144,3456]{1,0:T(8,128)(2,1)} %refs_3_), channel_id=1, source_target_pairs={{0,16},{4,20},{8,24},{12,28},{16,0},{20,4},{24,8},{28,12},{1,17},{... | collective-permute-start | bytes 2985992 | tf_op jit(solution)/shard_map/ppermute | solution.py:396
  191.6 30.6 %collective-permute-start.4 = (bf16[144,3456]{1,0:T(8,128)(2,1)}, bf16[144,3456]{1,0:T(8,128)(2,1)}, u32[]{:S(2)}, u32[]{:S(2)}) collective-permute-start(bf16[144,3456]{1,0:T(8,128)(2,1)} %refs_3_), channel_id=1, source_target_pairs={{0,8},{4,12},{8,0},{12,4},{16,24},{20,28},{24,16},{28,20},{1,9},{5... | collective-permute-start | bytes 2985992 | tf_op jit(solution)/shard_map/ppermute | solution.py:396
  192.8 28.8 %collective-permute-start.7 = (bf16[144,1152]{1,0:T(8,128)(2,1)S(1)}, bf16[144,1152]{1,0:T(8,128)(2,1)S(1)}, u32[]{:S(2)}, u32[]{:S(2)}) collective-permute-start(bf16[144,1152]{1,0:T(8,128)(2,1)S(1)} %copy-done.46), channel_id=1, source_target_pairs={{0,16},{4,20},{8,24},{12,28},{16,0},{20,4},{24,8},{28,12},{1,17},{... | collective-permute-start | bytes 995336 | tf_op jit(solution)/shard_map/ppermute | solution.py:396
  193.8 28.4 %collective-permute-start.6 = (bf16[144,1152]{1,0:T(8,128)(2,1)S(1)}, bf16[144,1152]{1,0:T(8,128)(2,1)S(1)}, u32[]{:S(2)}, u32[]{:S(2)}) collective-permute-start(bf16[144,1152]{1,0:T(8,128)(2,1)S(1)} %copy-done.46), channel_id=1, source_target_pairs={{0,8},{4,12},{8,0},{12,4},{16,24},{20,28},{24,16},{28,20},{1,9},{5... | collective-permute-start | bytes 995336 | tf_op jit(solution)/shard_map/ppermute | solution.py:396
  222.9 45.6 %copy-start.32 = (bf16[1152,1152]{1,0:T(8,128)(2,1)S(1)}, bf16[1152,1152]{1,0:T(8,128)(2,1)}, u32[]{:S(2)}) copy-start(bf16[1152,1152]{1,0:T(8,128)(2,1)} %get-tuple-element.88) | copy-start | bytes 7962628
  267.2 53.8 %collective-permute-start.9 = (bf16[144,4608]{1,0:T(8,128)(2,1)}, bf16[144,4608]{1,0:T(8,128)(2,1)}, u32[]{:S(2)}, u32[]{:S(2)}) collective-permute-start(bf16[144,4608]{1,0:T(8,128)(2,1)} %refs_0_.4), channel_id=1, source_target_pairs={{0,16},{4,20},{8,24},{12,28},{16,0},{20,4},{24,8},{28,12},{1,17},{... | collective-permute-start | bytes 3981320 | tf_op jit(solution)/shard_map/ppermute | solution.py:396
  267.3 53.7 %collective-permute-start.8 = (bf16[144,4608]{1,0:T(8,128)(2,1)}, bf16[144,4608]{1,0:T(8,128)(2,1)}, u32[]{:S(2)}, u32[]{:S(2)}) collective-permute-start(bf16[144,4608]{1,0:T(8,128)(2,1)} %refs_0_.4), channel_id=1, source_target_pairs={{0,8},{4,12},{8,0},{12,4},{16,24},{20,28},{24,16},{28,20},{1,9},{5... | collective-permute-start | bytes 3981320 | tf_op jit(solution)/shard_map/ppermute | solution.py:396
  272.0 12.2 %copy-start.2 = (f32[256,1152]{1,0:T(8,128)}, f32[256,1152]{1,0:T(8,128)S(1)}, u32[]{:S(2)}) copy-start(f32[256,1152]{1,0:T(8,128)S(1)} %get-tuple-element.155) | copy-start | bytes 3538948
  272.3 11.9 %slice-start = ((s8[10616832]{0:T(1024)(128)(4,1)}), s8[4194304]{0:T(1024)(128)(4,1)S(1)}, s32[]{:S(2)}) async-start(s8[10616832]{0:T(1024)(128)(4,1)} %bitcast.124), calls=%async_computation | async-start | bytes 8388608
  274.4 9.7 copy-start.34
  274.4 9.7 slice-start.1
  274.5 18.8 %slice-start.3 = ((s8[7962624]{0:T(1024)(128)(4,1)}), s8[4194304]{0:T(1024)(128)(4,1)S(1)}, s32[]{:S(2)}) async-start(s8[7962624]{0:T(1024)(128)(4,1)} %bitcast.126), calls=%async_computation.3 | async-start | bytes 8388608
  297.1 90.2 %collective-permute-start.11 = (bf16[576,1152]{1,0:T(8,128)(2,1)}, bf16[576,1152]{1,0:T(8,128)(2,1)}, u32[]{:S(2)}, u32[]{:S(2)}) collective-permute-start(bf16[576,1152]{1,0:T(8,128)(2,1)} %refs_0_.5), channel_id=1, source_target_pairs={{0,16},{4,20},{8,24},{12,28},{16,0},{20,4},{24,8},{28,12},{1,17},{... | collective-permute-start | bytes 3981320 | tf_op jit(solution)/shard_map/ppermute | solution.py:396
  298.0 89.4 %collective-permute-start.10 = (bf16[576,1152]{1,0:T(8,128)(2,1)}, bf16[576,1152]{1,0:T(8,128)(2,1)}, u32[]{:S(2)}, u32[]{:S(2)}) collective-permute-start(bf16[576,1152]{1,0:T(8,128)(2,1)} %refs_0_.5), channel_id=1, source_target_pairs={{0,8},{4,12},{8,0},{12,4},{16,24},{20,28},{24,16},{28,20},{1,9},{5... | collective-permute-start | bytes 3981320 | tf_op jit(solution)/shard_map/ppermute | solution.py:396
  474.1 10.2 copy-start.29
  474.1 10.1 copy-start.14
  484.2 100.0 %copy-start.18 = (f32[256,1152]{1,0:T(8,128)}, f32[256,1152]{1,0:T(8,128)S(1)}, u32[]{:S(2)}) copy-start(f32[256,1152]{1,0:T(8,128)S(1)} %get-tuple-element.149) | copy-start | bytes 3538948
  584.5 47.2 %copy-start.7 = (f32[256,1152]{1,0:T(8,128)}, f32[256,1152]{1,0:T(8,128)S(1)}, u32[]{:S(2)}) copy-start(f32[256,1152]{1,0:T(8,128)S(1)} %add_add_fusion.6) | copy-start | bytes 3538948
  633.3 14.4 %copy-start.3 = (f32[256,1152]{1,0:T(8,128)S(1)}, f32[256,1152]{1,0:T(8,128)}, u32[]{:S(2)}) copy-start(f32[256,1152]{1,0:T(8,128)} %copy-done.2) | copy-start | bytes 3538948
  633.3 14.4 %copy-start.53 = (f32[256]{0:T(256)S(1)}, f32[256]{0:T(256)}, u32[]{:S(2)}) copy-start(f32[256]{0:T(256)} %copy-done.52) | copy-start | bytes 3076
  642.1 14.4 %copy-start.69 = (bf16[256,4608]{1,0:T(8,128)(2,1)}, bf16[256,4608]{1,0:T(8,128)(2,1)S(1)}, u32[]{:S(2)}) copy-start(bf16[256,4608]{1,0:T(8,128)(2,1)S(1)} %get-tuple-element.132.refs_5_) | copy-start | bytes 7077892
  642.1 118.8 %collective-permute-start.13 = (bf16[12,2,64,1152]{3,2,1,0:T(8,128)(2,1)}, bf16[12,2,64,1152]{3,2,1,0:T(8,128)(2,1)}, u32[]{:S(2)}, u32[]{:S(2)}) collective-permute-start(bf16[12,2,64,1152]{3,2,1,0:T(8,128)(2,1)} %get-tuple-element.117), channel_id=1, source_target_pairs={{0,16},{4,20},{8,24},{12,28},{16,0},{20,4},{24,8},{28,12},{1,17},{... | collective-permute-start | bytes 10616840 | tf_op jit(solution)/shard_map/ppermute | solution.py:1416
  647.7 113.3 %collective-permute-start.12 = (bf16[12,2,80,1152]{3,2,1,0:T(8,128)(2,1)}, bf16[12,2,80,1152]{3,2,1,0:T(8,128)(2,1)}, u32[]{:S(2)}, u32[]{:S(2)}) collective-permute-start(bf16[12,2,80,1152]{3,2,1,0:T(8,128)(2,1)} %get-tuple-element.116), channel_id=1, source_target_pairs={{0,8},{4,12},{8,0},{12,4},{16,24},{20,28},{24,16},{28,20},{1,9},{5... | collective-permute-start | bytes 13271048 | tf_op jit(solution)/shard_map/ppermute | solution.py:1416
  714.6 40.3 %copy-start.22 = (f32[256,1152]{1,0:T(8,128)S(1)}, f32[256,1152]{1,0:T(8,128)}, u32[]{:S(2)}) copy-start(f32[256,1152]{1,0:T(8,128)} %copy-done.21) | copy-start | bytes 3538948
  714.6 40.3 %copy-start.45 = (s32[256]{0:T(256)S(1)}, s32[256]{0:T(256)}, u32[]{:S(2)}) copy-start(s32[256]{0:T(256)} %copy-done.44) | copy-start | bytes 3076
  (60 other events, 212.3 us)

commit v6 on v5

--- a/solution.py
+++ b/solution.py
@@ -524,13 +524,6 @@
     wide = x_ref.shape[2]
     width = qkv.shape[1] // 3
     hd = width // reps
-    for place in range(reps):
-        def pack(rows, place=place):
-            at = place * hd
-            pieces = [(qkv, width + at, 0, hd), (qkv, 2 * width + at, hd, hd), (qkv, at, 2 * hd, hd)]
-            x_ref[place, rows, :] = assemble(rows, wide, pieces).astype(jnp.bfloat16)
-
-        by_rows(size, pack)
     down, up = group > 0, group < groups - 1
     others = [(group, lax.rem(me + d, reps)) for d in range(1, reps)]
     greet(
@@ -546,10 +539,23 @@
             recv_sem=recv.at[part, me], device_id=(group, there), device_id_type=MESH,
         )
 
-    for part, span in enumerate(spans):
-        for _, there in others:
-            exchange(span, part, there).start()
-        pltpu.make_async_copy(x_ref.at[me, :, span], own.at[me, :, span], recv.at[part, me]).start()
+    def depart(place, part):
+        span = spans[part]
+        pl.when(me != place)(lambda: exchange(span, part, place).start())
+        keep = pltpu.make_async_copy(x_ref.at[place, :, span], own.at[place, :, span], recv.at[part, place])
+        pl.when(me == place)(keep.start)
+
+    for place in range(reps):
+        def pack(rows, place=place):
+            at = place * hd
+            pieces = [(qkv, width + at, 0, hd), (qkv, 2 * width + at, hd, hd), (qkv, at, 2 * hd, hd)]
+            x_ref[place, rows, :] = assemble(rows, wide, pieces).astype(jnp.bfloat16)
+
+        by_rows(size, pack)
+        depart(place, 0)
+    for part in range(1, len(spans)):
+        for place in range(reps):
+            depart(place, part)
 
     if count:
         gather.begin()
@@ -638,24 +644,22 @@
     others = [(group, lax.rem(me + d, reps)) for d in range(1, reps)]
     planar = [(there, me) for there in (gather.core, gather.x, gather.y)] if count else []
     size, lanes = held.shape[1:]
-    if out:
-        src, dst = x_ref, held
-        hd = y_ref.shape[1] // reps
-    else:
-        src, dst = held, y_ref
-        hd = x_ref.shape[1] // reps
-        for place in range(reps):
+    src, dst = (x_ref, held) if out else (held, y_ref)
+    hd = (y_ref if out else x_ref).shape[1] // reps
+    greet([(place, True) for place in others + planar], reps - 1 + len(planar))
+    for place in range(reps):
+        if not out:
             def pack(rows, place=place):
                 held[place, rows, :] = assemble(rows, lanes, [(x_ref, place * hd, 0, hd)]).astype(jnp.bfloat16)
 
             by_rows(size, pack)
-    greet([(place, True) for place in others + planar], reps - 1 + len(planar))
-    for _, there in others:
-        pltpu.make_async_remote_copy(
-            src_ref=src.at[there], dst_ref=dst.at[me], send_sem=send.at[there], recv_sem=recv.at[me],
-            device_id=(group, there), device_id_type=MESH,
-        ).start()
-    pltpu.make_async_copy(src.at[me], dst.at[me], recv.at[me]).start()
+        leave = pltpu.make_async_remote_copy(
+            src_ref=src.at[place], dst_ref=dst.at[me], send_sem=send.at[place], recv_sem=recv.at[me],
+            device_id=(group, place), device_id_type=MESH,
+        )
+        keep = pltpu.make_async_copy(src.at[place], dst.at[place], recv.at[place])
+        pl.when(me != place)(leave.start)
+        pl.when(me == place)(keep.start)
     if count:
         gather.begin()
     for at in range(count):
@@ -816,14 +820,14 @@
 
 
 MATRICES = 12
-UNIT_WIDTH = 1152
+CHIP_WIDTH, UNIT_WIDTH = 1152, 384
 LEFT_ROWS = 4
 PLACES = ((0, 0), (1, 0), (0, 1), (1, 1))
 
 
 class Terms:
-    def __init__(self, ins, left, right, rows, width, load_sem):
-        self.left, self.right, self.rows, self.width = left, right, rows, width
+    def __init__(self, ins, flat, left, right, rows, width, load_sem):
+        self.flat, self.left, self.right, self.rows, self.width = flat, left, right, rows, width
         self.unit = right.shape[2]
         self.parts = width // self.unit
         f = lax.axis_index("fsdp")
@@ -831,8 +835,8 @@
         self.core_at, self.x_at, self.y_at = f + 1 - 2 * self.c, f + 2 - 4 * self.x, f + 4 - 8 * self.y
         self.loads, place, slot = [], 0, 0
         for src in ins[:4]:
-            self.loads.append((src, left.at[pl.ds(place, src.shape[0]), :]))
-            place += src.shape[0]
+            self.loads.append((src, flat.at[:, pl.ds(place, src.shape[1])]))
+            place += src.shape[1]
         for src in ins[4:]:
             for part in range(src.shape[1] // self.unit):
                 self.loads.append((src.at[:, pl.ds(part * self.unit, self.unit)], right.at[slot]))
@@ -846,6 +850,13 @@
     def wait(self):
         for at, (src, dst) in enumerate(self.loads):
             pltpu.make_async_copy(src, dst, self.load_sem.at[at]).wait()
+
+        def turn(at, carry):
+            here = pl.ds(pl.multiple_of(at * LANES, LANES), LANES)
+            self.left[here, :] = self.flat[:, here].T
+            return carry
+
+        lax.fori_loop(0, self.left.shape[0] // LANES, turn, 0)
 
     def block(self, core, mx, my):
         x, y = self.x + mx * (1 - 2 * self.x), self.y + my * (1 - 2 * self.y)
@@ -867,9 +878,10 @@
 
 
 def term_scratch(ins, unit):
-    width, tokens = ins[1].shape
+    tokens, width = ins[1].shape
     parts = width // unit
     return [
+        pltpu.VMEM((tokens, (LEFT_ROWS + 3) * width), jnp.bfloat16),
         pltpu.VMEM(((LEFT_ROWS + 3) * width, tokens), jnp.bfloat16),
         pltpu.VMEM((9 * parts, tokens, unit), jnp.bfloat16),
         pltpu.SemaphoreType.DMA((4 + 9 * parts,)),
@@ -884,10 +896,10 @@
 
 def chip_kernel(width, half, *refs):
     ins, (own, xs, ys, tx, ty), refs = refs[:8], refs[8:13], refs[13:]
-    left, right, load_sem, csend, crecv, own_b, xs_b, ys_b, tx_b, ty_b, core_s, core_r, out_sem = refs
+    flat, left, right, load_sem, csend, crecv, own_b, xs_b, ys_b, tx_b, ty_b, core_s, core_r, out_sem = refs
     r = lax.axis_index("replica")
     count, rows = own.shape[:2]
-    terms = Terms(ins, left, right, rows, width, load_sem)
+    terms = Terms(ins, flat, left, right, rows, width, load_sem)
     where = (terms.core_at, r)
     greet([(where, True)], 1)
     terms.start()
@@ -941,8 +953,8 @@
 
 def chip_sums(lefts, rights, collective_id):
     ins = (*lefts, *rights)
-    width, tokens = lefts[1].shape
-    rows, unit = width // 8, UNIT_WIDTH
+    tokens, width = lefts[1].shape
+    rows, unit = width // 8, CHIP_WIDTH
     half = pad_to(rows // 2, 16)
     count = MATRICES * (width // unit)
     bf16 = jnp.bfloat16
@@ -970,8 +982,8 @@
 
 
 def reduce_kernel(width, half, *refs):
-    ins, (extra_in, own_in, xr_in, yr_in, tx_in, ty_in), (out, mine, shared), refs = refs[:8], refs[8:14], refs[14:17], refs[17:]
-    (left, right, load_sem, extra, extra_sem, cx_s, cx_r, cxs_sem, cxr_sem, share_s, share_r,
+    ins, (extra_in, own_in, xr_in, yr_in, tx_in, ty_in), (out, out_down, mine, shared), refs = refs[:8], refs[8:14], refs[14:18], refs[18:]
+    (flat, left, right, load_sem, extra, extra_sem, cx_s, cx_r, cxs_sem, cxr_sem, share_s, share_r,
      csend, crecv, own, xs, xr, ys, yr, tx, ty, x2s, x2r, y2s, y2r, zs, z1r, z2s, z2r, fin,
      own_l, xr_l, yr_l, tx_l, ty_l, ready_sem,
      core_s, core_r, x_s, x_r, y_s, y_r, x2_s, x2_r, y2_s, y2_r, z1_s, z1_r, z2_s, z2_r, fin_l, fin_s, fin_r,
@@ -979,9 +991,9 @@
     f, r = lax.axis_index("fsdp"), lax.axis_index("replica")
     rows = own.shape[1]
     extras = extra.shape[0]
-    count = extras + 2 * own_in.shape[0]
     unit = own.shape[2]
-    terms = Terms(ins, left, right, rows, width, load_sem)
+    count = extras + 2 * MATRICES * (width // unit)
+    terms = Terms(ins, flat, left, right, rows, width, load_sem)
     core_at, x_at, y_at = terms.core_at, terms.x_at, terms.y_at
     inner = jnp.logical_and(r > 0, r < 3)
     outer = jnp.logical_not(inner)
@@ -992,10 +1004,15 @@
         7 + (r > 0).astype(jnp.int32) + (r < 3).astype(jnp.int32),
     )
     few = extra.shape[2]
-    extra_load = pltpu.make_async_copy(extra_in, extra, extra_sem)
-    extra_load.start()
+    extra_loads = [
+        pltpu.make_async_copy(extra_in.at[:, :, pl.ds(at * unit, unit)], extra.at[at], extra_sem.at[at])
+        for at in range(extras)
+    ]
+    for load in extra_loads:
+        load.start()
     terms.start()
-    extra_load.wait()
+    for load in extra_loads:
+        load.wait()
     send = remote_copy
     top, low = pl.ds(0, half), pl.ds(half, rows - half)
 
@@ -1023,35 +1040,56 @@
     def z2_copy(slot):
         return send(z2s.at[slot], z2r.at[slot], z2_s.at[slot], z2_r.at[slot], (f, 3 - r))
 
-    def target(u):
+    def routed(u, action):
         v = u - extras
-        first = pl.multiple_of((v // 2) * unit, LANES)
-        return out.at[1 - lax.rem(v, 2), :, pl.ds(first, unit)]
-
-    def fin_copy(slot, u):
-        return send(fin.at[slot], target(u), fin_s.at[slot], fin_r.at[u], (f, z_at))
-
-    def keep_copy(slot, u):
-        return pltpu.make_async_copy(fin.at[slot], target(u), fin_l.at[slot])
+        w, layer = v // 2, 1 - lax.rem(v, 2)
+        parts = width // unit
+        m = w // parts
+
+        @pl.when(m < 4)
+        def _():
+            row = pl.multiple_of(m * rows, 16)
+            column = pl.multiple_of(lax.rem(w, parts) * unit, LANES)
+            action(out_down.at[layer, pl.ds(row, rows), pl.ds(column, unit)])
+
+        @pl.when(m >= 4)
+        def _():
+            column = pl.multiple_of((w - 4 * parts) * unit, LANES)
+            action(out.at[layer, :, pl.ds(column, unit)])
+
+    def fin_copy(slot, u, to):
+        return send(fin.at[slot], to, fin_s.at[slot], fin_r.at[u], (f, z_at))
+
+    def keep_copy(slot, to):
+        return pltpu.make_async_copy(fin.at[slot], to, fin_l.at[slot])
+
+    def columns(u):
+        return pl.ds(pl.multiple_of(u * unit, LANES), unit)
 
     def fin_extra(u):
         slot = lax.rem(u, 4)
-        return send(fin.at[slot, pl.ds(0, few), :], mine.at[u], fin_s.at[slot], fin_r.at[u], (f, z_at))
+        return send(fin.at[slot, pl.ds(0, few), :], mine.at[:, columns(u)], fin_s.at[slot], fin_r.at[u], (f, z_at))
 
     def keep_extra(u):
         slot = lax.rem(u, 4)
-        return pltpu.make_async_copy(fin.at[slot, pl.ds(0, few), :], mine.at[u], fin_l.at[slot])
+        return pltpu.make_async_copy(fin.at[slot, pl.ds(0, few), :], mine.at[:, columns(u)], fin_l.at[slot])
 
     def share_copy(u, there, where):
         return send(
-            mine.at[u], shared.at[u, there], share_s.at[u, where], share_r.at[u, there], (where, r)
+            mine.at[:, columns(u)], shared.at[there, :, columns(u)], share_s.at[u, where], share_r.at[u, there], (where, r)
         )
+
+    def piece(src, w):
+        whole = src.shape[-1]
+        here = pl.ds(pl.multiple_of(lax.rem(w, whole // unit) * unit, LANES), unit)
+        at = w // (whole // unit)
+        return src.at[at, :, here] if len(src.shape) == 3 else src.at[at, :, :, here]
 
     def ready_copies(u):
         slot = lax.rem(u, 4)
         buffers = ((own_in, own_l), (xr_in, xr_l), (yr_in, yr_l), (tx_in, tx_l), (ty_in, ty_l))
         return [
-            pltpu.make_async_copy(src.at[(u - extras) // 2], dst.at[slot], ready_sem.at[at, slot])
+            pltpu.make_async_copy(piece(src, (u - extras) // 2), dst.at[slot], ready_sem.at[at, slot])
             for at, (src, dst) in enumerate(buffers)
         ]
 
@@ -1062,17 +1100,25 @@
         live = jnp.logical_and(u >= first, u < last)
         pl.when(live if condition is None else jnp.logical_and(live, condition))(lambda: body(u))
 
+    def share_own(u):
+        return pltpu.make_async_copy(mine.at[:, columns(u)], shared.at[f, :, columns(u)], share_r.at[u, f])
+
     def share(u):
         for there in others:
             share_copy(u, f, there).start()
+        share_own(u).start()
 
     def close(u):
         slot = lax.rem(u, 4)
-        fin_copy(slot, u).wait_send()
-        keep_copy(slot, u).wait()
+
+        def action(to):
+            fin_copy(slot, u, to).wait_send()
+            keep_copy(slot, to).wait()
+
+        routed(u, action)
 
     def arrive(u):
-        fin_copy(lax.rem(u, 4), u).wait_recv()
+        routed(u, lambda to: fin_copy(lax.rem(u, 4), u, to).wait_recv())
 
     def close_extra(u):
         fin_extra(u).wait_send()
@@ -1088,8 +1134,11 @@
 
         @pl.when(u >= extras)
         def _():
-            fin_copy(slot, u).start()
-            keep_copy(slot, u).start()
+            def action(to):
+                fin_copy(slot, u, to).start()
+                keep_copy(slot, to).start()
+
+            routed(u, action)
 
         @pl.when(u < extras)
         def _():
@@ -1228,15 +1277,16 @@
         for there in others:
             share_copy(u, f, there).wait_send()
             share_copy(u, there, there).wait_recv()
+        share_own(u).wait()
 
 
 def reduce_grads(lefts, rights, ready, extra):
-    width, tokens = lefts[1].shape
+    tokens, width = lefts[1].shape
     rows, unit = width // 8, UNIT_WIDTH
     half = pad_to(rows // 2, 16)
     ins = (*lefts, *rights)
-    extras, _, few, _ = extra.shape
-    count = extras + ready[0].shape[0] + MATRICES * (width // unit)
+    extras, few = width // unit, extra.shape[1]
+    count = extras + 2 * MATRICES * (width // unit)
     bf16, f32 = jnp.bfloat16, jnp.float32
     buf = lambda dtype, *shape: pltpu.VMEM((*shape, unit), dtype)
     sem = lambda *size: pltpu.SemaphoreType.DMA(size)
@@ -1245,15 +1295,16 @@
     return pl.pallas_call(
         functools.partial(reduce_kernel, width, half),
         out_shape=(
-            jax.ShapeDtypeStruct((2, rows, MATRICES * width), bf16),
-            jax.ShapeDtypeStruct((extras, few, unit), bf16),
+            jax.ShapeDtypeStruct((2, rows, (MATRICES - 4) * width), bf16),
+            jax.ShapeDtypeStruct((2, 4 * rows, width), bf16),
+            jax.ShapeDtypeStruct((few, width), bf16),
             jax.ShapeDtypeStruct(extra.shape, bf16),
         ),
         in_specs=[HB] * 14,
-        out_specs=(HB, HB, HB),
+        out_specs=(HB, HB, HB, HB),
         scratch_shapes=[
             *term_scratch(ins, unit),
-            pltpu.VMEM(extra.shape, f32), pltpu.SemaphoreType.DMA, buf(bf16, extras, 4, few), buf(bf16, extras, 4, few),
+            buf(f32, extras, 8, few), sem(extras), buf(bf16, extras, 4, few), buf(bf16, extras, 4, few),
             sem(extras), sem(extras), sem(extras, 8), sem(extras, 8),
             buf(bf16, 2, 4, rows), buf(bf16, 2, 4, rows), buf(f32, 9, rows),
             buf(bf16, 4, 2, half), buf(bf16, 4, 2, half), buf(bf16, 4, 2, rest), buf(bf16, 4, 2, rest),
@@ -1280,10 +1331,6 @@
     return centred * lax.rsqrt(spread + NORM_EPS) * (1.0 + scale) + shift
 
 
-def gelu_tanh(values):
-    return jax.nn.gelu(values, approximate=True)
-
-
 def latent_ids(latent_len, positions, token_total):
     starts = jnp.cumsum(latent_len) - latent_len
     found = jnp.sum((starts[None, :] <= positions[:, None]).astype(jnp.int32), axis=1) - 1
@@ -1295,13 +1342,230 @@
     return jnp.dot(left, right, preferred_element_type=jnp.float32)
 
 
-def layer_forward(stream, mod_tok, full, plan, in_first, shards_first, shards_second, shards_ahead, collective_id):
+TILE = 512
+GELU_ROOT = math.sqrt(2.0 / math.pi)
+
+
+def thirds(values):
+    high = values.astype(jnp.bfloat16)
+    rest = values - high.astype(jnp.float32)
+    middle = rest.astype(jnp.bfloat16)
+    return high, middle, (rest - middle.astype(jnp.float32)).astype(jnp.bfloat16)
+
+
+def halves_across(width):
+    first = pad_to(width // 2, LANES)
+    return (pl.ds(0, first), pl.ds(first, width - first))
+
+
+def at_tile(at, size=TILE):
+    return pl.ds(pl.multiple_of(at * size, size), size)
+
+
+def tiles(count, body):
+    def run(at, carry):
+        body(at)
+        return carry
+
+    lax.fori_loop(0, count, run, 0)
+
+
+def norm_parts(stream):
+    centred = stream - jnp.mean(stream, axis=1, keepdims=True)
+    root = lax.rsqrt(jnp.mean(centred * centred, axis=1, keepdims=True) + NORM_EPS)
+    return centred * root, root
+
+
+class FeedForward:
+    def __init__(self, pick, mod, weights, held, sems):
+        self.pick, self.mod = pick, mod
+        self.out_w, self.up_w, self.down_w = held
+        self.width, self.hidden = held[1].shape
+        self.pieces = sems.shape[0] // 2
+        self.piece = self.hidden // self.pieces
+        cuts = [pl.ds(at * self.piece, self.piece) for at in range(self.pieces)]
+        copy = pltpu.make_async_copy
+        self.out_copy = copy(weights[0], held[0], sems.at[0])
+        self.up_copies = [copy(weights[1].at[:, cut], held[1].at[:, cut], sems.at[1 + at]) for at, cut in enumerate(cuts)]
+        self.down_copies = [
+            copy(weights[2].at[cut, :], held[2].at[cut, :], sems.at[1 + self.pieces + at]) for at, cut in enumerate(cuts)
+        ]
+
+    def start(self, forth):
+        order = [self.out_copy, *self.up_copies, *self.down_copies]
+        for part in order if forth else [*self.down_copies, *self.up_copies, self.out_copy]:
+            part.start()
+
+    def vector(self, rows, at):
+        return nn_dot(self.pick[rows, :], self.mod[:, at * self.width : (at + 1) * self.width])
+
+    def forward(self, stream, mixed, biases, branch, middle, normed, hidden, active, result, after):
+        out_b, up_b, down_b = biases
+        size, width = stream.shape
+        self.out_copy.wait()
+        for here in halves_across(width):
+            branch[:, here] = nn_dot(mixed[...], self.out_w[:, here]) + out_b[:, here].astype(jnp.float32)
+
+        def first_norm(rows):
+            total = stream[rows, :] + self.vector(rows, 2) * branch[rows, :]
+            middle[rows, :] = total
+            unit, _ = norm_parts(total)
+            normed[rows, :] = (unit * (1.0 + self.vector(rows, 4)) + self.vector(rows, 3)).astype(jnp.bfloat16)
+
+        by_rows(size, first_norm)
+        for piece in range(self.pieces):
+            self.up_copies[piece].wait()
+
+            def widen(at, piece=piece):
+                here = at_tile(piece * (self.piece // TILE) + at)
+                values = nn_dot(normed[...], self.up_w[:, here]) + up_b[:, here].astype(jnp.float32)
+                hidden[:, here] = values
+                inner = GELU_ROOT * (values + 0.044715 * values * values * values)
+                active[:, here] = (0.5 * values * (1.0 + jnp.tanh(inner))).astype(jnp.bfloat16)
+
+            tiles(self.piece // TILE, widen)
+        for part in self.down_copies:
+            part.wait()
+        for here in halves_across(width):
+            result[:, here] = nn_dot(active[...], self.down_w[:, here]) + down_b[:, here].astype(jnp.float32)
+
+        def leave(rows):
+            after[rows, :] = (middle[rows, :] + self.vector(rows, 5) * result[rows, :]).astype(after.dtype)
+
+        by_rows(size, leave)
+
+    def backward(self, grad, branch, middle, hidden, result, outs, work, fresh):
+        low_result, low_hidden, low_branch, low_mixed, grad_middle, grad_mod, out_sum, up_sum, down_sum = outs
+        size, width = middle.shape
+        grad_mod[...] = jnp.zeros_like(grad_mod)
+        for ref in (out_sum, up_sum, down_sum):
+            ref[...] = jnp.zeros_like(ref)
+
+        latents = grad_mod.shape[0] // 4
+
+        def collect(rows, at, values):
+            here = slice(at * latents, (at + 1) * latents)
+            ones = self.pick[rows, :latents]
+            for part in thirds(values)[:2]:
+                grad_mod[here, :] += lax.dot_general(
+                    ones, part, (((0,), (0,)), ((), ())), preferred_element_type=jnp.float32
+                )
+
+        def total(values):
+            return jnp.sum(values.astype(jnp.float32), axis=0, keepdims=True)
+
+        def enter(rows):
+            values = grad[rows, :].astype(jnp.float32)
+            low = (self.vector(rows, 5) * values).astype(jnp.bfloat16)
+            low_result[rows, :] = low
+            down_sum[...] += total(low)
+            collect(rows, 3, values * result[rows, :])
+
+        by_rows(size, enter)
+
+        def widen(at):
+            here = at_tile(at)
+            values = hidden[:, here]
+            square = values * values
+            bent = jnp.tanh(GELU_ROOT * (values + 0.044715 * values * square))
+            slope = 0.5 * (1.0 + bent) + 0.5 * values * (1.0 - bent * bent) * (GELU_ROOT * (1.0 + 3 * 0.044715 * square))
+            low = (nt_dot(low_result[...], self.down_w[here, :]) * slope).astype(jnp.bfloat16)
+            low_hidden[:, here] = low
+            up_sum[:, here] = total(low)
+
+        for part in self.down_copies if fresh else ():
+            part.wait()
+        tiles(self.hidden // TILE, widen)
+        for part in self.up_copies if fresh else ():
+            part.wait()
+        for here in halves_across(width):
+            work[:, here] = nt_dot(low_hidden[...], self.up_w[here, :])
+
+        def norm_back(rows):
+            unit, root = norm_parts(middle[rows, :])
+            values = work[rows, :]
+            collect(rows, 1, values)
+            collect(rows, 2, values * unit)
+            scaled = values * (1.0 + self.vector(rows, 4))
+            inside = scaled - jnp.mean(scaled, axis=1, keepdims=True)
+            inside = inside - unit * jnp.mean(scaled * unit, axis=1, keepdims=True)
+            here = grad[rows, :].astype(jnp.float32) + root * inside
+            grad_middle[rows, :] = here
+            low = (self.vector(rows, 2) * here).astype(jnp.bfloat16)
+            low_branch[rows, :] = low
+            out_sum[...] += total(low)
+            collect(rows, 0, here * branch[rows, :])
+
+        by_rows(size, norm_back)
+
+        if fresh:
+            self.out_copy.wait()
+        for here in halves_across(width):
+            low_mixed[:, here] = nt_dot(low_branch[...], self.out_w[here, :]).astype(jnp.bfloat16)
+
+
+def feed_kernel(forth, back, *refs):
+    pick, mod, out_w, up_w, down_w, out_b, up_b, down_b, *refs = refs
+    weights, biases = (out_w, up_w, down_w), (out_b, up_b, down_b)
+    if forth and not back:
+        stream, mixed, branch, middle, normed, hidden, active, result, after, *refs = refs
+        held, sems = refs[:3], refs[3]
+    elif back and not forth:
+        grad, branch, middle, hidden, result, *refs = refs
+        outs, (*held, sems, work) = refs[:9], refs[9:]
+    else:
+        stream, mixed, grad, normed, active, after, *refs = refs
+        outs, (*held, sems, work, branch, middle, hidden, result) = refs[:9], refs[9:]
+    feed = FeedForward(pick, mod, weights, held, sems)
+    feed.start(forth)
+    if forth:
+        feed.forward(stream, mixed, biases, branch, middle, normed, hidden, active, result, after)
+    if back:
+        feed.backward(grad, branch, middle, hidden, result, outs, work, not forth)
+
+
+def feed_call(forth, back, ins, full, pick, mod, dtype):
+    qkv_w, qkv_b, out_w, out_b, up_w, up_b, down_w, down_b = full
+    size, latents = pick.shape
+    width, hidden = up_w.shape
+    bf16, f32 = jnp.bfloat16, jnp.float32
+    shape = lambda columns, dtype, rows=size: jax.ShapeDtypeStruct((rows, columns), dtype)
+    saved = (shape(width, f32), shape(width, f32), shape(width, bf16), shape(hidden, f32), shape(hidden, bf16), shape(width, f32))
+    after = shape(width, dtype)
+    outs = (
+        shape(width, bf16), shape(hidden, bf16), shape(width, bf16), shape(width, bf16), shape(width, f32),
+        shape(width, f32, 4 * latents), shape(width, f32, 1), shape(hidden, f32, 1), shape(width, f32, 1),
+    )
+    scratch = [pltpu.VMEM(part.shape, part.dtype) for part in (out_w, up_w, down_w)]
+    scratch.append(pltpu.SemaphoreType.DMA((1 + 2 * (hidden // (3 * TILE)),)))
+    if back:
+        scratch.append(pltpu.VMEM((size, width), f32))
+    if forth and back:
+        scratch += [pltpu.VMEM((size, columns), f32) for columns in (width, width, hidden, width)]
+        shapes = (saved[2], saved[4], after, *outs)
+    else:
+        shapes = (*saved, after) if forth else outs
+    return pl.pallas_call(
+        functools.partial(feed_kernel, forth, back),
+        out_shape=shapes,
+        in_specs=[VM, VM, HB, HB, HB, VM, VM, VM] + [VM] * len(ins),
+        out_specs=(VM,) * len(shapes),
+        scratch_shapes=scratch,
+        compiler_params=pltpu.CompilerParams(vmem_limit_bytes=60 * 1024 * 1024),
+    )(
+        jnp.concatenate([pick.astype(bf16)] * 3, axis=1), jnp.concatenate(thirds(mod), axis=0), out_w, up_w, down_w,
+        out_b[None], up_b[None], down_b[None], *ins,
+    )
+
+
+def layer_forward(stream, modulation, full, plan, in_first, shards_first, shards_second, shards_ahead, collective_id):
     qkv_w, qkv_b, out_w, out_b, up_w, up_b, down_w, down_b = full
     reps, edge, bounds, ids = plan
     width = stream.shape[1]
     hd = width // reps
     nh = HEADS // reps
-    shift_one, scale_one, gate_one, shift_two, scale_two, gate_two = jnp.split(mod_tok, 6, axis=1)
+    mod, pick, front = modulation
+    shift_one, scale_one = jnp.split(front, 2, axis=1)
     normed = pre_norm(stream, shift_one, scale_one).astype(jnp.bfloat16)
     qkv_bias = qkv_b.astype(jnp.float32)
     bias_full = jnp.concatenate(
@@ -1317,44 +1581,21 @@
     if in_first:
         (up_w,), (down_w, *fulls) = first_gathered, fulls
     in_next = sent_ahead(shards_ahead, mixed) if shards_ahead else ()
-    branch = low_dot(mixed, out_w) + out_b.astype(jnp.float32)
-    middle = stream + gate_one * branch
-    normed_two = pre_norm(middle, shift_two, scale_two).astype(jnp.bfloat16)
-    hidden = low_dot(normed_two, up_w) + up_b.astype(jnp.float32)
-    active = gelu_tanh(hidden).astype(jnp.bfloat16)
-    result = low_dot(active, down_w) + down_b.astype(jnp.float32)
-    saved = (
-        normed, (prev, own, after), mixed, (mixed_t, log_norm), branch, middle, normed_two, hidden, active, result,
-    )
     full = (qkv_w, qkv_b, out_w, out_b, up_w, up_b, down_w, down_b)
-    return (middle + gate_two * result, saved, full, fulls, in_next)
-
-
-def layer_backward(stream, mod_tok, full, saved, plan, pick, grad_next, beside):
-    qkv_w, qkv_b, out_w, out_b, up_w, up_b, down_w, down_b = full
-    normed, window, mixed, kept, branch, middle, normed_two, hidden, active, result = saved
+    saved = (normed, (prev, own, after), mixed, (mixed_t, log_norm))
+    return (saved, full, fulls, in_next)
+
+
+def layer_backward(stream, modulation, full, saved, feed_grads, plan, beside):
+    qkv_w = full[0]
+    normed, window, mixed, kept = saved
+    normed_two, active, grad_result, grad_hidden, grad_branch, grad_mixed, grad_middle, grad_mod, *bias_sums = feed_grads
     reps, edge, bounds, ids = plan
     width = stream.shape[1]
     hd = width // reps
     nh = HEADS // reps
-    shift_one, scale_one, gate_one, shift_two, scale_two, gate_two = jnp.split(mod_tok, 6, axis=1)
-    grad_result = (gate_two * grad_next).astype(jnp.bfloat16)
-    grad_gate_two = grad_next * result
-    grad_down_b = jnp.sum(grad_result.astype(jnp.float32), axis=0)
-    grad_active = jnp.einsum("td,fd->tf", grad_result, down_w, preferred_element_type=jnp.float32)
-    _, gelu_back = jax.vjp(gelu_tanh, hidden)
-    grad_hidden = gelu_back(grad_active)[0].astype(jnp.bfloat16)
-    grad_up_b = jnp.sum(grad_hidden.astype(jnp.float32), axis=0)
-    grad_normed_two = jnp.einsum("tf,df->td", grad_hidden, up_w, preferred_element_type=jnp.float32)
-    _, norm_back_two = jax.vjp(pre_norm, middle, shift_two, scale_two)
-    grad_middle_part, grad_shift_two, grad_scale_two = norm_back_two(grad_normed_two)
-    grad_middle = grad_next + grad_middle_part
-    grad_branch = (gate_one * grad_middle).astype(jnp.bfloat16)
-    grad_gate_one = grad_middle * branch
-    grad_out_b = jnp.sum(grad_branch.astype(jnp.float32), axis=0)
-    grad_mixed = jnp.einsum(
-        "te,de->td", grad_branch, out_w, preferred_element_type=jnp.float32
-    ).astype(jnp.bfloat16)
+    mod, pick, front = modulation
+    shift_one, scale_one = jnp.split(front, 2, axis=1)
     grad_heads, _ = swap(grad_mixed, reps, False, (), 3)
     prev, own, after = window
     grad_q, grad_prev, grad_own, grad_after = attend_back(
@@ -1371,40 +1612,40 @@
     grad_mod = jnp.concatenate(
         [
             jnp.einsum("tl,tm->lm", pick, part, precision=HIGH, preferred_element_type=jnp.float32)
-            for part in (
-                grad_shift_one, grad_scale_one, grad_gate_one, grad_shift_two, grad_scale_two, grad_gate_two,
-            )
-        ],
-        axis=1,
+            for part in (grad_shift_one, grad_scale_one)
+        ]
+        + [grad_mod],
     )
     return (
         grad_stream, grad_mod,
-        ((active.T, normed_two.T, mixed.T, normed.T), (grad_result, grad_hidden, grad_branch, grad_projected)),
-        (grad_qkv_b, grad_out_b, grad_up_b, grad_down_b), beside,
+        ((active, normed_two, mixed, normed), (grad_result, grad_hidden, grad_branch, grad_projected)),
+        (grad_qkv_b, *(part[0] for part in bias_sums)), beside,
     )
 
 
 def bias_parts(stacked, params):
-    cuts = [0]
-    for at in (3, 5, 7, 9):
-        cuts.append(cuts[-1] + params[at].shape[0])
-    return [stacked[:, a:b].reshape(-1) for a, b in zip(cuts[:-1], cuts[1:])]
+    return [stacked[:, row, : params[at].shape[0]].reshape(-1) for row, at in enumerate((3, 5, 7, 9))]
 
 
 def modulation(partial_terms, layers):
-    shares = jnp.stack([jnp.concatenate([params[at] for at in (3, 5, 7, 9)]) for params in layers])
+    longest = pad_to(max(params[at].shape[0] for params in layers for at in (3, 5, 7, 9)), LANES)
+    shares = jnp.stack(
+        [jnp.pad(params[at], (0, longest - params[at].shape[0])) for params in layers for at in (3, 5, 7, 9)]
+    )
     if not on_planes():
         mods = lax.psum(tuple(partial_terms), "fsdp")
         stacked = lax.all_gather(shares, "fsdp", axis=0)
         fulls = [lax.all_gather(layers[0][at], "fsdp", axis=0, tiled=True) for at in (2, 4)]
     else:
         width = layers[0][4].shape[1]
-        parts = jnp.stack(partial_terms).reshape(8, -1, width)
+        parts = partial_terms[0].reshape(8, -1, width)
+        some = parts.shape[1]
+        parts = jnp.pad(parts, ((0, 0), (0, pad_to(some, 8) - some), (0, 0)))
         mod, stacked, *fulls = start(
             parts, jnp.pad(shares, ((0, 16 - shares.shape[0]), (0, 0))), [(layers[0][at],) for at in (2, 4)], 6
         )
-        mods = mod.reshape(len(layers), -1, partial_terms[0].shape[1])
-    return mods, [bias_parts(stacked[:, at], params) for at, params in enumerate(layers)], fulls
+        mods = [mod[:, :some].reshape(partial_terms[0].shape)] + [lax.psum(term, "fsdp") for term in partial_terms[1:]]
+    return mods, [bias_parts(stacked[:, 4 * at : 4 * at + 4], params) for at, params in enumerate(layers)], fulls
 
 
 def on_planes():
@@ -1419,33 +1660,25 @@
 
 def owner_sums(pairs, ready, grad_mods, grad_biases):
     groups = lax.axis_size("fsdp")
-    width = pairs[0][0][1].shape[0]
+    width = pairs[0][0][1].shape[1]
     if on_planes():
-        mods = jnp.stack(grad_mods).reshape(groups, -1, width)
+        mods = jnp.concatenate(grad_mods).reshape(groups, -1, width)
         biases = jnp.stack(
             [jnp.concatenate([part.reshape(groups, -1) for part in parts], axis=1) for parts in grad_biases], axis=1
         )
-        extra = jnp.concatenate([mods, biases], axis=1)
-        used, parts = extra.shape[1], width // UNIT_WIDTH
-        lines = pad_to(used, 16) * parts
-        extras = -(-lines // pad_to(width // 16, 16))
-        extra = jnp.pad(extra, ((0, 0), (0, lines // parts - used), (0, 0)))
-        extra = extra.reshape(groups, extras, -1, UNIT_WIDTH).transpose(1, 0, 2, 3)
-        out, mine, shared = reduce_grads(*pairs[0], ready, extra)
-        shared = lax.dynamic_update_slice_in_dim(shared, mine[:, None], lax.axis_index("fsdp"), 1)
-        shared = shared.transpose(1, 0, 2, 3).reshape(groups, -1, width)
-        mods = shared[:, : mods.shape[1]].reshape(len(pairs), -1, grad_mods[0].shape[1])
-        mine = mine.reshape(-1, width)
-        columns = lambda layer_at, first, last: out[layer_at, :, first * width : last * width].astype(jnp.float32)
+        used, lines = mods.shape[1], pad_to(mods.shape[1] + 2, 16)
+        biases = jnp.pad(biases, ((0, 0), (0, lines - used - 2), (0, 0)))
+        out, out_down, mine, shared = reduce_grads(*pairs[0], ready, jnp.concatenate([mods, biases], axis=1))
+        mods = shared[:, :used].reshape(2, -1, width)
+        shares = mine[used : used + 2].astype(jnp.float32)
         results = []
         for layer_at in range(2):
-            share = mine[used - 2 + layer_at].astype(jnp.float32)
+            columns = lambda first, last: out[layer_at, :, (first - 4) * width : (last - 4) * width].astype(jnp.float32)
             cuts = [0]
             for part in grad_biases[layer_at]:
                 cuts.append(cuts[-1] + part.shape[0] // groups)
-            down = jnp.stack([columns(layer_at, m, m + 1) for m in range(4)]).reshape(-1, width)
-            weights = (columns(layer_at, 9, 12), columns(layer_at, 8, 9), columns(layer_at, 4, 8), down)
-            results.append((weights, [share[i:j] for i, j in zip(cuts[:-1], cuts[1:])]))
+            weights = (columns(9, 12), columns(8, 9), columns(4, 8), out_down[layer_at].astype(jnp.float32))
+            results.append((weights, [shares[layer_at, i:j] for i, j in zip(cuts[:-1], cuts[1:])]))
         return results, mods
     flat = jnp.concatenate([part for parts in grad_biases for part in parts])
     *mods, flat = lax.psum((*grad_mods, flat), ("fsdp", "replica"))
@@ -1453,7 +1686,7 @@
     for (lefts, rights), parts in zip(pairs, grad_biases):
         grads, biases = [], []
         for left, right in zip(lefts, rights):
-            grad = low_dot(left, right).astype(jnp.bfloat16)
+            grad = low_dot(left.T, right).astype(jnp.bfloat16)
             part = lax.psum_scatter(grad, "fsdp", scatter_dimension=0, tiled=True)
             grads.append(lax.psum(part, "replica").astype(jnp.float32))
         for part in parts:
@@ -1565,9 +1798,9 @@
         )
         partial_terms.append(term + spread[None, :])
     (mod_first, mod_second), biases, attention_weights = modulation(partial_terms, layers)
-    mod_tokens = (
-        jnp.dot(pick, mod_first, precision=HIGH, preferred_element_type=jnp.float32),
-        jnp.dot(pick, mod_second, precision=HIGH, preferred_element_type=jnp.float32),
+    mod_tokens = tuple(
+        (mod, pick, jnp.dot(pick, mod[:, : 2 * tokens.shape[1]], precision=HIGH, preferred_element_type=jnp.float32))
+        for mod in (mod_first, mod_second)
     )
     stream = tokens.astype(jnp.float32)
     inputs = []
@@ -1588,22 +1821,35 @@
         else:
             up_w, down_w = whole(params[6]), whole(params[8])
         full = (qkv_w, qkv_b, out_w, out_b, up_w, up_b, down_w, down_b)
-        stream, saved, full, attention_weights, in_first = layer_forward(
+        saved, full, attention_weights, in_first = layer_forward(
             stream, mod_tokens[layer_at], full, plan, in_first, shards_first, shards_second, shards_ahead, 7 + 2 * layer_at
         )
+        if layer_at == 0:
+            *feed_saved, stream = feed_call(
+                True, False, (stream, saved[2]), full, pick, mod_tokens[0][0], jnp.float32
+            )
+        else:
+            normed_two, active, output, *feed_grads = feed_call(
+                True, True, (stream, saved[2], cotangent), full, pick, mod_tokens[1][0], jnp.bfloat16
+            )
+            feed_grads = [normed_two, active, *feed_grads]
         fulls.append(full)
         if ahead is not None and not on_planes():
             attention_weights = [whole(ahead[at]) for at in (2, 4)]
         kept.append(saved)
-    output = stream.astype(jnp.bfloat16)
-    grad_stream = cotangent.astype(jnp.float32)
     weight_pairs = [None, None]
     ready = ()
     mod_grads = [None, None]
     bias_grads = [None, None]
     for layer_at in (1, 0):
+        if layer_at == 0:
+            branch, middle, normed_two, hidden, active, result = feed_saved
+            feed_grads = feed_call(
+                False, True, (grad_stream, branch, middle, hidden, result), fulls[0], pick, mod_tokens[0][0], jnp.float32
+            )
+            feed_grads = [normed_two, active, *feed_grads]
         grad_stream, grad_mod, local_grads, local_biases, ready = layer_backward(
-            inputs[layer_at], mod_tokens[layer_at], fulls[layer_at], kept[layer_at], plan, pick, grad_stream, ready
+            inputs[layer_at], mod_tokens[layer_at], fulls[layer_at], kept[layer_at], feed_grads, plan, ready
         )
         weight_pairs[layer_at] = local_grads
         if layer_at == 1 and on_planes():
@@ -1615,7 +1861,7 @@
     grad_silu = jnp.zeros(own_cond.shape, jnp.float32)
     ada_grads = []
     for params, grad_mod in zip(layers, (grad_mod_first, grad_mod_second)):
-        low_mod = grad_mod.astype(jnp.bfloat16)
+        low_mod = grad_mod.astype(jnp.bfloat16).reshape(6, latent_count, -1).transpose(1, 0, 2).reshape(latent_count, -1)
         weight_grad = jnp.einsum("ld,lm->dm", own_silu, low_mod, preferred_element_type=jnp.float32)
         column_sums = jnp.sum(low_mod.astype(jnp.float32), axis=0)
         bias_rows = params[1].shape[0]

time: 1100 us -> 1040 us (0.945)
  matrix products: 136 us -> 49.1 us
  Pallas kernels: 792 us -> 857 us
  local copies, waits for them, and re-layouts: 62.9 us -> 30.3 us
  other arithmetic: 48.4 us -> 31.2 us
  between operations: 2.44 us -> 15.3 us
    pallas_call x0 -> x3, Pallas kernels: none -> 77 us  [feed_call(): pl.pallas_call(functools.partial(feed_kernel, forth, back), out_shape=sha...]
    dot_general x8 -> x2, matrix products: 48.9 us -> 4.59 us  [shards(): jnp.dot(pick, mod[:, :2 * tokens.shape[1]], precision=HIGH, preferred_ele...]
    dot_general x10 -> x4, matrix products: 55.4 us -> 17.6 us  [low_dot(): return jnp.dot(left, right, preferred_element_type=jnp.float32)]
    pallas_call x1, Pallas kernels: 278 us -> 251 us  [reduce_grads(): pl.pallas_call(functools.partial(reduce_kernel, width, half), out_shape=(...]
    convert_element_type x8 -> x0, local copies, waits for them, and re-layouts: 16.8 us -> none  [the longest x2 16.3 us: layer_forward(): active = gelu_tanh(hidden).astype(jnp.bfloat16)]
  transfers between devices with their start and end apart: 14 -> 15, of which waited for: 4 -> 2; matrix products, arithmetic and copies ran while one was open for 8% -> 5% of each run, Pallas kernels for 20% -> 26%
where the time goes in v6:
time: 1040 us; the launch traced here: 1030 us
  Pallas kernels  857 us (82%)
  matrix products  49.1 us (5%)
  starting transfers between devices  38.3 us (4%)
  other arithmetic  31.2 us (3%)
  local copies, waits for them, and re-layouts  30.3 us (3%)
  between operations  15.3 us (1%)
  waiting for transfers between devices  12.9 us (1%)
    pallas_call x1, Pallas kernels, reduce_grads(): pl.pallas_call(functools.partial(reduce_kernel, width, half), out_shape=(...  251 us
    pallas_call x4, Pallas kernels, swap(): pl.pallas_call(functools.partial(swap_kernel, reps, out, halves_of(shards...  135 us
    pallas_call x2, Pallas kernels, to_heads(): pl.pallas_call(functools.partial(to_heads_kernel, reps, size, edge, kv, h...  95.9 us
    pallas_call x2, Pallas kernels, from_heads(): pl.pallas_call(functools.partial(from_heads_kernel, reps, size, edge), ou...  88.5 us
    pallas_call x3, Pallas kernels, feed_call(): pl.pallas_call(functools.partial(feed_kernel, forth, back), out_shape=sha...  77 us
    pallas_call x1, Pallas kernels, start(): pl.pallas_call(functools.partial(start_kernel, halves_of(shards)), out_sh...  66.1 us
    pallas_call x2, Pallas kernels, attend_back(): pl.pallas_call(functools.partial(attend_back_kernel, nh, hd), out_shape=(...  56.6 us
    pallas_call x1, Pallas kernels, chip_sums(): pl.pallas_call(functools.partial(chip_kernel, width, half), out_shape=tup...  47.7 us
  transfers between devices with their start and end apart: 15, of which 2 were waited for; matrix products, arithmetic and copies ran while one was open for 5% of the time, Pallas kernels for 26%

profile of v6, /device:TPU:0, one launch (start us, length us, event | category | flops | bytes accessed | tf_op | source)
XLA Modules:
  0.0 1034.0 jit_solution(4554302246251170992)
XLA Ops:
  16.4 66.1 %shard_map.407 = (f32[8,16,1152]{2,1,0:T(8,128)}, bf16[8,16,640]{2,1,0:T(8,128)(2,1)}, bf16[1152,3456]{1,0:T(8,128)(2,1)}, bf16[1152,1152]{1,0:T(8,128)(2,1)}) custom-call(f32[8,16,1152]{2,1,0:T(8,128)} %pad.39.part_in, bf16[16,640]{1,0:T(8,128)(2,1)} %pad.48.bias_in, bf16[144,3456]{1,0:T(8,128)(2,1)} %refs_0_.1, bf16[144,1152]{1,0:T(8,128)(2,1)} %refs_1_.1), custom_call_target="tpu_custom_call" | custom-call | tf_op jit(solution)/shard_map/pallas_call | solution.py:496
  91.2 7.2 fusion.qkv
  106.6 11.3 %collective-permute-done.1.refs_2_ = bf16[144,4608]{1,0:T(8,128)(2,1)} collective-permute-done((bf16[144,4608]{1,0:T(8,128)(2,1)}, bf16[144,4608]{1,0:T(8,128)(2,1)}, u32[]{:S(2)}, u32[]{:S(2)}) %collective-permute-start.1) | collective-permute-done | bytes 1327136 | tf_op jit(solution)/shard_map/ppermute | solution.py:396
  119.5 48.7 %shard_map.408 = (bf16[4,256,896]{2,1,0:T(8,128)(2,1)}, bf16[1024,640]{1,0:T(8,128)(2,1)}, bf16[1024,640]{1,0:T(8,128)(2,1)}, bf16[1152,4608]{1,0:T(8,128)(2,1)}) custom-call(bf16[256,3456]{1,0:T(8,128)(2,1)} %fusion.qkv, bf16[144,4608]{1,0:T(8,128)(2,1)} %refs_0_.2, bf16[144,4608]{1,0:T(8,128)(2,1)} %collective-permute-done.refs_1_, ...), custom_call_target="tpu_custom_call" | custom-call | tf_op jit(solution)/shard_map/pallas_call | solution.py:619
  168.2 23.8 %collective-permute-start.5 = (bf16[144,3456]{1,0:T(8,128)(2,1)}, bf16[144,3456]{1,0:T(8,128)(2,1)}, u32[]{:S(2)}, u32[]{:S(2)}) collective-permute-start(bf16[144,3456]{1,0:T(8,128)(2,1)} %refs_3_), channel_id=1, source_target_pairs={{0,16},{4,20},{8,24},{12,28},{16,0},{20,4},{24,8},{28,12},{1,17},{... | collective-permute-start | bytes 2985992 | tf_op jit(solution)/shard_map/ppermute | solution.py:396
  201.9 3.4 fusion.19
  205.9 2.2 broadcast_in_dim.19.kid
  208.1 19.5 %shard_map.409 = (bf16[1024,384]{1,0:T(8,128)(2,1)}, f32[384,1024]{1,0:T(8,128)}, f32[8,1024]{1,0:T(8,128)}) custom-call(s32[4]{0:T(128)} %get-tuple-element.238.lo, s32[4]{0:T(128)} %get-tuple-element.237.hi, bf16[1024,640]{1,0:T(8,128)(2,1)} %get-tuple-element.109.prev, bf16[1024,896]{1,0:T(8,128)(2,1)} %bitcast.69, ...), custom_call_target="tpu_custom_call" | custom-call | tf_op jit(solution)/shard_map/pallas_call | solution.py:144
  228.4 44.3 %shard_map.410 = (bf16[256,1152]{1,0:T(8,128)(2,1)}, bf16[4608,1152]{1,0:T(8,128)(2,1)}, bf16[1152,3456]{1,0:T(8,128)(2,1)}, bf16[1152,1152]{1,0:T(8,128)(2,1)}) custom-call(bf16[4,256,384]{2,1,0:T(8,128)(2,1)} %bitcast.84, bf16[576,1152]{1,0:T(8,128)(2,1)} %refs_0_.3, bf16[576,1152]{1,0:T(8,128)(2,1)} %collective-permute-done.2.refs_1_, ...), custom_call_target="tpu_custom_call" | custom-call | tf_op jit(solution)/shard_map/pallas_call | solution.py:692
  274.7 20.1 %shard_map.411 = (f32[256,1152]{1,0:T(8,128)}, f32[256,1152]{1,0:T(8,128)}, bf16[256,1152]{1,0:T(8,128)(2,1)}, f32[256,4608]{1,0:T(8,128)}, bf16[256,4608]{1,0:T...) custom-call(bf16[256,48]{1,0:T(8,128)(2,1)} %copy.59.refs_0_, bf16[48,6912]{1,0:T(8,128)(2,1)} %pad_maximum_fusion.2.refs_1_, ...), custom_call_target="tpu_custom_call" | custom-call | tf_op jit(solution)/shard_map/pallas_call | solution.py:1548
  298.6 7.3 fusion.1.qkv
  309.0 47.2 %shard_map.412 = (bf16[4,256,896]{2,1,0:T(8,128)(2,1)}, bf16[1024,640]{1,0:T(8,128)(2,1)}, bf16[1024,640]{1,0:T(8,128)(2,1)}, bf16[1152,4608]{1,0:T(8,128)(2,1)}) custom-call(bf16[256,3456]{1,0:T(8,128)(2,1)} %fusion.1.qkv, bf16[144,4608]{1,0:T(8,128)(2,1)} %refs_0_.4, bf16[144,4608]{1,0:T(8,128)(2,1)} %collective-permute-done.8.refs_1_, ...), custom_call_target="tpu_custom_call" | custom-call | tf_op jit(solution)/shard_map/pallas_call | solution.py:619
  356.2 19.7 %shard_map.413 = (bf16[1024,384]{1,0:T(8,128)(2,1)}, f32[384,1024]{1,0:T(8,128)}, f32[8,1024]{1,0:T(8,128)}) custom-call(s32[4]{0:T(128)} %get-tuple-element.238.lo, s32[4]{0:T(128)} %get-tuple-element.237.hi, bf16[1024,640]{1,0:T(8,128)(2,1)} %get-tuple-element.125.prev, bf16[1024,896]{1,0:T(8,128)(2,1)} %bitcast.71, ...), custom_call_target="tpu_custom_call" | custom-call | tf_op jit(solution)/shard_map/pallas_call | solution.py:144
  377.4 50.1 %shard_map.414 = (bf16[256,1152]{1,0:T(8,128)(2,1)}, bf16[4608,1152]{1,0:T(8,128)(2,1)}) custom-call(bf16[4,256,384]{2,1,0:T(8,128)(2,1)} %bitcast.85, bf16[576,1152]{1,0:T(8,128)(2,1)} %refs_0_.5, bf16[576,1152]{1,0:T(8,128)(2,1)} %copy-done.21, bf16[576,1152]{1,0:T(8,128)(2,1)} %copy-done.20), custom_call_target="tpu_custom_call" | custom-call | tf_op jit(solution)/shard_map/pallas_call | solution.py:692
  427.6 33.0 %shard_map.415 = (bf16[256,1152]{1,0:T(8,128)(2,1)}, bf16[256,4608]{1,0:T(8,128)(2,1)}, bf16[256,1152]{1,0:T(8,128)(2,1)}, bf16[256,1152]{1,0:T(8,128)(2,1)}, bf...) custom-call(bf16[256,48]{1,0:T(8,128)(2,1)} %copy.59.refs_0_, ...), custom_call_target="tpu_custom_call" | custom-call | tf_op jit(solution)/shard_map/pallas_call | solution.py:1548
  460.5 19.2 %shard_map.416 = bf16[4,256,384]{2,1,0:T(8,128)(2,1)} custom-call(bf16[256,1152]{1,0:T(8,128)(2,1)} %get-tuple-element.134.x_ref), custom_call_target="tpu_custom_call" | custom-call | tf_op jit(solution)/shard_map/pallas_call | solution.py:692
  479.7 28.3 %shard_map.417 = (bf16[1024,384]{1,0:T(8,128)(2,1)}, bf16[1024,640]{1,0:T(8,128)(2,1)}, bf16[1024,640]{1,0:T(8,128)(2,1)}, bf16[1024,640]{1,0:T(8,128)(2,1)}) custom-call(s32[4]{0:T(128)} %get-tuple-element.238.lo, s32[4]{0:T(128)} %get-tuple-element.237.hi, bf16[1024,640]{1,0:T(8,128)(2,1)} %get-tuple-element.125.prev, bf16[1024,896]{1,0:T(8,128)(2,1)} %bitcast.72, ...), custom_call_target="tpu_custom_call" | custom-call | tf_op jit(solution)/shard_map/pallas_call | solution.py:237
  508.0 43.9 %shard_map.418.refs_7_ = bf16[256,3456]{1,0:T(8,128)(2,1)} custom-call(bf16[1024,640]{1,0:T(8,128)(2,1)} %get-tuple-element.137.dprev, bf16[1024,640]{1,0:T(8,128)(2,1)} %get-tuple-element.138.own, bf16[1024,640]{1,0:T(8,128)(2,1)} %get-tuple-element.139.dafter, bf16[1024,384]{1,0:T(8,128)(2,1)} %get-tuple-element.140.dq), custom_call_target="tpu_custom_call" | custom-call | tf_op jit(solution)/shard_map/pallas_call | solution.py:799
  552.0 47.7 %shard_map.419 = (bf16[12,144,1152]{2,1,0:T(8,128)(2,1)}, bf16[12,2,80,1152]{3,2,1,0:T(8,128)(2,1)}, bf16[12,2,64,1152]{3,2,1,0:T(8,128)(2,1)}, bf16[12,64,1152]{2,1,0:T(8,128)(2,1)}, bf16[12,80,1152]{2,1,0:T(8,128)(2,1)}) custom-call(bf16[256,4608]{1,0:T(8,128)(2,1)} %get-tuple-element.141.refs_0_, bf16[256,1152]{1,0:T(8,128)(2,1)} %get-tuple-element.142.refs_1_, ...), custom_call_target="tpu_custom_call" | custom-call | flops 43486543872 | bytes 41943040 | tf_op jit(solution)/shard_map/pallas_call | solution.py:963
  599.7 4.1 collective-permute-start.12
  606.2 6.9 multiply_reduce_fusion.1
  616.0 24.0 %shard_map.420 = (bf16[256,1152]{1,0:T(8,128)(2,1)}, bf16[256,4608]{1,0:T(8,128)(2,1)}, bf16[256,1152]{1,0:T(8,128)(2,1)}, bf16[256,1152]{1,0:T(8,128)(2,1)}, f3...) custom-call(bf16[256,48]{1,0:T(8,128)(2,1)} %copy.59.refs_0_, ...), custom_call_target="tpu_custom_call" | custom-call | tf_op jit(solution)/shard_map/pallas_call | solution.py:1548
  642.4 21.1 %shard_map.421 = bf16[4,256,384]{2,1,0:T(8,128)(2,1)} custom-call(bf16[256,1152]{1,0:T(8,128)(2,1)} %get-tuple-element.153.x_ref), custom_call_target="tpu_custom_call" | custom-call | tf_op jit(solution)/shard_map/pallas_call | solution.py:692
  663.6 28.3 %shard_map.422 = (bf16[1024,384]{1,0:T(8,128)(2,1)}, bf16[1024,640]{1,0:T(8,128)(2,1)}, bf16[1024,640]{1,0:T(8,128)(2,1)}, bf16[1024,640]{1,0:T(8,128)(2,1)}) custom-call(s32[4]{0:T(128)} %get-tuple-element.238.lo, s32[4]{0:T(128)} %get-tuple-element.237.hi, bf16[1024,640]{1,0:T(8,128)(2,1)} %get-tuple-element.109.prev, bf16[1024,896]{1,0:T(8,128)(2,1)} %bitcast.70, ...), custom_call_target="tpu_custom_call" | custom-call | tf_op jit(solution)/shard_map/pallas_call | solution.py:237
  691.9 44.6 %shard_map.423.refs_7_ = bf16[256,3456]{1,0:T(8,128)(2,1)} custom-call(bf16[1024,640]{1,0:T(8,128)(2,1)} %get-tuple-element.156.dprev, bf16[1024,640]{1,0:T(8,128)(2,1)} %get-tuple-element.157.own, bf16[1024,640]{1,0:T(8,128)(2,1)} %get-tuple-element.158.dafter, bf16[1024,384]{1,0:T(8,128)(2,1)} %get-tuple-element.159.dq), custom_call_target="tpu_custom_call" | custom-call | tf_op jit(solution)/shard_map/pallas_call | solution.py:799
  736.6 7.5 multiply_reduce_fusion
  751.4 251.0 %shard_map.424 = (bf16[2,144,9216]{2,1,0:T(8,128)(2,1)}, bf16[2,576,1152]{2,1,0:T(8,128)(2,1)}, bf16[32,1152]{1,0:T(8,128)(2,1)}, bf16[8,32,1152]{2,1,0:T(8,128)(2,1)}) custom-call(bf16[256,4608]{1,0:T(8,128)(2,1)} %get-tuple-element.165.refs_0_, bf16[256,1152]{1,0:T(8,128)(2,1)} %get-tuple-element.166.refs_1_, ...), custom_call_target="tpu_custom_call" | custom-call | flops 43486543872 | bytes 104857600 | tf_op jit(solution)/shard_map/pallas_call | solution.py:1295
  1006.9 2.7 fusion.41
  1010.7 2.2 bitcast_convert_fusion.4
  1012.9 3.1 bitcast_convert_fusion.1
  1018.7 2.8 fusion.39
  1022.8 2.7 bitcast_convert_fusion
  (243 shorter events, 74.5 us)
Async XLA Ops:
  7.2 7.1 copy-start
  7.2 194.7 %all-reduce.13.cloned.1.call-start = ((), (), s32[]{:S(2)}) async-start(), calls=%async_computation | async-start | bytes 884736 | tf_op jit(solution)/shard_map/psum | solution.py:1647
  16.4 69.5 %copy-start.3 = (bf16[256,1152]{1,0:T(8,128)(2,1)S(1)}, bf16[256,1152]{1,0:T(8,128)(2,1)}, u32[]{:S(2)}) copy-start(bf16[256,1152]{1,0:T(8,128)(2,1)} %param.24) | copy-start | bytes 1769476
  83.8 34.2 %collective-permute-start.1 = (bf16[144,4608]{1,0:T(8,128)(2,1)}, bf16[144,4608]{1,0:T(8,128)(2,1)}, u32[]{:S(2)}, u32[]{:S(2)}) collective-permute-start(bf16[144,4608]{1,0:T(8,128)(2,1)} %refs_0_.2), channel_id=1, source_target_pairs={{0,16},{4,20},{8,24},{12,28},{16,0},{20,4},{24,8},{28,12},{1,17},{... | collective-permute-start | bytes 3981320 | tf_op jit(solution)/shard_map/ppermute | solution.py:396
  85.3 34.1 %collective-permute-start = (bf16[144,4608]{1,0:T(8,128)(2,1)}, bf16[144,4608]{1,0:T(8,128)(2,1)}, u32[]{:S(2)}, u32[]{:S(2)}) collective-permute-start(bf16[144,4608]{1,0:T(8,128)(2,1)} %refs_0_.2), channel_id=1, source_target_pairs={{0,8},{4,12},{8,0},{12,4},{16,24},{20,28},{24,16},{28,20},{1,9},{5... | collective-permute-start | bytes 3981320 | tf_op jit(solution)/shard_map/ppermute | solution.py:396
  91.1 7.3 copy-start.26
  91.1 9.3 copy-start.37
  91.2 9.3 copy-start.14
  98.4 96.4 %collective-permute-start.3 = (bf16[576,1152]{1,0:T(8,128)(2,1)}, bf16[576,1152]{1,0:T(8,128)(2,1)}, u32[]{:S(2)}, u32[]{:S(2)}) collective-permute-start(bf16[576,1152]{1,0:T(8,128)(2,1)} %refs_0_.3), channel_id=1, source_target_pairs={{0,16},{4,20},{8,24},{12,28},{16,0},{20,4},{24,8},{28,12},{1,17},{... | collective-permute-start | bytes 3981320 | tf_op jit(solution)/shard_map/ppermute | solution.py:396
  98.9 128.7 %collective-permute-start.2 = (bf16[576,1152]{1,0:T(8,128)(2,1)}, bf16[576,1152]{1,0:T(8,128)(2,1)}, u32[]{:S(2)}, u32[]{:S(2)}) collective-permute-start(bf16[576,1152]{1,0:T(8,128)(2,1)} %refs_0_.3), channel_id=1, source_target_pairs={{0,8},{4,12},{8,0},{12,4},{16,24},{20,28},{24,16},{28,20},{1,9},{5... | collective-permute-start | bytes 3981320 | tf_op jit(solution)/shard_map/ppermute | solution.py:396
  106.6 87.2 %copy-start.27 = (bf16[144,1152]{1,0:T(8,128)(2,1)S(1)}, bf16[144,1152]{1,0:T(8,128)(2,1)}, u32[]{:S(2)}) copy-start(bf16[144,1152]{1,0:T(8,128)(2,1)} %refs_6_) | copy-start | bytes 995332
  168.2 59.5 %collective-permute-start.5 = (bf16[144,3456]{1,0:T(8,128)(2,1)}, bf16[144,3456]{1,0:T(8,128)(2,1)}, u32[]{:S(2)}, u32[]{:S(2)}) collective-permute-start(bf16[144,3456]{1,0:T(8,128)(2,1)} %refs_3_), channel_id=1, source_target_pairs={{0,16},{4,20},{8,24},{12,28},{16,0},{20,4},{24,8},{28,12},{1,17},{... | collective-permute-start | bytes 2985992 | tf_op jit(solution)/shard_map/ppermute | solution.py:396
  192.0 35.7 %collective-permute-start.4 = (bf16[144,3456]{1,0:T(8,128)(2,1)}, bf16[144,3456]{1,0:T(8,128)(2,1)}, u32[]{:S(2)}, u32[]{:S(2)}) collective-permute-start(bf16[144,3456]{1,0:T(8,128)(2,1)} %refs_3_), channel_id=1, source_target_pairs={{0,8},{4,12},{8,0},{12,4},{16,24},{20,28},{24,16},{28,20},{1,9},{5... | collective-permute-start | bytes 2985992 | tf_op jit(solution)/shard_map/ppermute | solution.py:396
  193.8 33.9 %collective-permute-start.7 = (bf16[144,1152]{1,0:T(8,128)(2,1)S(1)}, bf16[144,1152]{1,0:T(8,128)(2,1)S(1)}, u32[]{:S(2)}, u32[]{:S(2)}) collective-permute-start(bf16[144,1152]{1,0:T(8,128)(2,1)S(1)} %copy-done.27), channel_id=1, source_target_pairs={{0,16},{4,20},{8,24},{12,28},{16,0},{20,4},{24,8},{28,12},{1,17},{... | collective-permute-start | bytes 995336 | tf_op jit(solution)/shard_map/ppermute | solution.py:396
  194.8 32.9 %collective-permute-start.6 = (bf16[144,1152]{1,0:T(8,128)(2,1)S(1)}, bf16[144,1152]{1,0:T(8,128)(2,1)}, u32[]{:S(2)}, u32[]{:S(2)}) collective-permute-start(bf16[144,1152]{1,0:T(8,128)(2,1)S(1)} %copy-done.27), channel_id=1, source_target_pairs={{0,8},{4,12},{8,0},{12,4},{16,24},{20,28},{24,16},{28,20},{1,9},{5... | collective-permute-start | bytes 995336 | tf_op jit(solution)/shard_map/ppermute | solution.py:396
  272.7 36.3 %collective-permute-start.9 = (bf16[144,4608]{1,0:T(8,128)(2,1)}, bf16[144,4608]{1,0:T(8,128)(2,1)}, u32[]{:S(2)}, u32[]{:S(2)}) collective-permute-start(bf16[144,4608]{1,0:T(8,128)(2,1)} %refs_0_.4), channel_id=1, source_target_pairs={{0,16},{4,20},{8,24},{12,28},{16,0},{20,4},{24,8},{28,12},{1,17},{... | collective-permute-start | bytes 3981320 | tf_op jit(solution)/shard_map/ppermute | solution.py:396
  274.7 34.4 %collective-permute-start.8 = (bf16[144,4608]{1,0:T(8,128)(2,1)}, bf16[144,4608]{1,0:T(8,128)(2,1)}, u32[]{:S(2)}, u32[]{:S(2)}) collective-permute-start(bf16[144,4608]{1,0:T(8,128)(2,1)} %refs_0_.4), channel_id=1, source_target_pairs={{0,8},{4,12},{8,0},{12,4},{16,24},{20,28},{24,16},{28,20},{1,9},{5... | collective-permute-start | bytes 3981320 | tf_op jit(solution)/shard_map/ppermute | solution.py:396
  298.6 7.3 copy-start.25
  298.6 7.3 copy-start.19
  298.6 9.5 copy-start.24
  305.9 70.1 %collective-permute-start.11 = (bf16[576,1152]{1,0:T(8,128)(2,1)S(1)}, bf16[576,1152]{1,0:T(8,128)(2,1)S(1)}, u32[]{:S(2)}, u32[]{:S(2)}) collective-permute-start(bf16[576,1152]{1,0:T(8,128)(2,1)S(1)} %copy-done.19), channel_id=1, source_target_pairs={{0,16},{4,20},{8,24},{12,28},{16,0},{20,4},{24,8},{28,12},{1,17},{... | collective-permute-start | bytes 3981320 | tf_op jit(solution)/shard_map/ppermute | solution.py:396
  306.1 69.8 %collective-permute-start.10 = (bf16[576,1152]{1,0:T(8,128)(2,1)S(1)}, bf16[576,1152]{1,0:T(8,128)(2,1)S(1)}, u32[]{:S(2)}, u32[]{:S(2)}) collective-permute-start(bf16[576,1152]{1,0:T(8,128)(2,1)S(1)} %copy-done.19), channel_id=1, source_target_pairs={{0,8},{4,12},{8,0},{12,4},{16,24},{20,28},{24,16},{28,20},{1,9},{5... | collective-permute-start | bytes 3981320 | tf_op jit(solution)/shard_map/ppermute | solution.py:396
  552.0 51.8 %copy-start.36 = (f32[1,1152]{1,0:T(1,128)S(1)}, f32[1,1152]{1,0:T(1,128)}, u32[]{:S(2)}) copy-start(f32[1,1152]{1,0:T(1,128)} %get-tuple-element.175) | copy-start | bytes 13828
  552.0 51.9 %copy-start.35 = (f32[1,1152]{1,0:T(1,128)S(1)}, f32[1,1152]{1,0:T(1,128)}, u32[]{:S(2)}) copy-start(f32[1,1152]{1,0:T(1,128)} %get-tuple-element.177) | copy-start | bytes 13828
  552.0 52.0 %copy-start.32 = (f32[1,4608]{1,0:T(1,128)S(1)}, f32[1,4608]{1,0:T(1,128)}, u32[]{:S(2)}) copy-start(f32[1,4608]{1,0:T(1,128)} %get-tuple-element.176) | copy-start | bytes 55300
  599.7 6.5 copy-start.2
  599.7 136.9 %collective-permute-start.12 = (bf16[12,2,80,1152]{3,2,1,0:T(8,128)(2,1)}, bf16[12,2,80,1152]{3,2,1,0:T(8,128)(2,1)}, u32[]{:S(2)}, u32[]{:S(2)}) collective-permute-start(bf16[12,2,80,1152]{3,2,1,0:T(8,128)(2,1)} %get-tuple-element.160), channel_id=1, source_target_pairs={{0,8},{4,12},{8,0},{12,4},{16,24},{20,28},{24,16},{28,20},{1,9},{5... | collective-permute-start | bytes 13271048 | tf_op jit(solution)/shard_map/ppermute | solution.py:1657
  603.7 132.8 %collective-permute-start.13 = (bf16[12,2,64,1152]{3,2,1,0:T(8,128)(2,1)}, bf16[12,2,64,1152]{3,2,1,0:T(8,128)(2,1)}, u32[]{:S(2)}, u32[]{:S(2)}) collective-permute-start(bf16[12,2,64,1152]{3,2,1,0:T(8,128)(2,1)} %get-tuple-element.161), channel_id=1, source_target_pairs={{0,16},{4,20},{8,24},{12,28},{16,0},{20,4},{24,8},{28,12},{1,17},{... | collective-permute-start | bytes 10616840 | tf_op jit(solution)/shard_map/ppermute | solution.py:1657
  606.2 6.9 copy-start.10
  691.9 44.6 %copy-start.4 = (bf16[256,1152]{1,0:T(8,128)(2,1)S(1)}, bf16[256,1152]{1,0:T(8,128)(2,1)}, u32[]{:S(2)}) copy-start(bf16[256,1152]{1,0:T(8,128)(2,1)} %param.24) | copy-start | bytes 1769476
  691.9 44.6 %copy-start.8 = (f32[256,2304]{1,0:T(8,128)S(1)}, f32[256,2304]{1,0:T(8,128)}, u32[]{:S(2)}) copy-start(f32[256,2304]{1,0:T(8,128)} %copy-done.7) | copy-start | bytes 7077892
  736.6 7.6 copy-start.16
  (22 other events, 50.0 us)
Sparse Core Ops, SparseCore 0:
  102.6 56.3 all-reduce.12

commit v7 on v6

--- a/solution.py
+++ b/solution.py
@@ -421,12 +421,12 @@
     return tuple(jax.ShapeDtypeStruct((8 * part.shape[0], part.shape[1]), part.dtype) for part, *_ in shards)
 
 
-def halves_of(shards):
+def halves_of(shards, more=False):
     halves, ahead = [], 0
     for part, *_ in shards:
         rows, size = part.shape
-        half = rows // 32 * 16
-        if rows % 32 and ahead <= 0:
+        half = rows // 24 * 16 if more else rows // 32 * 16
+        if rows % 32 and ahead <= 0 and not more:
             half += 16
         ahead += (2 * half - rows) * size
         halves.append(half)
@@ -617,7 +617,7 @@
     size, wide = qkv.shape[0], pad_to(qkv.shape[1] // reps, LANES)
     sems = pltpu.SemaphoreType.DMA((2, reps))
     own, prev, after, *fulls = pl.pallas_call(
-        functools.partial(to_heads_kernel, reps, size, edge, kv, halves_of(shards)),
+        functools.partial(to_heads_kernel, reps, size, edge, kv, halves_of(shards, True)),
         out_shape=(
             jax.ShapeDtypeStruct((reps, size, wide), qkv.dtype),
             jax.ShapeDtypeStruct((edge, kv), qkv.dtype),
@@ -634,11 +634,35 @@
     return own.reshape(reps * size, wide), prev, after, fulls
 
 
+class Tails:
+    def __init__(self, hd, size):
+        self.main = hd // LANES * LANES
+        self.few = hd - self.main
+        self.fold = LANES // self.few
+        self.band = size // self.fold
+
+    def block(self, values, shift):
+        turned = pltpu.roll(values.astype(jnp.float32), shift % LANES, 1) if shift % LANES else values.astype(jnp.float32)
+        lane = lax.broadcasted_iota(jnp.int32, turned.shape, 1)
+        return jnp.where(lane < self.few, turned, 0.0)
+
+    def folded(self, ref):
+        total = None
+        for at in range(self.fold):
+            part = self.block(ref[at * self.band : (at + 1) * self.band, self.main : self.main + LANES], 0)
+            part = pltpu.roll(part, at * self.few, 1) if at else part
+            total = part if total is None else total + part
+        return total.astype(jnp.bfloat16)
+
+    def unfolded(self, tail, at):
+        return self.block(tail, -at * self.few).astype(jnp.bfloat16)
+
+
 def swap_kernel(reps, out, plan, x_ref, *refs):
     halves, sizes = plan
     count = len(halves)
     shards, refs = split_shards(refs, sizes)
-    y_ref, fulls, (held, send, recv, *sems) = refs[0], refs[1 : count + 1], refs[count + 1 :]
+    y_ref, fulls, (held, tail_out, tail_in, opened, send, recv, done, *sems) = refs[0], refs[1 : count + 1], refs[count + 1 :]
     gather = Gather(shards, fulls, halves, *sems) if count else None
     group, me = lax.axis_index("fsdp"), lax.axis_index("replica")
     others = [(group, lax.rem(me + d, reps)) for d in range(1, reps)]
@@ -646,6 +670,8 @@
     size, lanes = held.shape[1:]
     src, dst = (x_ref, held) if out else (held, y_ref)
     hd = (y_ref if out else x_ref).shape[1] // reps
+    tails = Tails(hd, size)
+    span = pl.ds(0, tails.main)
     greet([(place, True) for place in others + planar], reps - 1 + len(planar))
     for place in range(reps):
         if not out:
@@ -653,13 +679,16 @@
                 held[place, rows, :] = assemble(rows, lanes, [(x_ref, place * hd, 0, hd)]).astype(jnp.bfloat16)
 
             by_rows(size, pack)
-        leave = pltpu.make_async_remote_copy(
-            src_ref=src.at[place], dst_ref=dst.at[me], send_sem=send.at[place], recv_sem=recv.at[me],
-            device_id=(group, place), device_id_type=MESH,
-        )
-        keep = pltpu.make_async_copy(src.at[place], dst.at[place], recv.at[place])
-        pl.when(me != place)(leave.start)
-        pl.when(me == place)(keep.start)
+        tail_out[place] = tails.folded(src.at[place])
+        parts = ((src.at[place, :, span], lambda to: dst.at[to, :, span]), (tail_out.at[place], lambda to: tail_in.at[to]))
+        for at, (part, landing) in enumerate(parts):
+            leave = pltpu.make_async_remote_copy(
+                src_ref=part, dst_ref=landing(me), send_sem=send.at[at, place], recv_sem=recv.at[at, me],
+                device_id=(group, place), device_id_type=MESH,
+            )
+            keep = pltpu.make_async_copy(part, landing(place), recv.at[at, place])
+            pl.when(me != place)(leave.start)
+            pl.when(me == place)(keep.start)
     if count:
         gather.begin()
     for at in range(count):
@@ -667,15 +696,29 @@
     for at in range(count):
         gather.across(at)
     for piece in range(reps):
-        wait_for(dst.at[piece], recv.at[piece])
+        wait_for(dst.at[piece, :, span], recv.at[0, piece])
+        wait_for(tail_in.at[piece], recv.at[1, piece])
+        for at in range(tails.fold):
+            rows = slice(at * tails.band, (at + 1) * tails.band)
+            few = tails.unfolded(tail_in[piece], at)
+            if out:
+                held[piece, rows, tails.main : tails.main + LANES] = few
+            else:
+                opened[piece, rows, :] = few
+        if not out:
+            pltpu.make_async_copy(opened.at[piece], y_ref.at[piece, :, pl.ds(tails.main, LANES)], done.at[piece]).start()
     if out:
         def unpack(rows):
             pieces = [(held.at[place], 0, place * hd, hd) for place in range(reps)]
             y_ref[rows, :] = assemble(rows, y_ref.shape[1], pieces).astype(jnp.bfloat16)
 
         by_rows(size, unpack)
+    else:
+        for piece in range(reps):
+            wait_for(opened.at[piece], done.at[piece])
     for _, there in others:
-        wait_for(src.at[there], send.at[there])
+        wait_for(src.at[there, :, span], send.at[0, there])
+        wait_for(tail_out.at[there], send.at[1, there])
     for at in range(count):
         gather.end(at)
 
@@ -688,13 +731,18 @@
     else:
         size, lanes = x.shape[0], pad_to(x.shape[1] // reps, LANES)
         shape = (reps, size, lanes)
-    sems = pltpu.SemaphoreType.DMA((reps,))
+    band = Tails(HEADS * HEAD_DIM // reps, size).band
+    sems = pltpu.SemaphoreType.DMA((2, reps))
+    tail = pltpu.VMEM((reps, band, LANES), x.dtype)
     swapped, *fulls = pl.pallas_call(
         functools.partial(swap_kernel, reps, out, halves_of(shards)),
         out_shape=(jax.ShapeDtypeStruct(shape, x.dtype), *gathered_shapes(shards)),
-        in_specs=[HB if out else VM] + [HB] * sum(len(shard) for shard in shards),
+        in_specs=[VM] + [HB] * sum(len(shard) for shard in shards),
         out_specs=(VM if out else HB,) + (HB,) * len(shards),
-        scratch_shapes=[pltpu.VMEM((reps, size, lanes), x.dtype), sems, sems, *gather_scratch(shards)],
+        scratch_shapes=[
+            pltpu.VMEM((reps, size, lanes), x.dtype), tail, tail, pltpu.VMEM((reps, size, LANES), x.dtype), sems, sems,
+            pltpu.SemaphoreType.DMA((reps,)), *gather_scratch(shards),
+        ],
         compiler_params=pltpu.CompilerParams(
             collective_id=collective_id, has_side_effects=True, vmem_limit_bytes=VMEM_LIMIT
         ),
@@ -702,100 +750,146 @@
     return swapped, fulls
 
 
-def from_heads_kernel(reps, size, edge, dprev, own, dafter, dq, out, out_kv, out_q, from_up, from_down, total, mine, sends, recvs, send, recv):
+def from_heads_kernel(
+    reps, size, edge, dprev, own, dafter, dq, out, out_kv, out_q, dq_tail, from_up, from_down, total, mine,
+    sends, recvs, send, recv, tail_sem,
+):
     group, me = lax.axis_index("fsdp"), lax.axis_index("replica")
     groups = lax.axis_size("fsdp")
     rows = reps * size
     down, up = group > 0, group < groups - 1
     others = [(group, lax.rem(me + d, reps)) for d in range(1, reps)]
+    order = [lax.rem(me + d, reps) for d in range(1, reps + 1)]
     greet(
         [(place, True) for place in others] + [((group - 1, me), down), ((group + 1, me), up)],
         reps - 1 + down.astype(jnp.int32) + up.astype(jnp.int32),
     )
-    to_down = pltpu.make_async_remote_copy(
-        src_ref=dprev, dst_ref=from_up, send_sem=sends.at[0], recv_sem=recvs.at[0],
-        device_id=(group - 1, me), device_id_type=MESH,
-    )
-    to_up = pltpu.make_async_remote_copy(
-        src_ref=dafter, dst_ref=from_down, send_sem=sends.at[1], recv_sem=recvs.at[1],
-        device_id=(group + 1, me), device_id_type=MESH,
-    )
-    pl.when(down)(to_down.start)
-    pl.when(up)(to_up.start)
-    for _, there in others:
-        pltpu.make_async_remote_copy(
-            src_ref=dq.at[pl.ds(pl.multiple_of(there * size, size), size), :], dst_ref=out_q.at[me], send_sem=send.at[0, there],
-            recv_sem=recv.at[0, me], device_id=(group, there), device_id_type=MESH,
-        ).start()
-    pltpu.make_async_copy(dq.at[pl.ds(pl.multiple_of(me * size, size), size), :], out_q.at[me], recv.at[0, me]).start()
-    step = math.gcd(edge, 256)
-
-    def chunk(at, carry):
-        here = pl.ds(pl.multiple_of(at * step, step), step)
-        total[here, :] = own[here, :].astype(jnp.float32)
-        return carry
-
-    lax.fori_loop(0, rows // step, chunk, 0)
-
-    def add(ref, first):
-        def body(at, carry):
-            here = pl.ds(pl.multiple_of(first + at * step, step), step)
-            there = pl.ds(pl.multiple_of(at * step, step), step)
-            total[here, :] += ref[there, :].astype(jnp.float32)
-            return carry
-
-        lax.fori_loop(0, edge // step, body, 0)
-
-    @pl.when(down)
-    def _():
-        wait_for(from_down, recvs.at[1])
-        add(from_down, 0)
-
-    @pl.when(up)
-    def _():
-        wait_for(from_up, recvs.at[0])
-        add(from_up, rows - edge)
-
-    def narrow(at, carry):
-        here = pl.ds(pl.multiple_of(at * step, step), step)
-        mine[here, :] = total[here, :].astype(jnp.bfloat16)
-        return carry
-
-    lax.fori_loop(0, rows // step, narrow, 0)
-    for _, there in others:
-        pltpu.make_async_remote_copy(
-            src_ref=mine.at[pl.ds(pl.multiple_of(there * size, size), size), :], dst_ref=out_kv.at[me], send_sem=send.at[1, there],
-            recv_sem=recv.at[1, me], device_id=(group, there), device_id_type=MESH,
-        ).start()
-    pltpu.make_async_copy(mine.at[pl.ds(pl.multiple_of(me * size, size), size), :], out_kv.at[me], recv.at[1, me]).start()
+    edges = edge // size
     width = out.shape[1] // 3
     hd = width // reps
-
-    def unpack(ref, first, section):
+    tails = Tails(hd, size)
+
+    def at_piece(piece):
+        return pl.ds(pl.multiple_of(piece * size, size), size)
+
+    def to_down(piece):
+        return pltpu.make_async_remote_copy(
+            src_ref=dprev.at[at_piece(piece), :], dst_ref=from_up.at[at_piece(piece), :], send_sem=sends.at[0, piece],
+            recv_sem=recvs.at[0, piece], device_id=(group - 1, me), device_id_type=MESH,
+        )
+
+    def to_up(piece):
+        return pltpu.make_async_remote_copy(
+            src_ref=dafter.at[at_piece(piece), :], dst_ref=from_down.at[at_piece(piece), :], send_sem=sends.at[1, piece],
+            recv_sem=recvs.at[1, piece], device_id=(group + 1, me), device_id_type=MESH,
+        )
+
+    def edge_pieces(piece, when_up, when_down):
+        pl.when(jnp.logical_and(down, piece < edges))(lambda: when_down(piece))
+        late = piece - (reps - edges)
+        pl.when(jnp.logical_and(up, late >= 0))(lambda: when_up(late))
+
+    for piece in order:
+        late = piece - (reps - edges)
+        pl.when(jnp.logical_and(down, late >= 0))(lambda late=late: to_down(late).start())
+        pl.when(jnp.logical_and(up, piece < edges))(lambda piece=piece: to_up(piece).start())
+    tail_load = pltpu.make_async_copy(dq.at[:, pl.ds(tails.main, LANES)], dq_tail, tail_sem)
+    tail_load.start()
+
+    def query_copy(piece):
+        return pltpu.make_async_remote_copy(
+            src_ref=dq.at[at_piece(piece), pl.ds(0, tails.main)], dst_ref=out_q.at[me], send_sem=send.at[0, piece],
+            recv_sem=recv.at[0, me], device_id=(group, piece), device_id_type=MESH,
+        )
+
+    def sums_copy(piece):
+        return pltpu.make_async_remote_copy(
+            src_ref=mine.at[at_piece(piece), :], dst_ref=out_kv.at[me], send_sem=send.at[1, piece],
+            recv_sem=recv.at[1, me], device_id=(group, piece), device_id_type=MESH,
+        )
+
+    for piece in order[:-1]:
+        query_copy(piece).start()
+    pltpu.make_async_copy(dq.at[at_piece(me), pl.ds(0, tails.main)], out_q.at[me], recv.at[0, me]).start()
+    tail_load.wait()
+    step = math.gcd(size, 64)
+
+    def sum_up(piece):
+        def chunk(at, action):
+            here = pl.ds(pl.multiple_of(piece * size + at * step, step), step)
+            there = pl.ds(pl.multiple_of(at * step, step), step)
+            action(here, there)
+
+        def over(action):
+            def body(at, carry):
+                chunk(at, action)
+                return carry
+
+            lax.fori_loop(0, size // step, body, 0)
+
+        def begin(here, there):
+            total[there, :] = own[here, :].astype(jnp.float32)
+
+        over(begin)
+
+        def add(ref, sem, source):
+            wait_for(ref.at[at_piece(source), :], sem)
+
+            def body(at, carry):
+                there = pl.ds(pl.multiple_of(at * step, step), step)
+                here = pl.ds(pl.multiple_of(source * size + at * step, step), step)
+                total[there, :] += ref[here, :].astype(jnp.float32)
+                return carry
+
+            lax.fori_loop(0, size // step, body, 0)
+
+        edge_pieces(
+            piece, lambda late: add(from_up, recvs.at[0, late], late), lambda early: add(from_down, recvs.at[1, early], early)
+        )
+
+        def narrow(here, there):
+            mine[here, :] = total[there, :].astype(jnp.bfloat16)
+            first = 2 * hd // LANES * LANES
+            few = pltpu.roll(tails.block(dq_tail[here, :], 0), 2 * hd - first, 1)
+            last = slice(first, first + LANES)
+            mine[here, last] = (total[there, last] + few).astype(jnp.bfloat16)
+
+        over(narrow)
+
+    for piece in order[:-1]:
+        sum_up(piece)
+        sums_copy(piece).start()
+    sum_up(me)
+    pltpu.make_async_copy(mine.at[at_piece(me), :], out_kv.at[me], recv.at[1, me]).start()
+
+    def unpack(section, sources):
         def body(rows):
-            pieces = [(ref.at[place], first, place * hd, hd) for place in range(reps)]
+            pieces = [
+                (ref.at[place], first, place * hd + to, lanes) for place in range(reps) for ref, first, to, lanes in sources
+            ]
             out[rows, section * width : (section + 1) * width] = assemble(rows, width, pieces).astype(jnp.bfloat16)
 
         by_rows(size, body)
 
     for piece in range(reps):
         wait_for(out_q.at[piece], recv.at[0, piece])
-    unpack(out_q, 0, 0)
-    for piece in range(reps):
         wait_for(out_kv.at[piece], recv.at[1, piece])
-    unpack(out_kv, 0, 1)
-    unpack(out_kv, hd, 2)
-    for _, there in others:
-        wait_for(out_q.at[0], send.at[0, there])
-        wait_for(out_kv.at[0], send.at[1, there])
-    pl.when(down)(to_down.wait_send)
-    pl.when(up)(to_up.wait_send)
+    unpack(0, ((out_q, 0, 0, tails.main), (out_kv, 2 * hd, tails.main, tails.few)))
+    unpack(1, ((out_kv, 0, 0, hd),))
+    unpack(2, ((out_kv, hd, 0, hd),))
+    for piece in order[:-1]:
+        query_copy(piece).wait_send()
+        sums_copy(piece).wait_send()
+    for piece in order:
+        late = piece - (reps - edges)
+        pl.when(jnp.logical_and(down, late >= 0))(lambda late=late: to_down(late).wait_send())
+        pl.when(jnp.logical_and(up, piece < edges))(lambda piece=piece: to_up(piece).wait_send())
 
 
 def from_heads(reps, width, dprev, own, dafter, dq, collective_id):
     rows, kv = own.shape
     edge, size = dprev.shape[0], own.shape[0] // reps
-    pair, both = pltpu.SemaphoreType.DMA((2,)), pltpu.SemaphoreType.DMA((2, reps))
+    both = pltpu.SemaphoreType.DMA((2, reps))
     return pl.pallas_call(
         functools.partial(from_heads_kernel, reps, size, edge),
         out_shape=jax.ShapeDtypeStruct((size, 3 * width), own.dtype),
@@ -803,15 +897,17 @@
         out_specs=VM,
         scratch_shapes=[
             pltpu.VMEM((reps, size, kv), own.dtype),
-            pltpu.VMEM((reps, size, dq.shape[1]), own.dtype),
+            pltpu.VMEM((reps, size, width // reps // LANES * LANES), own.dtype),
+            pltpu.VMEM((rows, LANES), own.dtype),
             pltpu.VMEM((edge, kv), own.dtype),
             pltpu.VMEM((edge, kv), own.dtype),
-            pltpu.VMEM((rows, kv), jnp.float32),
+            pltpu.VMEM((size, kv), jnp.float32),
             pltpu.VMEM((rows, kv), own.dtype),
-            pair,
-            pair,
             both,
             both,
+            both,
+            both,
+            pltpu.SemaphoreType.DMA,
         ],
         compiler_params=pltpu.CompilerParams(
             collective_id=collective_id, has_side_effects=True, vmem_limit_bytes=VMEM_LIMIT
@@ -821,6 +917,7 @@
 
 MATRICES = 12
 CHIP_WIDTH, UNIT_WIDTH = 1152, 384
+SLACK = 4
 LEFT_ROWS = 4
 PLACES = ((0, 0), (1, 0), (0, 1), (1, 1))
 
@@ -992,6 +1089,7 @@
     rows = own.shape[1]
     extras = extra.shape[0]
     unit = own.shape[2]
+    slots, pairs, z_slots = xr.shape[0], crecv.shape[0], z1r.shape[0]
     count = extras + 2 * MATRICES * (width // unit)
     terms = Terms(ins, flat, left, right, rows, width, load_sem)
     core_at, x_at, y_at = terms.core_at, terms.x_at, terms.y_at
@@ -1067,11 +1165,11 @@
         return pl.ds(pl.multiple_of(u * unit, LANES), unit)
 
     def fin_extra(u):
-        slot = lax.rem(u, 4)
+        slot = lax.rem(u, slots)
         return send(fin.at[slot, pl.ds(0, few), :], mine.at[:, columns(u)], fin_s.at[slot], fin_r.at[u], (f, z_at))
 
     def keep_extra(u):
-        slot = lax.rem(u, 4)
+        slot = lax.rem(u, slots)
         return pltpu.make_async_copy(fin.at[slot, pl.ds(0, few), :], mine.at[:, columns(u)], fin_l.at[slot])
 
     def share_copy(u, there, where):
@@ -1086,7 +1184,7 @@
         return src.at[at, :, here] if len(src.shape) == 3 else src.at[at, :, :, here]
 
     def ready_copies(u):
-        slot = lax.rem(u, 4)
+        slot = lax.rem(u, slots)
         buffers = ((own_in, own_l), (xr_in, xr_l), (yr_in, yr_l), (tx_in, tx_l), (ty_in, ty_l))
         return [
             pltpu.make_async_copy(piece(src, (u - extras) // 2), dst.at[slot], ready_sem.at[at, slot])
@@ -1094,7 +1192,6 @@
         ]
 
     f32, bf16 = jnp.float32, jnp.bfloat16
-    z_slots = z1r.shape[0]
 
     def stage(u, condition, body, first=0, last=count):
         live = jnp.logical_and(u >= first, u < last)
@@ -1109,7 +1206,7 @@
         share_own(u).start()
 
     def close(u):
-        slot = lax.rem(u, 4)
+        slot = lax.rem(u, slots)
 
         def action(to):
             fin_copy(slot, u, to).wait_send()
@@ -1118,7 +1215,7 @@
         routed(u, action)
 
     def arrive(u):
-        routed(u, lambda to: fin_copy(lax.rem(u, 4), u, to).wait_recv())
+        routed(u, lambda to: fin_copy(lax.rem(u, slots), u, to).wait_recv())
 
     def close_extra(u):
         fin_extra(u).wait_send()
@@ -1128,7 +1225,7 @@
         fin_extra(u).wait_recv()
 
     def finish(u):
-        slot = lax.rem(u, 4)
+        slot = lax.rem(u, slots)
         z2_copy(slot).wait()
         fin[slot] = (z2s[slot].astype(f32) + z2r[slot].astype(f32)).astype(bf16)
 
@@ -1146,7 +1243,7 @@
             keep_extra(u).start()
 
     def middle(u):
-        slot, z_slot, at = lax.rem(u, 4), lax.rem(u, z_slots), lax.rem(u, own.shape[0])
+        slot, z_slot, at = lax.rem(u, slots), lax.rem(u, z_slots), lax.rem(u, own.shape[0])
         z1_copy(slot, z_slot).wait_recv()
         z2s[slot] = (own[at] + z1r[z_slot].astype(f32)).astype(bf16)
         z2_copy(slot).start()
@@ -1156,10 +1253,10 @@
             pl.semaphore_signal(credit, inc=1, device_id=(f, z_at), device_id_type=MESH)
 
     def sent(u):
-        z1_copy(lax.rem(u, 4), lax.rem(u, z_slots)).wait_send()
+        z1_copy(lax.rem(u, slots), lax.rem(u, z_slots)).wait_send()
 
     def plane(u):
-        slot, at = lax.rem(u, 4), lax.rem(u, own.shape[0])
+        slot, at = lax.rem(u, slots), lax.rem(u, own.shape[0])
         x2_copy(slot).wait()
         y2_copy(slot).wait()
         own[at, top, :] += y2r[slot].astype(f32)
@@ -1176,7 +1273,7 @@
             z1_copy(slot, lax.rem(u, z_slots)).start()
 
     def cross(u):
-        slot, at = lax.rem(u, 4), lax.rem(u, own.shape[0])
+        slot, at = lax.rem(u, slots), lax.rem(u, own.shape[0])
         x_copy(slot).wait()
         y_copy(slot).wait()
         y2s[slot] = (ty[slot] + xr[slot, 1].astype(f32)).astype(bf16)
@@ -1187,7 +1284,7 @@
         own[at, low, :] += yr[slot, 0].astype(f32)
 
     def cross_ready(u):
-        slot, at = lax.rem(u, 4), lax.rem(u, own.shape[0])
+        slot, at = lax.rem(u, slots), lax.rem(u, own.shape[0])
         for copy in ready_copies(u):
             copy.wait()
         y2s[slot] = (ty_l[slot].astype(f32) + xr_l[slot, 1].astype(f32)).astype(bf16)
@@ -1198,9 +1295,9 @@
         own[at, low, :] = own_l[slot, low, :].astype(f32) + yr_l[slot, 0].astype(f32)
 
     def chip(u):
-        slot, at = lax.rem(u, 4), lax.rem(u, own.shape[0])
+        slot, at = lax.rem(u, slots), lax.rem(u, own.shape[0])
         w = (u - extras) // 2
-        pair = lax.rem(w, 2)
+        pair = lax.rem(w, pairs)
         stacked = terms.stack(w, 0)
         core_copy(pair).wait()
         total = stacked[3 * rows :] + crecv[pair, 3].astype(f32)
@@ -1217,7 +1314,7 @@
         own[at] = stacked[:rows] + crecv[pair, 0].astype(f32)
 
     def chip_extra(u):
-        slot, at = lax.rem(u, 4), lax.rem(u, own.shape[0])
+        slot, at = lax.rem(u, slots), lax.rem(u, own.shape[0])
         extra_copy(u).wait()
         for m, (mx, my) in enumerate(PLACES):
             total = extra[u, terms.block(0, mx, my)] + cx_r[u, m].astype(f32)
@@ -1241,7 +1338,7 @@
 
     def open_unit(u):
         w = (u - extras) // 2
-        pair = lax.rem(w, 2)
+        pair = lax.rem(w, pairs)
         csend[pair] = terms.stack(w, 1).astype(bf16).reshape(csend.shape[1:])
         core_copy(pair).start()
 
@@ -1252,27 +1349,28 @@
         return lax.rem(u - extras, 2) == 0
 
     def step(t, carry):
-        stage(t - 13, None, share, 0, extras)
-        stage(t - 12, inner, close, extras)
-        stage(t - 12, outer, arrive, extras)
-        stage(t - 12, inner, close_extra, 0, extras)
-        stage(t - 12, outer, arrive_extra, 0, extras)
-        stage(t - 10, inner, finish)
-        stage(t - 8, inner, middle)
-        stage(t - 8, outer, sent)
-        stage(t - 6, None, plane)
-        stage(t - 4, full(t - 4), cross, extras)
-        stage(t - 4, None, cross, 0, extras)
-        stage(t - 4, prepared(t - 4), cross_ready, extras)
-        stage(t - 2, full(t - 2), chip, extras)
-        stage(t - 2, None, chip_extra, 0, extras)
-        pl.when(t == extras)(terms.wait)
+        at = [t - hop * SLACK for hop in range(7)]
+        stage(at[6] - 1, None, share, 0, extras)
+        stage(at[6], inner, close, extras)
+        stage(at[6], outer, arrive, extras)
+        stage(at[6], inner, close_extra, 0, extras)
+        stage(at[6], outer, arrive_extra, 0, extras)
+        stage(at[5], inner, finish)
+        stage(at[4], inner, middle)
+        stage(at[4], outer, sent)
+        stage(at[3], None, plane)
+        stage(at[2], full(at[2]), cross, extras)
+        stage(at[2], None, cross, 0, extras)
+        stage(at[2], prepared(at[2]), cross_ready, extras)
+        stage(at[1], full(at[1]), chip, extras)
+        stage(at[1], None, chip_extra, 0, extras)
+        pl.when(t == extras + 1)(terms.wait)
         stage(t, full(t), open_unit, extras)
         stage(t, prepared(t), open_ready, extras)
         stage(t, None, open_extra, 0, extras)
         return carry
 
-    lax.fori_loop(0, count + 12, step, 0)
+    lax.fori_loop(0, count + 6 * SLACK + 1, step, 0)
     for u in range(extras):
         for there in others:
             share_copy(u, f, there).wait_send()
@@ -1290,7 +1388,7 @@
     bf16, f32 = jnp.bfloat16, jnp.float32
     buf = lambda dtype, *shape: pltpu.VMEM((*shape, unit), dtype)
     sem = lambda *size: pltpu.SemaphoreType.DMA(size)
-    z_slots = 8
+    slots, z_slots = 2 * SLACK, 3 * SLACK
     rest = rows - half
     return pl.pallas_call(
         functools.partial(reduce_kernel, width, half),
@@ -1306,15 +1404,14 @@
             *term_scratch(ins, unit),
             buf(f32, extras, 8, few), sem(extras), buf(bf16, extras, 4, few), buf(bf16, extras, 4, few),
             sem(extras), sem(extras), sem(extras, 8), sem(extras, 8),
-            buf(bf16, 2, 4, rows), buf(bf16, 2, 4, rows), buf(f32, 9, rows),
-            buf(bf16, 4, 2, half), buf(bf16, 4, 2, half), buf(bf16, 4, 2, rest), buf(bf16, 4, 2, rest),
-            buf(f32, 4, rest), buf(f32, 4, half),
-            buf(bf16, 4, rest), buf(bf16, 4, rest), buf(bf16, 4, half), buf(bf16, 4, half),
-            buf(bf16, 4, rows), buf(bf16, z_slots, rows), buf(bf16, 4, rows), buf(bf16, 4, rows), buf(bf16, 4, rows),
-            buf(bf16, 4, rows), buf(bf16, 4, 2, half), buf(bf16, 4, 2, rest), buf(bf16, 4, rest), buf(bf16, 4, half),
-            sem(5, 4),
-            sem(2), sem(2), sem(4), sem(4), sem(4), sem(4), sem(4), sem(4), sem(4), sem(4),
-            sem(4), sem(z_slots), sem(4), sem(4), sem(4), sem(4), sem(count), pltpu.SemaphoreType.REGULAR,
+            buf(bf16, SLACK, 4, rows), buf(bf16, SLACK, 4, rows), buf(f32, 3 * SLACK + 1, rows),
+            buf(bf16, slots, 2, half), buf(bf16, slots, 2, half), buf(bf16, slots, 2, rest), buf(bf16, slots, 2, rest),
+            buf(f32, slots, rest), buf(f32, slots, half),
+            buf(bf16, slots, rest), buf(bf16, slots, rest), buf(bf16, slots, half), buf(bf16, slots, half),
+            buf(bf16, slots, rows), buf(bf16, z_slots, rows), buf(bf16, slots, rows), buf(bf16, slots, rows), buf(bf16, slots, rows),
+            buf(bf16, slots, rows), buf(bf16, slots, 2, half), buf(bf16, slots, 2, rest), buf(bf16, slots, rest), buf(bf16, slots, half),
+            sem(5, slots), sem(SLACK), sem(SLACK), *[sem(slots)] * 8,
+            sem(slots), sem(z_slots), *[sem(slots)] * 4, sem(count), pltpu.SemaphoreType.REGULAR,
         ],
         compiler_params=pltpu.CompilerParams(
             collective_id=5, has_side_effects=True, vmem_limit_bytes=60 * 1024 * 1024
@@ -1524,9 +1621,14 @@
         feed.backward(grad, branch, middle, hidden, result, outs, work, not forth)
 
 
-def feed_call(forth, back, ins, full, pick, mod, dtype):
+def feed_inputs(pick, mod, biases):
+    ones = jnp.concatenate([pick.astype(jnp.bfloat16)] * 3, axis=1)
+    return (ones, jnp.concatenate(thirds(mod), axis=0), *(part[None] for part in biases[1:]))
+
+
+def feed_call(forth, back, ins, full, given, dtype):
     qkv_w, qkv_b, out_w, out_b, up_w, up_b, down_w, down_b = full
-    size, latents = pick.shape
+    size, latents = given[0].shape[0], given[1].shape[0] // 3
     width, hidden = up_w.shape
     bf16, f32 = jnp.bfloat16, jnp.float32
     shape = lambda columns, dtype, rows=size: jax.ShapeDtypeStruct((rows, columns), dtype)
@@ -1552,15 +1654,12 @@
         out_specs=(VM,) * len(shapes),
         scratch_shapes=scratch,
         compiler_params=pltpu.CompilerParams(vmem_limit_bytes=60 * 1024 * 1024),
-    )(
-        jnp.concatenate([pick.astype(bf16)] * 3, axis=1), jnp.concatenate(thirds(mod), axis=0), out_w, up_w, down_w,
-        out_b[None], up_b[None], down_b[None], *ins,
-    )
-
-
-def layer_forward(stream, modulation, full, plan, in_first, shards_first, shards_second, shards_ahead, collective_id):
+    )(*given[:2], out_w, up_w, down_w, *given[2:], *ins)
+
+
+def layer_forward(stream, modulation, full, plan, in_first, shards_first, shards_second, shards_ahead, collective_id, beside):
     qkv_w, qkv_b, out_w, out_b, up_w, up_b, down_w, down_b = full
-    reps, edge, bounds, ids = plan
+    reps, edge = plan[:2]
     width = stream.shape[1]
     hd = width // reps
     nh = HEADS // reps
@@ -1572,6 +1671,8 @@
         [qkv_bias[:width], jnp.zeros((width,), jnp.float32), qkv_bias[width:]]
     )
     projected = (low_dot(normed, qkv_w) + bias_full).astype(jnp.bfloat16)
+    projected, plan, beside = lax.optimization_barrier((projected, plan[2:], beside))
+    bounds, ids = plan
     in_second = sent_ahead(shards_first, projected) if shards_first else []
     own, prev, after, fulls = to_heads(projected, reps, edge, pad_to(2 * hd, LANES), in_first, collective_id)
     first_gathered = fulls
@@ -1583,7 +1684,7 @@
     in_next = sent_ahead(shards_ahead, mixed) if shards_ahead else ()
     full = (qkv_w, qkv_b, out_w, out_b, up_w, up_b, down_w, down_b)
     saved = (normed, (prev, own, after), mixed, (mixed_t, log_norm))
-    return (saved, full, fulls, in_next)
+    return (saved, full, fulls, in_next, (reps, edge, bounds, ids), beside)
 
 
 def layer_backward(stream, modulation, full, saved, feed_grads, plan, beside):
@@ -1798,10 +1899,8 @@
         )
         partial_terms.append(term + spread[None, :])
     (mod_first, mod_second), biases, attention_weights = modulation(partial_terms, layers)
-    mod_tokens = tuple(
-        (mod, pick, jnp.dot(pick, mod[:, : 2 * tokens.shape[1]], precision=HIGH, preferred_element_type=jnp.float32))
-        for mod in (mod_first, mod_second)
-    )
+    mods = [mod_first, mod_second]
+    mod_tokens, feeds = [], []
     stream = tokens.astype(jnp.float32)
     inputs = []
     kept = []
@@ -1809,7 +1908,12 @@
     fulls = []
     in_first = sent_ahead((first_up_weight,), mod_first) if on_planes() else ()
     for layer_at, params in enumerate(layers):
+        if layer_at > 0:
+            stream, mods[layer_at] = lax.optimization_barrier((stream, mods[layer_at]))
         inputs.append(stream)
+        front = jnp.dot(pick, mods[layer_at][:, : 2 * tokens.shape[1]], precision=HIGH, preferred_element_type=jnp.float32)
+        mod_tokens.append((mods[layer_at], pick, front))
+        feed = feed_inputs(pick, mods[layer_at], biases[layer_at])
         ahead = layers[layer_at + 1] if layer_at + 1 < len(layers) else None
         qkv_w, out_w = attention_weights
         qkv_b, out_b, up_b, down_b = biases[layer_at]
@@ -1821,16 +1925,18 @@
         else:
             up_w, down_w = whole(params[6]), whole(params[8])
         full = (qkv_w, qkv_b, out_w, out_b, up_w, up_b, down_w, down_b)
-        saved, full, attention_weights, in_first = layer_forward(
-            stream, mod_tokens[layer_at], full, plan, in_first, shards_first, shards_second, shards_ahead, 7 + 2 * layer_at
+        saved, full, attention_weights, in_first, plan, feed = layer_forward(
+            stream, mod_tokens[layer_at], full, plan, in_first, shards_first, shards_second, shards_ahead, 7 + 2 * layer_at,
+            feed,
         )
+        feeds.append(feed)
         if layer_at == 0:
             *feed_saved, stream = feed_call(
-                True, False, (stream, saved[2]), full, pick, mod_tokens[0][0], jnp.float32
+                True, False, (stream, saved[2]), full, feeds[0], jnp.float32
             )
         else:
             normed_two, active, output, *feed_grads = feed_call(
-                True, True, (stream, saved[2], cotangent), full, pick, mod_tokens[1][0], jnp.bfloat16
+                True, True, (stream, saved[2], cotangent), full, feeds[1], jnp.bfloat16
             )
             feed_grads = [normed_two, active, *feed_grads]
         fulls.append(full)
@@ -1845,7 +1951,7 @@
         if layer_at == 0:
             branch, middle, normed_two, hidden, active, result = feed_saved
             feed_grads = feed_call(
-                False, True, (grad_stream, branch, middle, hidden, result), fulls[0], pick, mod_tokens[0][0], jnp.float32
+                False, True, (grad_stream, branch, middle, hidden, result), fulls[0], feeds[0], jnp.float32
             )
             feed_grads = [normed_two, active, *feed_grads]
         grad_stream, grad_mod, local_grads, local_biases, ready = layer_backward(

time: 1040 us -> 1010 us (0.971)
  Pallas kernels: 857 us -> 833 us
    pallas_call x2, Pallas kernels: 95.9 us -> 109 us  [to_heads(): pl.pallas_call(functools.partial(to_heads_kernel, reps, size, edge, kv, h...]
    pallas_call x4, Pallas kernels: 135 us -> 123 us  [swap(): pl.pallas_call(functools.partial(swap_kernel, reps, out, halves_of(shards...]
    ppermute x12, starting transfers between devices: 34.2 us -> 22.9 us  [sent_ahead(): lax.ppermute(shard, 'fsdp', [(at, at ^ step) for at in range(8)])]
  transfers between devices with their start and end apart: 15 -> 15, of which waited for: 2 -> 4; matrix products, arithmetic and copies ran while one was open for 5% -> 6% of each run, Pallas kernels for 26% -> 32%
where the time goes in v7:
time: 1010 us; the launch traced here: 1000 us
  Pallas kernels  833 us (82%)
  matrix products  50.2 us (5%)
  other arithmetic  32.7 us (3%)
  starting transfers between devices  30.6 us (3%)
  local copies, waits for them, and re-layouts  29.7 us (3%)
  between operations  15.4 us (2%)
  waiting for transfers between devices  11.2 us (1%)
    pallas_call x1, Pallas kernels, reduce_grads(): pl.pallas_call(functools.partial(reduce_kernel, width, half), out_shape=(...  241 us
    pallas_call x4, Pallas kernels, swap(): pl.pallas_call(functools.partial(swap_kernel, reps, out, halves_of(shards...  123 us
    pallas_call x2, Pallas kernels, to_heads(): pl.pallas_call(functools.partial(to_heads_kernel, reps, size, edge, kv, h...  109 us
    pallas_call x2, Pallas kernels, from_heads(): pl.pallas_call(functools.partial(from_heads_kernel, reps, size, edge), ou...  91.4 us
    pallas_call x3, Pallas kernels, feed_call(): pl.pallas_call(functools.partial(feed_kernel, forth, back), out_shape=sha...  77.1 us
    pallas_call x1, Pallas kernels, start(): pl.pallas_call(functools.partial(start_kernel, halves_of(shards)), out_sh...  66.1 us
    pallas_call x2, Pallas kernels, attend_back(): pl.pallas_call(functools.partial(attend_back_kernel, nh, hd), out_shape=(...  51.4 us
    pallas_call x1, Pallas kernels, chip_sums(): pl.pallas_call(functools.partial(chip_kernel, width, half), out_shape=tup...  38.9 us
  transfers between devices with their start and end apart: 15, of which 4 were waited for; matrix products, arithmetic and copies ran while one was open for 6% of the time, Pallas kernels for 32%

profile of v7, /device:TPU:0, one launch (start us, length us, event | category | flops | bytes accessed | tf_op | source)
XLA Modules:
  0.0 1002.8 jit_solution(11967719523881699422)
XLA Ops:
  16.4 66.1 %shard_map.407 = (f32[8,16,1152]{2,1,0:T(8,128)}, bf16[8,16,640]{2,1,0:T(8,128)(2,1)}, bf16[1152,3456]{1,0:T(8,128)(2,1)}, bf16[1152,1152]{1,0:T(8,128)(2,1)}) custom-call(f32[8,16,1152]{2,1,0:T(8,128)} %pad.39.part_in, bf16[16,640]{1,0:T(8,128)(2,1)} %pad.48.bias_in, bf16[144,3456]{1,0:T(8,128)(2,1)} %refs_0_.1, bf16[144,1152]{1,0:T(8,128)(2,1)} %refs_1_.1), custom_call_target="tpu_custom_call" | custom-call | tf_op jit(solution)/shard_map/pallas_call | solution.py:496
  91.1 2.5 fusion.19
  102.3 7.0 fusion.qkv
  109.9 2.2 broadcast_in_dim.19.kid
  117.6 53.8 %shard_map.408 = (bf16[4,256,896]{2,1,0:T(8,128)(2,1)}, bf16[1024,640]{1,0:T(8,128)(2,1)}, bf16[1024,640]{1,0:T(8,128)(2,1)}, bf16[1152,4608]{1,0:T(8,128)(2,1)}) custom-call(bf16[256,3456]{1,0:T(8,128)(2,1)} %fusion.qkv, bf16[144,4608]{1,0:T(8,128)(2,1)} %refs_0_.2, bf16[144,4608]{1,0:T(8,128)(2,1)} %collective-permute-done.refs_1_, ...), custom_call_target="tpu_custom_call" | custom-call | tf_op jit(solution)/shard_map/pallas_call | solution.py:619
  171.4 12.5 %collective-permute-start.5 = (bf16[144,3456]{1,0:T(8,128)(2,1)}, bf16[144,3456]{1,0:T(8,128)(2,1)}, u32[]{:S(2)}, u32[]{:S(2)}) collective-permute-start(bf16[144,3456]{1,0:T(8,128)(2,1)} %refs_3_), channel_id=1, source_target_pairs={{0,16},{4,20},{8,24},{12,28},{16,0},{20,4},{24,8},{28,12},{1,17},{... | collective-permute-start | bytes 2985992 | tf_op jit(solution)/shard_map/ppermute | solution.py:396
  192.0 17.4 %shard_map.409 = (bf16[1024,384]{1,0:T(8,128)(2,1)}, f32[384,1024]{1,0:T(8,128)}, f32[8,1024]{1,0:T(8,128)}) custom-call(s32[4]{0:T(128)} %get-tuple-element.162.lo, s32[4]{0:T(128)} %get-tuple-element.163.hi, bf16[1024,640]{1,0:T(8,128)(2,1)} %get-tuple-element.138.prev, bf16[1024,896]{1,0:T(8,128)(2,1)} %bitcast.69, ...), custom_call_target="tpu_custom_call" | custom-call | tf_op jit(solution)/shard_map/pallas_call | solution.py:144
  209.4 6.9 collective-permute-done.7.refs_8_
  217.2 45.1 %shard_map.410 = (bf16[256,1152]{1,0:T(8,128)(2,1)}, bf16[4608,1152]{1,0:T(8,128)(2,1)}, bf16[1152,3456]{1,0:T(8,128)(2,1)}, bf16[1152,1152]{1,0:T(8,128)(2,1)}) custom-call(bf16[4,256,384]{2,1,0:T(8,128)(2,1)} %bitcast.84, bf16[576,1152]{1,0:T(8,128)(2,1)} %refs_0_.3, bf16[576,1152]{1,0:T(8,128)(2,1)} %collective-permute-done.2.refs_1_, ...), custom_call_target="tpu_custom_call" | custom-call | tf_op jit(solution)/shard_map/pallas_call | solution.py:737
  263.9 20.1 %shard_map.411 = (f32[256,1152]{1,0:T(8,128)}, f32[256,1152]{1,0:T(8,128)}, bf16[256,1152]{1,0:T(8,128)(2,1)}, f32[256,4608]{1,0:T(8,128)}, bf16[256,4608]{1,0:T...) custom-call(bf16[256,48]{1,0:T(8,128)(2,1)} %copy.58.refs_0_, bf16[48,6912]{1,0:T(8,128)(2,1)} %pad_maximum_fusion.1.refs_1_, ...), custom_call_target="tpu_custom_call" | custom-call | tf_op jit(solution)/shard_map/pallas_call | solution.py:1650
  286.0 3.5 fusion.21
  293.1 7.1 fusion.1.qkv
  303.3 55.1 %shard_map.412 = (bf16[4,256,896]{2,1,0:T(8,128)(2,1)}, bf16[1024,640]{1,0:T(8,128)(2,1)}, bf16[1024,640]{1,0:T(8,128)(2,1)}, bf16[1152,4608]{1,0:T(8,128)(2,1)}) custom-call(bf16[256,3456]{1,0:T(8,128)(2,1)} %fusion.1.qkv, bf16[144,4608]{1,0:T(8,128)(2,1)} %refs_0_.4, bf16[144,4608]{1,0:T(8,128)(2,1)} %collective-permute-done.8.refs_1_, ...), custom_call_target="tpu_custom_call" | custom-call | tf_op jit(solution)/shard_map/pallas_call | solution.py:619
  358.5 17.3 %shard_map.413 = (bf16[1024,384]{1,0:T(8,128)(2,1)}, f32[384,1024]{1,0:T(8,128)}, f32[8,1024]{1,0:T(8,128)}) custom-call(s32[4]{0:T(128)} %get-tuple-element.162.lo, s32[4]{0:T(128)} %get-tuple-element.163.hi, bf16[1024,640]{1,0:T(8,128)(2,1)} %get-tuple-element.164.prev, bf16[1024,896]{1,0:T(8,128)(2,1)} %bitcast.71, ...), custom_call_target="tpu_custom_call" | custom-call | tf_op jit(solution)/shard_map/pallas_call | solution.py:144
  375.8 42.6 %shard_map.414 = (bf16[256,1152]{1,0:T(8,128)(2,1)}, bf16[4608,1152]{1,0:T(8,128)(2,1)}) custom-call(bf16[4,256,384]{2,1,0:T(8,128)(2,1)} %bitcast.85, bf16[576,1152]{1,0:T(8,128)(2,1)} %refs_0_.5, bf16[576,1152]{1,0:T(8,128)(2,1)} %collective-permute-done.10.refs_1_, bf16[576,1152]{1,0:T(8,128)(2,1)} %collective-permute-done.11.refs_2_), custom_call_target="tpu_custom_call" | custom-call | tf_op jit(solution)/shard_map/pallas_call | solution.py:737
  418.5 33.0 %shard_map.415 = (bf16[256,1152]{1,0:T(8,128)(2,1)}, bf16[256,4608]{1,0:T(8,128)(2,1)}, bf16[256,1152]{1,0:T(8,128)(2,1)}, bf16[256,1152]{1,0:T(8,128)(2,1)}, bf...) custom-call(bf16[256,48]{1,0:T(8,128)(2,1)} %copy.59.refs_0_, ...), custom_call_target="tpu_custom_call" | custom-call | tf_op jit(solution)/shard_map/pallas_call | solution.py:1650
  451.4 16.1 %shard_map.416 = bf16[4,256,384]{2,1,0:T(8,128)(2,1)} custom-call(bf16[256,1152]{1,0:T(8,128)(2,1)} %get-tuple-element.178.x_ref), custom_call_target="tpu_custom_call" | custom-call | tf_op jit(solution)/shard_map/pallas_call | solution.py:737
  467.6 25.7 %shard_map.417 = (bf16[1024,384]{1,0:T(8,128)(2,1)}, bf16[1024,640]{1,0:T(8,128)(2,1)}, bf16[1024,640]{1,0:T(8,128)(2,1)}, bf16[1024,640]{1,0:T(8,128)(2,1)}) custom-call(s32[4]{0:T(128)} %get-tuple-element.162.lo, s32[4]{0:T(128)} %get-tuple-element.163.hi, bf16[1024,640]{1,0:T(8,128)(2,1)} %get-tuple-element.164.prev, bf16[1024,896]{1,0:T(8,128)(2,1)} %bitcast.72, ...), custom_call_target="tpu_custom_call" | custom-call | tf_op jit(solution)/shard_map/pallas_call | solution.py:237
  493.3 45.2 %shard_map.418.refs_7_ = bf16[256,3456]{1,0:T(8,128)(2,1)} custom-call(bf16[1024,640]{1,0:T(8,128)(2,1)} %get-tuple-element.181.dprev, bf16[1024,640]{1,0:T(8,128)(2,1)} %get-tuple-element.182.own, bf16[1024,640]{1,0:T(8,128)(2,1)} %get-tuple-element.183.dafter, bf16[1024,384]{1,0:T(8,128)(2,1)} %get-tuple-element.184.dq), custom_call_target="tpu_custom_call" | custom-call | tf_op jit(solution)/shard_map/pallas_call | solution.py:893
  538.6 38.9 %shard_map.419 = (bf16[12,144,1152]{2,1,0:T(8,128)(2,1)}, bf16[12,2,80,1152]{3,2,1,0:T(8,128)(2,1)}, bf16[12,2,64,1152]{3,2,1,0:T(8,128)(2,1)}, bf16[12,64,1152]{2,1,0:T(8,128)(2,1)}, bf16[12,80,1152]{2,1,0:T(8,128)(2,1)}) custom-call(bf16[256,4608]{1,0:T(8,128)(2,1)} %get-tuple-element.185.refs_0_, bf16[256,1152]{1,0:T(8,128)(2,1)} %get-tuple-element.186.refs_1_, ...), custom_call_target="tpu_custom_call" | custom-call | flops 43486543872 | bytes 41943040 | tf_op jit(solution)/shard_map/pallas_call | solution.py:1060
  579.6 5.5 collective-permute-start.13
  587.6 6.9 multiply_reduce_fusion.1
  597.4 24.1 %shard_map.420 = (bf16[256,1152]{1,0:T(8,128)(2,1)}, bf16[256,4608]{1,0:T(8,128)(2,1)}, bf16[256,1152]{1,0:T(8,128)(2,1)}, bf16[256,1152]{1,0:T(8,128)(2,1)}, f3...) custom-call(bf16[256,48]{1,0:T(8,128)(2,1)} %copy.58.refs_0_, ...), custom_call_target="tpu_custom_call" | custom-call | tf_op jit(solution)/shard_map/pallas_call | solution.py:1650
  623.9 19.2 %shard_map.421 = bf16[4,256,384]{2,1,0:T(8,128)(2,1)} custom-call(bf16[256,1152]{1,0:T(8,128)(2,1)} %get-tuple-element.197.x_ref), custom_call_target="tpu_custom_call" | custom-call | tf_op jit(solution)/shard_map/pallas_call | solution.py:737
  643.1 25.7 %shard_map.422 = (bf16[1024,384]{1,0:T(8,128)(2,1)}, bf16[1024,640]{1,0:T(8,128)(2,1)}, bf16[1024,640]{1,0:T(8,128)(2,1)}, bf16[1024,640]{1,0:T(8,128)(2,1)}) custom-call(s32[4]{0:T(128)} %get-tuple-element.162.lo, s32[4]{0:T(128)} %get-tuple-element.163.hi, bf16[1024,640]{1,0:T(8,128)(2,1)} %get-tuple-element.138.prev, bf16[1024,896]{1,0:T(8,128)(2,1)} %bitcast.70, ...), custom_call_target="tpu_custom_call" | custom-call | tf_op jit(solution)/shard_map/pallas_call | solution.py:237
  668.8 46.2 %shard_map.423.refs_7_ = bf16[256,3456]{1,0:T(8,128)(2,1)} custom-call(bf16[1024,640]{1,0:T(8,128)(2,1)} %get-tuple-element.200.dprev, bf16[1024,640]{1,0:T(8,128)(2,1)} %get-tuple-element.201.own, bf16[1024,640]{1,0:T(8,128)(2,1)} %get-tuple-element.202.dafter, bf16[1024,384]{1,0:T(8,128)(2,1)} %get-tuple-element.203.dq), custom_call_target="tpu_custom_call" | custom-call | tf_op jit(solution)/shard_map/pallas_call | solution.py:893
  715.1 7.5 multiply_reduce_fusion
  729.9 241.3 %shard_map.424 = (bf16[2,144,9216]{2,1,0:T(8,128)(2,1)}, bf16[2,576,1152]{2,1,0:T(8,128)(2,1)}, bf16[32,1152]{1,0:T(8,128)(2,1)}, bf16[8,32,1152]{2,1,0:T(8,128)(2,1)}) custom-call(bf16[256,4608]{1,0:T(8,128)(2,1)} %get-tuple-element.209.refs_0_, bf16[256,1152]{1,0:T(8,128)(2,1)} %get-tuple-element.210.refs_1_, ...), custom_call_target="tpu_custom_call" | custom-call | flops 43486543872 | bytes 104857600 | tf_op jit(solution)/shard_map/pallas_call | solution.py:1393
  975.7 2.7 fusion.41
  981.8 3.1 bitcast_convert_fusion.1
  987.5 2.8 fusion.39
  991.6 2.7 bitcast_convert_fusion
  (258 shorter events, 81.2 us)
Async XLA Ops:
  7.2 276.8 %all-reduce.13.cloned.1.call-start = ((), (), s32[]{:S(2)}) async-start(), calls=%async_computation | async-start | bytes 884736 | tf_op jit(solution)/shard_map/psum | solution.py:1748
  16.4 69.5 %copy-start.45 = (s32[16]{0:T(128)S(1)}, s32[16]{0:T(128)}, u32[]{:S(2)}) copy-start(s32[16]{0:T(128)} %param.26) | copy-start | bytes 196
  83.7 32.3 %collective-permute-start.1 = (bf16[144,4608]{1,0:T(8,128)(2,1)}, bf16[144,4608]{1,0:T(8,128)(2,1)}, u32[]{:S(2)}, u32[]{:S(2)}) collective-permute-start(bf16[144,4608]{1,0:T(8,128)(2,1)} %refs_0_.2), channel_id=1, source_target_pairs={{0,16},{4,20},{8,24},{12,28},{16,0},{20,4},{24,8},{28,12},{1,17},{... | collective-permute-start | bytes 3981320 | tf_op jit(solution)/shard_map/ppermute | solution.py:396
  85.3 32.3 %collective-permute-start = (bf16[144,4608]{1,0:T(8,128)(2,1)}, bf16[144,4608]{1,0:T(8,128)(2,1)}, u32[]{:S(2)}, u32[]{:S(2)}) collective-permute-start(bf16[144,4608]{1,0:T(8,128)(2,1)} %refs_0_.2), channel_id=1, source_target_pairs={{0,8},{4,12},{8,0},{12,4},{16,24},{20,28},{24,16},{28,20},{1,9},{5... | collective-permute-start | bytes 3981320 | tf_op jit(solution)/shard_map/ppermute | solution.py:396
  93.8 7.5 copy-start.31
  94.1 7.1 copy-start.34
  101.3 8.1 copy-start.25
  112.1 71.8 %copy-start.44 = (bf16[864]{0:T(1024)(128)(2,1)S(1)}, bf16[864]{0:T(1024)(128)(2,1)}, u32[]{:S(2)}) copy-start(bf16[864]{0:T(1024)(128)(2,1)} %param.38) | copy-start | bytes 5188
  112.1 71.9 %copy-start.26 = (bf16[144,1152]{1,0:T(8,128)(2,1)S(1)}, bf16[144,1152]{1,0:T(8,128)(2,1)}, u32[]{:S(2)}) copy-start(bf16[144,1152]{1,0:T(8,128)(2,1)} %refs_6_) | copy-start | bytes 995332
  112.1 74.1 %copy-start.13 = (bf16[144,6912]{1,0:T(8,128)(2,1)S(1)}, bf16[144,6912]{1,0:T(8,128)(2,1)}, u32[]{:S(2)}) copy-start(bf16[144,6912]{1,0:T(8,128)(2,1)} %param.37) | copy-start | bytes 5971972
  112.1 72.9 %collective-permute-start.3 = (bf16[576,1152]{1,0:T(8,128)(2,1)}, bf16[576,1152]{1,0:T(8,128)(2,1)}, u32[]{:S(2)}, u32[]{:S(2)}) collective-permute-start(bf16[576,1152]{1,0:T(8,128)(2,1)} %refs_0_.3), channel_id=1, source_target_pairs={{0,16},{4,20},{8,24},{12,28},{16,0},{20,4},{24,8},{28,12},{1,17},{... | collective-permute-start | bytes 3981320 | tf_op jit(solution)/shard_map/ppermute | solution.py:396
  112.7 96.8 %collective-permute-start.2 = (bf16[576,1152]{1,0:T(8,128)(2,1)}, bf16[576,1152]{1,0:T(8,128)(2,1)}, u32[]{:S(2)}, u32[]{:S(2)}) collective-permute-start(bf16[576,1152]{1,0:T(8,128)(2,1)} %refs_0_.3), channel_id=1, source_target_pairs={{0,8},{4,12},{8,0},{12,4},{16,24},{20,28},{24,16},{28,20},{1,9},{5... | collective-permute-start | bytes 3981320 | tf_op jit(solution)/shard_map/ppermute | solution.py:396
  171.4 45.8 %collective-permute-start.5 = (bf16[144,3456]{1,0:T(8,128)(2,1)}, bf16[144,3456]{1,0:T(8,128)(2,1)}, u32[]{:S(2)}, u32[]{:S(2)}) collective-permute-start(bf16[144,3456]{1,0:T(8,128)(2,1)} %refs_3_), channel_id=1, source_target_pairs={{0,16},{4,20},{8,24},{12,28},{16,0},{20,4},{24,8},{28,12},{1,17},{... | collective-permute-start | bytes 2985992 | tf_op jit(solution)/shard_map/ppermute | solution.py:396
  183.9 33.2 %collective-permute-start.4 = (bf16[144,3456]{1,0:T(8,128)(2,1)}, bf16[144,3456]{1,0:T(8,128)(2,1)}, u32[]{:S(2)}, u32[]{:S(2)}) collective-permute-start(bf16[144,3456]{1,0:T(8,128)(2,1)} %refs_3_), channel_id=1, source_target_pairs={{0,8},{4,12},{8,0},{12,4},{16,24},{20,28},{24,16},{28,20},{1,9},{5... | collective-permute-start | bytes 2985992 | tf_op jit(solution)/shard_map/ppermute | solution.py:396
  184.1 32.3 %collective-permute-start.7 = (bf16[144,1152]{1,0:T(8,128)(2,1)S(1)}, bf16[144,1152]{1,0:T(8,128)(2,1)S(1)}, u32[]{:S(2)}, u32[]{:S(2)}) collective-permute-start(bf16[144,1152]{1,0:T(8,128)(2,1)S(1)} %copy-done.26), channel_id=1, source_target_pairs={{0,16},{4,20},{8,24},{12,28},{16,0},{20,4},{24,8},{28,12},{1,17},{... | collective-permute-start | bytes 995336 | tf_op jit(solution)/shard_map/ppermute | solution.py:396
  185.1 32.1 %collective-permute-start.6 = (bf16[144,1152]{1,0:T(8,128)(2,1)S(1)}, bf16[144,1152]{1,0:T(8,128)(2,1)}, u32[]{:S(2)}, u32[]{:S(2)}) collective-permute-start(bf16[144,1152]{1,0:T(8,128)(2,1)S(1)} %copy-done.26), channel_id=1, source_target_pairs={{0,8},{4,12},{8,0},{12,4},{16,24},{20,28},{24,16},{28,20},{1,9},{5... | collective-permute-start | bytes 995336 | tf_op jit(solution)/shard_map/ppermute | solution.py:396
  262.2 41.1 %collective-permute-start.9 = (bf16[144,4608]{1,0:T(8,128)(2,1)}, bf16[144,4608]{1,0:T(8,128)(2,1)}, u32[]{:S(2)}, u32[]{:S(2)}) collective-permute-start(bf16[144,4608]{1,0:T(8,128)(2,1)} %refs_0_.4), channel_id=1, source_target_pairs={{0,16},{4,20},{8,24},{12,28},{16,0},{20,4},{24,8},{28,12},{1,17},{... | collective-permute-start | bytes 3981320 | tf_op jit(solution)/shard_map/ppermute | solution.py:396
  263.0 40.3 %collective-permute-start.8 = (bf16[144,4608]{1,0:T(8,128)(2,1)}, bf16[144,4608]{1,0:T(8,128)(2,1)}, u32[]{:S(2)}, u32[]{:S(2)}) collective-permute-start(bf16[144,4608]{1,0:T(8,128)(2,1)} %refs_0_.4), channel_id=1, source_target_pairs={{0,8},{4,12},{8,0},{12,4},{16,24},{20,28},{24,16},{28,20},{1,9},{5... | collective-permute-start | bytes 3981320 | tf_op jit(solution)/shard_map/ppermute | solution.py:396
  292.0 8.2 copy-start.24
  293.1 7.1 copy-start.18
  300.2 75.6 %collective-permute-start.11 = (bf16[576,1152]{1,0:T(8,128)(2,1)S(1)}, bf16[576,1152]{1,0:T(8,128)(2,1)}, u32[]{:S(2)}, u32[]{:S(2)}) collective-permute-start(bf16[576,1152]{1,0:T(8,128)(2,1)S(1)} %copy-done.18), channel_id=1, source_target_pairs={{0,16},{4,20},{8,24},{12,28},{16,0},{20,4},{24,8},{28,12},{1,17},{... | collective-permute-start | bytes 3981320 | tf_op jit(solution)/shard_map/ppermute | solution.py:396
  301.0 74.8 %collective-permute-start.10 = (bf16[576,1152]{1,0:T(8,128)(2,1)S(1)}, bf16[576,1152]{1,0:T(8,128)(2,1)}, u32[]{:S(2)}, u32[]{:S(2)}) collective-permute-start(bf16[576,1152]{1,0:T(8,128)(2,1)S(1)} %copy-done.18), channel_id=1, source_target_pairs={{0,8},{4,12},{8,0},{12,4},{16,24},{20,28},{24,16},{28,20},{1,9},{5... | collective-permute-start | bytes 3981320 | tf_op jit(solution)/shard_map/ppermute | solution.py:396
  538.5 46.6 %copy-start.43 = (f32[1,1152]{1,0:T(1,128)S(1)}, f32[1,1152]{1,0:T(1,128)}, u32[]{:S(2)}) copy-start(f32[1,1152]{1,0:T(1,128)} %get-tuple-element.219) | copy-start | bytes 13828
  538.5 46.7 %copy-start.42 = (f32[1,1152]{1,0:T(1,128)S(1)}, f32[1,1152]{1,0:T(1,128)}, u32[]{:S(2)}) copy-start(f32[1,1152]{1,0:T(1,128)} %get-tuple-element.221) | copy-start | bytes 13828
  538.5 46.8 %copy-start.33 = (f32[1,4608]{1,0:T(1,128)S(1)}, f32[1,4608]{1,0:T(1,128)}, u32[]{:S(2)}) copy-start(f32[1,4608]{1,0:T(1,128)} %get-tuple-element.220) | copy-start | bytes 55300
  577.5 10.1 %copy-start.2 = (f32[256,1152]{1,0:T(8,128)S(1)}, f32[256,1152]{1,0:T(8,128)}, u32[]{:S(2)}) copy-start(f32[256,1152]{1,0:T(8,128)} %get-tuple-element.153.refs_8_) | copy-start | bytes 3538948
  577.5 137.5 %collective-permute-start.12 = (bf16[12,2,80,1152]{3,2,1,0:T(8,128)(2,1)}, bf16[12,2,80,1152]{3,2,1,0:T(8,128)(2,1)}, u32[]{:S(2)}, u32[]{:S(2)}) collective-permute-start(bf16[12,2,80,1152]{3,2,1,0:T(8,128)(2,1)} %get-tuple-element.204), channel_id=1, source_target_pairs={{0,8},{4,12},{8,0},{12,4},{16,24},{20,28},{24,16},{28,20},{1,9},{5... | collective-permute-start | bytes 13271048 | tf_op jit(solution)/shard_map/ppermute | solution.py:1758
  579.6 135.4 %collective-permute-start.13 = (bf16[12,2,64,1152]{3,2,1,0:T(8,128)(2,1)}, bf16[12,2,64,1152]{3,2,1,0:T(8,128)(2,1)}, u32[]{:S(2)}, u32[]{:S(2)}) collective-permute-start(bf16[12,2,64,1152]{3,2,1,0:T(8,128)(2,1)} %get-tuple-element.205), channel_id=1, source_target_pairs={{0,16},{4,20},{8,24},{12,28},{16,0},{20,4},{24,8},{28,12},{1,17},{... | collective-permute-start | bytes 10616840 | tf_op jit(solution)/shard_map/ppermute | solution.py:1758
  668.8 46.3 %copy-start.4 = (bf16[256,1152]{1,0:T(8,128)(2,1)S(1)}, bf16[256,1152]{1,0:T(8,128)(2,1)}, u32[]{:S(2)}) copy-start(bf16[256,1152]{1,0:T(8,128)(2,1)} %param.24) | copy-start | bytes 1769476
  668.8 46.3 %copy-start.7 = (f32[256,2304]{1,0:T(8,128)S(1)}, f32[256,2304]{1,0:T(8,128)}, u32[]{:S(2)}) copy-start(f32[256,2304]{1,0:T(8,128)} %fusion.19) | copy-start | bytes 7077892
  668.8 46.3 %copy-start.32 = (f32[256]{0:T(256)S(1)}, f32[256]{0:T(256)}, u32[]{:S(2)}) copy-start(f32[256]{0:T(256)} %copy-done.31) | copy-start | bytes 3076
  715.1 7.6 copy-start.15
  (29 other events, 81.8 us)
Sparse Core Ops, SparseCore 0:
  188.3 56.3 all-reduce.12

commit v8 on v7

--- a/solution.py
+++ b/solution.py
@@ -658,15 +658,21 @@
         return self.block(tail, -at * self.few).astype(jnp.bfloat16)
 
 
-def swap_kernel(reps, out, plan, x_ref, *refs):
+def swap_kernel(reps, out, plan, chip, x_ref, *refs):
     halves, sizes = plan
     count = len(halves)
     shards, refs = split_shards(refs, sizes)
-    y_ref, fulls, (held, tail_out, tail_in, opened, send, recv, done, *sems) = refs[0], refs[1 : count + 1], refs[count + 1 :]
+    have = sum(chip[2]) if chip else 0
+    chip_ins, refs = refs[:have], refs[have:]
+    y_ref, fulls, refs = refs[0], refs[1 : count + 1], refs[count + 1 :]
+    chip_outs, refs = (refs[:5], refs[5:]) if chip else ((), refs)
+    (held, tail_out, tail_in, opened, send, recv, done), sems = refs[:7], refs[7:]
     gather = Gather(shards, fulls, halves, *sems) if count else None
     group, me = lax.axis_index("fsdp"), lax.axis_index("replica")
     others = [(group, lax.rem(me + d, reps)) for d in range(1, reps)]
     planar = [(there, me) for there in (gather.core, gather.x, gather.y)] if count else []
+    if chip:
+        planar.append((group + 1 - 2 * lax.rem(group, 2), me))
     size, lanes = held.shape[1:]
     src, dst = (x_ref, held) if out else (held, y_ref)
     hd = (y_ref if out else x_ref).shape[1] // reps
@@ -695,6 +701,11 @@
         gather.onward(at)
     for at in range(count):
         gather.across(at)
+    if chip:
+        terms, run = chip_steps(*chip, (*chip_ins, *chip_outs, *sems))
+        terms.start()
+        terms.wait()
+        run((0, MATRICES + 3))
     for piece in range(reps):
         wait_for(dst.at[piece, :, span], recv.at[0, piece])
         wait_for(tail_in.at[piece], recv.at[1, piece])
@@ -723,7 +734,7 @@
         gather.end(at)
 
 
-def swap(x, reps, out, shards, collective_id):
+def swap(x, reps, out, shards, collective_id, pair=None):
     if out:
         size, lanes = x.shape[0] // reps, x.shape[1]
         x = x.reshape(reps, size, lanes)
@@ -734,26 +745,29 @@
     band = Tails(HEADS * HEAD_DIM // reps, size).band
     sems = pltpu.SemaphoreType.DMA((2, reps))
     tail = pltpu.VMEM((reps, band, LANES), x.dtype)
+    late = ((None, None, None, pair[0][3]), (None, None, None, pair[1][3])) if pair else None
+    chip, chip_ins, chip_shapes, chip_scratch = chip_parts(*late, EARLY, MATRICES) if pair else (None, (), (), [])
     swapped, *fulls = pl.pallas_call(
-        functools.partial(swap_kernel, reps, out, halves_of(shards)),
-        out_shape=(jax.ShapeDtypeStruct(shape, x.dtype), *gathered_shapes(shards)),
-        in_specs=[VM] + [HB] * sum(len(shard) for shard in shards),
-        out_specs=(VM if out else HB,) + (HB,) * len(shards),
+        functools.partial(swap_kernel, reps, out, halves_of(shards), chip),
+        out_shape=(jax.ShapeDtypeStruct(shape, x.dtype), *gathered_shapes(shards), *chip_shapes),
+        in_specs=[VM] + [HB] * (sum(len(shard) for shard in shards) + len(chip_ins)),
+        out_specs=(VM if out else HB,) + (HB,) * (len(shards) + len(chip_shapes)),
         scratch_shapes=[
             pltpu.VMEM((reps, size, lanes), x.dtype), tail, tail, pltpu.VMEM((reps, size, LANES), x.dtype), sems, sems,
-            pltpu.SemaphoreType.DMA((reps,)), *gather_scratch(shards),
+            pltpu.SemaphoreType.DMA((reps,)), *gather_scratch(shards), *chip_scratch,
         ],
         compiler_params=pltpu.CompilerParams(
             collective_id=collective_id, has_side_effects=True, vmem_limit_bytes=VMEM_LIMIT
         ),
-    )(x, *(part for shard in shards for part in shard))
+    )(x, *(part for shard in shards for part in shard), *chip_ins)
     return swapped, fulls
 
 
-def from_heads_kernel(
-    reps, size, edge, dprev, own, dafter, dq, out, out_kv, out_q, dq_tail, from_up, from_down, total, mine,
-    sends, recvs, send, recv, tail_sem,
-):
+def from_heads_kernel(reps, size, edge, chip, dprev, own, dafter, dq, *refs):
+    have = sum(chip[2]) if chip else 0
+    chip_ins, out, refs = refs[:have], refs[have], refs[have + 1 :]
+    chip_outs, refs = (refs[:5], refs[5:]) if chip else ((), refs)
+    (out_kv, out_q, dq_tail, from_up, from_down, total, mine, sends, recvs, send, recv, tail_sem), refs = refs[:12], refs[12:]
     group, me = lax.axis_index("fsdp"), lax.axis_index("replica")
     groups = lax.axis_size("fsdp")
     rows = reps * size
@@ -761,9 +775,13 @@
     others = [(group, lax.rem(me + d, reps)) for d in range(1, reps)]
     order = [lax.rem(me + d, reps) for d in range(1, reps + 1)]
     greet(
-        [(place, True) for place in others] + [((group - 1, me), down), ((group + 1, me), up)],
-        reps - 1 + down.astype(jnp.int32) + up.astype(jnp.int32),
+        [(place, True) for place in others] + [((group - 1, me), down), ((group + 1, me), up)]
+        + ([((group + 1 - 2 * lax.rem(group, 2), me), True)] if chip else []),
+        reps - 1 + down.astype(jnp.int32) + up.astype(jnp.int32) + (1 if chip else 0),
     )
+    terms, run = chip_steps(*chip, (*chip_ins, *chip_outs, *refs)) if chip else (None, lambda some: None)
+    if chip:
+        terms.start()
     edges = edge // size
     width = out.shape[1] // 3
     hd = width // reps
@@ -856,11 +874,15 @@
 
         over(narrow)
 
-    for piece in order[:-1]:
+    if chip:
+        terms.wait()
+    for at, piece in enumerate(order[:-1]):
+        run((2 * at, 2 * at + 2))
         sum_up(piece)
         sums_copy(piece).start()
     sum_up(me)
     pltpu.make_async_copy(mine.at[at_piece(me), :], out_kv.at[me], recv.at[1, me]).start()
+    run((2 * (reps - 1), MATRICES + 3))
 
     def unpack(section, sources):
         def body(rows):
@@ -886,15 +908,16 @@
         pl.when(jnp.logical_and(up, piece < edges))(lambda piece=piece: to_up(piece).wait_send())
 
 
-def from_heads(reps, width, dprev, own, dafter, dq, collective_id):
+def from_heads(reps, width, dprev, own, dafter, dq, collective_id, pair=None):
     rows, kv = own.shape
     edge, size = dprev.shape[0], own.shape[0] // reps
     both = pltpu.SemaphoreType.DMA((2, reps))
+    chip, chip_ins, chip_shapes, chip_scratch = chip_parts(*pair, 0, EARLY) if pair else (None, (), (), [])
     return pl.pallas_call(
-        functools.partial(from_heads_kernel, reps, size, edge),
-        out_shape=jax.ShapeDtypeStruct((size, 3 * width), own.dtype),
-        in_specs=[HB, VM, HB, HB],
-        out_specs=VM,
+        functools.partial(from_heads_kernel, reps, size, edge, chip),
+        out_shape=(jax.ShapeDtypeStruct((size, 3 * width), own.dtype), *chip_shapes),
+        in_specs=[HB, VM, HB, HB] + [HB] * len(chip_ins),
+        out_specs=(VM,) + (HB,) * len(chip_shapes),
         scratch_shapes=[
             pltpu.VMEM((reps, size, kv), own.dtype),
             pltpu.VMEM((reps, size, width // reps // LANES * LANES), own.dtype),
@@ -908,17 +931,20 @@
             both,
             both,
             pltpu.SemaphoreType.DMA,
+            *chip_scratch,
         ],
         compiler_params=pltpu.CompilerParams(
             collective_id=collective_id, has_side_effects=True, vmem_limit_bytes=VMEM_LIMIT
         ),
-    )(dprev, own, dafter, dq)
+    )(dprev, own, dafter, dq, *chip_ins)
 
 
 MATRICES = 12
 CHIP_WIDTH, UNIT_WIDTH = 1152, 384
 SLACK = 4
 LEFT_ROWS = 4
+LEFT_SIZES, RIGHT_SIZES = (4, 1, 1, 1), (1, 4, 1, 3)
+EARLY = 9
 PLACES = ((0, 0), (1, 0), (0, 1), (1, 1))
 
 
@@ -930,13 +956,16 @@
         f = lax.axis_index("fsdp")
         self.c, self.x, self.y = lax.rem(f, 2), lax.rem(f // 2, 2), f // 4
         self.core_at, self.x_at, self.y_at = f + 1 - 2 * self.c, f + 2 - 4 * self.x, f + 4 - 8 * self.y
-        self.loads, place, slot = [], 0, 0
-        for src in ins[:4]:
-            self.loads.append((src, flat.at[:, pl.ds(place, src.shape[1])]))
-            place += src.shape[1]
-        for src in ins[4:]:
-            for part in range(src.shape[1] // self.unit):
-                self.loads.append((src.at[:, pl.ds(part * self.unit, self.unit)], right.at[slot]))
+        self.loads, self.turns, place, slot = [], [], 0, 0
+        for src, size in zip(ins[:4], LEFT_SIZES):
+            if src is not None:
+                self.loads.append((src, flat.at[:, pl.ds(place, size * width)]))
+                self.turns.append((place // LANES, size * width // LANES))
+            place += size * width
+        for src, size in zip(ins[4:], RIGHT_SIZES):
+            for part in range(size * self.parts):
+                if src is not None:
+                    self.loads.append((src.at[:, pl.ds(part * self.unit, self.unit)], right.at[slot]))
                 slot += 1
         self.load_sem = load_sem
 
@@ -953,7 +982,8 @@
             self.left[here, :] = self.flat[:, here].T
             return carry
 
-        lax.fori_loop(0, self.left.shape[0] // LANES, turn, 0)
+        for first, count in self.turns:
+            lax.fori_loop(first, first + count, turn, 0)
 
     def block(self, core, mx, my):
         x, y = self.x + mx * (1 - 2 * self.x), self.y + my * (1 - 2 * self.y)
@@ -974,8 +1004,7 @@
         return nn_dot(jnp.concatenate(blocks, axis=0), self.right[other])
 
 
-def term_scratch(ins, unit):
-    tokens, width = ins[1].shape
+def term_scratch(tokens, width, unit):
     parts = width // unit
     return [
         pltpu.VMEM((tokens, (LEFT_ROWS + 3) * width), jnp.bfloat16),
@@ -991,16 +1020,15 @@
     )
 
 
-def chip_kernel(width, half, *refs):
-    ins, (own, xs, ys, tx, ty), refs = refs[:8], refs[8:13], refs[13:]
+def chip_steps(width, half, given, first, refs):
+    have = sum(given)
+    sides, (own, xs, ys, tx, ty), refs = iter(refs[:have]), refs[have : have + 5], refs[have + 5 :]
+    ins = [next(sides) if there else None for there in given]
     flat, left, right, load_sem, csend, crecv, own_b, xs_b, ys_b, tx_b, ty_b, core_s, core_r, out_sem = refs
     r = lax.axis_index("replica")
     count, rows = own.shape[:2]
     terms = Terms(ins, flat, left, right, rows, width, load_sem)
     where = (terms.core_at, r)
-    greet([(where, True)], 1)
-    terms.start()
-    terms.wait()
     bf16, f32 = jnp.bfloat16, jnp.float32
 
     def core_copy(u):
@@ -1020,7 +1048,7 @@
 
     def chip(u):
         pair, four = lax.rem(u, 2), lax.rem(u, 4)
-        stacked = terms.stack(u, 0)
+        stacked = terms.stack(first + u, 0)
         core_copy(u).wait()
         totals = [stacked[m * rows : (m + 1) * rows] + crecv[four, m].astype(f32) for m in range(4)]
         mine, along_x, along_y, opposite = [total.astype(bf16) for total in totals]
@@ -1036,7 +1064,7 @@
 
     def open_unit(u):
         pair = lax.rem(u, 2)
-        csend[pair] = terms.stack(u, 1).astype(bf16).reshape(csend.shape[1:])
+        csend[pair] = terms.stack(first + u, 1).astype(bf16).reshape(csend.shape[1:])
         core_copy(u).start()
 
     def step(t, carry):
@@ -1045,41 +1073,38 @@
         pl.when(jnp.logical_and(t >= 1, t <= count))(lambda: chip(t - 1))
         return carry
 
-    lax.fori_loop(0, count + 3, step, 0)
-
-
-def chip_sums(lefts, rights, collective_id):
+    def run(some):
+        lax.fori_loop(min(some[0], count + 3), min(some[1], count + 3), step, 0)
+
+    return terms, run
+
+
+def chip_parts(lefts, rights, first, last):
     ins = (*lefts, *rights)
-    tokens, width = lefts[1].shape
+    given = tuple(part is not None for part in ins)
+    width = next(part for part in rights if part is not None).shape[1] // RIGHT_SIZES[given[4:].index(True)]
+    tokens = next(part for part in ins if part is not None).shape[0]
     rows, unit = width // 8, CHIP_WIDTH
     half = pad_to(rows // 2, 16)
-    count = MATRICES * (width // unit)
+    count = last - first
     bf16 = jnp.bfloat16
     shapes = ((rows, unit), (2, half, unit), (2, rows - half, unit), (rows - half, unit), (half, unit))
-    pair = pltpu.SemaphoreType.DMA((2,))
-    return pl.pallas_call(
-        functools.partial(chip_kernel, width, half),
-        out_shape=tuple(jax.ShapeDtypeStruct((count, *shape), bf16) for shape in shapes),
-        in_specs=[HB] * 8,
-        out_specs=(HB,) * 5,
-        scratch_shapes=[
-            *term_scratch(ins, unit),
-            pltpu.VMEM((2, 4, rows, unit), bf16),
-            pltpu.VMEM((4, 4, rows, unit), bf16),
-            *(pltpu.VMEM((2, *shape), bf16) for shape in shapes),
-            pair,
-            pltpu.SemaphoreType.DMA((4,)),
-            pltpu.SemaphoreType.DMA((5, 2)),
-        ],
-        compiler_params=pltpu.CompilerParams(
-            collective_id=collective_id, has_side_effects=True, vmem_limit_bytes=VMEM_LIMIT
-        ),
-        cost_estimate=pl.CostEstimate(flops=2 * 64 * width * width * tokens, bytes_accessed=40 << 20, transcendentals=0),
-    )(*ins)
+    scratch = [
+        *term_scratch(tokens, width, unit),
+        pltpu.VMEM((2, 4, rows, unit), bf16),
+        pltpu.VMEM((4, 4, rows, unit), bf16),
+        *(pltpu.VMEM((2, *shape), bf16) for shape in shapes),
+        pltpu.SemaphoreType.DMA((2,)),
+        pltpu.SemaphoreType.DMA((4,)),
+        pltpu.SemaphoreType.DMA((5, 2)),
+    ]
+    ins = tuple(part for part in ins if part is not None)
+    return (width, half, given, first), ins, tuple(jax.ShapeDtypeStruct((count, *shape), bf16) for shape in shapes), scratch
 
 
 def reduce_kernel(width, half, *refs):
-    ins, (extra_in, own_in, xr_in, yr_in, tx_in, ty_in), (out, out_down, mine, shared), refs = refs[:8], refs[8:14], refs[14:18], refs[18:]
+    ins, extra_in, early, late, refs = refs[:8], refs[8], refs[9:14], refs[14:19], refs[19:]
+    (out, out_down, mine, shared), refs = refs[:4], refs[4:]
     (flat, left, right, load_sem, extra, extra_sem, cx_s, cx_r, cxs_sem, cxr_sem, share_s, share_r,
      csend, crecv, own, xs, xr, ys, yr, tx, ty, x2s, x2r, y2s, y2r, zs, z1r, z2s, z2r, fin,
      own_l, xr_l, yr_l, tx_l, ty_l, ready_sem,
@@ -1177,19 +1202,21 @@
             mine.at[:, columns(u)], shared.at[there, :, columns(u)], share_s.at[u, where], share_r.at[u, there], (where, r)
         )
 
-    def piece(src, w):
-        whole = src.shape[-1]
-        here = pl.ds(pl.multiple_of(lax.rem(w, whole // unit) * unit, LANES), unit)
-        at = w // (whole // unit)
-        return src.at[at, :, here] if len(src.shape) == 3 else src.at[at, :, :, here]
-
-    def ready_copies(u):
-        slot = lax.rem(u, slots)
-        buffers = ((own_in, own_l), (xr_in, xr_l), (yr_in, yr_l), (tx_in, tx_l), (ty_in, ty_l))
-        return [
-            pltpu.make_async_copy(piece(src, (u - extras) // 2), dst.at[slot], ready_sem.at[at, slot])
-            for at, (src, dst) in enumerate(buffers)
-        ]
+    def piece(src, m, part):
+        here = pl.ds(pl.multiple_of(part * unit, LANES), unit)
+        return src.at[m, :, here] if len(src.shape) == 3 else src.at[m, :, :, here]
+
+    def ready_copies(u, action):
+        slot, w = lax.rem(u, slots), (u - extras) // 2
+        parts = width // unit
+        m, part = w // parts, lax.rem(w, parts)
+
+        def over(sources, m):
+            for at, (src, dst) in enumerate(zip(sources, (own_l, xr_l, yr_l, tx_l, ty_l))):
+                action(pltpu.make_async_copy(piece(src, m, part), dst.at[slot], ready_sem.at[at, slot]))
+
+        pl.when(m < EARLY)(lambda: over(early, m))
+        pl.when(m >= EARLY)(lambda: over(late, m - EARLY))
 
     f32, bf16 = jnp.float32, jnp.bfloat16
 
@@ -1285,8 +1312,7 @@
 
     def cross_ready(u):
         slot, at = lax.rem(u, slots), lax.rem(u, own.shape[0])
-        for copy in ready_copies(u):
-            copy.wait()
+        ready_copies(u, lambda copy: copy.wait())
         y2s[slot] = (ty_l[slot].astype(f32) + xr_l[slot, 1].astype(f32)).astype(bf16)
         y2_copy(slot).start()
         x2s[slot] = (tx_l[slot].astype(f32) + yr_l[slot, 1].astype(f32)).astype(bf16)
@@ -1333,8 +1359,7 @@
         extra_copy(u).start()
 
     def open_ready(u):
-        for copy in ready_copies(u):
-            copy.start()
+        ready_copies(u, lambda copy: copy.start())
 
     def open_unit(u):
         w = (u - extras) // 2
@@ -1398,10 +1423,10 @@
             jax.ShapeDtypeStruct((few, width), bf16),
             jax.ShapeDtypeStruct(extra.shape, bf16),
         ),
-        in_specs=[HB] * 14,
+        in_specs=[HB] * 19,
         out_specs=(HB, HB, HB, HB),
         scratch_shapes=[
-            *term_scratch(ins, unit),
+            *term_scratch(tokens, width, unit),
             buf(f32, extras, 8, few), sem(extras), buf(bf16, extras, 4, few), buf(bf16, extras, 4, few),
             sem(extras), sem(extras), sem(extras, 8), sem(extras, 8),
             buf(bf16, SLACK, 4, rows), buf(bf16, SLACK, 4, rows), buf(f32, 3 * SLACK + 1, rows),
@@ -1687,7 +1712,7 @@
     return (saved, full, fulls, in_next, (reps, edge, bounds, ids), beside)
 
 
-def layer_backward(stream, modulation, full, saved, feed_grads, plan, beside):
+def layer_backward(stream, modulation, full, saved, feed_grads, plan, pair, last, hops):
     qkv_w = full[0]
     normed, window, mixed, kept = saved
     normed_two, active, grad_result, grad_hidden, grad_branch, grad_mixed, grad_middle, grad_mod, *bias_sums = feed_grads
@@ -1697,13 +1722,20 @@
     nh = HEADS // reps
     mod, pick, front = modulation
     shift_one, scale_one = jnp.split(front, 2, axis=1)
-    grad_heads, _ = swap(grad_mixed, reps, False, (), 3)
+    grad_heads, sums = swap(grad_mixed, reps, False, (), 13 if pair else 3, pair)
+    beside = first_hop(*sums) if pair else ()
+    grad_heads, hops = lax.optimization_barrier((grad_heads, hops))
     prev, own, after = window
     grad_q, grad_prev, grad_own, grad_after = attend_back(
         nh, hd, *bounds, prev, own, after, *ids, grad_heads.reshape(own.shape[0], -1), *kept
     )
-    grad_projected = from_heads(reps, width, grad_prev, grad_own, grad_after, grad_q, 4)
-    grad_projected, beside = lax.optimization_barrier((grad_projected, beside))
+    early = ((active, normed_two, mixed, None), (grad_result, grad_hidden, grad_branch, None)) if last else None
+    grad_projected, *early = from_heads(
+        reps, width, grad_prev, grad_own, grad_after, grad_q, 14 if last else 4, early
+    )
+    beside = first_hop(*early) if last else beside
+    if not last:
+        grad_projected, beside = lax.optimization_barrier((grad_projected, beside))
     sums = jnp.sum(grad_projected.astype(jnp.float32), axis=0)
     grad_qkv_b = jnp.concatenate([sums[:width], sums[2 * width :]])
     grad_normed = jnp.einsum("te,de->td", grad_projected, qkv_w, preferred_element_type=jnp.float32)
@@ -1720,7 +1752,7 @@
     return (
         grad_stream, grad_mod,
         ((active, normed_two, mixed, normed), (grad_result, grad_hidden, grad_branch, grad_projected)),
-        (grad_qkv_b, *(part[0] for part in bias_sums)), beside,
+        (grad_qkv_b, *(part[0] for part in bias_sums)), (*hops, *beside),
     )
 
 
@@ -1753,10 +1785,9 @@
     return lax.axis_size("fsdp") == 8 and lax.axis_size("replica") == 4
 
 
-def first_hop(lefts, rights):
-    own, xs, ys, tx, ty = chip_sums(lefts, rights, 11)
+def first_hop(own, xs, ys, tx, ty):
     hop = lambda value, step: lax.ppermute(value, "fsdp", [(at, at ^ step) for at in range(8)])
-    return (own, hop(xs, 2), hop(ys, 4), tx, ty), own
+    return (own, hop(xs, 2), hop(ys, 4), tx, ty)
 
 
 def owner_sums(pairs, ready, grad_mods, grad_biases):
@@ -1955,12 +1986,10 @@
             )
             feed_grads = [normed_two, active, *feed_grads]
         grad_stream, grad_mod, local_grads, local_biases, ready = layer_backward(
-            inputs[layer_at], mod_tokens[layer_at], fulls[layer_at], kept[layer_at], feed_grads, plan, ready
+            inputs[layer_at], mod_tokens[layer_at], fulls[layer_at], kept[layer_at], feed_grads, plan,
+            weight_pairs[1] if layer_at == 0 and on_planes() else None, layer_at == 1 and on_planes(), ready,
         )
         weight_pairs[layer_at] = local_grads
-        if layer_at == 1 and on_planes():
-            ready, own = first_hop(*local_grads)
-            grad_stream, _ = lax.optimization_barrier((grad_stream, own))
         mod_grads[layer_at] = grad_mod
         bias_grads[layer_at] = local_biases
     sums, (grad_mod_first, grad_mod_second) = owner_sums(weight_pairs, ready, mod_grads, bias_grads)

time: 1010 us -> 991 us (0.981)
  Pallas kernels: 833 us -> 798 us
  waiting for transfers between devices: 11.2 us -> 25.3 us
    pallas_call x3 -> x2, Pallas kernels: 130 us -> 97.9 us  [from_heads(): pl.pallas_call(functools.partial(from_heads_kernel, reps, size, edge, chi...]
    ppermute x2 -> x4, waiting for transfers between devices: 0.01 us -> 14 us  [first_hop(): lax.ppermute(value, 'fsdp', [(at, at ^ step) for at in range(8)])]
  transfers between devices with their start and end apart: 15 -> 17, of which waited for: 4 -> 5; matrix products, arithmetic and copies ran while one was open for 6% -> 6% of each run, Pallas kernels for 32% -> 34%
where the time goes in v8:
time: 991 us; the launch traced here: 974 us
  Pallas kernels  798 us (81%)
  matrix products  49.2 us (5%)
  other arithmetic  30.6 us (3%)
  local copies, waits for them, and re-layouts  29.6 us (3%)
  starting transfers between devices  26.2 us (3%)
  waiting for transfers between devices  25.3 us (3%)
  between operations  15.4 us (2%)
    pallas_call x1, Pallas kernels, reduce_grads(): pl.pallas_call(functools.partial(reduce_kernel, width, half), out_shape=(...  239 us
    pallas_call x4, Pallas kernels, swap(): pl.pallas_call(functools.partial(swap_kernel, reps, out, halves_of(shards...  122 us
    pallas_call x2, Pallas kernels, to_heads(): pl.pallas_call(functools.partial(to_heads_kernel, reps, size, edge, kv, h...  109 us
    pallas_call x2, Pallas kernels, from_heads(): pl.pallas_call(functools.partial(from_heads_kernel, reps, size, edge, chi...  97.9 us
    pallas_call x3, Pallas kernels, feed_call(): pl.pallas_call(functools.partial(feed_kernel, forth, back), out_shape=sha...  77 us
    pallas_call x1, Pallas kernels, start(): pl.pallas_call(functools.partial(start_kernel, halves_of(shards)), out_sh...  66.1 us
    pallas_call x2, Pallas kernels, attend_back(): pl.pallas_call(functools.partial(attend_back_kernel, nh, hd), out_shape=(...  51.2 us
    pallas_call x2, Pallas kernels, attend(): pl.pallas_call(functools.partial(attend_kernel, nh, hd), out_shape=(jax.S...  35.9 us
  transfers between devices with their start and end apart: 17, of which 5 were waited for; matrix products, arithmetic and copies ran while one was open for 6% of the time, Pallas kernels for 34%

profile of v8, /device:TPU:0, one launch (start us, length us, event | category | flops | bytes accessed | tf_op | source)
XLA Modules:
  0.0 974.3 jit_solution(13306596350833459625)
XLA Ops:
  16.4 66.1 %shard_map.407 = (f32[8,16,1152]{2,1,0:T(8,128)}, bf16[8,16,640]{2,1,0:T(8,128)(2,1)}, bf16[1152,3456]{1,0:T(8,128)(2,1)}, bf16[1152,1152]{1,0:T(8,128)(2,1)}) custom-call(f32[8,16,1152]{2,1,0:T(8,128)} %pad.39.part_in, bf16[16,640]{1,0:T(8,128)(2,1)} %pad.48.bias_in, bf16[144,3456]{1,0:T(8,128)(2,1)} %refs_0_.1, bf16[144,1152]{1,0:T(8,128)(2,1)} %refs_1_.1), custom_call_target="tpu_custom_call" | custom-call | tf_op jit(solution)/shard_map/pallas_call | solution.py:496
  91.1 2.5 fusion.19
  102.3 7.0 fusion.qkv
  109.9 2.2 broadcast_in_dim.19.kid
  117.6 53.8 %shard_map.408 = (bf16[4,256,896]{2,1,0:T(8,128)(2,1)}, bf16[1024,640]{1,0:T(8,128)(2,1)}, bf16[1024,640]{1,0:T(8,128)(2,1)}, bf16[1152,4608]{1,0:T(8,128)(2,1)}) custom-call(bf16[256,3456]{1,0:T(8,128)(2,1)} %fusion.qkv, bf16[144,4608]{1,0:T(8,128)(2,1)} %refs_0_.2, bf16[144,4608]{1,0:T(8,128)(2,1)} %collective-permute-done.refs_1_, ...), custom_call_target="tpu_custom_call" | custom-call | tf_op jit(solution)/shard_map/pallas_call | solution.py:619
  171.4 12.5 %collective-permute-start.5 = (bf16[144,3456]{1,0:T(8,128)(2,1)}, bf16[144,3456]{1,0:T(8,128)(2,1)}, u32[]{:S(2)}, u32[]{:S(2)}) collective-permute-start(bf16[144,3456]{1,0:T(8,128)(2,1)} %refs_3_), channel_id=1, source_target_pairs={{0,16},{4,20},{8,24},{12,28},{16,0},{20,4},{24,8},{28,12},{1,17},{... | collective-permute-start | bytes 2985992 | tf_op jit(solution)/shard_map/ppermute | solution.py:396
  191.3 18.0 %shard_map.409 = (bf16[1024,384]{1,0:T(8,128)(2,1)}, f32[384,1024]{1,0:T(8,128)}, f32[8,1024]{1,0:T(8,128)}) custom-call(s32[4]{0:T(128)} %get-tuple-element.174.lo, s32[4]{0:T(128)} %get-tuple-element.175.hi, bf16[1024,640]{1,0:T(8,128)(2,1)} %get-tuple-element.150.prev, bf16[1024,896]{1,0:T(8,128)(2,1)} %bitcast.69, ...), custom_call_target="tpu_custom_call" | custom-call | tf_op jit(solution)/shard_map/pallas_call | solution.py:144
  209.3 7.1 collective-permute-done.7.refs_8_
  217.2 45.1 %shard_map.410 = (bf16[256,1152]{1,0:T(8,128)(2,1)}, bf16[4608,1152]{1,0:T(8,128)(2,1)}, bf16[1152,3456]{1,0:T(8,128)(2,1)}, bf16[1152,1152]{1,0:T(8,128)(2,1)}) custom-call(bf16[4,256,384]{2,1,0:T(8,128)(2,1)} %bitcast.84, bf16[576,1152]{1,0:T(8,128)(2,1)} %refs_0_.3, bf16[576,1152]{1,0:T(8,128)(2,1)} %collective-permute-done.2.refs_1_, ...), custom_call_target="tpu_custom_call" | custom-call | tf_op jit(solution)/shard_map/pallas_call | solution.py:750
  264.0 20.1 %shard_map.411 = (f32[256,1152]{1,0:T(8,128)}, f32[256,1152]{1,0:T(8,128)}, bf16[256,1152]{1,0:T(8,128)(2,1)}, f32[256,4608]{1,0:T(8,128)}, bf16[256,4608]{1,0:T...) custom-call(bf16[256,48]{1,0:T(8,128)(2,1)} %copy.58.refs_0_, bf16[48,6912]{1,0:T(8,128)(2,1)} %pad_maximum_fusion.1.refs_1_, ...), custom_call_target="tpu_custom_call" | custom-call | tf_op jit(solution)/shard_map/pallas_call | solution.py:1675
  286.1 3.5 fusion.21
  293.1 7.1 fusion.1.qkv
  303.3 55.2 %shard_map.412 = (bf16[4,256,896]{2,1,0:T(8,128)(2,1)}, bf16[1024,640]{1,0:T(8,128)(2,1)}, bf16[1024,640]{1,0:T(8,128)(2,1)}, bf16[1152,4608]{1,0:T(8,128)(2,1)}) custom-call(bf16[256,3456]{1,0:T(8,128)(2,1)} %fusion.1.qkv, bf16[144,4608]{1,0:T(8,128)(2,1)} %refs_0_.4, bf16[144,4608]{1,0:T(8,128)(2,1)} %collective-permute-done.8.refs_1_, ...), custom_call_target="tpu_custom_call" | custom-call | tf_op jit(solution)/shard_map/pallas_call | solution.py:619
  358.6 17.9 %shard_map.413 = (bf16[1024,384]{1,0:T(8,128)(2,1)}, f32[384,1024]{1,0:T(8,128)}, f32[8,1024]{1,0:T(8,128)}) custom-call(s32[4]{0:T(128)} %get-tuple-element.174.lo, s32[4]{0:T(128)} %get-tuple-element.175.hi, bf16[1024,640]{1,0:T(8,128)(2,1)} %get-tuple-element.176.prev, bf16[1024,896]{1,0:T(8,128)(2,1)} %bitcast.71, ...), custom_call_target="tpu_custom_call" | custom-call | tf_op jit(solution)/shard_map/pallas_call | solution.py:144
  376.5 38.2 %shard_map.414 = (bf16[256,1152]{1,0:T(8,128)(2,1)}, bf16[4608,1152]{1,0:T(8,128)(2,1)}) custom-call(bf16[4,256,384]{2,1,0:T(8,128)(2,1)} %bitcast.85, bf16[576,1152]{1,0:T(8,128)(2,1)} %refs_0_.5, bf16[576,1152]{1,0:T(8,128)(2,1)} %collective-permute-done.10.refs_1_, bf16[576,1152]{1,0:T(8,128)(2,1)} %collective-permute-done.11.refs_2_), custom_call_target="tpu_custom_call" | custom-call | tf_op jit(solution)/shard_map/pallas_call | solution.py:750
  414.7 33.0 %shard_map.415 = (bf16[256,1152]{1,0:T(8,128)(2,1)}, bf16[256,4608]{1,0:T(8,128)(2,1)}, bf16[256,1152]{1,0:T(8,128)(2,1)}, bf16[256,1152]{1,0:T(8,128)(2,1)}, bf...) custom-call(bf16[256,48]{1,0:T(8,128)(2,1)} %copy.59.refs_0_, ...), custom_call_target="tpu_custom_call" | custom-call | tf_op jit(solution)/shard_map/pallas_call | solution.py:1675
  447.7 16.3 %shard_map.416 = bf16[4,256,384]{2,1,0:T(8,128)(2,1)} custom-call(bf16[256,1152]{1,0:T(8,128)(2,1)} %get-tuple-element.190.x_ref), custom_call_target="tpu_custom_call" | custom-call | tf_op jit(solution)/shard_map/pallas_call | solution.py:750
  464.0 25.6 %shard_map.417 = (bf16[1024,384]{1,0:T(8,128)(2,1)}, bf16[1024,640]{1,0:T(8,128)(2,1)}, bf16[1024,640]{1,0:T(8,128)(2,1)}, bf16[1024,640]{1,0:T(8,128)(2,1)}) custom-call(s32[4]{0:T(128)} %get-tuple-element.174.lo, s32[4]{0:T(128)} %get-tuple-element.175.hi, bf16[1024,640]{1,0:T(8,128)(2,1)} %get-tuple-element.176.prev, bf16[1024,896]{1,0:T(8,128)(2,1)} %bitcast.72, ...), custom_call_target="tpu_custom_call" | custom-call | tf_op jit(solution)/shard_map/pallas_call | solution.py:237
  489.6 51.6 %shard_map.418 = (bf16[256,3456]{1,0:T(8,128)(2,1)}, bf16[9,144,1152]{2,1,0:T(8,128)(2,1)}, bf16[9,2,80,1152]{3,2,1,0:T(8,128)(2,1)}, bf16[9,2,64,1152]{3,2,1,0:...) custom-call(bf16[1024,640]{1,0:T(8,128)(2,1)} %get-tuple-element.193.dprev, ...), custom_call_target="tpu_custom_call" | custom-call | tf_op jit(solution)/shard_map/pallas_call | solution.py:916
  544.1 6.5 multiply_reduce_fusion.1
  553.6 24.0 %shard_map.419 = (bf16[256,1152]{1,0:T(8,128)(2,1)}, bf16[256,4608]{1,0:T(8,128)(2,1)}, bf16[256,1152]{1,0:T(8,128)(2,1)}, bf16[256,1152]{1,0:T(8,128)(2,1)}, f3...) custom-call(bf16[256,48]{1,0:T(8,128)(2,1)} %copy.58.refs_0_, ...), custom_call_target="tpu_custom_call" | custom-call | tf_op jit(solution)/shard_map/pallas_call | solution.py:1675
  577.6 22.5 %shard_map.420 = (bf16[4,256,384]{2,1,0:T(8,128)(2,1)}, bf16[3,144,1152]{2,1,0:T(8,128)(2,1)}, bf16[3,2,80,1152]{3,2,1,0:T(8,128)(2,1)}, bf16[3,2,64,1152]{3,2,1...) custom-call(bf16[256,1152]{1,0:T(8,128)(2,1)} %get-tuple-element.208.x_ref, ...), custom_call_target="tpu_custom_call" | custom-call | tf_op jit(solution)/shard_map/pallas_call | solution.py:750
  603.2 14.0 %collective-permute-done.12.refs_10_ = bf16[9,2,80,1152]{3,2,1,0:T(8,128)(2,1)} collective-permute-done((bf16[9,2,80,1152]{3,2,1,0:T(8,128)(2,1)}, bf16[9,2,80,1152]{3,2,1,0:T(8,128)(2,1)}, u32[]{:S(2)}, u32[]{:S(2)}) %collective-permute-start.12) | collective-permute-done | bytes 3317792 | tf_op jit(solution)/shard_map/ppermute | solution.py:1789
  617.2 25.7 %shard_map.421 = (bf16[1024,384]{1,0:T(8,128)(2,1)}, bf16[1024,640]{1,0:T(8,128)(2,1)}, bf16[1024,640]{1,0:T(8,128)(2,1)}, bf16[1024,640]{1,0:T(8,128)(2,1)}) custom-call(s32[4]{0:T(128)} %get-tuple-element.174.lo, s32[4]{0:T(128)} %get-tuple-element.175.hi, bf16[1024,640]{1,0:T(8,128)(2,1)} %get-tuple-element.150.prev, bf16[1024,896]{1,0:T(8,128)(2,1)} %bitcast.70, ...), custom_call_target="tpu_custom_call" | custom-call | tf_op jit(solution)/shard_map/pallas_call | solution.py:237
  642.9 46.4 %shard_map.422.refs_7_ = bf16[256,3456]{1,0:T(8,128)(2,1)} custom-call(bf16[1024,640]{1,0:T(8,128)(2,1)} %get-tuple-element.218.dprev, bf16[1024,640]{1,0:T(8,128)(2,1)} %get-tuple-element.219.own, bf16[1024,640]{1,0:T(8,128)(2,1)} %get-tuple-element.220.dafter, bf16[1024,384]{1,0:T(8,128)(2,1)} %get-tuple-element.221.dq), custom_call_target="tpu_custom_call" | custom-call | tf_op jit(solution)/shard_map/pallas_call | solution.py:916
  689.3 7.5 multiply_reduce_fusion
  704.1 238.7 %shard_map.423 = (bf16[2,144,9216]{2,1,0:T(8,128)(2,1)}, bf16[2,576,1152]{2,1,0:T(8,128)(2,1)}, bf16[32,1152]{1,0:T(8,128)(2,1)}, bf16[8,32,1152]{2,1,0:T(8,128)(2,1)}) custom-call(bf16[256,4608]{1,0:T(8,128)(2,1)} %get-tuple-element.228.refs_0_, bf16[256,1152]{1,0:T(8,128)(2,1)} %get-tuple-element.229.refs_1_, ...), custom_call_target="tpu_custom_call" | custom-call | flops 43486543872 | bytes 104857600 | tf_op jit(solution)/shard_map/pallas_call | solution.py:1418
  947.1 2.8 fusion.41
  951.1 2.2 bitcast_convert_fusion.4
  953.3 3.1 bitcast_convert_fusion.1
  959.0 2.8 fusion.39
  963.1 2.7 bitcast_convert_fusion
  (267 shorter events, 77.2 us)
Async XLA Ops:
  7.2 276.9 %all-reduce.13.cloned.1.call-start = ((), (), s32[]{:S(2)}) async-start(), calls=%async_computation | async-start | bytes 884736 | tf_op jit(solution)/shard_map/psum | solution.py:1780
  16.4 69.5 %copy-start.48 = (s32[16]{0:T(128)S(1)}, s32[16]{0:T(128)}, u32[]{:S(2)}) copy-start(s32[16]{0:T(128)} %param.26) | copy-start | bytes 196
  83.7 32.3 %collective-permute-start.1 = (bf16[144,4608]{1,0:T(8,128)(2,1)}, bf16[144,4608]{1,0:T(8,128)(2,1)}, u32[]{:S(2)}, u32[]{:S(2)}) collective-permute-start(bf16[144,4608]{1,0:T(8,128)(2,1)} %refs_0_.2), channel_id=1, source_target_pairs={{0,16},{4,20},{8,24},{12,28},{16,0},{20,4},{24,8},{28,12},{1,17},{... | collective-permute-start | bytes 3981320 | tf_op jit(solution)/shard_map/ppermute | solution.py:396
  85.3 32.3 %collective-permute-start = (bf16[144,4608]{1,0:T(8,128)(2,1)}, bf16[144,4608]{1,0:T(8,128)(2,1)}, u32[]{:S(2)}, u32[]{:S(2)}) collective-permute-start(bf16[144,4608]{1,0:T(8,128)(2,1)} %refs_0_.2), channel_id=1, source_target_pairs={{0,8},{4,12},{8,0},{12,4},{16,24},{20,28},{24,16},{28,20},{1,9},{5... | collective-permute-start | bytes 3981320 | tf_op jit(solution)/shard_map/ppermute | solution.py:396
  112.1 71.8 %copy-start.47 = (bf16[864]{0:T(1024)(128)(2,1)S(1)}, bf16[864]{0:T(1024)(128)(2,1)}, u32[]{:S(2)}) copy-start(bf16[864]{0:T(1024)(128)(2,1)} %param.38) | copy-start | bytes 5188
  112.1 71.9 %copy-start.26 = (bf16[144,1152]{1,0:T(8,128)(2,1)S(1)}, bf16[144,1152]{1,0:T(8,128)(2,1)}, u32[]{:S(2)}) copy-start(bf16[144,1152]{1,0:T(8,128)(2,1)} %refs_6_) | copy-start | bytes 995332
  112.1 74.1 %copy-start.13 = (bf16[144,6912]{1,0:T(8,128)(2,1)S(1)}, bf16[144,6912]{1,0:T(8,128)(2,1)}, u32[]{:S(2)}) copy-start(bf16[144,6912]{1,0:T(8,128)(2,1)} %param.37) | copy-start | bytes 5971972
  112.1 74.1 %copy-start.30 = (bf16[16,1152]{1,0:T(8,128)(2,1)S(1)}, bf16[16,1152]{1,0:T(8,128)(2,1)}, u32[]{:S(2)}) copy-start(bf16[16,1152]{1,0:T(8,128)(2,1)} %param.25) | copy-start | bytes 110596
  112.1 72.9 %collective-permute-start.3 = (bf16[576,1152]{1,0:T(8,128)(2,1)}, bf16[576,1152]{1,0:T(8,128)(2,1)}, u32[]{:S(2)}, u32[]{:S(2)}) collective-permute-start(bf16[576,1152]{1,0:T(8,128)(2,1)} %refs_0_.3), channel_id=1, source_target_pairs={{0,16},{4,20},{8,24},{12,28},{16,0},{20,4},{24,8},{28,12},{1,17},{... | collective-permute-start | bytes 3981320 | tf_op jit(solution)/shard_map/ppermute | solution.py:396
  112.7 96.6 %collective-permute-start.2 = (bf16[576,1152]{1,0:T(8,128)(2,1)}, bf16[576,1152]{1,0:T(8,128)(2,1)}, u32[]{:S(2)}, u32[]{:S(2)}) collective-permute-start(bf16[576,1152]{1,0:T(8,128)(2,1)} %refs_0_.3), channel_id=1, source_target_pairs={{0,8},{4,12},{8,0},{12,4},{16,24},{20,28},{24,16},{28,20},{1,9},{5... | collective-permute-start | bytes 3981320 | tf_op jit(solution)/shard_map/ppermute | solution.py:396
  171.4 45.8 %collective-permute-start.5 = (bf16[144,3456]{1,0:T(8,128)(2,1)}, bf16[144,3456]{1,0:T(8,128)(2,1)}, u32[]{:S(2)}, u32[]{:S(2)}) collective-permute-start(bf16[144,3456]{1,0:T(8,128)(2,1)} %refs_3_), channel_id=1, source_target_pairs={{0,16},{4,20},{8,24},{12,28},{16,0},{20,4},{24,8},{28,12},{1,17},{... | collective-permute-start | bytes 2985992 | tf_op jit(solution)/shard_map/ppermute | solution.py:396
  183.9 33.2 %collective-permute-start.4 = (bf16[144,3456]{1,0:T(8,128)(2,1)}, bf16[144,3456]{1,0:T(8,128)(2,1)}, u32[]{:S(2)}, u32[]{:S(2)}) collective-permute-start(bf16[144,3456]{1,0:T(8,128)(2,1)} %refs_3_), channel_id=1, source_target_pairs={{0,8},{4,12},{8,0},{12,4},{16,24},{20,28},{24,16},{28,20},{1,9},{5... | collective-permute-start | bytes 2985992 | tf_op jit(solution)/shard_map/ppermute | solution.py:396
  184.1 32.3 %collective-permute-start.7 = (bf16[144,1152]{1,0:T(8,128)(2,1)S(1)}, bf16[144,1152]{1,0:T(8,128)(2,1)S(1)}, u32[]{:S(2)}, u32[]{:S(2)}) collective-permute-start(bf16[144,1152]{1,0:T(8,128)(2,1)S(1)} %copy-done.26), channel_id=1, source_target_pairs={{0,16},{4,20},{8,24},{12,28},{16,0},{20,4},{24,8},{28,12},{1,17},{... | collective-permute-start | bytes 995336 | tf_op jit(solution)/shard_map/ppermute | solution.py:396
  185.1 32.1 %collective-permute-start.6 = (bf16[144,1152]{1,0:T(8,128)(2,1)S(1)}, bf16[144,1152]{1,0:T(8,128)(2,1)}, u32[]{:S(2)}, u32[]{:S(2)}) collective-permute-start(bf16[144,1152]{1,0:T(8,128)(2,1)S(1)} %copy-done.26), channel_id=1, source_target_pairs={{0,8},{4,12},{8,0},{12,4},{16,24},{20,28},{24,16},{28,20},{1,9},{5... | collective-permute-start | bytes 995336 | tf_op jit(solution)/shard_map/ppermute | solution.py:396
  262.2 41.1 %collective-permute-start.9 = (bf16[144,4608]{1,0:T(8,128)(2,1)}, bf16[144,4608]{1,0:T(8,128)(2,1)}, u32[]{:S(2)}, u32[]{:S(2)}) collective-permute-start(bf16[144,4608]{1,0:T(8,128)(2,1)} %refs_0_.4), channel_id=1, source_target_pairs={{0,16},{4,20},{8,24},{12,28},{16,0},{20,4},{24,8},{28,12},{1,17},{... | collective-permute-start | bytes 3981320 | tf_op jit(solution)/shard_map/ppermute | solution.py:396
  263.0 40.3 %collective-permute-start.8 = (bf16[144,4608]{1,0:T(8,128)(2,1)}, bf16[144,4608]{1,0:T(8,128)(2,1)}, u32[]{:S(2)}, u32[]{:S(2)}) collective-permute-start(bf16[144,4608]{1,0:T(8,128)(2,1)} %refs_0_.4), channel_id=1, source_target_pairs={{0,8},{4,12},{8,0},{12,4},{16,24},{20,28},{24,16},{28,20},{1,9},{5... | collective-permute-start | bytes 3981320 | tf_op jit(solution)/shard_map/ppermute | solution.py:396
  300.2 76.3 %collective-permute-start.11 = (bf16[576,1152]{1,0:T(8,128)(2,1)S(1)}, bf16[576,1152]{1,0:T(8,128)(2,1)}, u32[]{:S(2)}, u32[]{:S(2)}) collective-permute-start(bf16[576,1152]{1,0:T(8,128)(2,1)S(1)} %copy-done.19), channel_id=1, source_target_pairs={{0,16},{4,20},{8,24},{12,28},{16,0},{20,4},{24,8},{28,12},{1,17},{... | collective-permute-start | bytes 3981320 | tf_op jit(solution)/shard_map/ppermute | solution.py:396
  301.1 75.4 %collective-permute-start.10 = (bf16[576,1152]{1,0:T(8,128)(2,1)S(1)}, bf16[576,1152]{1,0:T(8,128)(2,1)}, u32[]{:S(2)}, u32[]{:S(2)}) collective-permute-start(bf16[576,1152]{1,0:T(8,128)(2,1)S(1)} %copy-done.19), channel_id=1, source_target_pairs={{0,8},{4,12},{8,0},{12,4},{16,24},{20,28},{24,16},{28,20},{1,9},{5... | collective-permute-start | bytes 3981320 | tf_op jit(solution)/shard_map/ppermute | solution.py:396
  489.6 54.5 %copy-start.2 = (f32[256,1152]{1,0:T(8,128)S(1)}, f32[256,1152]{1,0:T(8,128)}, u32[]{:S(2)}) copy-start(f32[256,1152]{1,0:T(8,128)} %get-tuple-element.165.refs_8_) | copy-start | bytes 3538948
  489.6 54.5 %copy-start.9 = (f32[256,2304]{1,0:T(8,128)S(1)}, f32[256,2304]{1,0:T(8,128)}, u32[]{:S(2)}) copy-start(f32[256,2304]{1,0:T(8,128)} %fusion.21) | copy-start | bytes 7077892
  541.2 62.1 %collective-permute-start.13 = (bf16[9,2,64,1152]{3,2,1,0:T(8,128)(2,1)}, bf16[9,2,64,1152]{3,2,1,0:T(8,128)(2,1)}, u32[]{:S(2)}, u32[]{:S(2)}) collective-permute-start(bf16[9,2,64,1152]{3,2,1,0:T(8,128)(2,1)} %get-tuple-element.212), channel_id=1, source_target_pairs={{0,16},{4,20},{8,24},{12,28},{16,0},{20,4},{24,8},{28,12},{1,17},{... | collective-permute-start | bytes 7962632 | tf_op jit(solution)/shard_map/ppermute | solution.py:1789
  542.2 75.0 %collective-permute-start.12 = (bf16[9,2,80,1152]{3,2,1,0:T(8,128)(2,1)}, bf16[9,2,80,1152]{3,2,1,0:T(8,128)(2,1)}, u32[]{:S(2)}, u32[]{:S(2)}) collective-permute-start(bf16[9,2,80,1152]{3,2,1,0:T(8,128)(2,1)} %get-tuple-element.211), channel_id=1, source_target_pairs={{0,8},{4,12},{8,0},{12,4},{16,24},{20,28},{24,16},{28,20},{1,9},{5... | collective-permute-start | bytes 9953288 | tf_op jit(solution)/shard_map/ppermute | solution.py:1789
  577.6 23.0 %copy-start.43 = (f32[1,1152]{1,0:T(1,128)S(1)}, f32[1,1152]{1,0:T(1,128)}, u32[]{:S(2)}) copy-start(f32[1,1152]{1,0:T(1,128)} %get-tuple-element.240) | copy-start | bytes 13828
  577.6 23.1 %copy-start.33 = (f32[1,4608]{1,0:T(1,128)S(1)}, f32[1,4608]{1,0:T(1,128)}, u32[]{:S(2)}) copy-start(f32[1,4608]{1,0:T(1,128)} %get-tuple-element.239) | copy-start | bytes 55300
  577.6 23.2 %copy-start.46 = (f32[1,1152]{1,0:T(1,128)S(1)}, f32[1,1152]{1,0:T(1,128)}, u32[]{:S(2)}) copy-start(f32[1,1152]{1,0:T(1,128)} %get-tuple-element.235) | copy-start | bytes 13828
  577.6 23.3 %copy-start.45 = (f32[1,1152]{1,0:T(1,128)S(1)}, f32[1,1152]{1,0:T(1,128)}, u32[]{:S(2)}) copy-start(f32[1,1152]{1,0:T(1,128)} %get-tuple-element.237) | copy-start | bytes 13828
  577.6 23.4 %copy-start.34 = (f32[1,4608]{1,0:T(1,128)S(1)}, f32[1,4608]{1,0:T(1,128)}, u32[]{:S(2)}) copy-start(f32[1,4608]{1,0:T(1,128)} %get-tuple-element.236) | copy-start | bytes 55300
  600.2 89.1 %collective-permute-start.14 = (bf16[3,2,80,1152]{3,2,1,0:T(8,128)(2,1)}, bf16[3,2,80,1152]{3,2,1,0:T(8,128)(2,1)}, u32[]{:S(2)}, u32[]{:S(2)}) collective-permute-start(bf16[3,2,80,1152]{3,2,1,0:T(8,128)(2,1)} %get-tuple-element.223), channel_id=1, source_target_pairs={{0,8},{4,12},{8,0},{12,4},{16,24},{20,28},{24,16},{28,20},{1,9},{5... | collective-permute-start | bytes 3317768 | tf_op jit(solution)/shard_map/ppermute | solution.py:1789
  600.3 89.0 %collective-permute-start.15 = (bf16[3,2,64,1152]{3,2,1,0:T(8,128)(2,1)}, bf16[3,2,64,1152]{3,2,1,0:T(8,128)(2,1)}, u32[]{:S(2)}, u32[]{:S(2)}) collective-permute-start(bf16[3,2,64,1152]{3,2,1,0:T(8,128)(2,1)} %get-tuple-element.224), channel_id=1, source_target_pairs={{0,16},{4,20},{8,24},{12,28},{16,0},{20,4},{24,8},{28,12},{1,17},{... | collective-permute-start | bytes 2654216 | tf_op jit(solution)/shard_map/ppermute | solution.py:1789
  642.9 46.4 %copy-start.4 = (bf16[256,1152]{1,0:T(8,128)(2,1)S(1)}, bf16[256,1152]{1,0:T(8,128)(2,1)}, u32[]{:S(2)}) copy-start(bf16[256,1152]{1,0:T(8,128)(2,1)} %param.24) | copy-start | bytes 1769476
  642.9 46.4 %copy-start.7 = (f32[256,2304]{1,0:T(8,128)S(1)}, f32[256,2304]{1,0:T(8,128)}, u32[]{:S(2)}) copy-start(f32[256,2304]{1,0:T(8,128)} %fusion.19) | copy-start | bytes 7077892
  642.9 46.4 %copy-start.32 = (f32[256]{0:T(256)S(1)}, f32[256]{0:T(256)}, u32[]{:S(2)}) copy-start(f32[256]{0:T(256)} %copy-done.31) | copy-start | bytes 3076
  (34 other events, 142.4 us)
Sparse Core Ops, SparseCore 0:
  187.6 56.4 all-reduce.12
